TPU v7x, 32 devices: a whole 2x2x4 slice. The times are simulated.
32 devices in a mesh: dp: 8 (over z, core), expert: 4 (over y, x).
Axes of the slice: x: 2, y: 2, z: 4, core: 2. Of those that a mesh axis runs over, the one named last changes fastest.
Arguments:
- tokens: bfloat16 [1024, 2048], P(('dp', 'expert')), may hold values from -6 to 6
- routes: int32 [1024, 6], P(('dp', 'expert')), may hold values from 0 to 31, all different within a row; in each aligned block of 32 rows (0 to 31, 32 to 63, ...) at most 7 rows name the same one
- weights_fwd: float32 [1024, 6], P(('dp', 'expert')), may hold values from 0.05 to 0.45
- cotangent: bfloat16 [1024, 2048], P(('dp', 'expert')), may hold values from -6 to 6
- routes_back: int32 [1024, 6], P(('dp', 'expert')), may hold values from 0 to 31, all different within a row; in each aligned block of 32 rows (0 to 31, 32 to 63, ...) at most 7 rows name the same one
- weights_back: float32 [1024, 6], P(('dp', 'expert')), may hold values from 0.05 to 0.45
- saved_gate: bfloat16 [8, 4, 32, 7, 704], P('dp', None, 'expert'), may hold values from -5 to 5
- saved_up: bfloat16 [8, 4, 32, 7, 704], P('dp', None, 'expert'), may hold values from -5 to 5
- w_gate: bfloat16 [32, 2048, 704], P('expert'), may hold values from -0.125 to 0.125
- w_up: bfloat16 [32, 2048, 704], P('expert'), may hold values from -0.125 to 0.125
- w_down: bfloat16 [32, 704, 2048], P('expert'), may hold values from -0.21875 to 0.21875
Outputs:
- mixed: bfloat16 [1024, 2048], P(('dp', 'expert'))
- input_grad: bfloat16 [1024, 2048], P(('dp', 'expert'))
- weight_grad: float32 [1024, 6], P(('dp', 'expert'))
Inputs may be any that keep to these rules, and one draw needn't show every extreme that they name: `routes`: each row names 6 different experts; among the 32 rows of one device no expert is named more than 7 times, and in every draw some expert is named exactly 7 times by one device. `routes_back`: each row names 6 different experts; among the 32 rows of one device no expert is named more than 7 times, and in every draw some expert is named exactly 7 times by one device.
All inputs are finite; a program needn't handle non-finite values.
Results may differ from a plain program's by a relative error of at most 0.0057.
Values may be sent and summed in bfloat16 or wider, within the bound.
No kernel may reach another device: no remote copies, remote signals or barrier semaphores. Data moves between devices by JAX's collectives and lax.ppermute only.
A program may use at most 128 MiB of HBM per device.

v0:
```python
import jax
import jax.numpy as jnp
from jax import lax
from jax.sharding import PartitionSpec as P

EXPERTS = 32
CAP = 7


def slot_places(ids):
    count, top = ids.shape
    flat = ids.reshape(-1)
    onehot = (flat[:, None] == jnp.arange(EXPERTS, dtype=jnp.int32)[None, :]).astype(jnp.int32)
    before = jnp.cumsum(onehot, axis=0) - onehot
    slot = jnp.sum(before * onehot, axis=1)
    return (flat * CAP + slot).reshape(count, top)


def dispatch(places, rows, owners):
    count, top = places.shape
    table = places.reshape(-1)[None, :] == jnp.arange(EXPERTS * CAP, dtype=jnp.int32)[:, None]
    table = jnp.sum(table.reshape(EXPERTS * CAP, count, top).astype(jnp.int32), axis=2).astype(
        jnp.bfloat16
    )
    packed = jnp.dot(table, rows, preferred_element_type=jnp.float32).astype(jnp.bfloat16)
    return packed.reshape(owners, EXPERTS // owners, CAP, rows.shape[1])


def combine(flat_out, places, factors):
    picked = flat_out[places].astype(jnp.float32)
    return jnp.sum(factors[:, :, None] * picked, axis=1)


def expert_forward(received, w_gate, w_up, w_down):
    gate = jnp.einsum("secd,edf->secf", received, w_gate, preferred_element_type=jnp.float32)
    up = jnp.einsum("secd,edf->secf", received, w_up, preferred_element_type=jnp.float32)
    hidden = (jax.nn.silu(gate) * up).astype(jnp.bfloat16)
    return jnp.einsum("secf,efd->secd", hidden, w_down, preferred_element_type=jnp.float32).astype(
        jnp.bfloat16
    )


def expert_backward(received, saved_gate, saved_up, w_gate, w_up, w_down):
    act_in = saved_gate.astype(jnp.float32)
    up_in = saved_up.astype(jnp.float32)
    grad_hidden = jnp.einsum("secd,efd->secf", received, w_down, preferred_element_type=jnp.float32)
    sig = jax.nn.sigmoid(act_in)
    silu_in = act_in * sig
    score = jnp.sum(silu_in * up_in * grad_hidden, axis=3)
    grad_gate = (grad_hidden * up_in * sig * (1.0 + act_in * (1.0 - sig))).astype(jnp.bfloat16)
    grad_up = (grad_hidden * silu_in).astype(jnp.bfloat16)
    result = jnp.einsum("secf,edf->secd", grad_gate, w_gate, preferred_element_type=jnp.float32)
    result = result + jnp.einsum(
        "secf,edf->secd", grad_up, w_up, preferred_element_type=jnp.float32
    )
    return (result.astype(jnp.bfloat16), score)


def body(
    tokens,
    routes,
    weights_fwd,
    cotangent,
    routes_back,
    weights_back,
    saved_gate,
    saved_up,
    w_gate,
    w_up,
    w_down,
):
    owners = lax.axis_size("expert")
    places = slot_places(routes)
    places_back = slot_places(routes_back)
    buffer = dispatch(places, tokens, owners)
    grad_buffer = dispatch(places_back, cotangent, owners)
    kept_gate = saved_gate[0]
    kept_up = saved_up[0]
    outputs = expert_forward(
        lax.all_to_all(buffer, "expert", split_axis=0, concat_axis=0, tiled=True),
        w_gate,
        w_up,
        w_down,
    )
    returned = lax.all_to_all(outputs, "expert", split_axis=0, concat_axis=0, tiled=True)
    grad_in = lax.all_to_all(grad_buffer, "expert", split_axis=0, concat_axis=0, tiled=True)
    expert_grad, score = expert_backward(grad_in, kept_gate, kept_up, w_gate, w_up, w_down)
    grad_back, score_back = (
        lax.all_to_all(
            expert_grad.astype(jnp.float32), "expert", split_axis=0, concat_axis=0, tiled=True
        ).astype(expert_grad.dtype),
        lax.all_to_all(score, "expert", split_axis=0, concat_axis=0, tiled=True),
    )
    width = tokens.shape[1]
    mixed = combine(returned.reshape(EXPERTS * CAP, width), places, weights_fwd).astype(
        jnp.bfloat16
    )
    input_grad = combine(grad_back.reshape(EXPERTS * CAP, width), places_back, weights_back).astype(
        jnp.bfloat16
    )
    weight_grad = score_back.reshape(EXPERTS * CAP)[places_back]
    return (mixed, input_grad, weight_grad)


def solution(mesh):
    return jax.shard_map(
        body,
        mesh=mesh,
        in_specs=(
            P(("dp", "expert"), None),
            P(("dp", "expert"), None),
            P(("dp", "expert"), None),
            P(("dp", "expert"), None),
            P(("dp", "expert"), None),
            P(("dp", "expert"), None),
            P("dp", None, "expert", None, None),
            P("dp", None, "expert", None, None),
            P("expert", None, None),
            P("expert", None, None),
            P("expert", None, None),
        ),
        out_specs=(P(("dp", "expert"), None), P(("dp", "expert"), None), P(("dp", "expert"), None)),
        check_vma=False,
    )
```

profile of v0, /device:TPU:0, one launch (start us, length us, event | category | flops | bytes accessed | tf_op | source)
XLA Modules:
  0.0 133.5 jit_solution(15173159059820518315)
XLA Ops:
  3.6 1.5 %copy.102 = bf16[4,8,7,2048]{3,1,2,0:T(8,128)(2,1)} copy(bf16[4,8,7,2048]{3,2,1,0:T(8,128)(2,1)S(1)} %reshape.97) | data formatting | bytes 1835008 | tf_op jit(solution)/shard_map/reshape | solution.py:26
  5.1 5.2 %all-to-all-start.2 = ((bf16[4,8,7,2048]{3,1,2,0:T(8,128)(2,1)}), bf16[4,8,7,2048]{3,1,2,0:T(8,128)(2,1)S(1)}, u32[]{:S(2)}, u32[]{:S(2)}) async-start(bf16[4,8,7,2048]{3,1,2,0:T(8,128)(2,1)} %copy.102), calls=%async_computation.2 | async-start | bytes 1835008 | tf_op jit(solution)/shard_map/all_to_all | solution.py:86
  12.4 1.3 convolution_convert_fusion.1
  14.1 1.6 %copy.91 = bf16[4,8,7,2048]{3,1,2,0:T(8,128)(2,1)} copy(bf16[4,8,7,2048]{3,2,1,0:T(8,128)(2,1)S(1)} %reshape.93) | data formatting | bytes 1835008 | tf_op jit(solution)/shard_map/reshape | solution.py:26
  15.6 6.9 %all-to-all-done.2 = bf16[4,8,7,2048]{3,1,2,0:T(8,128)(2,1)S(1)} async-done(((bf16[4,8,7,2048]{3,1,2,0:T(8,128)(2,1)}), bf16[4,8,7,2048]{3,1,2,0:T(8,128)(2,1)S(1)}, u32[]{:S(2)}, u32[]{:S(2)}) %all-to-all-start.2) | async-done | bytes 917536 | tf_op jit(solution)/shard_map/all_to_all | solution.py:86
  22.5 3.7 %all-to-all-start = ((bf16[4,8,7,2048]{3,1,2,0:T(8,128)(2,1)}), bf16[4,8,7,2048]{3,1,2,0:T(8,128)(2,1)S(1)}, u32[]{:S(2)}, u32[]{:S(2)}) async-start(bf16[4,8,7,2048]{3,1,2,0:T(8,128)(2,1)} %copy.91), calls=%async_computation | async-start | bytes 1835008 | tf_op jit(solution)/shard_map/all_to_all | solution.py:80
  26.2 12.1 %fusion.52 = (f32[4,8,7]{2,0,1:T(4,128)S(1)}, f32[4,8,7,704]{3,2,0,1:T(8,128)S(1)}) fusion(bf16[1,4,8,7,704]{4,2,3,1,0:T(8,128)(2,1)} %param.18, bf16[1,4,8,7,704]{4,2,3,1,0:T(8,128)(2,1)} %param.17, bf16[8,704,2048]{2,1,0:T(8,128)(2,1)} %param.21, bf16[4,8,7,2048]{3,1,2,0:T(8,128)(2,1)S(1)} %all-to-all-done.2), kind=kOutput, calls=%fused_computation.42 | convolution fusion | flops 647341824 | bytes 25248640 | tf_op jit(solution)/shard_map/secd,efd->secf/dot_general | solution.py:46
  38.3 9.6 %fusion = f32[8,4,7,2048]{3,2,1,0:T(8,128)S(1)} fusion(bf16[8,2048,704]{1,2,0:T(8,128)(2,1)} %param.20, f32[4,8,7,704]{3,2,0,1:T(8,128)S(1)} %get-tuple-element.20, bf16[1,4,8,7,704]{4,2,3,1,0:T(8,128)(2,1)S(1)} %copy-done.2), kind=kOutput, calls=%fused_computation.3 | convolution fusion | flops 647026688 | bytes 25849856 | tf_op jit(solution)/shard_map/secf,edf->secd/dot_general | solution.py:53
  47.9 11.4 %fusion.21 = bf16[4,8,7,2048]{3,2,0,1:T(8,128)(2,1)S(1)} fusion(f32[8,4,7,2048]{3,2,1,0:T(8,128)S(1)} %fusion, bf16[8,2048,704]{1,2,0:T(8,128)(2,1)} %param.19, f32[4,8,7,704]{3,2,0,1:T(8,128)S(1)} %get-tuple-element.20, bf16[1,4,8,7,704]{4,2,3,1,0:T(8,128)(2,1)S(1)} %copy-done.2, bf16[1,4,8,7,704]{4,2,3,1,0:T(8,128)(2,1)S(1)} %copy-done.3), kind=kOutput, calls=%fused_computation.18 | convolution fusion | flops 648732672 | bytes 27082752 | tf_op jit(solution)/shard_map/secf,edf->secd/dot_general | solution.py:52
  60.0 4.0 %all-to-all-start.4 = ((f32[4,8,7]{2,1,0:T(8,128)}), f32[4,8,7]{2,1,0:T(8,128)S(1)}, u32[]{:S(2)}, u32[]{:S(2)}) async-start(f32[4,8,7]{2,1,0:T(8,128)} %copy.108), calls=%async_computation.4 | async-start | bytes 32768 | tf_op jit(solution)/shard_map/all_to_all | solution.py:92
  63.9 11.6 %fusion.33 = f32[4,8,7,704]{3,2,0,1:T(8,128)S(1)} fusion(bf16[8,2048,704]{1,2,0:T(8,128)(2,1)} %param.19, bf16[4,8,7,2048]{3,1,2,0:T(8,128)(2,1)S(1)} %all-to-all-done), kind=kOutput, calls=%fused_computation.26 | convolution fusion | flops 645922816 | bytes 24616960 | tf_op jit(solution)/shard_map/secd,edf->secf/dot_general | solution.py:35
  75.5 11.7 %fusion.42 = bf16[4,8,7,704]{3,2,0,1:T(8,128)(2,1)S(1)} fusion(bf16[8,2048,704]{1,2,0:T(8,128)(2,1)} %param.20, bf16[4,8,7,2048]{3,1,2,0:T(8,128)(2,1)S(1)} %all-to-all-done, f32[4,8,7,704]{3,2,0,1:T(8,128)S(1)} %fusion.33), kind=kOutput, calls=%fused_computation.29 | convolution fusion | flops 646868992 | bytes 24932352 | tf_op jit(solution)/shard_map/secd,edf->secf/dot_general | solution.py:36
  87.3 1.6 %copy.106 = bf16[4,8,7,2048]{3,1,2,0:T(8,128)(2,1)} copy(bf16[4,8,7,2048]{3,2,0,1:T(8,128)(2,1)S(1)} %fusion.21) | data formatting | bytes 1835008 | tf_op jit(solution)/shard_map/convert_element_type | solution.py:90
  88.8 4.2 %all-to-all-start.3 = ((bf16[4,8,7,2048]{3,1,2,0:T(8,128)(2,1)}), bf16[4,8,7,2048]{3,1,2,0:T(8,128)(2,1)S(1)}, u32[]{:S(2)}, u32[]{:S(2)}) async-start(bf16[4,8,7,2048]{3,1,2,0:T(8,128)(2,1)} %copy.106), calls=%async_computation.3 | async-start | bytes 1835008 | tf_op jit(solution)/shard_map/all_to_all | solution.py:89
  93.0 11.2 %fusion.27 = bf16[4,8,7,2048]{3,2,0,1:T(8,128)(2,1)S(1)} fusion(bf16[4,8,7,704]{3,2,0,1:T(8,128)(2,1)S(1)} %fusion.42, bf16[8,704,2048]{2,1,0:T(8,128)(2,1)} %param.21), kind=kOutput, calls=%fused_computation.22 | convolution fusion | flops 646381568 | bytes 24301568 | tf_op jit(solution)/shard_map/secf,efd->secd/dot_general | solution.py:38
  104.2 1.5 %copy.94 = bf16[4,8,7,2048]{3,1,2,0:T(8,128)(2,1)} copy(bf16[4,8,7,2048]{3,2,0,1:T(8,128)(2,1)S(1)} %fusion.27) | data formatting | bytes 1835008 | tf_op jit(solution)/shard_map/convert_element_type | solution.py:38
  105.7 4.5 %all-to-all-start.1 = ((bf16[4,8,7,2048]{3,1,2,0:T(8,128)(2,1)}), bf16[4,8,7,2048]{3,1,2,0:T(8,128)(2,1)}, u32[]{:S(2)}, u32[]{:S(2)}) async-start(bf16[4,8,7,2048]{3,1,2,0:T(8,128)(2,1)} %copy.94), calls=%async_computation.1 | async-start | bytes 1835008 | tf_op jit(solution)/shard_map/all_to_all | solution.py:85
  110.8 1.6 %gather_fusion.2 = f32[192]{0:T(256)S(1)} fusion(f32[224]{0:T(256)S(1)} %reshape.99, s32[1024]{0:T(1024)S(1)} %pad_clamp_fusion), kind=kCustom, calls=%fused_computation.2 | custom fusion | bytes 2304 | tf_op jit(solution)/shard_map/gather | solution.py:101
  115.4 5.5 %all-to-all-done.1 = bf16[4,8,7,2048]{3,1,2,0:T(8,128)(2,1)} async-done(((bf16[4,8,7,2048]{3,1,2,0:T(8,128)(2,1)}), bf16[4,8,7,2048]{3,1,2,0:T(8,128)(2,1)}, u32[]{:S(2)}, u32[]{:S(2)}) %all-to-all-start.1) | async-done | bytes 917536 | tf_op jit(solution)/shard_map/all_to_all | solution.py:85
  120.9 2.7 %copy.95 = bf16[4,8,7,2048]{3,2,1,0:T(8,128)(2,1)} copy(bf16[4,8,7,2048]{3,1,2,0:T(8,128)(2,1)} %all-to-all-done.1) | data formatting | bytes 1835008 | tf_op jit(solution)/shard_map/all_to_all | solution.py:85
  123.6 1.5 %reshape.94 = bf16[224,2048]{1,0:T(8,128)(2,1)S(1)} reshape(bf16[4,8,7,2048]{3,2,1,0:T(8,128)(2,1)} %copy.95) | data formatting | bytes 1835008 | tf_op jit(solution)/shard_map/reshape | solution.py:95
  125.1 2.1 %gather_fusion = bf16[192,2048]{1,0:T(8,128)(2,1)} fusion(bf16[224,2048]{1,0:T(8,128)(2,1)S(1)} %reshape.94, s32[1024]{0:T(1024)S(1)} %pad_clamp_fusion.1), kind=kCustom, calls=%fused_computation | custom fusion | bytes 1573632 | tf_op jit(solution)/shard_map/gather | solution.py:30
  127.1 2.5 %reshape.134 = f32[32,6,2048]{2,1,0:T(8,128)} reshape(bf16[192,2048]{1,0:T(8,128)(2,1)} %gather_fusion) | data formatting | bytes 2359296 | tf_op jit(solution)/shard_map/convert_element_type | solution.py:30
  129.6 3.8 %multiply_reduce_fusion = (bf16[32,2048]{1,0:T(8,128)(2,1)}, bf16[32,2048]{1,0:T(8,128)(2,1)}) fusion(f32[32,6,2048]{2,1,0:T(8,128)S(1)} %reshape.135, f32[32,6]{1,0:T(8,128)S(1)} %copy.96, f32[32,6,2048]{2,1,0:T(8,128)} %reshape.134, f32[32,6]{1,0:T(8,128)S(1)} %copy.85), kind=kLoop, calls=%fused_computation.23 | loop fusion | flops 1441792 | bytes 3409408 | tf_op jit(solution)/shard_map/reduce_sum | solution.py:31
  (60 shorter events, 9.4 us)
Async XLA Ops:
  0.6 2.2 %copy-start = (bf16[32,2048]{1,0:T(8,128)(2,1)S(1)}, bf16[32,2048]{1,0:T(8,128)(2,1)}, u32[]{:S(2)}) copy-start(bf16[32,2048]{1,0:T(8,128)(2,1)} %param.14) | copy-start | bytes 393220
  0.6 37.7 %copy-start.2 = (bf16[1,4,8,7,704]{4,2,3,1,0:T(8,128)(2,1)S(1)}, bf16[1,4,8,7,704]{4,2,3,1,0:T(8,128)(2,1)}, u32[]{:S(2)}) copy-start(bf16[1,4,8,7,704]{4,2,3,1,0:T(8,128)(2,1)} %param.17) | copy-start | bytes 946180
  5.1 17.4 %all-to-all-start.2 = ((bf16[4,8,7,2048]{3,1,2,0:T(8,128)(2,1)}), bf16[4,8,7,2048]{3,1,2,0:T(8,128)(2,1)S(1)}, u32[]{:S(2)}, u32[]{:S(2)}) async-start(bf16[4,8,7,2048]{3,1,2,0:T(8,128)(2,1)} %copy.102), calls=%async_computation.2 | async-start | bytes 1835008 | tf_op jit(solution)/shard_map/all_to_all | solution.py:86
  22.5 37.5 %all-to-all-start = ((bf16[4,8,7,2048]{3,1,2,0:T(8,128)(2,1)}), bf16[4,8,7,2048]{3,1,2,0:T(8,128)(2,1)S(1)}, u32[]{:S(2)}, u32[]{:S(2)}) async-start(bf16[4,8,7,2048]{3,1,2,0:T(8,128)(2,1)} %copy.91), calls=%async_computation | async-start | bytes 1835008 | tf_op jit(solution)/shard_map/all_to_all | solution.py:80
  26.2 21.7 %copy-start.3 = (bf16[1,4,8,7,704]{4,2,3,1,0:T(8,128)(2,1)S(1)}, bf16[1,4,8,7,704]{4,2,3,1,0:T(8,128)(2,1)}, u32[]{:S(2)}) copy-start(bf16[1,4,8,7,704]{4,2,3,1,0:T(8,128)(2,1)} %param.18) | copy-start | bytes 946180
  60.0 28.9 %all-to-all-start.4 = ((f32[4,8,7]{2,1,0:T(8,128)}), f32[4,8,7]{2,1,0:T(8,128)S(1)}, u32[]{:S(2)}, u32[]{:S(2)}) async-start(f32[4,8,7]{2,1,0:T(8,128)} %copy.108), calls=%async_computation.4 | async-start | bytes 32768 | tf_op jit(solution)/shard_map/all_to_all | solution.py:92
  75.5 34.9 %copy-start.4 = (f32[32,6]{0,1:T(8,128)S(1)}, f32[32,6]{0,1:T(8,128)}, u32[]{:S(2)}) copy-start(f32[32,6]{0,1:T(8,128)} %param.13) | copy-start | bytes 2308
  75.5 35.0 %copy-start.5 = (f32[32,6]{0,1:T(8,128)S(1)}, f32[32,6]{0,1:T(8,128)}, u32[]{:S(2)}) copy-start(f32[32,6]{0,1:T(8,128)} %param.16) | copy-start | bytes 2308
  88.8 16.9 %all-to-all-start.3 = ((bf16[4,8,7,2048]{3,1,2,0:T(8,128)(2,1)}), bf16[4,8,7,2048]{3,1,2,0:T(8,128)(2,1)S(1)}, u32[]{:S(2)}, u32[]{:S(2)}) async-start(bf16[4,8,7,2048]{3,1,2,0:T(8,128)(2,1)} %copy.106), calls=%async_computation.3 | async-start | bytes 1835008 | tf_op jit(solution)/shard_map/all_to_all | solution.py:89
  105.7 15.1 %all-to-all-start.1 = ((bf16[4,8,7,2048]{3,1,2,0:T(8,128)(2,1)}), bf16[4,8,7,2048]{3,1,2,0:T(8,128)(2,1)}, u32[]{:S(2)}, u32[]{:S(2)}) async-start(bf16[4,8,7,2048]{3,1,2,0:T(8,128)(2,1)} %copy.94), calls=%async_computation.1 | async-start | bytes 1835008 | tf_op jit(solution)/shard_map/all_to_all | solution.py:85
  110.6 22.8 %copy-start.1 = (bf16[32,2048]{1,0:T(8,128)(2,1)S(1)}, bf16[32,2048]{1,0:T(8,128)(2,1)}, u32[]{:S(2)}) copy-start(bf16[32,2048]{1,0:T(8,128)(2,1)} %param.14) | copy-start | bytes 393220
where the time goes:
time: 134 us; the launch traced here: 133 us
  matrix products  69.3 us (52%)
  local copies, waits for them, and re-layouts  23.7 us (18%)
  starting transfers between devices  21.5 us (16%)
  waiting for transfers between devices  12.4 us (9%)
  other arithmetic  5.58 us (4%)
    dot_general x1, matrix products, expert_backward(): jnp.einsum('secd,efd->secf', received, w_down, preferred_element_type=jnp...  12.1 us
    dot_general x1, matrix products, expert_forward(): jnp.einsum('secd,edf->secf', received, w_up, preferred_element_type=jnp.f...  11.7 us
    dot_general x1, matrix products, expert_forward(): jnp.einsum('secd,edf->secf', received, w_gate, preferred_element_type=jnp...  11.6 us
    dot_general x1, matrix products, expert_backward(): jnp.einsum('secf,edf->secd', grad_gate, w_gate, preferred_element_type=jn...  11.4 us
    dot_general x1, matrix products, expert_forward(): jnp.einsum('secf,efd->secd', hidden, w_down, preferred_element_type=jnp.f...  11.2 us
    dot_general x1, matrix products, expert_backward(): jnp.einsum('secf,edf->secd', grad_up, w_up, preferred_element_type=jnp.fl...  9.59 us
    all_to_all x1, waiting for transfers between devices, body(): lax.all_to_all(grad_buffer, 'expert', split_axis=0, concat_axis=0, tiled=...  6.9 us
    all_to_all x1, waiting for transfers between devices, body(): lax.all_to_all(outputs, 'expert', split_axis=0, concat_axis=0, tiled=True)  5.5 us
  transfers between devices with their start and end apart: 5, of which 2 were waited for; matrix products, arithmetic and copies ran while one was open for 61% of the time, Pallas kernels for 0%

commit v1 on v0

v1 whole, which is shorter than its diff:
```python
import functools
import jax
import jax.numpy as jnp
from jax import lax
from jax.experimental import pallas as pl
from jax.experimental.pallas import tpu as pltpu
from jax.sharding import PartitionSpec as P

F32 = jnp.float32
BF16 = jnp.bfloat16
LANES = 128
MIB = 1 << 20


def round_up(value, unit):
    return -(-value // unit) * unit


def dot(a, b):
    return jnp.dot(a, b, preferred_element_type=F32)


def dot_tb(a, b):
    return lax.dot_general(a, b, (((1,), (1,)), ((), ())), preferred_element_type=F32)


def dot_ta(a, b):
    return lax.dot_general(a, b, (((0,), (0,)), ((), ())), preferred_element_type=F32)


def iota(shape, dim):
    return lax.broadcasted_iota(jnp.int32, shape, dim)


def vmem():
    return pl.BlockSpec(memory_space=pltpu.VMEM)


class Plan:
    def __init__(self, tokens, routes, saved_gate, w_gate):
        self.owners = lax.axis_size("expert")
        self.groups = lax.axis_size("dp")
        self.count, self.width = tokens.shape
        self.top = routes.shape[1]
        self.local = w_gate.shape[0]
        self.hidden = w_gate.shape[2]
        self.experts = self.owners * self.local
        self.cap = saved_gate.shape[3]
        self.cap_rows = round_up(self.cap, 8)
        self.split = 2 if self.groups % 2 == 0 and self.local % 2 == 0 else 1
        self.mine = self.local // self.split
        self.meta = round_up(3 * self.experts, LANES)
        self.blocks = self.split * self.owners
        self.source_rows = self.owners * self.cap_rows
        self.expert_rows = self.split * self.source_rows
        self.rows = self.mine * self.expert_rows
        self.cols = self.blocks * self.count

    def peer(self, index, step):
        if self.owners & (self.owners - 1) == 0:
            return index ^ step
        return (index + step) % self.owners

    def over_expert(self, x, step):
        pairs = [(self.peer(i, step), i) for i in range(self.owners)]
        return lax.ppermute(x, "expert", pairs)

    def back_over_expert(self, x, step):
        pairs = [(i, self.peer(i, step)) for i in range(self.owners)]
        return lax.ppermute(x, "expert", pairs)

    def over_pair(self, x):
        return lax.ppermute(x, "dp", [(i, i ^ 1) for i in range(self.groups)])


def pack_kernel(plan, x_ref, routes_ref, factors_ref, out_ref):
    experts, top = plan.experts, plan.top
    count = plan.count
    out_ref[:, : plan.width] = x_ref[...]
    lane = iota((plan.meta, count), 0)
    chosen = jnp.zeros((plan.meta, count), F32)
    parts = jnp.zeros((plan.meta, count), F32)
    for k in range(top):
        route = routes_ref[k : k + 1, :]
        factor = factors_ref[k : k + 1, :]
        high = factor.astype(BF16).astype(F32)
        low = factor - high
        chosen = chosen + jnp.where(lane == route, 1.0, 0.0)
        parts = parts + jnp.where(lane == route + experts, high, 0.0)
        parts = parts + jnp.where(lane == route + 2 * experts, low, 0.0)
    earlier = jnp.where(iota((count, count), 0) < iota((count, count), 1), 1.0, 0.0)
    before = dot(chosen.astype(BF16), earlier.astype(BF16))
    facts = (chosen * (before + 1.0) + parts).astype(BF16)
    shape = (plan.meta, plan.meta)
    same = jnp.where(iota(shape, 0) == iota(shape, 1), 1.0, 0.0).astype(BF16)
    out_ref[:, plan.width :] = dot_ta(facts, same).astype(BF16)


def pack(plan, x, routes, factors):
    return pl.pallas_call(
        functools.partial(pack_kernel, plan),
        out_shape=jax.ShapeDtypeStruct((plan.count, plan.width + plan.meta), BF16),
        in_specs=[vmem()] * 3,
        out_specs=vmem(),
        name="pack",
    )(x, routes.T, factors.T)


def first_expert(plan):
    core = lax.rem(lax.axis_index("dp"), plan.split)
    return lax.axis_index("expert") * plan.local + core * plan.mine, core * plan.mine


def tables(plan, meta, first):
    me = lax.axis_index("expert")
    row = iota((plan.rows, plan.meta), 0)
    lane = iota((plan.rows, plan.meta), 1)
    expert = first + row // plan.expert_rows
    pick_slot = jnp.where(lane == expert, 1.0, 0.0).astype(BF16)
    pick_part = jnp.where(
        (lane == expert + plan.experts) | (lane == expert + 2 * plan.experts), 1.0, 0.0
    ).astype(BF16)
    slot = dot_tb(pick_slot, meta)
    part = dot_tb(pick_part, meta)
    shape = (plan.rows, plan.cols)
    row = iota(shape, 0)
    col = iota(shape, 1)
    block = col // plan.count
    source = plan.peer(me, block % plan.owners)
    place = row % plan.expert_rows
    want = (row % plan.cap_rows + 1).astype(F32)
    same = (place // plan.cap_rows) == (block // plan.owners) * plan.owners + source
    hit = same & (slot == want)
    factor = jnp.sum(jnp.where(hit, part, 0.0), axis=1, keepdims=True)
    return jnp.where(hit, 1.0, 0.0).astype(BF16), factor


def weight_copies(plan, offset, arrays, slots, sems):
    copies = []
    for e in range(plan.mine):
        copies.append(
            [
                pltpu.make_async_copy(array.at[offset + e], slot.at[e], sems.at[e, i])
                for i, (array, slot) in enumerate(zip(arrays, slots))
            ]
        )
    for group in copies:
        for copy in group:
            copy.start()
    return copies


def forward_kernel(plan, *refs):
    blocks = refs[: plan.blocks]
    w_gate, w_up, w_down = refs[plan.blocks : plan.blocks + 3]
    outs = refs[plan.blocks + 3 : 2 * plan.blocks + 3]
    gate_s, up_s, down_s, x_s, y_s, sems = refs[2 * plan.blocks + 3 :]
    first, offset = first_expert(plan)
    copies = weight_copies(
        plan, offset, (w_gate, w_up, w_down), (gate_s, up_s, down_s), sems
    )
    meta = jnp.concatenate([b[:, plan.width :] for b in blocks], axis=0)
    rows = jnp.concatenate([b[:, : plan.width] for b in blocks], axis=0)
    table, factor = tables(plan, meta, first)
    x_s[...] = dot(table, rows).astype(BF16)
    n = plan.expert_rows
    for e in range(plan.mine):
        x = x_s[e * n : (e + 1) * n, :]
        copies[e][0].wait()
        gate = dot_tb(x, gate_s[e])
        copies[e][1].wait()
        up = dot_tb(x, up_s[e])
        hidden = (gate / (1.0 + jnp.exp(-gate)) * up).astype(BF16)
        copies[e][2].wait()
        out = dot(hidden, down_s[e])
        y_s[e * n : (e + 1) * n, :] = (out * factor[e * n : (e + 1) * n]).astype(BF16)
    mixed = dot_ta(table, y_s[...]).astype(BF16)
    for i, out in enumerate(outs):
        out[...] = mixed[i * plan.count : (i + 1) * plan.count, :]


def backward_kernel(plan, *refs):
    blocks = refs[: plan.blocks]
    refs = refs[plan.blocks :]
    saved = refs[: plan.split]
    w_gate, w_up, w_down = refs[plan.split : plan.split + 3]
    refs = refs[plan.split + 3 :]
    outs = refs[: plan.blocks]
    gate_s, up_s, down_s, x_s, y_s, score_s, sems = refs[plan.blocks :]
    first, offset = first_expert(plan)
    copies = weight_copies(
        plan, offset, (w_down, w_gate, w_up), (down_s, gate_s, up_s), sems
    )
    meta = jnp.concatenate([b[:, plan.width :] for b in blocks], axis=0)
    rows = jnp.concatenate([b[:, : plan.width] for b in blocks], axis=0)
    table, factor = tables(plan, meta, first)
    x_s[...] = dot(table, rows).astype(BF16)
    n = plan.expert_rows
    lane = iota((n, plan.meta), 1)
    for e in range(plan.mine):
        x = x_s[e * n : (e + 1) * n, :]
        act = jnp.concatenate([s[0, e] for s in saved], axis=0).astype(F32)
        up = jnp.concatenate([s[1, e] for s in saved], axis=0).astype(F32)
        sig = 1.0 / (1.0 + jnp.exp(-act))
        silu = act * sig
        copies[e][0].wait()
        grad = dot_tb(x, down_s[e])
        score = jnp.sum(silu * up * grad, axis=1, keepdims=True)
        grad_gate = (grad * up * sig * (1.0 + act * (1.0 - sig))).astype(BF16)
        grad_up = (grad * silu).astype(BF16)
        copies[e][1].wait()
        result = dot(grad_gate, gate_s[e])
        copies[e][2].wait()
        result = result + dot(grad_up, up_s[e])
        y_s[e * n : (e + 1) * n, :] = (result * factor[e * n : (e + 1) * n]).astype(BF16)
        expert = first + e
        high = score.astype(BF16).astype(F32)
        middle = (score - high).astype(BF16).astype(F32)
        low = score - high - middle
        spread = jnp.where(lane == expert, high, 0.0)
        spread = jnp.where(lane == expert + plan.experts, middle, spread)
        spread = jnp.where(lane == expert + 2 * plan.experts, low, spread)
        score_s[e * n : (e + 1) * n, :] = spread.astype(BF16)
    grads = dot_ta(table, y_s[...]).astype(BF16)
    scores = dot_ta(table, score_s[...]).astype(BF16)
    for i, out in enumerate(outs):
        out[:, : plan.width] = grads[i * plan.count : (i + 1) * plan.count, :]
        out[:, plan.width :] = scores[i * plan.count : (i + 1) * plan.count, :]


def expert_call(plan, kernel, name, width, vmem_inputs, weights, extra_scratch):
    any_spec = pl.BlockSpec(memory_space=pl.ANY)
    shape = (plan.mine, plan.hidden, plan.width)
    matrices = 3 * plan.mine
    return pl.pallas_call(
        functools.partial(kernel, plan),
        out_shape=[jax.ShapeDtypeStruct((plan.count, width), BF16)] * plan.blocks,
        in_specs=[vmem()] * len(vmem_inputs) + [any_spec] * 3,
        out_specs=[vmem()] * plan.blocks,
        scratch_shapes=[
            pltpu.VMEM(shape, BF16),
            pltpu.VMEM(shape, BF16),
            pltpu.VMEM(shape, BF16),
            pltpu.VMEM((plan.rows, plan.width), BF16),
            pltpu.VMEM((plan.rows, plan.width), BF16),
        ]
        + extra_scratch
        + [pltpu.SemaphoreType.DMA((plan.mine, 3))],
        compiler_params=pltpu.CompilerParams(vmem_limit_bytes=46 * MIB),
        cost_estimate=pl.CostEstimate(
            flops=2 * matrices * plan.expert_rows * plan.width * plan.hidden,
            bytes_accessed=2 * matrices * plan.width * plan.hidden,
            transcendentals=0,
        ),
        name=name,
    )(*vmem_inputs, *weights)


def gather(plan, block):
    own = [block] + [plan.over_expert(block, d) for d in range(1, plan.owners)]
    if plan.split == 1:
        return own
    return own + [plan.over_pair(b) for b in own]


def scatter(plan, parts):
    own = parts[: plan.owners]
    if plan.split > 1:
        other = [plan.over_pair(p) for p in parts[plan.owners :]]
        own = [
            (a.astype(F32) + b.astype(F32)).astype(BF16) if d else a
            for d, (a, b) in enumerate(zip(own, other))
        ]
    arrived = [own[0]]
    if plan.split > 1:
        arrived.append(other[0])
    return arrived + [plan.back_over_expert(own[d], d) for d in range(1, plan.owners)]


def sum_kernel(count, *refs):
    total = refs[0][...].astype(F32)
    for ref in refs[1:count]:
        total = total + ref[...].astype(F32)
    refs[count][...] = total.astype(BF16)


def sum_parts(plan, parts):
    return pl.pallas_call(
        functools.partial(sum_kernel, len(parts)),
        out_shape=jax.ShapeDtypeStruct((plan.count, plan.width), BF16),
        in_specs=[vmem()] * len(parts),
        out_specs=vmem(),
        name="sum_forward",
    )(*parts)


def sum_back_kernel(plan, count, *refs):
    routes, out, score = refs[count:]
    total = refs[0][...].astype(F32)
    for ref in refs[1:count]:
        total = total + ref[...].astype(F32)
    out[...] = total[:, : plan.width].astype(BF16)
    spread = total[:, plan.width :]
    lane = iota(spread.shape, 1)
    lane = jnp.where(lane < 3 * plan.experts, lane % plan.experts, -1)
    for k in range(plan.top):
        hit = lane == routes[:, k : k + 1]
        score[:, k : k + 1] = jnp.sum(jnp.where(hit, spread, 0.0), axis=1, keepdims=True)


def sum_back(plan, parts, routes):
    return pl.pallas_call(
        functools.partial(sum_back_kernel, plan, len(parts)),
        out_shape=(
            jax.ShapeDtypeStruct((plan.count, plan.width), BF16),
            jax.ShapeDtypeStruct((plan.count, plan.top), F32),
        ),
        in_specs=[vmem()] * (len(parts) + 1),
        out_specs=(vmem(), vmem()),
        name="sum_backward",
    )(*parts, routes)


def split_saved(plan, saved_gate, saved_up):
    both = jnp.stack([saved_gate[0], saved_up[0]])

    def part(core):
        piece = lax.dynamic_slice_in_dim(both, core * plan.mine, plan.mine, axis=2)
        piece = jnp.swapaxes(piece, 1, 2)
        short = plan.cap_rows - plan.cap
        return jnp.pad(piece, ((0, 0),) * 3 + ((0, short), (0, 0))).reshape(
            2, plan.mine, plan.source_rows, plan.hidden
        )

    if plan.split == 1:
        return [part(0)]
    core = lax.axis_index("dp") % 2
    return [part(core), plan.over_pair(part(1 - core))]


def body(
    tokens,
    routes,
    weights_fwd,
    cotangent,
    routes_back,
    weights_back,
    saved_gate,
    saved_up,
    w_gate,
    w_up,
    w_down,
):
    plan = Plan(tokens, routes, saved_gate, w_gate)
    weights = (jnp.swapaxes(w_gate, 1, 2), jnp.swapaxes(w_up, 1, 2), w_down)
    blocks = gather(plan, pack(plan, tokens, routes, weights_fwd))
    blocks_back = gather(plan, pack(plan, cotangent, routes_back, weights_back))
    saved = split_saved(plan, saved_gate, saved_up)
    parts = expert_call(plan, forward_kernel, "forward", plan.width, blocks, weights, [])
    mixed = sum_parts(plan, scatter(plan, parts))
    parts_back = expert_call(
        plan,
        backward_kernel,
        "backward",
        plan.width + plan.meta,
        [*blocks_back, *saved],
        weights,
        [pltpu.VMEM((plan.rows, plan.meta), BF16)],
    )
    input_grad, weight_grad = sum_back(plan, scatter(plan, parts_back), routes_back)
    return (mixed, input_grad, weight_grad)


def solution(mesh):
    spec = P(("dp", "expert"), None)
    saved = P("dp", None, "expert", None, None)
    weight = P("expert", None, None)
    return jax.shard_map(
        body,
        mesh=mesh,
        in_specs=(spec,) * 6 + (saved,) * 2 + (weight,) * 3,
        out_specs=(spec,) * 3,
        check_vma=False,
    )
```

time: 134 us -> 80.3 us (0.60)
  matrix products: 69.3 us -> 0 us
  Pallas kernels: 0 us -> 36.7 us
  local copies, waits for them, and re-layouts: 23.7 us -> 7.67 us
  other arithmetic: 5.58 us -> 0.21 us
  waiting for transfers between devices: 12.4 us -> 16.5 us
  starting transfers between devices: 21.5 us -> 17.9 us
    dot_general x8 -> x0, matrix products: 69.3 us -> none  [the longest x1 12.1 us: expert_backward(): jnp.einsum('secd,efd->secf', received, w_down, preferred_element_type=jnp...]
    pallas_call x0 -> x6, Pallas kernels: none -> 36.7 us  [the longest x2 28.8 us: expert_call(): pl.pallas_call(functools.partial(kernel, plan), out_shape=[jax.ShapeDtype...]
    all_to_all x5 -> x0, starting transfers between devices: 21.5 us -> none  [the longest x1 5.16 us: body(): lax.all_to_all(grad_buffer, 'expert', split_axis=0, concat_axis=0, tiled=...]
    ppermute x0 -> x29, starting transfers between devices: none -> 17.9 us  [the longest x6 8.02 us: over_expert(): return lax.ppermute(x, 'expert', pairs)]
    ppermute x0 -> x29, waiting for transfers between devices: none -> 16.5 us  [the longest x6 11 us: back_over_expert(): return lax.ppermute(x, 'expert', pairs)]
    all_to_all x5 -> x0, waiting for transfers between devices: 12.4 us -> none  [the longest x1 6.9 us: body(): lax.all_to_all(grad_buffer, 'expert', split_axis=0, concat_axis=0, tiled=...]
    convert_element_type x5 -> x0, local copies, waits for them, and re-layouts: 6.3 us -> none  [the longest x2 2.7 us: combine(): picked = flat_out[places].astype(jnp.float32)]
    reshape x7 -> x2, local copies, waits for them, and re-layouts: 5.55 us -> 0.14 us  [part(): jnp.pad(piece, ((0, 0),) * 3 + ((0, short), (0, 0)))]
  transfers between devices with their start and end apart: 5 -> 29, of which waited for: 2 -> 7; matrix products, arithmetic and copies ran while one was open for 61% -> 4% of each run, Pallas kernels for 0% -> 41%
where the time goes in v1:
time: 80.3 us; the launch traced here: 79.9 us
  Pallas kernels  36.7 us (46%)
  starting transfers between devices  17.9 us (22%)
  waiting for transfers between devices  16.5 us (21%)
  local copies, waits for them, and re-layouts  7.67 us (10%)
  between operations  0.92 us (1%)
    pallas_call x2, Pallas kernels, expert_call(): pl.pallas_call(functools.partial(kernel, plan), out_shape=[jax.ShapeDtype...  28.8 us
    ppermute x6, waiting for transfers between devices, back_over_expert(): return lax.ppermute(x, 'expert', pairs)  11 us
    ppermute x6, starting transfers between devices, over_expert(): return lax.ppermute(x, 'expert', pairs)  8.02 us
    unnamed x31, local copies, waits for them, and re-layouts  6.16 us
    ppermute x6, starting transfers between devices, back_over_expert(): return lax.ppermute(x, 'expert', pairs)  5.67 us
    ppermute x6, waiting for transfers between devices, over_expert(): return lax.ppermute(x, 'expert', pairs)  5.02 us
    ppermute x17, starting transfers between devices, over_pair(): return lax.ppermute(x, 'dp', [(i, i ^ 1) for i in range(self.groups)])  4.23 us
    pallas_call x2, Pallas kernels, pack(): pl.pallas_call(functools.partial(pack_kernel, plan), out_shape=jax.ShapeD...  3.82 us
  transfers between devices with their start and end apart: 29, of which 7 were waited for; matrix products, arithmetic and copies ran while one was open for 4% of the time, Pallas kernels for 41%

profile of v1, /device:TPU:0, one launch (start us, length us, event | category | flops | bytes accessed | tf_op | source)
XLA Modules:
  0.0 79.9 jit_solution(11422399582361645625)
XLA Ops:
  0.6 1.9 %pack.3.refs_0_ = bf16[32,2176]{1,0:T(8,128)(2,1)} custom-call(bf16[32,2048]{1,0:T(8,128)(2,1)} %x_ref.3, s32[6,32]{1,0:T(8,128)} %bitcast.18, f32[6,32]{1,0:T(8,128)} %bitcast.19), custom_call_target="tpu_custom_call" | custom-call | tf_op jit(solution)/shard_map/pack/pallas_call | solution.py:100
  2.5 2.9 %collective-permute-start.14 = (bf16[32,2176]{1,0:T(8,128)(2,1)}, bf16[32,2176]{1,0:T(8,128)(2,1)S(1)}, u32[]{:S(2)}, u32[]{:S(2)}) collective-permute-start(bf16[32,2176]{1,0:T(8,128)(2,1)} %pack.3.refs_0_), channel_id=1, source_target_pairs={{1,0},{0,1},{3,2},{2,3},{5,4},{4,5},{7,6},{6,7},{9,8},{8,9},{11,10... | collective-permute-start | bytes 417800 | tf_op jit(solution)/shard_map/ppermute | solution.py:66
  5.5 1.5 %collective-permute-start.15 = (bf16[32,2176]{1,0:T(8,128)(2,1)}, bf16[32,2176]{1,0:T(8,128)(2,1)S(1)}, u32[]{:S(2)}, u32[]{:S(2)}) collective-permute-start(bf16[32,2176]{1,0:T(8,128)(2,1)} %pack.3.refs_0_), channel_id=1, source_target_pairs={{2,0},{3,1},{0,2},{1,3},{6,4},{7,5},{4,6},{5,7},{10,8},{11,9},{8,1... | collective-permute-start | bytes 417800 | tf_op jit(solution)/shard_map/ppermute | solution.py:66
  7.0 1.9 %pack.2.refs_0_ = bf16[32,2176]{1,0:T(8,128)(2,1)} custom-call(bf16[32,2048]{1,0:T(8,128)(2,1)} %x_ref.2, s32[6,32]{1,0:T(8,128)} %bitcast.20, f32[6,32]{1,0:T(8,128)} %bitcast.21), custom_call_target="tpu_custom_call" | custom-call | tf_op jit(solution)/shard_map/pack/pallas_call | solution.py:100
  8.9 2.0 %collective-permute-start = (bf16[32,2176]{1,0:T(8,128)(2,1)}, bf16[32,2176]{1,0:T(8,128)(2,1)S(1)}, u32[]{:S(2)}, u32[]{:S(2)}) collective-permute-start(bf16[32,2176]{1,0:T(8,128)(2,1)} %pack.2.refs_0_), channel_id=1, source_target_pairs={{1,0},{0,1},{3,2},{2,3},{5,4},{4,5},{7,6},{6,7},{9,8},{8,9},{11,10... | collective-permute-start | bytes 417800 | tf_op jit(solution)/shard_map/ppermute | solution.py:66
  10.9 1.5 %collective-permute-start.1 = (bf16[32,2176]{1,0:T(8,128)(2,1)}, bf16[32,2176]{1,0:T(8,128)(2,1)S(1)}, u32[]{:S(2)}, u32[]{:S(2)}) collective-permute-start(bf16[32,2176]{1,0:T(8,128)(2,1)} %pack.2.refs_0_), channel_id=1, source_target_pairs={{2,0},{3,1},{0,2},{1,3},{6,4},{7,5},{4,6},{5,7},{10,8},{11,9},{8,1... | collective-permute-start | bytes 417800 | tf_op jit(solution)/shard_map/ppermute | solution.py:66
  12.4 1.0 %constant_dynamic-update-slice_fusion.1 = bf16[2,4,8,7,704]{4,2,3,1,0:T(8,128)(2,1)S(1)} fusion(bf16[1,4,8,7,704]{4,2,3,1,0:T(8,128)(2,1)} %param.17), kind=kLoop, calls=%fused_computation.11 | loop fusion | bytes 659456
  13.4 1.0 %constant_dynamic-update-slice_fusion = bf16[2,4,8,7,704]{4,2,3,1,0:T(8,128)(2,1)S(1)} fusion(bf16[2,4,8,7,704]{4,2,3,1,0:T(8,128)(2,1)S(1)} %constant_dynamic-update-slice_fusion.1, bf16[1,4,8,7,704]{4,2,3,1,0:T(8,128)(2,1)} %param.18), kind=kLoop, calls=%fused_computation.10 | loop fusion | bytes 659456 | tf_op jit(solution)/shard_map/stack | solution.py:325
  15.7 2.6 %collective-permute-done.1.refs_2_ = bf16[32,2176]{1,0:T(8,128)(2,1)S(1)} collective-permute-done((bf16[32,2176]{1,0:T(8,128)(2,1)}, bf16[32,2176]{1,0:T(8,128)(2,1)S(1)}, u32[]{:S(2)}, u32[]{:S(2)}) %collective-permute-start.1) | collective-permute-done | bytes 139296 | tf_op jit(solution)/shard_map/ppermute | solution.py:66
  18.3 2.4 %collective-permute-done.2.refs_3_ = bf16[32,2176]{1,0:T(8,128)(2,1)S(1)} collective-permute-done((bf16[32,2176]{1,0:T(8,128)(2,1)}, bf16[32,2176]{1,0:T(8,128)(2,1)S(1)}, u32[]{:S(2)}, u32[]{:S(2)}) %collective-permute-start.2) | collective-permute-done | bytes 139296 | tf_op jit(solution)/shard_map/ppermute | solution.py:66
  22.2 0.9 %copy-done.1 = bf16[32,2176]{1,0:T(8,128)(2,1)S(1)} copy-done((bf16[32,2176]{1,0:T(8,128)(2,1)S(1)}, bf16[32,2176]{1,0:T(8,128)(2,1)}, u32[]{:S(2)}) %copy-start.1) | copy-done | bytes 139288
  23.1 14.5 %forward.1 = (bf16[32,2048]{1,0:T(8,128)(2,1)S(1)}, bf16[32,2048]{1,0:T(8,128)(2,1)S(1)}, bf16[32,2048]{1,0:T(8,128)(2,1)S(1)}, bf16[32,2048]{1,0:T(8,128)(2,1)S...) custom-call(bf16[32,2176]{1,0:T(8,128)(2,1)S(1)} %copy-done.1, ...), custom_call_target="tpu_custom_call" | custom-call | flops 2214592512 | bytes 34603008 | tf_op jit(solution)/shard_map/forward/pallas_call | solution.py:235
  38.7 14.2 %backward.1 = (bf16[32,2176]{1,0:T(8,128)(2,1)S(1)}, bf16[32,2176]{1,0:T(8,128)(2,1)S(1)}, bf16[32,2176]{1,0:T(8,128)(2,1)S(1)}, bf16[32,2176]{1,0:T(8,128)(2,1)...) custom-call(bf16[32,2176]{1,0:T(8,128)(2,1)S(1)} %copy-done, ...), custom_call_target="tpu_custom_call" | custom-call | flops 2214592512 | bytes 34603008 | tf_op jit(solution)/shard_map/backward/pallas_call | solution.py:235
  55.4 0.8 %collective-permute-start.13 = (bf16[32,2048]{1,0:T(8,128)(2,1)S(1)}, bf16[32,2048]{1,0:T(8,128)(2,1)S(1)}, u32[]{:S(2)}, u32[]{:S(2)}) collective-permute-start(bf16[32,2048]{1,0:T(8,128)(2,1)S(1)} %add_convert_fusion.3), channel_id=1, source_target_pairs={{0,3},{1,2},{2,1},{3,0},{4,7},{5,6},{6,5},{7,4},{8,11},{9,10},{10,... | collective-permute-start | bytes 393224 | tf_op jit(solution)/shard_map/ppermute | solution.py:70
  56.3 1.3 %collective-permute-start.11 = (bf16[32,2048]{1,0:T(8,128)(2,1)S(1)}, bf16[32,2048]{1,0:T(8,128)(2,1)S(1)}, u32[]{:S(2)}, u32[]{:S(2)}) collective-permute-start(bf16[32,2048]{1,0:T(8,128)(2,1)S(1)} %add_convert_fusion.4), channel_id=1, source_target_pairs={{0,2},{1,3},{2,0},{3,1},{4,6},{5,7},{6,4},{7,5},{8,10},{9,11},{10,... | collective-permute-start | bytes 393224 | tf_op jit(solution)/shard_map/ppermute | solution.py:70
  57.7 1.8 %collective-permute-start.28 = (bf16[32,2176]{1,0:T(8,128)(2,1)S(1)}, bf16[32,2176]{1,0:T(8,128)(2,1)S(1)}, u32[]{:S(2)}, u32[]{:S(2)}) collective-permute-start(bf16[32,2176]{1,0:T(8,128)(2,1)S(1)} %add_convert_fusion), channel_id=1, source_target_pairs={{0,3},{1,2},{2,1},{3,0},{4,7},{5,6},{6,5},{7,4},{8,11},{9,10},{10,... | collective-permute-start | bytes 417800 | tf_op jit(solution)/shard_map/ppermute | solution.py:70
  59.5 1.2 %collective-permute-start.26 = (bf16[32,2176]{1,0:T(8,128)(2,1)S(1)}, bf16[32,2176]{1,0:T(8,128)(2,1)S(1)}, u32[]{:S(2)}, u32[]{:S(2)}) collective-permute-start(bf16[32,2176]{1,0:T(8,128)(2,1)S(1)} %add_convert_fusion.1), channel_id=1, source_target_pairs={{0,2},{1,3},{2,0},{3,1},{4,6},{5,7},{6,4},{7,5},{8,10},{9,11},{10,... | collective-permute-start | bytes 417800 | tf_op jit(solution)/shard_map/ppermute | solution.py:70
  60.7 2.2 %collective-permute-done.13.refs_4_ = bf16[32,2048]{1,0:T(8,128)(2,1)S(1)} collective-permute-done((bf16[32,2048]{1,0:T(8,128)(2,1)S(1)}, bf16[32,2048]{1,0:T(8,128)(2,1)S(1)}, u32[]{:S(2)}, u32[]{:S(2)}) %collective-permute-start.13) | collective-permute-done | bytes 131104 | tf_op jit(solution)/shard_map/ppermute | solution.py:70
  62.9 5.0 %collective-permute-done.11.refs_3_ = bf16[32,2048]{1,0:T(8,128)(2,1)S(1)} collective-permute-done((bf16[32,2048]{1,0:T(8,128)(2,1)S(1)}, bf16[32,2048]{1,0:T(8,128)(2,1)S(1)}, u32[]{:S(2)}, u32[]{:S(2)}) %collective-permute-start.11) | collective-permute-done | bytes 131104 | tf_op jit(solution)/shard_map/ppermute | solution.py:70
  68.4 0.7 copy.16.refs_5_
  69.1 3.9 %collective-permute-done.9.refs_2_ = bf16[32,2048]{1,0:T(8,128)(2,1)S(1)} collective-permute-done((bf16[32,2048]{1,0:T(8,128)(2,1)S(1)}, bf16[32,2048]{1,0:T(8,128)(2,1)S(1)}, u32[]{:S(2)}, u32[]{:S(2)}) %collective-permute-start.9) | collective-permute-done | bytes 131104 | tf_op jit(solution)/shard_map/ppermute | solution.py:70
  73.6 1.9 %sum_forward.1 = bf16[32,2048]{1,0:T(8,128)(2,1)} custom-call(bf16[32,2048]{1,0:T(8,128)(2,1)} %copy-done.3, bf16[32,2048]{1,0:T(8,128)(2,1)} %copy-done.8, bf16[32,2048]{1,0:T(8,128)(2,1)} %copy-done.11, bf16[32,2048]{1,0:T(8,128)(2,1)} %copy-done.10, bf16[32,2048]{1,0:T(8,128)(2,1)} %copy-done.9), custom_call_target="tpu_custom_call" | custom-call | tf_op jit(solution)/shard_map/sum_forward/pallas_call | solution.py:288
  76.3 2.2 %sum_backward.1 = (bf16[32,2048]{1,0:T(8,128)(2,1)}, f32[32,6]{1,0:T(8,128)}) custom-call(bf16[32,2176]{1,0:T(8,128)(2,1)} %copy-done.2, bf16[32,2176]{1,0:T(8,128)(2,1)} %copy-done.4, bf16[32,2176]{1,0:T(8,128)(2,1)} %copy-done.7, bf16[32,2176]{1,0:T(8,128)(2,1)} %copy-done.6, bf16[32,2176]{1,0:T(8,128)(2,1)} %copy-done.5, s32[32,6]{1,0:T(8,128)} %copy.16.refs_5_), custom_call_target="tpu_custom_call" | custom-call | tf_op jit(solution)/shard_map/sum_backward/pallas_call | solution.py:312
  78.5 1.4 %copy.17 = f32[32,6]{0,1:T(8,128)} copy(f32[32,6]{1,0:T(8,128)} %get-tuple-element.41) | data formatting | bytes 1536
  (81 shorter events, 8.3 us)
Async XLA Ops:
  2.5 11.9 %collective-permute-start.14 = (bf16[32,2176]{1,0:T(8,128)(2,1)}, bf16[32,2176]{1,0:T(8,128)(2,1)S(1)}, u32[]{:S(2)}, u32[]{:S(2)}) collective-permute-start(bf16[32,2176]{1,0:T(8,128)(2,1)} %pack.3.refs_0_), channel_id=1, source_target_pairs={{1,0},{0,1},{3,2},{2,3},{5,4},{4,5},{7,6},{6,7},{9,8},{8,9},{11,10... | collective-permute-start | bytes 417800 | tf_op jit(solution)/shard_map/ppermute | solution.py:66
  5.5 9.6 %collective-permute-start.15 = (bf16[32,2176]{1,0:T(8,128)(2,1)}, bf16[32,2176]{1,0:T(8,128)(2,1)S(1)}, u32[]{:S(2)}, u32[]{:S(2)}) collective-permute-start(bf16[32,2176]{1,0:T(8,128)(2,1)} %pack.3.refs_0_), channel_id=1, source_target_pairs={{2,0},{3,1},{0,2},{1,3},{6,4},{7,5},{4,6},{5,7},{10,8},{11,9},{8,1... | collective-permute-start | bytes 417800 | tf_op jit(solution)/shard_map/ppermute | solution.py:66
  7.0 8.1 %collective-permute-start.16 = (bf16[32,2176]{1,0:T(8,128)(2,1)}, bf16[32,2176]{1,0:T(8,128)(2,1)S(1)}, u32[]{:S(2)}, u32[]{:S(2)}) collective-permute-start(bf16[32,2176]{1,0:T(8,128)(2,1)} %pack.3.refs_0_), channel_id=1, source_target_pairs={{3,0},{2,1},{1,2},{0,3},{7,4},{6,5},{5,6},{4,7},{11,8},{10,9},{9,1... | collective-permute-start | bytes 417800 | tf_op jit(solution)/shard_map/ppermute | solution.py:66
  8.9 6.7 %collective-permute-start = (bf16[32,2176]{1,0:T(8,128)(2,1)}, bf16[32,2176]{1,0:T(8,128)(2,1)S(1)}, u32[]{:S(2)}, u32[]{:S(2)}) collective-permute-start(bf16[32,2176]{1,0:T(8,128)(2,1)} %pack.2.refs_0_), channel_id=1, source_target_pairs={{1,0},{0,1},{3,2},{2,3},{5,4},{4,5},{7,6},{6,7},{9,8},{8,9},{11,10... | collective-permute-start | bytes 417800 | tf_op jit(solution)/shard_map/ppermute | solution.py:66
  10.9 7.4 %collective-permute-start.1 = (bf16[32,2176]{1,0:T(8,128)(2,1)}, bf16[32,2176]{1,0:T(8,128)(2,1)S(1)}, u32[]{:S(2)}, u32[]{:S(2)}) collective-permute-start(bf16[32,2176]{1,0:T(8,128)(2,1)} %pack.2.refs_0_), channel_id=1, source_target_pairs={{2,0},{3,1},{0,2},{1,3},{6,4},{7,5},{4,6},{5,7},{10,8},{11,9},{8,1... | collective-permute-start | bytes 417800 | tf_op jit(solution)/shard_map/ppermute | solution.py:66
  14.4 6.2 %collective-permute-start.2 = (bf16[32,2176]{1,0:T(8,128)(2,1)}, bf16[32,2176]{1,0:T(8,128)(2,1)S(1)}, u32[]{:S(2)}, u32[]{:S(2)}) collective-permute-start(bf16[32,2176]{1,0:T(8,128)(2,1)} %pack.2.refs_0_), channel_id=1, source_target_pairs={{3,0},{2,1},{1,2},{0,3},{7,4},{6,5},{5,6},{4,7},{11,8},{10,9},{9,1... | collective-permute-start | bytes 417800 | tf_op jit(solution)/shard_map/ppermute | solution.py:66
  15.0 23.7 %collective-permute-start.21 = (bf16[2,4,32,704]{3,2,1,0:T(8,128)(2,1)S(1)}, bf16[2,4,32,704]{3,2,1,0:T(8,128)(2,1)S(1)}, u32[]{:S(2)}, u32[]{:S(2)}) collective-permute-start(bf16[2,4,32,704]{3,2,1,0:T(8,128)(2,1)S(1)} %pad_bitcast_fusion), channel_id=1, source_target_pairs={{0,4},{4,0},{8,12},{12,8},{16,20},{20,16},{24,28},{28,24},{1,5},{5... | collective-permute-start | bytes 1081352 | tf_op jit(solution)/shard_map/ppermute | solution.py:73
  15.1 5.7 %collective-permute-start.3 = (bf16[32,2176]{1,0:T(8,128)(2,1)}, bf16[32,2176]{1,0:T(8,128)(2,1)S(1)}, u32[]{:S(2)}, u32[]{:S(2)}) collective-permute-start(bf16[32,2176]{1,0:T(8,128)(2,1)} %pack.2.refs_0_), channel_id=1, source_target_pairs={{0,4},{4,0},{8,12},{12,8},{16,20},{20,16},{24,28},{28,24},{1,5},{5... | collective-permute-start | bytes 417800 | tf_op jit(solution)/shard_map/ppermute | solution.py:73
  15.7 5.7 %collective-permute-start.4 = (bf16[32,2176]{1,0:T(8,128)(2,1)S(1)}, bf16[32,2176]{1,0:T(8,128)(2,1)S(1)}, u32[]{:S(2)}, u32[]{:S(2)}) collective-permute-start(bf16[32,2176]{1,0:T(8,128)(2,1)S(1)} %collective-permute-done.refs_1_), channel_id=1, source_target_pairs={{0,4},{4,0},{8,12},{12,8},{16,20},{20,16},{24,28},{28,24},{1,5},{5... | collective-permute-start | bytes 417800 | tf_op jit(solution)/shard_map/ppermute | solution.py:73
  20.8 16.8 %collective-permute-start.17 = (bf16[32,2176]{1,0:T(8,128)(2,1)}, bf16[32,2176]{1,0:T(8,128)(2,1)S(1)}, u32[]{:S(2)}, u32[]{:S(2)}) collective-permute-start(bf16[32,2176]{1,0:T(8,128)(2,1)} %pack.3.refs_0_), channel_id=1, source_target_pairs={{0,4},{4,0},{8,12},{12,8},{16,20},{20,16},{24,28},{28,24},{1,5},{5... | collective-permute-start | bytes 417800 | tf_op jit(solution)/shard_map/ppermute | solution.py:73
  21.4 16.7 %collective-permute-start.18 = (bf16[32,2176]{1,0:T(8,128)(2,1)S(1)}, bf16[32,2176]{1,0:T(8,128)(2,1)S(1)}, u32[]{:S(2)}, u32[]{:S(2)}) collective-permute-start(bf16[32,2176]{1,0:T(8,128)(2,1)S(1)} %collective-permute-done.14.refs_1_), channel_id=1, source_target_pairs={{0,4},{4,0},{8,12},{12,8},{16,20},{20,16},{24,28},{28,24},{1,5},{5... | collective-permute-start | bytes 417800 | tf_op jit(solution)/shard_map/ppermute | solution.py:73
  21.5 16.7 %collective-permute-start.19 = (bf16[32,2176]{1,0:T(8,128)(2,1)S(1)}, bf16[32,2176]{1,0:T(8,128)(2,1)S(1)}, u32[]{:S(2)}, u32[]{:S(2)}) collective-permute-start(bf16[32,2176]{1,0:T(8,128)(2,1)S(1)} %collective-permute-done.15.refs_2_), channel_id=1, source_target_pairs={{0,4},{4,0},{8,12},{12,8},{16,20},{20,16},{24,28},{28,24},{1,5},{5... | collective-permute-start | bytes 417800 | tf_op jit(solution)/shard_map/ppermute | solution.py:73
  22.0 16.6 %collective-permute-start.20 = (bf16[32,2176]{1,0:T(8,128)(2,1)S(1)}, bf16[32,2176]{1,0:T(8,128)(2,1)S(1)}, u32[]{:S(2)}, u32[]{:S(2)}) collective-permute-start(bf16[32,2176]{1,0:T(8,128)(2,1)S(1)} %collective-permute-done.16.refs_3_), channel_id=1, source_target_pairs={{0,4},{4,0},{8,12},{12,8},{16,20},{20,16},{24,28},{28,24},{1,5},{5... | collective-permute-start | bytes 417800 | tf_op jit(solution)/shard_map/ppermute | solution.py:73
  37.6 16.4 %collective-permute-start.12 = (bf16[32,2048]{1,0:T(8,128)(2,1)S(1)}, bf16[32,2048]{1,0:T(8,128)(2,1)S(1)}, u32[]{:S(2)}, u32[]{:S(2)}) collective-permute-start(bf16[32,2048]{1,0:T(8,128)(2,1)S(1)} %get-tuple-element.28), channel_id=1, source_target_pairs={{0,4},{4,0},{8,12},{12,8},{16,20},{20,16},{24,28},{28,24},{1,5},{5... | collective-permute-start | bytes 393224 | tf_op jit(solution)/shard_map/ppermute | solution.py:73
  38.1 16.1 %collective-permute-start.10 = (bf16[32,2048]{1,0:T(8,128)(2,1)S(1)}, bf16[32,2048]{1,0:T(8,128)(2,1)S(1)}, u32[]{:S(2)}, u32[]{:S(2)}) collective-permute-start(bf16[32,2048]{1,0:T(8,128)(2,1)S(1)} %get-tuple-element.26), channel_id=1, source_target_pairs={{0,4},{4,0},{8,12},{12,8},{16,20},{20,16},{24,28},{28,24},{1,5},{5... | collective-permute-start | bytes 393224 | tf_op jit(solution)/shard_map/ppermute | solution.py:73
  38.2 19.4 %collective-permute-start.8 = (bf16[32,2048]{1,0:T(8,128)(2,1)S(1)}, bf16[32,2048]{1,0:T(8,128)(2,1)S(1)}, u32[]{:S(2)}, u32[]{:S(2)}) collective-permute-start(bf16[32,2048]{1,0:T(8,128)(2,1)S(1)} %get-tuple-element.24), channel_id=1, source_target_pairs={{0,4},{4,0},{8,12},{12,8},{16,20},{20,16},{24,28},{28,24},{1,5},{5... | collective-permute-start | bytes 393224 | tf_op jit(solution)/shard_map/ppermute | solution.py:73
  38.6 20.9 %collective-permute-start.7 = (bf16[32,2048]{1,0:T(8,128)(2,1)S(1)}, bf16[32,2048]{1,0:T(8,128)(2,1)S(1)}, u32[]{:S(2)}, u32[]{:S(2)}) collective-permute-start(bf16[32,2048]{1,0:T(8,128)(2,1)S(1)} %get-tuple-element.22), channel_id=1, source_target_pairs={{0,4},{4,0},{8,12},{12,8},{16,20},{20,16},{24,28},{28,24},{1,5},{5... | collective-permute-start | bytes 393224 | tf_op jit(solution)/shard_map/ppermute | solution.py:73
  55.0 20.5 %collective-permute-start.22 = (bf16[32,2176]{1,0:T(8,128)(2,1)S(1)}, bf16[32,2176]{1,0:T(8,128)(2,1)S(1)}, u32[]{:S(2)}, u32[]{:S(2)}) collective-permute-start(bf16[32,2176]{1,0:T(8,128)(2,1)S(1)} %get-tuple-element.30), channel_id=1, source_target_pairs={{0,4},{4,0},{8,12},{12,8},{16,20},{20,16},{24,28},{28,24},{1,5},{5... | collective-permute-start | bytes 417800 | tf_op jit(solution)/shard_map/ppermute | solution.py:73
  55.4 7.4 %collective-permute-start.13 = (bf16[32,2048]{1,0:T(8,128)(2,1)S(1)}, bf16[32,2048]{1,0:T(8,128)(2,1)S(1)}, u32[]{:S(2)}, u32[]{:S(2)}) collective-permute-start(bf16[32,2048]{1,0:T(8,128)(2,1)S(1)} %add_convert_fusion.3), channel_id=1, source_target_pairs={{0,3},{1,2},{2,1},{3,0},{4,7},{5,6},{6,5},{7,4},{8,11},{9,10},{10,... | collective-permute-start | bytes 393224 | tf_op jit(solution)/shard_map/ppermute | solution.py:70
  56.3 11.5 %collective-permute-start.11 = (bf16[32,2048]{1,0:T(8,128)(2,1)S(1)}, bf16[32,2048]{1,0:T(8,128)(2,1)S(1)}, u32[]{:S(2)}, u32[]{:S(2)}) collective-permute-start(bf16[32,2048]{1,0:T(8,128)(2,1)S(1)} %add_convert_fusion.4), channel_id=1, source_target_pairs={{0,2},{1,3},{2,0},{3,1},{4,6},{5,7},{6,4},{7,5},{8,10},{9,11},{10,... | collective-permute-start | bytes 393224 | tf_op jit(solution)/shard_map/ppermute | solution.py:70
  57.7 17.8 %collective-permute-start.28 = (bf16[32,2176]{1,0:T(8,128)(2,1)S(1)}, bf16[32,2176]{1,0:T(8,128)(2,1)S(1)}, u32[]{:S(2)}, u32[]{:S(2)}) collective-permute-start(bf16[32,2176]{1,0:T(8,128)(2,1)S(1)} %add_convert_fusion), channel_id=1, source_target_pairs={{0,3},{1,2},{2,1},{3,0},{4,7},{5,6},{6,5},{7,4},{8,11},{9,10},{10,... | collective-permute-start | bytes 417800 | tf_op jit(solution)/shard_map/ppermute | solution.py:70
  59.5 16.0 %collective-permute-start.26 = (bf16[32,2176]{1,0:T(8,128)(2,1)S(1)}, bf16[32,2176]{1,0:T(8,128)(2,1)S(1)}, u32[]{:S(2)}, u32[]{:S(2)}) collective-permute-start(bf16[32,2176]{1,0:T(8,128)(2,1)S(1)} %add_convert_fusion.1), channel_id=1, source_target_pairs={{0,2},{1,3},{2,0},{3,1},{4,6},{5,7},{6,4},{7,5},{8,10},{9,11},{10,... | collective-permute-start | bytes 417800 | tf_op jit(solution)/shard_map/ppermute | solution.py:70
  62.9 12.7 %collective-permute-start.24 = (bf16[32,2176]{1,0:T(8,128)(2,1)S(1)}, bf16[32,2176]{1,0:T(8,128)(2,1)S(1)}, u32[]{:S(2)}, u32[]{:S(2)}) collective-permute-start(bf16[32,2176]{1,0:T(8,128)(2,1)S(1)} %add_convert_fusion.2), channel_id=1, source_target_pairs={{0,1},{1,0},{2,3},{3,2},{4,5},{5,4},{6,7},{7,6},{8,9},{9,8},{10,11... | collective-permute-start | bytes 417800 | tf_op jit(solution)/shard_map/ppermute | solution.py:70
  67.9 5.1 %collective-permute-start.9 = (bf16[32,2048]{1,0:T(8,128)(2,1)S(1)}, bf16[32,2048]{1,0:T(8,128)(2,1)S(1)}, u32[]{:S(2)}, u32[]{:S(2)}) collective-permute-start(bf16[32,2048]{1,0:T(8,128)(2,1)S(1)} %add_convert_fusion.5), channel_id=1, source_target_pairs={{0,1},{1,0},{2,3},{3,2},{4,5},{5,4},{6,7},{7,6},{8,9},{9,8},{10,11... | collective-permute-start | bytes 393224 | tf_op jit(solution)/shard_map/ppermute | solution.py:70
  (18 other events, 104.1 us)

commit v2 on v1

--- a/solution.py
+++ b/solution.py
@@ -102,6 +102,7 @@
         out_shape=jax.ShapeDtypeStruct((plan.count, plan.width + plan.meta), BF16),
         in_specs=[vmem()] * 3,
         out_specs=vmem(),
+        compiler_params=pltpu.CompilerParams(vmem_limit_bytes=4 * MIB),
         name="pack",
     )(x, routes.T, factors.T)
 
@@ -111,8 +112,15 @@
     return lax.axis_index("expert") * plan.local + core * plan.mine, core * plan.mine
 
 
-def tables(plan, meta, first):
+def whole_block(plan, index):
+    core = lax.rem(lax.axis_index("dp"), plan.split)
+    group, step = index // plan.owners, index % plan.owners
+    return (group ^ core) * plan.owners + plan.peer(lax.axis_index("expert"), step)
+
+
+def tables(plan, meta, first, whole):
     me = lax.axis_index("expert")
+    core = lax.rem(lax.axis_index("dp"), plan.split)
     row = iota((plan.rows, plan.meta), 0)
     lane = iota((plan.rows, plan.meta), 1)
     expert = first + row // plan.expert_rows
@@ -126,10 +134,15 @@
     row = iota(shape, 0)
     col = iota(shape, 1)
     block = col // plan.count
-    source = plan.peer(me, block % plan.owners)
+    source = block % plan.owners
+    group = block // plan.owners
+    if whole:
+        group = group ^ core
+    else:
+        source = plan.peer(me, source)
     place = row % plan.expert_rows
     want = (row % plan.cap_rows + 1).astype(F32)
-    same = (place // plan.cap_rows) == (block // plan.owners) * plan.owners + source
+    same = (place // plan.cap_rows) == group * plan.owners + source
     hit = same & (slot == want)
     factor = jnp.sum(jnp.where(hit, part, 0.0), axis=1, keepdims=True)
     return jnp.where(hit, 1.0, 0.0).astype(BF16), factor
@@ -153,48 +166,45 @@
 def forward_kernel(plan, *refs):
     blocks = refs[: plan.blocks]
     w_gate, w_up, w_down = refs[plan.blocks : plan.blocks + 3]
-    outs = refs[plan.blocks + 3 : 2 * plan.blocks + 3]
-    gate_s, up_s, down_s, x_s, y_s, sems = refs[2 * plan.blocks + 3 :]
+    out_ref, gate_s, up_s, down_s, x_s, y_s, sems = refs[plan.blocks + 3 :]
     first, offset = first_expert(plan)
     copies = weight_copies(
         plan, offset, (w_gate, w_up, w_down), (gate_s, up_s, down_s), sems
     )
     meta = jnp.concatenate([b[:, plan.width :] for b in blocks], axis=0)
     rows = jnp.concatenate([b[:, : plan.width] for b in blocks], axis=0)
-    table, factor = tables(plan, meta, first)
+    table, factor = tables(plan, meta, first, False)
     x_s[...] = dot(table, rows).astype(BF16)
     n = plan.expert_rows
     for e in range(plan.mine):
         x = x_s[e * n : (e + 1) * n, :]
         copies[e][0].wait()
-        gate = dot_tb(x, gate_s[e])
+        gate = dot_tb(gate_s[e], x)
         copies[e][1].wait()
-        up = dot_tb(x, up_s[e])
+        up = dot_tb(up_s[e], x)
         hidden = (gate / (1.0 + jnp.exp(-gate)) * up).astype(BF16)
         copies[e][2].wait()
-        out = dot(hidden, down_s[e])
+        out = dot_ta(hidden, down_s[e])
         y_s[e * n : (e + 1) * n, :] = (out * factor[e * n : (e + 1) * n]).astype(BF16)
     mixed = dot_ta(table, y_s[...]).astype(BF16)
-    for i, out in enumerate(outs):
-        out[...] = mixed[i * plan.count : (i + 1) * plan.count, :]
+    for i in range(plan.blocks):
+        start = pl.multiple_of(whole_block(plan, i) * plan.count, plan.count)
+        out_ref[pl.ds(start, plan.count), :] = mixed[i * plan.count : (i + 1) * plan.count, :]
 
 
 def backward_kernel(plan, *refs):
-    blocks = refs[: plan.blocks]
-    refs = refs[plan.blocks :]
+    block_ref, refs = refs[0], refs[1:]
     saved = refs[: plan.split]
     w_gate, w_up, w_down = refs[plan.split : plan.split + 3]
     refs = refs[plan.split + 3 :]
     outs = refs[: plan.blocks]
-    gate_s, up_s, down_s, x_s, y_s, score_s, sems = refs[plan.blocks :]
+    gate_s, up_s, down_s, x_s, y_s, score_s, grad_s, sems = refs[plan.blocks :]
     first, offset = first_expert(plan)
     copies = weight_copies(
         plan, offset, (w_down, w_gate, w_up), (down_s, gate_s, up_s), sems
     )
-    meta = jnp.concatenate([b[:, plan.width :] for b in blocks], axis=0)
-    rows = jnp.concatenate([b[:, : plan.width] for b in blocks], axis=0)
-    table, factor = tables(plan, meta, first)
-    x_s[...] = dot(table, rows).astype(BF16)
+    table, factor = tables(plan, block_ref[:, plan.width :], first, True)
+    x_s[...] = dot(table, block_ref[:, : plan.width]).astype(BF16)
     n = plan.expert_rows
     lane = iota((n, plan.meta), 1)
     for e in range(plan.mine):
@@ -221,22 +231,22 @@
         spread = jnp.where(lane == expert + plan.experts, middle, spread)
         spread = jnp.where(lane == expert + 2 * plan.experts, low, spread)
         score_s[e * n : (e + 1) * n, :] = spread.astype(BF16)
-    grads = dot_ta(table, y_s[...]).astype(BF16)
-    scores = dot_ta(table, score_s[...]).astype(BF16)
+    grad_s[:, : plan.width] = dot_ta(table, y_s[...]).astype(BF16)
+    grad_s[:, plan.width :] = dot_ta(table, score_s[...]).astype(BF16)
     for i, out in enumerate(outs):
-        out[:, : plan.width] = grads[i * plan.count : (i + 1) * plan.count, :]
-        out[:, plan.width :] = scores[i * plan.count : (i + 1) * plan.count, :]
-
-
-def expert_call(plan, kernel, name, width, vmem_inputs, weights, extra_scratch):
+        start = pl.multiple_of(whole_block(plan, i) * plan.count, plan.count)
+        out[...] = grad_s[pl.ds(start, plan.count), :]
+
+
+def expert_call(plan, kernel, name, out_shape, vmem_inputs, weights, extra_scratch):
     any_spec = pl.BlockSpec(memory_space=pl.ANY)
     shape = (plan.mine, plan.hidden, plan.width)
     matrices = 3 * plan.mine
     return pl.pallas_call(
         functools.partial(kernel, plan),
-        out_shape=[jax.ShapeDtypeStruct((plan.count, width), BF16)] * plan.blocks,
+        out_shape=out_shape,
         in_specs=[vmem()] * len(vmem_inputs) + [any_spec] * 3,
-        out_specs=[vmem()] * plan.blocks,
+        out_specs=[vmem()] * len(out_shape),
         scratch_shapes=[
             pltpu.VMEM(shape, BF16),
             pltpu.VMEM(shape, BF16),
@@ -256,6 +266,14 @@
     )(*vmem_inputs, *weights)
 
 
+def pair_groups(plan):
+    size = plan.blocks
+    return [
+        list(range(start, start + size))
+        for start in range(0, plan.groups * plan.owners, size)
+    ]
+
+
 def gather(plan, block):
     own = [block] + [plan.over_expert(block, d) for d in range(1, plan.owners)]
     if plan.split == 1:
@@ -263,74 +281,46 @@
     return own + [plan.over_pair(b) for b in own]
 
 
+def gather_whole(plan, block):
+    axes = ("dp", "expert")
+    return lax.all_gather(block, axes, axis_index_groups=pair_groups(plan), tiled=True)
+
+
+def scatter_whole(plan, parts):
+    axes = ("dp", "expert")
+    groups = pair_groups(plan)
+    return lax.psum_scatter(parts, axes, axis_index_groups=groups, tiled=True)
+
+
 def scatter(plan, parts):
     own = parts[: plan.owners]
+    arrived = [own[0]]
     if plan.split > 1:
         other = [plan.over_pair(p) for p in parts[plan.owners :]]
-        own = [
-            (a.astype(F32) + b.astype(F32)).astype(BF16) if d else a
-            for d, (a, b) in enumerate(zip(own, other))
-        ]
-    arrived = [own[0]]
-    if plan.split > 1:
         arrived.append(other[0])
+        own = [(a.astype(F32) + b.astype(F32)).astype(BF16) for a, b in zip(own, other)]
     return arrived + [plan.back_over_expert(own[d], d) for d in range(1, plan.owners)]
 
 
-def sum_kernel(count, *refs):
-    total = refs[0][...].astype(F32)
-    for ref in refs[1:count]:
-        total = total + ref[...].astype(F32)
-    refs[count][...] = total.astype(BF16)
-
-
-def sum_parts(plan, parts):
-    return pl.pallas_call(
-        functools.partial(sum_kernel, len(parts)),
-        out_shape=jax.ShapeDtypeStruct((plan.count, plan.width), BF16),
-        in_specs=[vmem()] * len(parts),
-        out_specs=vmem(),
-        name="sum_forward",
-    )(*parts)
-
-
-def sum_back_kernel(plan, count, *refs):
-    routes, out, score = refs[count:]
-    total = refs[0][...].astype(F32)
-    for ref in refs[1:count]:
-        total = total + ref[...].astype(F32)
-    out[...] = total[:, : plan.width].astype(BF16)
-    spread = total[:, plan.width :]
-    lane = iota(spread.shape, 1)
-    lane = jnp.where(lane < 3 * plan.experts, lane % plan.experts, -1)
-    for k in range(plan.top):
-        hit = lane == routes[:, k : k + 1]
-        score[:, k : k + 1] = jnp.sum(jnp.where(hit, spread, 0.0), axis=1, keepdims=True)
-
-
-def sum_back(plan, parts, routes):
-    return pl.pallas_call(
-        functools.partial(sum_back_kernel, plan, len(parts)),
-        out_shape=(
-            jax.ShapeDtypeStruct((plan.count, plan.width), BF16),
-            jax.ShapeDtypeStruct((plan.count, plan.top), F32),
-        ),
-        in_specs=[vmem()] * (len(parts) + 1),
-        out_specs=(vmem(), vmem()),
-        name="sum_backward",
-    )(*parts, routes)
+def finish_back(plan, parts, routes):
+    total = sum(p.astype(F32) for p in parts)
+    spread = total[:, plan.width : plan.width + 3 * plan.experts]
+    spread = jnp.sum(spread.reshape(plan.count, 3, plan.experts), axis=1)
+    lane = iota((plan.top, plan.count, plan.experts), 2)
+    hit = lane == routes.T[:, :, None]
+    score = jnp.sum(jnp.where(hit, spread[None], 0.0), axis=2).T
+    return total[:, : plan.width].astype(BF16), score
 
 
 def split_saved(plan, saved_gate, saved_up):
-    both = jnp.stack([saved_gate[0], saved_up[0]])
+    def piece(array, core):
+        rows = lax.dynamic_slice_in_dim(array[0], core * plan.mine, plan.mine, axis=1)
+        short = plan.cap_rows - plan.cap
+        rows = jnp.pad(jnp.swapaxes(rows, 0, 1), ((0, 0), (0, 0), (0, short), (0, 0)))
+        return rows.reshape(1, plan.mine, plan.source_rows, plan.hidden)
 
     def part(core):
-        piece = lax.dynamic_slice_in_dim(both, core * plan.mine, plan.mine, axis=2)
-        piece = jnp.swapaxes(piece, 1, 2)
-        short = plan.cap_rows - plan.cap
-        return jnp.pad(piece, ((0, 0),) * 3 + ((0, short), (0, 0))).reshape(
-            2, plan.mine, plan.source_rows, plan.hidden
-        )
+        return jnp.concatenate([piece(saved_gate, core), piece(saved_up, core)])
 
     if plan.split == 1:
         return [part(0)]
@@ -353,21 +343,33 @@
 ):
     plan = Plan(tokens, routes, saved_gate, w_gate)
     weights = (jnp.swapaxes(w_gate, 1, 2), jnp.swapaxes(w_up, 1, 2), w_down)
-    blocks = gather(plan, pack(plan, tokens, routes, weights_fwd))
-    blocks_back = gather(plan, pack(plan, cotangent, routes_back, weights_back))
+    packed = pack(plan, tokens, routes, weights_fwd)
+    packed, cotangent = lax.optimization_barrier((packed, cotangent))
+    packed_back = pack(plan, cotangent, routes_back, weights_back)
+    blocks = gather(plan, packed)
+    whole_back = gather_whole(plan, packed_back)
     saved = split_saved(plan, saved_gate, saved_up)
-    parts = expert_call(plan, forward_kernel, "forward", plan.width, blocks, weights, [])
-    mixed = sum_parts(plan, scatter(plan, parts))
+    whole_shape = jax.ShapeDtypeStruct((plan.cols, plan.width), BF16)
+    (partial,) = expert_call(
+        plan, forward_kernel, "forward", [whole_shape], blocks, weights, []
+    )
+    partial, saved = lax.optimization_barrier((partial, saved))
+    mixed = scatter_whole(plan, partial)
+    block_shape = jax.ShapeDtypeStruct((plan.count, plan.width + plan.meta), BF16)
     parts_back = expert_call(
         plan,
         backward_kernel,
         "backward",
-        plan.width + plan.meta,
-        [*blocks_back, *saved],
+        [block_shape] * plan.blocks,
+        [whole_back, *saved],
         weights,
-        [pltpu.VMEM((plan.rows, plan.meta), BF16)],
-    )
-    input_grad, weight_grad = sum_back(plan, scatter(plan, parts_back), routes_back)
+        [
+            pltpu.VMEM((plan.rows, plan.meta), BF16),
+            pltpu.VMEM((plan.cols, plan.width + plan.meta), BF16),
+        ],
+    )
+    parts_back, mixed = lax.optimization_barrier((parts_back, mixed))
+    input_grad, weight_grad = finish_back(plan, scatter(plan, parts_back), routes_back)
     return (mixed, input_grad, weight_grad)
 
 

time: 80.3 us -> 102 us (1.27)
  waiting for transfers between devices: 16.5 us -> 33.8 us
  between operations: 0.92 us -> 14.3 us
  starting transfers between devices: 17.9 us -> 9.78 us
  Pallas kernels: 36.7 us -> 34.7 us
    reduce_scatter x0 -> x1, waiting for transfers between devices: none -> 21.3 us  [scatter_whole(): return lax.psum_scatter(parts, axes, axis_index_groups=groups, tiled=True)]
    ppermute x6 -> x3, waiting for transfers between devices: 11 us -> 6.25 us  [back_over_expert(): return lax.ppermute(x, 'expert', pairs)]
    ppermute x6 -> x3, starting transfers between devices: 8.02 us -> 4.16 us  [over_expert(): return lax.ppermute(x, 'expert', pairs)]
    pallas_call x2, Pallas kernels: 3.82 us -> 1.31 us  [pack(): pl.pallas_call(functools.partial(pack_kernel, plan), out_shape=jax.ShapeD...]
    ppermute x17 -> x9, starting transfers between devices: 4.23 us -> 1.85 us  [over_pair(): return lax.ppermute(x, 'dp', [(i, i ^ 1) for i in range(self.groups)])]
    ppermute x6 -> x3, starting transfers between devices: 5.67 us -> 3.68 us  [back_over_expert(): return lax.ppermute(x, 'expert', pairs)]
    transpose x1, local copies, waits for them, and re-layouts: 0.36 us -> 1.7 us  [piece(): jnp.swapaxes(rows, 0, 1)]
    pallas_call x4 -> x2, Pallas kernels: 32.9 us -> 33.4 us  [expert_call(): pl.pallas_call(functools.partial(kernel, plan), out_shape=out_shape, in_s...]
  transfers between devices with their start and end apart: 29 -> 17, of which waited for: 7 -> 9; matrix products, arithmetic and copies ran while one was open for 4% -> 2% of each run, Pallas kernels for 41% -> 33%
where the time goes in v2:
time: 102 us
  Pallas kernels  34.7 us (34%)
  waiting for transfers between devices  33.8 us (33%)
  between operations  14.3 us (14%)
  starting transfers between devices  9.78 us (10%)
  local copies, waits for them, and re-layouts  8.5 us (8%)
  other arithmetic  1.09 us (1%)
    pallas_call x2, Pallas kernels, expert_call(): pl.pallas_call(functools.partial(kernel, plan), out_shape=out_shape, in_s...  33.4 us
    reduce_scatter x1, waiting for transfers between devices, scatter_whole(): return lax.psum_scatter(parts, axes, axis_index_groups=groups, tiled=True)  21.3 us
    ppermute x3, waiting for transfers between devices, back_over_expert(): return lax.ppermute(x, 'expert', pairs)  6.25 us
    unnamed x20, local copies, waits for them, and re-layouts  5.88 us
    ppermute x3, waiting for transfers between devices, over_expert(): return lax.ppermute(x, 'expert', pairs)  4.78 us
    ppermute x3, starting transfers between devices, over_expert(): return lax.ppermute(x, 'expert', pairs)  4.16 us
    ppermute x3, starting transfers between devices, back_over_expert(): return lax.ppermute(x, 'expert', pairs)  3.68 us
  transfers between devices with their start and end apart: 17, of which 9 were waited for; matrix products, arithmetic and copies ran while one was open for 2% of the time, Pallas kernels for 33%

profile of v2, /device:TPU:0, one launch (start us, length us, event | category | flops | bytes accessed | tf_op | source)
XLA Modules:
  0.0 102.1 jit_solution(7084819714512843763)
XLA Ops:
  7.2 0.9 copy-done.1
  8.1 0.7 copy-done.5
  8.8 0.7 copy-done.6
  9.8 0.9 copy-done.2
  10.7 0.7 copy-done.3
  11.4 0.7 copy-done.7
  12.1 1.0 pack.3
  13.2 0.5 collective-permute-start.3
  13.7 3.5 %collective-permute-start.2 = (bf16[32,2176]{1,0:T(8,128)(2,1)S(1)}, bf16[32,2176]{1,0:T(8,128)(2,1)S(1)}, u32[]{:S(2)}, u32[]{:S(2)}) collective-permute-start(bf16[32,2176]{1,0:T(8,128)(2,1)S(1)} %pack.2.refs_0_), channel_id=1, source_target_pairs={{3,0},{2,1},{1,2},{0,3},{7,4},{6,5},{5,6},{4,7},{11,8},{10,9},{9,1... | collective-permute-start | bytes 417800 | tf_op jit(solution)/shard_map/ppermute | solution.py:66
  17.8 1.7 %dynamic-slice_bitcast_fusion = (bf16[4,4,7,704]{3,0,2,1:T(4,128)(2,1)S(1)}, bf16[4,4,7,704]{3,0,2,1:T(4,128)(2,1)S(1)}, bf16[4,4,7,704]{3,0,2,1:T(4,128)(2,1)S(1)}, bf16[4,4,7,704]{3,0,2,1:T(4,128)(2,1)S(1)}) fusion(bf16[1,4,8,7,704]{4,2,3,1,0:T(8,128)(2,1)} %param.18, s32[]{:T(128)S(6)} %select_n.21, s32[]{:T(128)S(6)} %select_n.20, ...), kind=kLoop, calls=%fused_computation.11 | loop fusion | bytes 1261576 | tf_op jit(solution)/shard_map/transpose | solution.py:319
  19.9 1.8 %collective-permute-done.2.refs_3_ = bf16[32,2176]{1,0:T(8,128)(2,1)S(1)} collective-permute-done((bf16[32,2176]{1,0:T(8,128)(2,1)S(1)}, bf16[32,2176]{1,0:T(8,128)(2,1)S(1)}, u32[]{:S(2)}, u32[]{:S(2)}) %collective-permute-start.2) | collective-permute-done | bytes 139296 | tf_op jit(solution)/shard_map/ppermute | solution.py:66
  21.7 2.7 %collective-permute-done.1.refs_2_ = bf16[32,2176]{1,0:T(8,128)(2,1)S(1)} collective-permute-done((bf16[32,2176]{1,0:T(8,128)(2,1)S(1)}, bf16[32,2176]{1,0:T(8,128)(2,1)S(1)}, u32[]{:S(2)}, u32[]{:S(2)}) %collective-permute-start.1) | collective-permute-done | bytes 139296 | tf_op jit(solution)/shard_map/ppermute | solution.py:66
  25.1 0.7 collective-permute-done.5.refs_6_
  26.1 19.1 %forward.1 = bf16[256,2048]{1,0:T(8,128)(2,1)} custom-call(bf16[32,2176]{1,0:T(8,128)(2,1)S(1)} %pack.2.refs_0_, bf16[32,2176]{1,0:T(8,128)(2,1)S(1)} %collective-permute-done.refs_1_, bf16[32,2176]{1,0:T(8,128)(2,1)S(1)} %collective-permute-done.1.refs_2_, bf16[32,2176]{1,0:T(8,128)(2,1)S(1)} %collective-permute-done.2.refs_3_, ...), custom_call_target="tpu_custom_call" | custom-call | flops 2214592512 | bytes 34603008 | tf_op jit(solution)/shard_map/forward/pallas_call | solution.py:245
  45.3 1.2 %copy-done = bf16[256,2176]{1,0:T(8,128)(2,1)S(1)} copy-done((bf16[256,2176]{1,0:T(8,128)(2,1)S(1)}, bf16[256,2176]{1,0:T(8,128)(2,1)}, u32[]{:S(2)}) %copy-start) | copy-done | bytes 1114136
  46.5 14.3 %backward.1 = (bf16[32,2176]{1,0:T(8,128)(2,1)S(1)}, bf16[32,2176]{1,0:T(8,128)(2,1)S(1)}, bf16[32,2176]{1,0:T(8,128)(2,1)S(1)}, bf16[32,2176]{1,0:T(8,128)(2,1)...) custom-call(bf16[256,2176]{1,0:T(8,128)(2,1)S(1)} %copy-done, ...), custom_call_target="tpu_custom_call" | custom-call | flops 2214592512 | bytes 34603008 | tf_op jit(solution)/shard_map/backward/pallas_call | solution.py:245
  60.9 21.3 %reduce-scatter.2.cloned.1.call-done = bf16[32,2048]{1,0:T(8,128)(2,1)} async-done(((bf16[256,2048]{1,0:T(8,128)(2,1)}), bf16[32,2048]{1,0:T(8,128)(2,1)}) %reduce-scatter.2.cloned.1.call-update) | async-done | bytes 131088 | tf_op jit(solution)/shard_map/reduce_scatter | solution.py:292
  83.5 1.5 %collective-permute-start.10 = (bf16[32,2176]{1,0:T(8,128)(2,1)S(1)}, bf16[32,2176]{1,0:T(8,128)(2,1)S(1)}, u32[]{:S(2)}, u32[]{:S(2)}) collective-permute-start(bf16[32,2176]{1,0:T(8,128)(2,1)S(1)} %add_convert_fusion.2), channel_id=1, source_target_pairs={{0,1},{1,0},{2,3},{3,2},{4,5},{5,4},{6,7},{7,6},{8,9},{9,8},{10,11... | collective-permute-start | bytes 417800 | tf_op jit(solution)/shard_map/ppermute | solution.py:70
  85.1 0.7 collective-permute-start.12
  85.8 1.5 %collective-permute-start.14 = (bf16[32,2176]{1,0:T(8,128)(2,1)S(1)}, bf16[32,2176]{1,0:T(8,128)(2,1)S(1)}, u32[]{:S(2)}, u32[]{:S(2)}) collective-permute-start(bf16[32,2176]{1,0:T(8,128)(2,1)S(1)} %add_convert_fusion), channel_id=1, source_target_pairs={{0,3},{1,2},{2,1},{3,0},{4,7},{5,6},{6,5},{7,4},{8,11},{9,10},{10,... | collective-permute-start | bytes 417800 | tf_op jit(solution)/shard_map/ppermute | solution.py:70
  87.3 2.4 %collective-permute-done.10 = bf16[32,2176]{1,0:T(8,128)(2,1)S(1)} collective-permute-done((bf16[32,2176]{1,0:T(8,128)(2,1)S(1)}, bf16[32,2176]{1,0:T(8,128)(2,1)S(1)}, u32[]{:S(2)}, u32[]{:S(2)}) %collective-permute-start.10) | collective-permute-done | bytes 139296 | tf_op jit(solution)/shard_map/ppermute | solution.py:70
  89.7 3.9 %collective-permute-done.12 = bf16[32,2176]{1,0:T(8,128)(2,1)S(1)} collective-permute-done((bf16[32,2176]{1,0:T(8,128)(2,1)S(1)}, bf16[32,2176]{1,0:T(8,128)(2,1)S(1)}, u32[]{:S(2)}, u32[]{:S(2)}) %collective-permute-start.12) | collective-permute-done | bytes 139296 | tf_op jit(solution)/shard_map/ppermute | solution.py:70
  93.7 0.7 slice.12
  94.5 0.8 select_reduce_fusion
  (52 shorter events, 4.0 us)
Async XLA Ops:
  7.2 38.1 %all-gather.2.cloned.1.call-start = ((), (), s32[]{:S(2)}) async-start(), calls=%async_computation.1 | async-start | bytes 1253376 | tf_op jit(solution)/shard_map/all_gather | solution.py:286
  7.2 0.9 copy-start.1
  8.1 0.7 copy-start.5
  8.8 0.7 copy-start.6
  9.8 0.9 copy-start.2
  10.7 0.7 copy-start.3
  13.1 69.0 %reduce-scatter.2.cloned.1.call-start = ((), (), s32[]{:S(2)}) async-start(), calls=%async_computation.2 | async-start | bytes 1179648 | tf_op jit(solution)/shard_map/reduce_scatter | solution.py:292
  13.2 11.9 %collective-permute-start.3 = (bf16[32,2176]{1,0:T(8,128)(2,1)S(1)}, bf16[32,2176]{1,0:T(8,128)(2,1)S(1)}, u32[]{:S(2)}, u32[]{:S(2)}) collective-permute-start(bf16[32,2176]{1,0:T(8,128)(2,1)S(1)} %pack.2.refs_0_), channel_id=1, source_target_pairs={{0,4},{4,0},{8,12},{12,8},{16,20},{20,16},{24,28},{28,24},{1,5},{5... | collective-permute-start | bytes 417800 | tf_op jit(solution)/shard_map/ppermute | solution.py:73
  13.7 8.0 %collective-permute-start.2 = (bf16[32,2176]{1,0:T(8,128)(2,1)S(1)}, bf16[32,2176]{1,0:T(8,128)(2,1)S(1)}, u32[]{:S(2)}, u32[]{:S(2)}) collective-permute-start(bf16[32,2176]{1,0:T(8,128)(2,1)S(1)} %pack.2.refs_0_), channel_id=1, source_target_pairs={{3,0},{2,1},{1,2},{0,3},{7,4},{6,5},{5,6},{4,7},{11,8},{10,9},{9,1... | collective-permute-start | bytes 417800 | tf_op jit(solution)/shard_map/ppermute | solution.py:66
  17.2 7.2 %collective-permute-start.1 = (bf16[32,2176]{1,0:T(8,128)(2,1)S(1)}, bf16[32,2176]{1,0:T(8,128)(2,1)S(1)}, u32[]{:S(2)}, u32[]{:S(2)}) collective-permute-start(bf16[32,2176]{1,0:T(8,128)(2,1)S(1)} %pack.2.refs_0_), channel_id=1, source_target_pairs={{2,0},{3,1},{0,2},{1,3},{6,4},{7,5},{4,6},{5,7},{10,8},{11,9},{8,1... | collective-permute-start | bytes 417800 | tf_op jit(solution)/shard_map/ppermute | solution.py:66
  17.7 7.1 %collective-permute-start = (bf16[32,2176]{1,0:T(8,128)(2,1)S(1)}, bf16[32,2176]{1,0:T(8,128)(2,1)S(1)}, u32[]{:S(2)}, u32[]{:S(2)}) collective-permute-start(bf16[32,2176]{1,0:T(8,128)(2,1)S(1)} %pack.2.refs_0_), channel_id=1, source_target_pairs={{1,0},{0,1},{3,2},{2,3},{5,4},{4,5},{7,6},{6,7},{9,8},{8,9},{11,10... | collective-permute-start | bytes 417800 | tf_op jit(solution)/shard_map/ppermute | solution.py:66
  19.7 25.5 %collective-permute-start.7 = (bf16[2,4,32,704]{3,2,1,0:T(8,128)(2,1)S(1)}, bf16[2,4,32,704]{3,2,1,0:T(8,128)(2,1)S(1)}, u32[]{:S(2)}, u32[]{:S(2)}) collective-permute-start(bf16[2,4,32,704]{3,2,1,0:T(8,128)(2,1)S(1)} %pad_maximum_fusion.1), channel_id=1, source_target_pairs={{0,4},{4,0},{8,12},{12,8},{16,20},{20,16},{24,28},{28,24},{1,5},{5... | collective-permute-start | bytes 1081352 | tf_op jit(solution)/shard_map/ppermute | solution.py:73
  21.7 3.3 %collective-permute-start.6 = (bf16[32,2176]{1,0:T(8,128)(2,1)S(1)}, bf16[32,2176]{1,0:T(8,128)(2,1)S(1)}, u32[]{:S(2)}, u32[]{:S(2)}) collective-permute-start(bf16[32,2176]{1,0:T(8,128)(2,1)S(1)} %collective-permute-done.2.refs_3_), channel_id=1, source_target_pairs={{0,4},{4,0},{8,12},{12,8},{16,20},{20,16},{24,28},{28,24},{1,5},{5... | collective-permute-start | bytes 417800 | tf_op jit(solution)/shard_map/ppermute | solution.py:73
  24.4 1.4 %collective-permute-start.5 = (bf16[32,2176]{1,0:T(8,128)(2,1)S(1)}, bf16[32,2176]{1,0:T(8,128)(2,1)S(1)}, u32[]{:S(2)}, u32[]{:S(2)}) collective-permute-start(bf16[32,2176]{1,0:T(8,128)(2,1)S(1)} %collective-permute-done.1.refs_2_), channel_id=1, source_target_pairs={{0,4},{4,0},{8,12},{12,8},{16,20},{20,16},{24,28},{28,24},{1,5},{5... | collective-permute-start | bytes 417800 | tf_op jit(solution)/shard_map/ppermute | solution.py:73
  24.8 1.4 %collective-permute-start.4 = (bf16[32,2176]{1,0:T(8,128)(2,1)S(1)}, bf16[32,2176]{1,0:T(8,128)(2,1)S(1)}, u32[]{:S(2)}, u32[]{:S(2)}) collective-permute-start(bf16[32,2176]{1,0:T(8,128)(2,1)S(1)} %collective-permute-done.refs_1_), channel_id=1, source_target_pairs={{0,4},{4,0},{8,12},{12,8},{16,20},{20,16},{24,28},{28,24},{1,5},{5... | collective-permute-start | bytes 417800 | tf_op jit(solution)/shard_map/ppermute | solution.py:73
  45.3 1.2 %copy-start = (bf16[256,2176]{1,0:T(8,128)(2,1)S(1)}, bf16[256,2176]{1,0:T(8,128)(2,1)}, u32[]{:S(2)}) copy-start(bf16[256,2176]{1,0:T(8,128)(2,1)} %all-gather.2.cloned.1.call-done.refs_0_) | copy-start | bytes 3342340
  46.5 48.0 %copy-start.4 = (s32[32,6]{0,1:T(8,128)S(1)}, s32[32,6]{0,1:T(8,128)}, u32[]{:S(2)}) copy-start(s32[32,6]{0,1:T(8,128)} %param.15) | copy-start | bytes 2308
  82.1 1.4 %collective-permute-start.9 = (bf16[32,2176]{1,0:T(8,128)(2,1)S(1)}, bf16[32,2176]{1,0:T(8,128)(2,1)S(1)}, u32[]{:S(2)}, u32[]{:S(2)}) collective-permute-start(bf16[32,2176]{1,0:T(8,128)(2,1)S(1)} %get-tuple-element.42), channel_id=1, source_target_pairs={{0,4},{4,0},{8,12},{12,8},{16,20},{20,16},{24,28},{28,24},{1,5},{5... | collective-permute-start | bytes 417800 | tf_op jit(solution)/shard_map/ppermute | solution.py:73
  82.1 5.2 %collective-permute-start.8 = (bf16[32,2176]{1,0:T(8,128)(2,1)S(1)}, bf16[32,2176]{1,0:T(8,128)(2,1)S(1)}, u32[]{:S(2)}, u32[]{:S(2)}) collective-permute-start(bf16[32,2176]{1,0:T(8,128)(2,1)S(1)} %get-tuple-element.40), channel_id=1, source_target_pairs={{0,4},{4,0},{8,12},{12,8},{16,20},{20,16},{24,28},{28,24},{1,5},{5... | collective-permute-start | bytes 417800 | tf_op jit(solution)/shard_map/ppermute | solution.py:73
  82.7 2.4 %collective-permute-start.11 = (bf16[32,2176]{1,0:T(8,128)(2,1)S(1)}, bf16[32,2176]{1,0:T(8,128)(2,1)S(1)}, u32[]{:S(2)}, u32[]{:S(2)}) collective-permute-start(bf16[32,2176]{1,0:T(8,128)(2,1)S(1)} %get-tuple-element.44), channel_id=1, source_target_pairs={{0,4},{4,0},{8,12},{12,8},{16,20},{20,16},{24,28},{28,24},{1,5},{5... | collective-permute-start | bytes 417800 | tf_op jit(solution)/shard_map/ppermute | solution.py:73
  82.7 3.1 %collective-permute-start.13 = (bf16[32,2176]{1,0:T(8,128)(2,1)S(1)}, bf16[32,2176]{1,0:T(8,128)(2,1)S(1)}, u32[]{:S(2)}, u32[]{:S(2)}) collective-permute-start(bf16[32,2176]{1,0:T(8,128)(2,1)S(1)} %get-tuple-element.46), channel_id=1, source_target_pairs={{0,4},{4,0},{8,12},{12,8},{16,20},{20,16},{24,28},{28,24},{1,5},{5... | collective-permute-start | bytes 417800 | tf_op jit(solution)/shard_map/ppermute | solution.py:73
  83.5 6.2 %collective-permute-start.10 = (bf16[32,2176]{1,0:T(8,128)(2,1)S(1)}, bf16[32,2176]{1,0:T(8,128)(2,1)S(1)}, u32[]{:S(2)}, u32[]{:S(2)}) collective-permute-start(bf16[32,2176]{1,0:T(8,128)(2,1)S(1)} %add_convert_fusion.2), channel_id=1, source_target_pairs={{0,1},{1,0},{2,3},{3,2},{4,5},{5,4},{6,7},{7,6},{8,9},{9,8},{10,11... | collective-permute-start | bytes 417800 | tf_op jit(solution)/shard_map/ppermute | solution.py:70
  85.1 8.5 %collective-permute-start.12 = (bf16[32,2176]{1,0:T(8,128)(2,1)S(1)}, bf16[32,2176]{1,0:T(8,128)(2,1)S(1)}, u32[]{:S(2)}, u32[]{:S(2)}) collective-permute-start(bf16[32,2176]{1,0:T(8,128)(2,1)S(1)} %add_convert_fusion.1), channel_id=1, source_target_pairs={{0,2},{1,3},{2,0},{3,1},{4,6},{5,7},{6,4},{7,5},{8,10},{9,11},{10,... | collective-permute-start | bytes 417800 | tf_op jit(solution)/shard_map/ppermute | solution.py:70
  85.8 7.8 %collective-permute-start.14 = (bf16[32,2176]{1,0:T(8,128)(2,1)S(1)}, bf16[32,2176]{1,0:T(8,128)(2,1)S(1)}, u32[]{:S(2)}, u32[]{:S(2)}) collective-permute-start(bf16[32,2176]{1,0:T(8,128)(2,1)S(1)} %add_convert_fusion), channel_id=1, source_target_pairs={{0,3},{1,2},{2,1},{3,0},{4,7},{5,6},{6,5},{7,4},{8,11},{9,10},{10,... | collective-permute-start | bytes 417800 | tf_op jit(solution)/shard_map/ppermute | solution.py:70
  (1 other events, 0.7 us)
Sparse Core Ops, SparseCore 0:
  13.2 26.5 all-gather.1
  45.4 36.7 reduce-scatter.1

commit v3 on v2

v3 whole, which is shorter than its diff:
```python
import functools
import jax
import jax.numpy as jnp
from jax import lax
from jax.experimental import pallas as pl
from jax.experimental.pallas import tpu as pltpu
from jax.sharding import PartitionSpec as P

F32 = jnp.float32
BF16 = jnp.bfloat16
LANES = 128
MIB = 1 << 20


def round_up(value, unit):
    return -(-value // unit) * unit


def dot(a, b):
    return jnp.dot(a, b, preferred_element_type=F32)


def dot_tb(a, b):
    return lax.dot_general(a, b, (((1,), (1,)), ((), ())), preferred_element_type=F32)


def dot_ta(a, b):
    return lax.dot_general(a, b, (((0,), (0,)), ((), ())), preferred_element_type=F32)


def iota(shape, dim):
    return lax.broadcasted_iota(jnp.int32, shape, dim)


def vmem():
    return pl.BlockSpec(memory_space=pltpu.VMEM)


def hbm():
    return pl.BlockSpec(memory_space=pltpu.HBM)


def in_vmem(x):
    return pltpu.with_memory_space_constraint(x, pltpu.VMEM)


def in_hbm(x):
    return pltpu.with_memory_space_constraint(x, pltpu.HBM)


class Plan:
    def __init__(self, tokens, routes, saved_gate, w_gate):
        self.owners = lax.axis_size("expert")
        self.groups = lax.axis_size("dp")
        self.count, self.width = tokens.shape
        self.top = routes.shape[1]
        self.local = w_gate.shape[0]
        self.hidden = w_gate.shape[2]
        self.experts = self.owners * self.local
        self.cap = saved_gate.shape[3]
        self.cap_rows = round_up(self.cap, 8)
        self.split = 2 if self.groups % 2 == 0 and self.local % 2 == 0 else 1
        self.mine = self.local // self.split
        self.meta = round_up(3 * self.experts, LANES)
        self.blocks = self.split * self.owners
        self.source_rows = self.owners * self.cap_rows
        self.expert_rows = self.split * self.source_rows
        self.rows = self.mine * self.expert_rows
        self.cols = self.blocks * self.count

    def peer(self, index, step):
        if self.owners & (self.owners - 1) == 0:
            return index ^ step
        return (index + step) % self.owners

    def over_expert(self, x, step):
        pairs = [(self.peer(i, step), i) for i in range(self.owners)]
        return lax.ppermute(x, "expert", pairs)

    def back_over_expert(self, x, step):
        pairs = [(i, self.peer(i, step)) for i in range(self.owners)]
        return lax.ppermute(x, "expert", pairs)

    def over_pair(self, x):
        return lax.ppermute(x, "dp", [(i, i ^ 1) for i in range(self.groups)])


def pack_kernel(plan, x_hbm, routes_hbm, factors_hbm, out_ref, routes_ref, factors_ref, sems):
    experts, top = plan.experts, plan.top
    count = plan.count
    x_copy = pltpu.make_async_copy(x_hbm, out_ref.at[:, : plan.width], sems.at[0])
    small = [
        pltpu.make_async_copy(routes_hbm, routes_ref, sems.at[1]),
        pltpu.make_async_copy(factors_hbm, factors_ref, sems.at[2]),
    ]
    for copy in (*small, x_copy):
        copy.start()
    for copy in small:
        copy.wait()
    lane = iota((plan.meta, count), 0)
    chosen = jnp.zeros((plan.meta, count), F32)
    parts = jnp.zeros((plan.meta, count), F32)
    for k in range(top):
        route = routes_ref[k : k + 1, :]
        factor = factors_ref[k : k + 1, :]
        high = factor.astype(BF16).astype(F32)
        low = factor - high
        chosen = chosen + jnp.where(lane == route, 1.0, 0.0)
        parts = parts + jnp.where(lane == route + experts, high, 0.0)
        parts = parts + jnp.where(lane == route + 2 * experts, low, 0.0)
    earlier = jnp.where(iota((count, count), 0) < iota((count, count), 1), 1.0, 0.0)
    before = dot(chosen.astype(BF16), earlier.astype(BF16))
    facts = (chosen * (before + 1.0) + parts).astype(BF16)
    shape = (plan.meta, plan.meta)
    same = jnp.where(iota(shape, 0) == iota(shape, 1), 1.0, 0.0).astype(BF16)
    out_ref[:, plan.width :] = dot_ta(facts, same).astype(BF16)
    x_copy.wait()


def pack(plan, x, routes, factors):
    return pl.pallas_call(
        functools.partial(pack_kernel, plan),
        out_shape=jax.ShapeDtypeStruct((plan.count, plan.width + plan.meta), BF16),
        in_specs=[hbm()] * 3,
        out_specs=vmem(),
        scratch_shapes=[
            pltpu.VMEM((plan.top, plan.count), jnp.int32),
            pltpu.VMEM((plan.top, plan.count), F32),
            pltpu.SemaphoreType.DMA((3,)),
        ],
        compiler_params=pltpu.CompilerParams(vmem_limit_bytes=4 * MIB),
        name="pack",
    )(in_hbm(x), in_hbm(routes.T), in_hbm(factors.T))


def first_expert(plan):
    core = lax.rem(lax.axis_index("dp"), plan.split)
    return lax.axis_index("expert") * plan.local + core * plan.mine, core * plan.mine


def tables(plan, meta, first):
    me = lax.axis_index("expert")
    row = iota((plan.rows, plan.meta), 0)
    lane = iota((plan.rows, plan.meta), 1)
    expert = first + row // plan.expert_rows
    pick_slot = jnp.where(lane == expert, 1.0, 0.0).astype(BF16)
    pick_part = jnp.where(
        (lane == expert + plan.experts) | (lane == expert + 2 * plan.experts), 1.0, 0.0
    ).astype(BF16)
    slot = dot_tb(pick_slot, meta)
    part = dot_tb(pick_part, meta)
    shape = (plan.rows, plan.cols)
    row = iota(shape, 0)
    col = iota(shape, 1)
    block = col // plan.count
    source = plan.peer(me, block % plan.owners)
    group = block // plan.owners
    place = row % plan.expert_rows
    want = (row % plan.cap_rows + 1).astype(F32)
    same = (place // plan.cap_rows) == group * plan.owners + source
    hit = same & (slot == want)
    factor = jnp.sum(jnp.where(hit, part, 0.0), axis=1, keepdims=True)
    return jnp.where(hit, 1.0, 0.0).astype(BF16), factor


def fetch_kernel(plan, gate_hbm, up_hbm, after, gate_ref, up_ref, done_ref, sems):
    done_ref[...] = jnp.zeros_like(done_ref)
    offset = first_expert(plan)[1]
    copies = []
    for i, (array, ref) in enumerate(((gate_hbm, gate_ref), (up_hbm, up_ref))):
        for e in range(plan.mine):
            copies.append(
                pltpu.make_async_copy(array.at[offset + e], ref.at[e], sems.at[i, e])
            )
    for copy in copies:
        copy.start()
    for copy in copies:
        copy.wait()


def fetch(plan, w_gate, w_up, after):
    shape = pltpu.VMEM((plan.mine, plan.hidden, plan.width), BF16)
    return pl.pallas_call(
        functools.partial(fetch_kernel, plan),
        out_shape=(shape, shape, jax.ShapeDtypeStruct((8, LANES), F32)),
        in_specs=[hbm(), hbm(), pl.BlockSpec(memory_space=pl.ANY)],
        out_specs=(vmem(), vmem(), vmem()),
        scratch_shapes=[pltpu.SemaphoreType.DMA((2, plan.mine))],
        compiler_params=pltpu.CompilerParams(vmem_limit_bytes=MIB),
        cost_estimate=pl.CostEstimate(
            flops=0,
            bytes_accessed=4 * plan.mine * plan.hidden * plan.width * 2,
            transcendentals=0,
        ),
        name="fetch",
    )(in_hbm(w_gate), in_hbm(w_up), after)


def forward_kernel(plan, count, *refs):
    blocks, refs = refs[:count], refs[count:]
    gate_ref, up_ref, down_hbm, *refs = refs
    outs, (kept_ref, rest_ref, x_s, y_s, sems) = refs[:-5], refs[-5:]
    first, offset = first_expert(plan)
    downs = [kept_ref.at[0]] + [rest_ref.at[e - 1] for e in range(1, plan.mine)]
    copies = [
        pltpu.make_async_copy(down_hbm.at[offset + e], down, sems.at[e])
        for e, down in enumerate(downs)
    ]
    for copy in copies:
        copy.start()
    meta = jnp.concatenate([b[:, plan.width :] for b in blocks], axis=0)
    rows = jnp.concatenate([b[:, : plan.width] for b in blocks], axis=0)
    table, factor = tables(plan, meta, first)
    x_s[...] = dot(table, rows).astype(BF16)
    n = plan.expert_rows
    hiddens = []
    for e in range(plan.mine):
        x = x_s[e * n : (e + 1) * n, :]
        gate = dot_tb(x, gate_ref[e])
        up = dot_tb(x, up_ref[e])
        hiddens.append((gate / (1.0 + jnp.exp(-gate)) * up).astype(BF16))
    for e in range(plan.mine):
        copies[e].wait()
        out = dot(hiddens[e], downs[e][...])
        y_s[e * n : (e + 1) * n, :] = (out * factor[e * n : (e + 1) * n]).astype(BF16)
    put_rows(plan, outs, slice(None), dot_ta(table, y_s[...]).astype(BF16))


def put_rows(plan, outs, columns, rows):
    start = 0
    for out in outs:
        stop = start + out.shape[0]
        out[:, columns] = rows[start:stop, :]
        start = stop


def backward_kernel(plan, count, *refs):
    blocks, refs = refs[:count], refs[count:]
    saved, refs = refs[: plan.split], refs[plan.split :]
    gate_ref, up_ref, kept_ref, down_hbm, *refs = refs
    outs, (rest_ref, x_s, y_s, score_s, sems) = refs[:-5], refs[-5:]
    first, offset = first_expert(plan)
    downs = [kept_ref.at[0]] + [rest_ref.at[e - 1] for e in range(1, plan.mine)]
    copies = [
        pltpu.make_async_copy(down_hbm.at[offset + e], downs[e], sems.at[e])
        for e in range(1, plan.mine)
    ]
    for copy in copies:
        copy.start()
    meta = jnp.concatenate([b[:, plan.width :] for b in blocks], axis=0)
    rows = jnp.concatenate([b[:, : plan.width] for b in blocks], axis=0)
    table, factor = tables(plan, meta, first)
    x_s[...] = dot(table, rows).astype(BF16)
    n = plan.expert_rows
    lane = iota((n, plan.meta), 1)
    for e in range(plan.mine):
        x = x_s[e * n : (e + 1) * n, :]
        act = jnp.concatenate([s[0, e] for s in saved], axis=0).astype(F32)
        up = jnp.concatenate([s[1, e] for s in saved], axis=0).astype(F32)
        sig = 1.0 / (1.0 + jnp.exp(-act))
        silu = act * sig
        if e > 0:
            copies[e - 1].wait()
        grad = dot_tb(x, downs[e][...])
        score = jnp.sum(silu * up * grad, axis=1, keepdims=True)
        grad_gate = (grad * up * sig * (1.0 + act * (1.0 - sig))).astype(BF16)
        grad_up = (grad * silu).astype(BF16)
        result = dot(grad_gate, gate_ref[e]) + dot(grad_up, up_ref[e])
        y_s[e * n : (e + 1) * n, :] = (result * factor[e * n : (e + 1) * n]).astype(BF16)
        expert = first + e
        high = score.astype(BF16).astype(F32)
        middle = (score - high).astype(BF16).astype(F32)
        low = score - high - middle
        spread = jnp.where(lane == expert, high, 0.0)
        spread = jnp.where(lane == expert + plan.experts, middle, spread)
        spread = jnp.where(lane == expert + 2 * plan.experts, low, spread)
        score_s[e * n : (e + 1) * n, :] = spread.astype(BF16)
    put_rows(plan, outs, slice(0, plan.width), dot_ta(table, y_s[...]).astype(BF16))
    scores = dot_ta(table, score_s[...]).astype(BF16)
    put_rows(plan, outs, slice(plan.width, plan.width + plan.meta), scores)


def part_shapes(plan, width):
    block = jax.ShapeDtypeStruct((plan.count, width), BF16)
    other = jax.ShapeDtypeStruct((plan.owners * plan.count, width), BF16)
    return [block] * plan.owners + [other] * (plan.split - 1)


def expert_params(plan, matrices):
    held = 2 * plan.mine * plan.width * plan.hidden * 2
    return dict(
        compiler_params=pltpu.CompilerParams(vmem_limit_bytes=40 * MIB - held),
        cost_estimate=pl.CostEstimate(
            flops=2 * 3 * plan.mine * plan.expert_rows * plan.width * plan.hidden,
            bytes_accessed=2 * matrices * plan.mine * plan.width * plan.hidden,
            transcendentals=0,
        ),
    )


def forward(plan, blocks, gate, up, w_down):
    kept = pltpu.VMEM((1, plan.hidden, plan.width), BF16)
    shapes = part_shapes(plan, plan.width) + [kept]
    *parts, kept = pl.pallas_call(
        functools.partial(forward_kernel, plan, len(blocks)),
        out_shape=shapes,
        in_specs=[vmem()] * (len(blocks) + 2) + [hbm()],
        out_specs=[vmem()] * len(shapes),
        scratch_shapes=[
            rest_shape(plan),
            pltpu.VMEM((plan.rows, plan.width), BF16),
            pltpu.VMEM((plan.rows, plan.width), BF16),
            pltpu.SemaphoreType.DMA((plan.mine,)),
        ],
        name="forward",
        **expert_params(plan, 1),
    )(*blocks, in_vmem(gate), in_vmem(up), in_hbm(w_down))
    return parts, kept


def rest_shape(plan):
    return pltpu.VMEM((max(plan.mine - 1, 1), plan.hidden, plan.width), BF16)


def backward(plan, blocks, saved, weights, w_down):
    shapes = part_shapes(plan, plan.width + plan.meta)
    return pl.pallas_call(
        functools.partial(backward_kernel, plan, len(blocks)),
        out_shape=shapes,
        in_specs=[vmem()] * (len(blocks) + len(saved) + 3) + [hbm()],
        out_specs=[vmem()] * len(shapes),
        scratch_shapes=[
            rest_shape(plan),
            pltpu.VMEM((plan.rows, plan.width), BF16),
            pltpu.VMEM((plan.rows, plan.width), BF16),
            pltpu.VMEM((plan.rows, plan.meta), BF16),
            pltpu.SemaphoreType.DMA((plan.mine,)),
        ],
        name="backward",
        **expert_params(plan, 1),
    )(*blocks, *saved, *[in_vmem(w) for w in weights], in_hbm(w_down))


def gather_group(plan, block):
    return [block] + [plan.over_expert(block, d) for d in range(1, plan.owners)]


def sum_pair(plan, parts):
    own = [[p] for p in parts[: plan.owners]]
    if plan.split > 1:
        other = plan.over_pair(parts[plan.owners])
        for d in range(plan.owners):
            own[d].append(other[d * plan.count : (d + 1) * plan.count])
    return own


def total(terms):
    return sum(t.astype(F32) for t in terms)


def scatter_group(plan, own):
    sent = [total(own[d]).astype(BF16) for d in range(1, plan.owners)]
    return own[0] + [plan.back_over_expert(x, d) for d, x in enumerate(sent, 1)]


def finish_back(plan, parts, routes):
    whole = total(parts)
    spread = whole[:, plan.width : plan.width + 3 * plan.experts]
    spread = jnp.sum(spread.reshape(plan.count, 3, plan.experts), axis=1)
    lane = iota((plan.top, plan.count, plan.experts), 2)
    hit = lane == routes.T[:, :, None]
    score = jnp.sum(jnp.where(hit, spread[None], 0.0), axis=2).T
    return whole[:, : plan.width].astype(BF16), score


def split_saved(plan, saved_gate, saved_up):
    def piece(array, core):
        rows = lax.dynamic_slice_in_dim(array[0], core * plan.mine, plan.mine, axis=1)
        short = plan.cap_rows - plan.cap
        rows = jnp.pad(jnp.swapaxes(rows, 0, 1), ((0, 0), (0, 0), (0, short), (0, 0)))
        return rows.reshape(1, plan.mine, plan.source_rows, plan.hidden)

    def part(core):
        return jnp.concatenate([piece(saved_gate, core), piece(saved_up, core)])

    if plan.split == 1:
        return [part(0)]
    core = lax.axis_index("dp") % 2
    return [part(core), plan.over_pair(part(1 - core))]


def body(
    tokens,
    routes,
    weights_fwd,
    cotangent,
    routes_back,
    weights_back,
    saved_gate,
    saved_up,
    w_gate,
    w_up,
    w_down,
):
    plan = Plan(tokens, routes, saved_gate, w_gate)
    packed = pack(plan, tokens, routes, weights_fwd)
    packed, cotangent = lax.optimization_barrier((packed, cotangent))
    packed_back = pack(plan, cotangent, routes_back, weights_back)
    gate, up, done = fetch(
        plan, jnp.swapaxes(w_gate, 1, 2), jnp.swapaxes(w_up, 1, 2), packed_back
    )
    blocks = gather_group(plan, packed)
    saved = split_saved(plan, saved_gate, saved_up)
    blocks_back = gather_group(plan, packed_back)
    if plan.split > 1:
        zero = done[0, 0].astype(BF16)
        blocks = blocks + [plan.over_pair(b + zero) for b in blocks]
    parts, kept = forward(plan, blocks, gate, up, w_down)
    parts, blocks_back, saved = lax.optimization_barrier((parts, blocks_back, saved))
    if plan.split > 1:
        blocks_back = blocks_back + [plan.over_pair(jnp.concatenate(blocks_back))]
    terms = scatter_group(plan, sum_pair(plan, parts))
    parts_back = backward(plan, blocks_back, saved, (gate, up, kept), w_down)
    parts_back, terms = lax.optimization_barrier((parts_back, terms))
    mixed = total(terms).astype(BF16)
    terms_back = scatter_group(plan, sum_pair(plan, parts_back))
    input_grad, weight_grad = finish_back(plan, terms_back, routes_back)
    return (mixed, input_grad, weight_grad)


def solution(mesh):
    spec = P(("dp", "expert"), None)
    saved = P("dp", None, "expert", None, None)
    weight = P("expert", None, None)
    return jax.shard_map(
        body,
        mesh=mesh,
        in_specs=(spec,) * 6 + (saved,) * 2 + (weight,) * 3,
        out_specs=(spec,) * 3,
        check_vma=False,
    )
```

time: 102 us -> 70.1 us (0.69)
  waiting for transfers between devices: 33.8 us -> 10.5 us
  between operations: 14.3 us -> 0.97 us
  starting transfers between devices: 9.78 us -> 17.3 us
  local copies, waits for them, and re-layouts: 8.5 us -> 3.24 us
  other arithmetic: 1.09 us -> 4.63 us
  Pallas kernels: 34.7 us -> 33.1 us
    reduce_scatter x1 -> x0, waiting for transfers between devices: 21.3 us -> none  [scatter_whole(): return lax.psum_scatter(parts, axes, axis_index_groups=groups, tiled=True)]
    unnamed x20 -> x8, local copies, waits for them, and re-layouts: 5.88 us -> 0.1 us
    ppermute x3 -> x6, waiting for transfers between devices: 4.78 us -> 0.02 us  [over_expert(): return lax.ppermute(x, 'expert', pairs)]
    ppermute x3 -> x6, starting transfers between devices: 4.16 us -> 8.16 us  [over_expert(): return lax.ppermute(x, 'expert', pairs)]
    ppermute x3 -> x6, starting transfers between devices: 3.68 us -> 7.11 us  [back_over_expert(): return lax.ppermute(x, 'expert', pairs)]
    add x1 -> x5, other arithmetic: 0.09 us -> 2.74 us  [the longest x4 2.65 us: body(): blocks = blocks + [plan.over_pair(b + zero) for b in blocks]]
    pallas_call x2 -> x3, Pallas kernels: 33.4 us -> 31 us  [the longest x1 12.4 us: forward(): pl.pallas_call(functools.partial(forward_kernel, plan, len(blocks)), out_...]
    ppermute x9 -> x8, waiting for transfers between devices: 1.4 us -> 3.25 us  [over_pair(): return lax.ppermute(x, 'dp', [(i, i ^ 1) for i in range(self.groups)])]
  transfers between devices with their start and end apart: 17 -> 20, of which waited for: 9 -> 5; matrix products, arithmetic and copies ran while one was open for 2% -> 9% of each run, Pallas kernels for 33% -> 46%
where the time goes in v3:
time: 70.1 us; the launch traced here: 69.8 us
  Pallas kernels  33.1 us (47%)
  starting transfers between devices  17.3 us (25%)
  waiting for transfers between devices  10.5 us (15%)
  other arithmetic  4.63 us (7%)
  local copies, waits for them, and re-layouts  3.24 us (5%)
  between operations  0.97 us (1%)
    pallas_call x1, Pallas kernels, forward(): pl.pallas_call(functools.partial(forward_kernel, plan, len(blocks)), out_...  12.4 us
    pallas_call x1, Pallas kernels, backward(): pl.pallas_call(functools.partial(backward_kernel, plan, len(blocks)), out...  10.9 us
    ppermute x6, starting transfers between devices, over_expert(): return lax.ppermute(x, 'expert', pairs)  8.16 us
    pallas_call x1, Pallas kernels, fetch(): pl.pallas_call(functools.partial(fetch_kernel, plan), out_shape=(shape, s...  7.72 us
    ppermute x6, waiting for transfers between devices, back_over_expert(): return lax.ppermute(x, 'expert', pairs)  7.28 us
    ppermute x6, starting transfers between devices, back_over_expert(): return lax.ppermute(x, 'expert', pairs)  7.11 us
    ppermute x8, waiting for transfers between devices, over_pair(): return lax.ppermute(x, 'dp', [(i, i ^ 1) for i in range(self.groups)])  3.25 us
    add x4, other arithmetic, body(): blocks = blocks + [plan.over_pair(b + zero) for b in blocks]  2.65 us
  transfers between devices with their start and end apart: 20, of which 5 were waited for; matrix products, arithmetic and copies ran while one was open for 9% of the time, Pallas kernels for 46%

profile of v3, /device:TPU:0, one launch (start us, length us, event | category | flops | bytes accessed | tf_op | source)
XLA Modules:
  0.0 69.8 jit_solution(11063489910356965161)
XLA Ops:
  0.6 1.1 %pack.2.refs_0_ = bf16[32,2176]{1,0:T(8,128)(2,1)S(1)} custom-call(bf16[32,2048]{1,0:T(8,128)(2,1)} %x_hbm.1, s32[6,32]{1,0:T(8,128)} %bitcast.36, f32[6,32]{1,0:T(8,128)} %bitcast.37), custom_call_target="tpu_custom_call" | custom-call | tf_op jit(solution)/shard_map/pack/pallas_call | solution.py:121
  1.7 4.0 %collective-permute-start.2 = (bf16[32,2176]{1,0:T(8,128)(2,1)S(1)}, bf16[32,2176]{1,0:T(8,128)(2,1)S(1)}, u32[]{:S(2)}, u32[]{:S(2)}) collective-permute-start(bf16[32,2176]{1,0:T(8,128)(2,1)S(1)} %pack.2.refs_0_), channel_id=1, source_target_pairs={{3,0},{2,1},{1,2},{0,3},{7,4},{6,5},{5,6},{4,7},{11,8},{10,9},{9,1... | collective-permute-start | bytes 417800 | tf_op jit(solution)/shard_map/ppermute | solution.py:78
  6.3 1.7 %dynamic-slice_bitcast_fusion = (bf16[4,4,7,704]{3,0,2,1:T(4,128)(2,1)S(1)}, bf16[4,4,7,704]{3,0,2,1:T(4,128)(2,1)S(1)}, bf16[4,4,7,704]{3,0,2,1:T(4,128)(2,1)S(1)}, bf16[4,4,7,704]{3,0,2,1:T(4,128)(2,1)S(1)}) fusion(bf16[1,4,8,7,704]{4,2,3,1,0:T(8,128)(2,1)} %param.18, s32[]{:T(128)S(6)} %select_n.21, s32[]{:T(128)S(6)} %select_n.20, ...), kind=kLoop, calls=%fused_computation.16 | loop fusion | bytes 1261576 | tf_op jit(solution)/shard_map/transpose | solution.py:380
  8.3 1.1 %pack.3.after.refs_0_ = bf16[32,2176]{1,0:T(8,128)(2,1)S(1)} custom-call(bf16[32,2048]{1,0:T(8,128)(2,1)} %x_hbm.2, s32[6,32]{1,0:T(8,128)} %bitcast.34, f32[6,32]{1,0:T(8,128)} %bitcast.38), custom_call_target="tpu_custom_call" | custom-call | tf_op jit(solution)/shard_map/pack/pallas_call | solution.py:121
  9.4 7.7 %fetch.1 = (bf16[4,704,2048]{2,1,0:T(8,128)(2,1)S(1)}, bf16[4,704,2048]{2,1,0:T(8,128)(2,1)S(1)}, f32[8,128]{1,0:T(8,128)S(1)}) custom-call(bf16[8,704,2048]{2,1,0:T(8,128)(2,1)} %bitcast.32, bf16[8,704,2048]{2,1,0:T(8,128)(2,1)} %bitcast.33, bf16[32,2176]{1,0:T(8,128)(2,1)S(1)} %pack.3.after.refs_0_), custom_call_target="tpu_custom_call" | custom-call | bytes 46137344 | tf_op jit(solution)/shard_map/fetch/pallas_call | solution.py:183
  17.6 0.7 broadcast_add_fusion.3
  18.3 0.6 collective-permute-start.3
  18.9 0.7 broadcast_add_fusion
  19.7 0.7 broadcast_add_fusion.1
  20.9 0.7 broadcast_add_fusion.2
  21.8 2.9 %collective-permute-start.9 = (bf16[32,2176]{1,0:T(8,128)(2,1)S(1)}, bf16[32,2176]{1,0:T(8,128)(2,1)S(1)}, u32[]{:S(2)}, u32[]{:S(2)}) collective-permute-start(bf16[32,2176]{1,0:T(8,128)(2,1)S(1)} %pack.3.after.refs_0_), channel_id=1, source_target_pairs={{3,0},{2,1},{1,2},{0,3},{7,4},{6,5},{5,6},{4,7},{11,8},{10,9},{9,1... | collective-permute-start | bytes 417800 | tf_op jit(solution)/shard_map/ppermute | solution.py:78
  25.4 12.4 %forward.1 = (bf16[32,2048]{1,0:T(8,128)(2,1)S(1)}, bf16[32,2048]{1,0:T(8,128)(2,1)S(1)}, bf16[32,2048]{1,0:T(8,128)(2,1)S(1)}, bf16[32,2048]{1,0:T(8,128)(2,1)S...) custom-call(bf16[32,2176]{1,0:T(8,128)(2,1)S(1)} %pack.2.refs_0_, ...), custom_call_target="tpu_custom_call" | custom-call | flops 2214592512 | bytes 11534336 | tf_op jit(solution)/shard_map/forward/pallas_call | solution.py:304
  38.5 1.3 %collective-permute-done.12 = bf16[128,2048]{1,0:T(8,128)(2,1)S(1)} collective-permute-done((bf16[128,2048]{1,0:T(8,128)(2,1)S(1)}, bf16[128,2048]{1,0:T(8,128)(2,1)S(1)}, u32[]{:S(2)}, u32[]{:S(2)}) %collective-permute-start.12) | collective-permute-done | bytes 524320 | tf_op jit(solution)/shard_map/ppermute | solution.py:85
  39.9 2.9 %collective-permute-start.15 = (bf16[32,2048]{1,0:T(8,128)(2,1)S(1)}, bf16[32,2048]{1,0:T(8,128)(2,1)S(1)}, u32[]{:S(2)}, u32[]{:S(2)}) collective-permute-start(bf16[32,2048]{1,0:T(8,128)(2,1)S(1)} %get-tuple-element.80), channel_id=1, source_target_pairs={{0,3},{1,2},{2,1},{3,0},{4,7},{5,6},{6,5},{7,4},{8,11},{9,10},{10,... | collective-permute-start | bytes 393224 | tf_op jit(solution)/shard_map/ppermute | solution.py:82
  43.4 10.9 %backward.1 = (bf16[32,2176]{1,0:T(8,128)(2,1)S(1)}, bf16[32,2176]{1,0:T(8,128)(2,1)S(1)}, bf16[32,2176]{1,0:T(8,128)(2,1)S(1)}, bf16[32,2176]{1,0:T(8,128)(2,1)S(1)}, bf16[128,2176]{1,0:T(8,128)(2,1)S(1)}) custom-call(bf16[32,2176]{1,0:T(8,128)(2,1)S(1)} %pack.3.after.refs_0_, bf16[32,2176]{1,0:T(8,128)(2,1)S(1)} %collective-permute-done.7.refs_1_, ...), custom_call_target="tpu_custom_call" | custom-call | flops 2214592512 | bytes 11534336 | tf_op jit(solution)/shard_map/backward/pallas_call | solution.py:327
  54.5 1.9 %collective-permute-done.16 = bf16[128,2176]{1,0:T(8,128)(2,1)S(1)} collective-permute-done((bf16[128,2176]{1,0:T(8,128)(2,1)S(1)}, bf16[128,2176]{1,0:T(8,128)(2,1)S(1)}, u32[]{:S(2)}, u32[]{:S(2)}) %collective-permute-start.16) | collective-permute-done | bytes 557088 | tf_op jit(solution)/shard_map/ppermute | solution.py:85
  56.6 1.9 %collective-permute-start.17 = (bf16[32,2176]{1,0:T(8,128)(2,1)S(1)}, bf16[32,2176]{1,0:T(8,128)(2,1)S(1)}, u32[]{:S(2)}, u32[]{:S(2)}) collective-permute-start(bf16[32,2176]{1,0:T(8,128)(2,1)S(1)} %get-tuple-element.77), channel_id=1, source_target_pairs={{0,1},{1,0},{2,3},{3,2},{4,5},{5,4},{6,7},{7,6},{8,9},{9,8},{10,11... | collective-permute-start | bytes 417800 | tf_op jit(solution)/shard_map/ppermute | solution.py:82
  58.5 1.5 %collective-permute-start.19 = (bf16[32,2176]{1,0:T(8,128)(2,1)S(1)}, bf16[32,2176]{1,0:T(8,128)(2,1)S(1)}, u32[]{:S(2)}, u32[]{:S(2)}) collective-permute-start(bf16[32,2176]{1,0:T(8,128)(2,1)S(1)} %get-tuple-element.78), channel_id=1, source_target_pairs={{0,3},{1,2},{2,1},{3,0},{4,7},{5,6},{6,5},{7,4},{8,11},{9,10},{10,... | collective-permute-start | bytes 417800 | tf_op jit(solution)/shard_map/ppermute | solution.py:82
  60.1 0.7 %add_convert_fusion.3 = bf16[32,2048]{1,0:T(8,128)(2,1)} fusion(bf16[32,2048]{1,0:T(8,128)(2,1)S(1)} %collective-permute-done.15, bf16[32,2048]{1,0:T(8,128)(2,1)S(1)} %collective-permute-done.14, bf16[32,2048]{1,0:T(8,128)(2,1)S(1)} %collective-permute-done.13, bf16[32,2048]{1,0:T(8,128)(2,1)S(1)} %slice-done, bf16[32,2048]{1,0:T(8,128)(2,1)S(1)} %get-tuple-element.67), kind=kLoop, calls=%fused_computation.8 | loop fusion | flops 655360 | bytes 786432 | tf_op jit(solution)/shard_map/convert_element_type | solution.py:425
  60.9 2.1 %collective-permute-done.17 = bf16[32,2176]{1,0:T(8,128)(2,1)S(1)} collective-permute-done((bf16[32,2176]{1,0:T(8,128)(2,1)S(1)}, bf16[32,2176]{1,0:T(8,128)(2,1)S(1)}, u32[]{:S(2)}, u32[]{:S(2)}) %collective-permute-start.17) | collective-permute-done | bytes 139296 | tf_op jit(solution)/shard_map/ppermute | solution.py:82
  63.0 3.8 %collective-permute-done.19 = bf16[32,2176]{1,0:T(8,128)(2,1)S(1)} collective-permute-done((bf16[32,2176]{1,0:T(8,128)(2,1)S(1)}, bf16[32,2176]{1,0:T(8,128)(2,1)S(1)}, u32[]{:S(2)}, u32[]{:S(2)}) %collective-permute-start.19) | collective-permute-done | bytes 139296 | tf_op jit(solution)/shard_map/ppermute | solution.py:82
  66.8 1.4 %collective-permute-done.18 = bf16[32,2176]{1,0:T(8,128)(2,1)S(1)} collective-permute-done((bf16[32,2176]{1,0:T(8,128)(2,1)S(1)}, bf16[32,2176]{1,0:T(8,128)(2,1)S(1)}, u32[]{:S(2)}, u32[]{:S(2)}) %collective-permute-start.18) | collective-permute-done | bytes 139296 | tf_op jit(solution)/shard_map/ppermute | solution.py:82
  68.2 0.7 slice.64
  69.1 0.8 %select_reduce_fusion = f32[6,32]{1,0:T(8,128)} fusion(f32[32,32]{1,0:T(8,128)S(1)} %reduce_sum.18, s32[6,32]{1,0:T(8,128)S(1)} %bitcast.35), kind=kLoop, calls=%fused_computation.20 | loop fusion | flops 18240 | bytes 5632 | tf_op jit(solution)/shard_map/reduce_sum | solution.py:372
  (54 shorter events, 4.9 us)
Async XLA Ops:
  1.7 17.2 %collective-permute-start.2 = (bf16[32,2176]{1,0:T(8,128)(2,1)S(1)}, bf16[32,2176]{1,0:T(8,128)(2,1)S(1)}, u32[]{:S(2)}, u32[]{:S(2)}) collective-permute-start(bf16[32,2176]{1,0:T(8,128)(2,1)S(1)} %pack.2.refs_0_), channel_id=1, source_target_pairs={{3,0},{2,1},{1,2},{0,3},{7,4},{6,5},{5,6},{4,7},{11,8},{10,9},{9,1... | collective-permute-start | bytes 417800 | tf_op jit(solution)/shard_map/ppermute | solution.py:78
  5.7 14.1 %collective-permute-start.1 = (bf16[32,2176]{1,0:T(8,128)(2,1)S(1)}, bf16[32,2176]{1,0:T(8,128)(2,1)S(1)}, u32[]{:S(2)}, u32[]{:S(2)}) collective-permute-start(bf16[32,2176]{1,0:T(8,128)(2,1)S(1)} %pack.2.refs_0_), channel_id=1, source_target_pairs={{2,0},{3,1},{0,2},{1,3},{6,4},{7,5},{4,6},{5,7},{10,8},{11,9},{8,1... | collective-permute-start | bytes 417800 | tf_op jit(solution)/shard_map/ppermute | solution.py:78
  6.2 14.8 %collective-permute-start = (bf16[32,2176]{1,0:T(8,128)(2,1)S(1)}, bf16[32,2176]{1,0:T(8,128)(2,1)S(1)}, u32[]{:S(2)}, u32[]{:S(2)}) collective-permute-start(bf16[32,2176]{1,0:T(8,128)(2,1)S(1)} %pack.2.refs_0_), channel_id=1, source_target_pairs={{1,0},{0,1},{3,2},{2,3},{5,4},{4,5},{7,6},{6,7},{9,8},{8,9},{11,10... | collective-permute-start | bytes 417800 | tf_op jit(solution)/shard_map/ppermute | solution.py:78
  8.2 29.6 %collective-permute-start.10 = (bf16[2,4,32,704]{3,2,1,0:T(8,128)(2,1)S(1)}, bf16[2,4,32,704]{3,2,1,0:T(8,128)(2,1)S(1)}, u32[]{:S(2)}, u32[]{:S(2)}) collective-permute-start(bf16[2,4,32,704]{3,2,1,0:T(8,128)(2,1)S(1)} %pad_maximum_fusion.2), channel_id=1, source_target_pairs={{0,4},{4,0},{8,12},{12,8},{16,20},{20,16},{24,28},{28,24},{1,5},{5... | collective-permute-start | bytes 1081352 | tf_op jit(solution)/shard_map/ppermute | solution.py:85
  18.3 3.5 %collective-permute-start.3 = (bf16[32,2176]{1,0:T(8,128)(2,1)S(1)}, bf16[32,2176]{1,0:T(8,128)(2,1)S(1)}, u32[]{:S(2)}, u32[]{:S(2)}) collective-permute-start(bf16[32,2176]{1,0:T(8,128)(2,1)S(1)} %broadcast_add_fusion.3), channel_id=1, source_target_pairs={{0,4},{4,0},{8,12},{12,8},{16,20},{20,16},{24,28},{28,24},{1,5},{5... | collective-permute-start | bytes 417800 | tf_op jit(solution)/shard_map/ppermute | solution.py:85
  19.6 5.1 %collective-permute-start.6 = (bf16[32,2176]{1,0:T(8,128)(2,1)S(1)}, bf16[32,2176]{1,0:T(8,128)(2,1)S(1)}, u32[]{:S(2)}, u32[]{:S(2)}) collective-permute-start(bf16[32,2176]{1,0:T(8,128)(2,1)S(1)} %broadcast_add_fusion), channel_id=1, source_target_pairs={{0,4},{4,0},{8,12},{12,8},{16,20},{20,16},{24,28},{28,24},{1,5},{5... | collective-permute-start | bytes 417800 | tf_op jit(solution)/shard_map/ppermute | solution.py:85
  20.4 4.8 %collective-permute-start.5 = (bf16[32,2176]{1,0:T(8,128)(2,1)S(1)}, bf16[32,2176]{1,0:T(8,128)(2,1)S(1)}, u32[]{:S(2)}, u32[]{:S(2)}) collective-permute-start(bf16[32,2176]{1,0:T(8,128)(2,1)S(1)} %broadcast_add_fusion.1), channel_id=1, source_target_pairs={{0,4},{4,0},{8,12},{12,8},{16,20},{20,16},{24,28},{28,24},{1,5},{5... | collective-permute-start | bytes 417800 | tf_op jit(solution)/shard_map/ppermute | solution.py:85
  21.6 3.8 %collective-permute-start.4 = (bf16[32,2176]{1,0:T(8,128)(2,1)S(1)}, bf16[32,2176]{1,0:T(8,128)(2,1)S(1)}, u32[]{:S(2)}, u32[]{:S(2)}) collective-permute-start(bf16[32,2176]{1,0:T(8,128)(2,1)S(1)} %broadcast_add_fusion.2), channel_id=1, source_target_pairs={{0,4},{4,0},{8,12},{12,8},{16,20},{20,16},{24,28},{28,24},{1,5},{5... | collective-permute-start | bytes 417800 | tf_op jit(solution)/shard_map/ppermute | solution.py:85
  21.8 16.0 %collective-permute-start.9 = (bf16[32,2176]{1,0:T(8,128)(2,1)S(1)}, bf16[32,2176]{1,0:T(8,128)(2,1)S(1)}, u32[]{:S(2)}, u32[]{:S(2)}) collective-permute-start(bf16[32,2176]{1,0:T(8,128)(2,1)S(1)} %pack.3.after.refs_0_), channel_id=1, source_target_pairs={{3,0},{2,1},{1,2},{0,3},{7,4},{6,5},{5,6},{4,7},{11,8},{10,9},{9,1... | collective-permute-start | bytes 417800 | tf_op jit(solution)/shard_map/ppermute | solution.py:78
  24.7 13.1 %collective-permute-start.8 = (bf16[32,2176]{1,0:T(8,128)(2,1)S(1)}, bf16[32,2176]{1,0:T(8,128)(2,1)S(1)}, u32[]{:S(2)}, u32[]{:S(2)}) collective-permute-start(bf16[32,2176]{1,0:T(8,128)(2,1)S(1)} %pack.3.after.refs_0_), channel_id=1, source_target_pairs={{2,0},{3,1},{0,2},{1,3},{6,4},{7,5},{4,6},{5,7},{10,8},{11,9},{8,1... | collective-permute-start | bytes 417800 | tf_op jit(solution)/shard_map/ppermute | solution.py:78
  25.2 12.6 %collective-permute-start.7 = (bf16[32,2176]{1,0:T(8,128)(2,1)S(1)}, bf16[32,2176]{1,0:T(8,128)(2,1)S(1)}, u32[]{:S(2)}, u32[]{:S(2)}) collective-permute-start(bf16[32,2176]{1,0:T(8,128)(2,1)S(1)} %pack.3.after.refs_0_), channel_id=1, source_target_pairs={{1,0},{0,1},{3,2},{2,3},{5,4},{4,5},{7,6},{6,7},{9,8},{8,9},{11,10... | collective-permute-start | bytes 417800 | tf_op jit(solution)/shard_map/ppermute | solution.py:78
  37.8 2.0 %collective-permute-start.12 = (bf16[128,2048]{1,0:T(8,128)(2,1)S(1)}, bf16[128,2048]{1,0:T(8,128)(2,1)S(1)}, u32[]{:S(2)}, u32[]{:S(2)}) collective-permute-start(bf16[128,2048]{1,0:T(8,128)(2,1)S(1)} %get-tuple-element.63), channel_id=1, source_target_pairs={{0,4},{4,0},{8,12},{12,8},{16,20},{20,16},{24,28},{28,24},{1,5},{5... | collective-permute-start | bytes 1572872 | tf_op jit(solution)/shard_map/ppermute | solution.py:85
  37.9 5.5 %collective-permute-start.11 = (bf16[128,2176]{1,0:T(8,128)(2,1)S(1)}, bf16[128,2176]{1,0:T(8,128)(2,1)S(1)}, u32[]{:S(2)}, u32[]{:S(2)}) collective-permute-start(bf16[128,2176]{1,0:T(8,128)(2,1)S(1)} %pad_maximum_fusion), channel_id=1, source_target_pairs={{0,4},{4,0},{8,12},{12,8},{16,20},{20,16},{24,28},{28,24},{1,5},{5... | collective-permute-start | bytes 1671176 | tf_op jit(solution)/shard_map/ppermute | solution.py:85
  39.8 14.6 %copy-start = (bf16[128,2048]{1,0:T(8,128)(2,1)}, bf16[128,2048]{1,0:T(8,128)(2,1)S(1)}, u32[]{:S(2)}) copy-start(bf16[128,2048]{1,0:T(8,128)(2,1)S(1)} %collective-permute-done.12) | copy-start | bytes 1572868
  39.9 14.5 %collective-permute-start.15 = (bf16[32,2048]{1,0:T(8,128)(2,1)S(1)}, bf16[32,2048]{1,0:T(8,128)(2,1)S(1)}, u32[]{:S(2)}, u32[]{:S(2)}) collective-permute-start(bf16[32,2048]{1,0:T(8,128)(2,1)S(1)} %get-tuple-element.80), channel_id=1, source_target_pairs={{0,3},{1,2},{2,1},{3,0},{4,7},{5,6},{6,5},{7,4},{8,11},{9,10},{10,... | collective-permute-start | bytes 393224 | tf_op jit(solution)/shard_map/ppermute | solution.py:82
  42.8 11.6 %collective-permute-start.14 = (bf16[32,2048]{1,0:T(8,128)(2,1)S(1)}, bf16[32,2048]{1,0:T(8,128)(2,1)S(1)}, u32[]{:S(2)}, u32[]{:S(2)}) collective-permute-start(bf16[32,2048]{1,0:T(8,128)(2,1)S(1)} %get-tuple-element.81), channel_id=1, source_target_pairs={{0,2},{1,3},{2,0},{3,1},{4,6},{5,7},{6,4},{7,5},{8,10},{9,11},{10,... | collective-permute-start | bytes 393224 | tf_op jit(solution)/shard_map/ppermute | solution.py:82
  43.3 11.1 %collective-permute-start.13 = (bf16[32,2048]{1,0:T(8,128)(2,1)S(1)}, bf16[32,2048]{1,0:T(8,128)(2,1)S(1)}, u32[]{:S(2)}, u32[]{:S(2)}) collective-permute-start(bf16[32,2048]{1,0:T(8,128)(2,1)S(1)} %get-tuple-element.82), channel_id=1, source_target_pairs={{0,1},{1,0},{2,3},{3,2},{4,5},{5,4},{6,7},{7,6},{8,9},{9,8},{10,11... | collective-permute-start | bytes 393224 | tf_op jit(solution)/shard_map/ppermute | solution.py:82
  54.4 5.7 %slice-start = ((bf16[128,2048]{1,0:T(8,128)(2,1)}), bf16[32,2048]{1,0:T(8,128)(2,1)S(1)}, s32[]{:S(2)}) async-start(bf16[128,2048]{1,0:T(8,128)(2,1)} %copy-done), calls=%async_computation | async-start | bytes 262144 | tf_op jit(solution)/shard_map/slice | solution.py:353
  54.4 2.0 %collective-permute-start.16 = (bf16[128,2176]{1,0:T(8,128)(2,1)S(1)}, bf16[128,2176]{1,0:T(8,128)(2,1)S(1)}, u32[]{:S(2)}, u32[]{:S(2)}) collective-permute-start(bf16[128,2176]{1,0:T(8,128)(2,1)S(1)} %get-tuple-element.73), channel_id=1, source_target_pairs={{0,4},{4,0},{8,12},{12,8},{16,20},{20,16},{24,28},{28,24},{1,5},{5... | collective-permute-start | bytes 1671176 | tf_op jit(solution)/shard_map/ppermute | solution.py:85
  56.5 12.5 %copy-start.1 = (s32[32,6]{0,1:T(8,128)S(1)}, s32[32,6]{0,1:T(8,128)}, u32[]{:S(2)}) copy-start(s32[32,6]{0,1:T(8,128)} %param.15) | copy-start | bytes 2308
  56.6 6.4 %collective-permute-start.17 = (bf16[32,2176]{1,0:T(8,128)(2,1)S(1)}, bf16[32,2176]{1,0:T(8,128)(2,1)S(1)}, u32[]{:S(2)}, u32[]{:S(2)}) collective-permute-start(bf16[32,2176]{1,0:T(8,128)(2,1)S(1)} %get-tuple-element.77), channel_id=1, source_target_pairs={{0,1},{1,0},{2,3},{3,2},{4,5},{5,4},{6,7},{7,6},{8,9},{9,8},{10,11... | collective-permute-start | bytes 417800 | tf_op jit(solution)/shard_map/ppermute | solution.py:82
  58.5 8.3 %collective-permute-start.19 = (bf16[32,2176]{1,0:T(8,128)(2,1)S(1)}, bf16[32,2176]{1,0:T(8,128)(2,1)S(1)}, u32[]{:S(2)}, u32[]{:S(2)}) collective-permute-start(bf16[32,2176]{1,0:T(8,128)(2,1)S(1)} %get-tuple-element.78), channel_id=1, source_target_pairs={{0,3},{1,2},{2,1},{3,0},{4,7},{5,6},{6,5},{7,4},{8,11},{9,10},{10,... | collective-permute-start | bytes 417800 | tf_op jit(solution)/shard_map/ppermute | solution.py:82
  60.0 8.1 %collective-permute-start.18 = (bf16[32,2176]{1,0:T(8,128)(2,1)S(1)}, bf16[32,2176]{1,0:T(8,128)(2,1)S(1)}, u32[]{:S(2)}, u32[]{:S(2)}) collective-permute-start(bf16[32,2176]{1,0:T(8,128)(2,1)S(1)} %get-tuple-element.79), channel_id=1, source_target_pairs={{0,2},{1,3},{2,0},{3,1},{4,6},{5,7},{6,4},{7,5},{8,10},{9,11},{10,... | collective-permute-start | bytes 417800 | tf_op jit(solution)/shard_map/ppermute | solution.py:82

commit v4 on v3

v4 whole, which is shorter than its diff:
```python
import functools
import jax
import jax.numpy as jnp
from jax import lax
from jax.experimental import pallas as pl
from jax.experimental.pallas import tpu as pltpu
from jax.sharding import PartitionSpec as P

F32 = jnp.float32
BF16 = jnp.bfloat16
LANES = 128
MIB = 1 << 20


def round_up(value, unit):
    return -(-value // unit) * unit


def dot(a, b):
    return jnp.dot(a, b, preferred_element_type=F32)


def dot_tb(a, b):
    return lax.dot_general(a, b, (((1,), (1,)), ((), ())), preferred_element_type=F32)


def dot_ta(a, b):
    return lax.dot_general(a, b, (((0,), (0,)), ((), ())), preferred_element_type=F32)


def iota(shape, dim):
    return lax.broadcasted_iota(jnp.int32, shape, dim)


def vmem():
    return pl.BlockSpec(memory_space=pltpu.VMEM)


def hbm():
    return pl.BlockSpec(memory_space=pltpu.HBM)


def in_vmem(x):
    return pltpu.with_memory_space_constraint(x, pltpu.VMEM)


def in_hbm(x):
    return pltpu.with_memory_space_constraint(x, pltpu.HBM)


class Plan:
    def __init__(self, tokens, routes, saved_gate, w_gate):
        self.owners = lax.axis_size("expert")
        self.groups = lax.axis_size("dp")
        self.count, self.width = tokens.shape
        self.top = routes.shape[1]
        self.local = w_gate.shape[0]
        self.hidden = w_gate.shape[2]
        self.experts = self.owners * self.local
        self.cap = saved_gate.shape[3]
        self.cap_rows = round_up(self.cap, 8)
        self.split = 2 if self.groups % 2 == 0 and self.local % 2 == 0 else 1
        self.mine = self.local // self.split
        self.meta = round_up(3 * self.experts, LANES)
        self.blocks = self.split * self.owners
        self.source_rows = self.owners * self.cap_rows
        self.expert_rows = self.split * self.source_rows
        self.paired = self.owners & (self.owners - 1) == 0
        self.sent = self.width + self.meta
        self.rows = self.mine * self.expert_rows
        self.cols = self.blocks * self.count

    def peer(self, index, step, core):
        bits = self.owners.bit_length() - 1
        if self.owners != 1 << bits:
            return (index + step) % self.owners
        turned = sum(((step >> i) & 1) << (bits - 1 - i) for i in range(bits))
        return index ^ (step + (turned - step) * core)

    def over_expert(self, x, step, back=False):
        pairs = []
        for group in range(self.groups):
            for i in range(self.owners):
                near = group * self.owners + i
                far = self.peer(i, step, group % self.split) + group * self.owners
                pairs.append((near, far) if back else (far, near))
        return lax.ppermute(x, ("dp", "expert"), pairs)

    def over_pair(self, x):
        return lax.ppermute(x, "dp", [(i, i ^ 1) for i in range(self.groups)])


def pack_body(plan, x_hbm, routes_hbm, factors_hbm, out_ref, routes_ref, factors_ref, sems):
    experts, count = plan.experts, plan.count
    x_copy = pltpu.make_async_copy(x_hbm, out_ref.at[:, : plan.width], sems.at[0])
    small = [
        pltpu.make_async_copy(routes_hbm, routes_ref, sems.at[1]),
        pltpu.make_async_copy(factors_hbm, factors_ref, sems.at[2]),
    ]
    for copy in (*small, x_copy):
        copy.start()
    for copy in small:
        copy.wait()
    lane = iota((plan.meta, count), 0)
    chosen = jnp.zeros((plan.meta, count), F32)
    parts = jnp.zeros((plan.meta, count), F32)
    for k in range(plan.top):
        route = routes_ref[k : k + 1, :]
        factor = factors_ref[k : k + 1, :]
        high = factor.astype(BF16).astype(F32)
        low = factor - high
        chosen = chosen + jnp.where(lane == route, 1.0, 0.0)
        parts = parts + jnp.where(lane == route + experts, high, 0.0)
        parts = parts + jnp.where(lane == route + 2 * experts, low, 0.0)
    earlier = jnp.where(iota((count, count), 0) < iota((count, count), 1), 1.0, 0.0)
    before = dot(chosen.astype(BF16), earlier.astype(BF16))
    facts = (chosen * (before + 1.0) + parts).astype(BF16)
    shape = (plan.meta, plan.meta)
    same = jnp.where(iota(shape, 0) == iota(shape, 1), 1.0, 0.0).astype(BF16)
    out_ref[:, plan.width :] = dot_ta(facts, same).astype(BF16)
    x_copy.wait()


def pack_scratch(plan):
    return [
        pltpu.VMEM((plan.top, plan.count), jnp.int32),
        pltpu.VMEM((plan.top, plan.count), F32),
        pltpu.SemaphoreType.DMA((3,)),
    ]


def pack(plan, x, routes, factors):
    return pl.pallas_call(
        functools.partial(pack_body, plan),
        out_shape=jax.ShapeDtypeStruct((plan.count, plan.width + plan.meta), BF16),
        in_specs=[hbm()] * 3,
        out_specs=vmem(),
        scratch_shapes=pack_scratch(plan),
        compiler_params=pltpu.CompilerParams(vmem_limit_bytes=4 * MIB),
        name="pack",
    )(in_hbm(x), in_hbm(routes.T), in_hbm(factors.T))


def first_expert(plan):
    core = lax.rem(lax.axis_index("dp"), plan.split)
    return lax.axis_index("expert") * plan.local + core * plan.mine, core * plan.mine


def tables(plan, meta, first):
    me = lax.axis_index("expert")
    core = lax.rem(lax.axis_index("dp"), plan.split)
    row = iota((plan.rows, plan.meta), 0)
    lane = iota((plan.rows, plan.meta), 1)
    expert = first + row // plan.expert_rows
    pick_slot = jnp.where(lane == expert, 1.0, 0.0).astype(BF16)
    pick_part = jnp.where(
        (lane == expert + plan.experts) | (lane == expert + 2 * plan.experts), 1.0, 0.0
    ).astype(BF16)
    slot = dot_tb(pick_slot, meta)
    part = dot_tb(pick_part, meta)
    shape = (plan.rows, plan.cols)
    row = iota(shape, 0)
    col = iota(shape, 1)
    block = col // plan.count
    group = block // plan.owners
    source = plan.peer(me, block % plan.owners, core ^ group)
    place = row % plan.expert_rows
    want = (row % plan.cap_rows + 1).astype(F32)
    same = (place // plan.cap_rows) == group * plan.owners + source
    hit = same & (slot == want)
    factor = jnp.sum(jnp.where(hit, part, 0.0), axis=1, keepdims=True)
    return jnp.where(hit, 1.0, 0.0).astype(BF16), factor


def weight_copies(plan, array, ref, sems):
    offset = first_expert(plan)[1]
    copies = [
        pltpu.make_async_copy(array.at[offset + e], ref.at[e], sems.at[e])
        for e in range(plan.mine)
    ]
    for copy in copies:
        copy.start()
    return copies


def prepare_kernel(plan, x_hbm, routes_hbm, factors_hbm, gate_hbm, up_hbm, after, *refs):
    packed_ref, done_ref, own_ref = refs[:3]
    other_ref = refs[3] if plan.split > 1 else None
    gate_s, up_s, saved_sems, routes_ref, factors_ref, pack_sems = refs[plan.split + 2 :]
    done_ref[...] = jnp.zeros_like(done_ref)
    saved = [
        pltpu.make_async_copy(gate_hbm, gate_s, saved_sems.at[0]),
        pltpu.make_async_copy(up_hbm, up_s, saved_sems.at[1]),
    ]
    for copy in saved:
        copy.start()
    pack_body(
        plan, x_hbm, routes_hbm, factors_hbm, packed_ref, routes_ref, factors_ref, pack_sems
    )
    _, offset = first_expert(plan)
    shape = (plan.mine * plan.source_rows, gate_s.shape[0])
    row, col = iota(shape, 0), iota(shape, 1)
    slot = row % plan.cap_rows
    source = row % plan.source_rows // plan.cap_rows
    place = (source * plan.cap + slot) * plan.local + row // plan.source_rows
    place = jnp.where(slot < plan.cap, place, -plan.local)

    def pick(start, ref):
        table = jnp.where(col == place + start, 1.0, 0.0).astype(BF16)
        return dot(table, ref[...]).astype(BF16)

    for copy in saved:
        copy.wait()
    own_ref[0] = pick(offset, gate_s)
    own_ref[1] = pick(offset, up_s)
    if other_ref is not None:
        other_ref[0] = pick(plan.mine - offset, gate_s)
        other_ref[1] = pick(plan.mine - offset, up_s)


def prepare(plan, x, routes, factors, saved_gate, saved_up, after):
    flat = (plan.owners * plan.cap * plan.local, plan.hidden)

    def flatten(saved):
        return in_hbm(jnp.swapaxes(saved[0], 1, 2).reshape(flat))

    part = jax.ShapeDtypeStruct((2, plan.mine * plan.source_rows, plan.hidden), BF16)
    packed_shape = jax.ShapeDtypeStruct((plan.count, plan.sent), BF16)
    done_shape = jax.ShapeDtypeStruct((16, plan.sent), BF16)
    out_shape = [packed_shape, done_shape] + [part] * plan.split
    packed, done, *saved = pl.pallas_call(
        functools.partial(prepare_kernel, plan),
        out_shape=out_shape,
        in_specs=[hbm()] * 5 + [pl.BlockSpec(memory_space=pl.ANY)],
        out_specs=[vmem()] * len(out_shape),
        scratch_shapes=[
            pltpu.VMEM(flat, BF16),
            pltpu.VMEM(flat, BF16),
            pltpu.SemaphoreType.DMA((2,)),
            *pack_scratch(plan),
        ],
        compiler_params=pltpu.CompilerParams(vmem_limit_bytes=8 * MIB),
        cost_estimate=pl.CostEstimate(
            flops=0, bytes_accessed=plan.owners * plan.width * plan.sent, transcendentals=0
        ),
        name="prepare",
    )(
        in_hbm(x),
        in_hbm(routes.T),
        in_hbm(factors.T),
        flatten(saved_gate),
        flatten(saved_up),
        after,
    )
    return packed, saved, done


def fetch_kernel(plan, w_hbm, after, w_ref, done_ref, sems):
    copies = weight_copies(plan, w_hbm, w_ref, sems)
    done_ref[...] = jnp.zeros_like(done_ref)
    for copy in copies:
        copy.wait()


def fetch(plan, w, after):
    return pl.pallas_call(
        functools.partial(fetch_kernel, plan),
        out_shape=(
            pltpu.VMEM((plan.mine, plan.hidden, plan.width), BF16),
            jax.ShapeDtypeStruct((16, plan.sent), BF16),
        ),
        in_specs=[hbm(), pl.BlockSpec(memory_space=pl.ANY)],
        out_specs=(vmem(), vmem()),
        scratch_shapes=[pltpu.SemaphoreType.DMA((plan.mine,))],
        compiler_params=pltpu.CompilerParams(vmem_limit_bytes=MIB),
        cost_estimate=pl.CostEstimate(
            flops=0,
            bytes_accessed=2 * plan.mine * plan.hidden * plan.width * 2,
            transcendentals=0,
        ),
        name="fetch",
    )(in_hbm(w), after)


def arrived(plan, blocks, first):
    left, metas, rows = plan.cols, [], []
    for block in blocks:
        count = min(left, block.shape[0])
        metas.append(block[:count, plan.width :])
        rows.append(block[:count, : plan.width])
        left -= count
    table, factor = tables(plan, jnp.concatenate(metas, axis=0), first)
    return table, factor, jnp.concatenate(rows, axis=0)


def forward_kernel(plan, count, *refs):
    blocks, refs = refs[:count], refs[count:]
    gate_ref, up_hbm, down_hbm, *refs = refs
    outs, (up_s, down_s, x_s, y_s, gate_s, sems) = refs[:-6], refs[-6:]
    first, _ = first_expert(plan)
    up_copies = weight_copies(plan, up_hbm, up_s, sems.at[0])
    down_copies = weight_copies(plan, down_hbm, down_s, sems.at[1])
    table, factor, rows = arrived(plan, blocks, first)
    x_s[...] = dot(table, rows).astype(BF16)
    n = plan.expert_rows
    for e in range(plan.mine):
        gate_s[e] = dot_tb(x_s[e * n : (e + 1) * n, :], gate_ref[e])
    for e in range(plan.mine):
        up_copies[e].wait()
        up = dot_tb(x_s[e * n : (e + 1) * n, :], up_s[e])
        gate = gate_s[e]
        hidden = (gate / (1.0 + jnp.exp(-gate)) * up).astype(BF16)
        down_copies[e].wait()
        out = dot(hidden, down_s[e])
        y_s[e * n : (e + 1) * n, :] = (out * factor[e * n : (e + 1) * n]).astype(BF16)
    put_rows(plan, outs, slice(None), dot_ta(table, y_s[...]).astype(BF16))


def put_rows(plan, outs, columns, rows):
    start = 0
    for out in outs:
        stop = start + out.shape[0]
        out[:, columns] = rows[start:stop, :]
        start = stop


def backward_kernel(plan, count, *refs):
    blocks, refs = refs[:count], refs[count:]
    saved_ref, other_ref, refs = refs[0], refs[plan.split - 1], refs[plan.split :]
    gate_ref, up_hbm, down_hbm, *refs = refs
    held = plan.source_rows
    outs, (up_s, down_s, x_s, y_s, score_s, sems) = refs[:-6], refs[-6:]
    first, offset = first_expert(plan)
    copies = []
    for e in range(plan.mine):
        for i, (array, slot) in enumerate(((down_hbm, down_s), (up_hbm, up_s))):
            copy = pltpu.make_async_copy(array.at[offset + e], slot.at[e], sems.at[i, e])
            copy.start()
            copies.append(copy)
    table, factor, rows = arrived(plan, blocks, first)
    x_s[...] = dot(table, rows).astype(BF16)
    n = plan.expert_rows
    lane = iota((n, plan.meta), 1)
    for e in range(plan.mine):
        x = x_s[e * n : (e + 1) * n, :]
        own = slice(e * held, (e + 1) * held)
        act, up = saved_ref[0, own, :], saved_ref[1, own, :]
        if plan.split > 1:
            act = jnp.concatenate([act, other_ref[0, own, :]], axis=0)
            up = jnp.concatenate([up, other_ref[1, own, :]], axis=0)
        act, up = act.astype(F32), up.astype(F32)
        sig = 1.0 / (1.0 + jnp.exp(-act))
        silu = act * sig
        copies[2 * e].wait()
        grad = dot_tb(x, down_s[e])
        score = jnp.sum(silu * up * grad, axis=1, keepdims=True)
        grad_gate = (grad * up * sig * (1.0 + act * (1.0 - sig))).astype(BF16)
        grad_up = (grad * silu).astype(BF16)
        result = dot(grad_gate, gate_ref[e])
        copies[2 * e + 1].wait()
        result = result + dot(grad_up, up_s[e])
        y_s[e * n : (e + 1) * n, :] = (result * factor[e * n : (e + 1) * n]).astype(BF16)
        expert = first + e
        high = score.astype(BF16).astype(F32)
        middle = (score - high).astype(BF16).astype(F32)
        low = score - high - middle
        spread = jnp.where(lane == expert, high, 0.0)
        spread = jnp.where(lane == expert + plan.experts, middle, spread)
        spread = jnp.where(lane == expert + 2 * plan.experts, low, spread)
        score_s[e * n : (e + 1) * n, :] = spread.astype(BF16)
    put_rows(plan, outs, slice(0, plan.width), dot_ta(table, y_s[...]).astype(BF16))
    scores = dot_ta(table, score_s[...]).astype(BF16)
    put_rows(plan, outs, slice(plan.width, plan.width + plan.meta), scores)


def part_shapes(plan, width):
    block = jax.ShapeDtypeStruct((plan.count, width), BF16)
    other = jax.ShapeDtypeStruct((plan.owners * plan.count, width), BF16)
    return [block] * plan.owners + [other] * (plan.split - 1)


def expert_call(plan, kernel, name, inputs, gate, up_hbm, down_hbm, width, scratch):
    shapes = part_shapes(plan, width)
    weight = pltpu.VMEM((plan.mine, plan.hidden, plan.width), BF16)
    rows = pltpu.VMEM((plan.rows, plan.width), BF16)
    return pl.pallas_call(
        kernel,
        out_shape=shapes,
        in_specs=[vmem()] * (len(inputs) + 1) + [hbm()] * 2,
        out_specs=[vmem()] * len(shapes),
        scratch_shapes=[
            *[weight, weight, rows, rows],
            scratch,
            pltpu.SemaphoreType.DMA((2, plan.mine)),
        ],
        compiler_params=pltpu.CompilerParams(vmem_limit_bytes=36 * MIB),
        cost_estimate=pl.CostEstimate(
            flops=2 * 3 * plan.mine * plan.expert_rows * plan.width * plan.hidden,
            bytes_accessed=2 * 2 * plan.mine * plan.width * plan.hidden,
            transcendentals=0,
        ),
        name=name,
    )(*inputs, in_vmem(gate), in_hbm(up_hbm), in_hbm(down_hbm))


def forward(plan, blocks, *weights):
    kernel = functools.partial(forward_kernel, plan, len(blocks))
    gates = pltpu.VMEM((plan.mine, plan.expert_rows, plan.hidden), F32)
    return expert_call(plan, kernel, "forward", blocks, *weights, plan.width, gates)


def backward(plan, blocks, saved, *weights):
    kernel = functools.partial(backward_kernel, plan, len(blocks))
    scores = pltpu.VMEM((plan.rows, plan.meta), BF16)
    inputs = [*blocks, *saved]
    return expert_call(plan, kernel, "backward", inputs, *weights, plan.sent, scores)


def gather_group(plan, block):
    return [block] + [plan.over_expert(block, d) for d in range(1, plan.owners)]


def sum_pair(plan, parts):
    own = [[p] for p in parts[: plan.owners]]
    if plan.split > 1:
        other = plan.over_pair(parts[plan.owners])
        for d in range(plan.owners):
            own[d].append(other[d * plan.count : (d + 1) * plan.count])
    return own


def total(terms):
    return sum(t.astype(F32) for t in terms)


def scatter_group(plan, own):
    sent = [total(own[d]).astype(BF16) for d in range(1, plan.owners)]
    return own[0] + [plan.over_expert(x, d, True) for d, x in enumerate(sent, 1)]


def scatter_steps(plan, own):
    if not plan.paired:
        return scatter_group(plan, own)
    step = 1
    while step < plan.owners:
        away = [d for d in range(0, plan.owners, step) if d & step]
        sent = jnp.concatenate([total(own[d]).astype(BF16) for d in away])
        back = plan.over_expert(sent, step, True)
        for i, d in enumerate(away):
            own[d ^ step].append(back[i * plan.count : (i + 1) * plan.count])
        step *= 2
    return own[0]


def finish_kernel(plan, count, *refs):
    parts, (routes_ref, out_hbm, score_hbm, out_s, score_s, sems) = refs[:count], refs[count:]
    whole = parts[0][: plan.count, :].astype(F32)
    for part in parts[1:]:
        whole = whole + part[: plan.count, :].astype(F32)
    out_s[...] = whole[:, : plan.width].astype(BF16)
    out_copy = pltpu.make_async_copy(out_s, out_hbm, sems.at[0])
    out_copy.start()
    shape = (plan.meta, plan.meta)
    same = jnp.where(iota(shape, 0) == iota(shape, 1), 1.0, 0.0).astype(BF16)
    spread = dot_tb(same, whole[:, plan.width :].astype(BF16))
    experts = plan.experts
    score = spread[:experts] + spread[experts : 2 * experts] + spread[2 * experts : 3 * experts]
    row = iota((experts, plan.count), 0)
    for k in range(plan.top):
        hit = row == routes_ref[k : k + 1, :]
        score_s[k : k + 1, :] = jnp.sum(jnp.where(hit, score, 0.0), axis=0, keepdims=True)
    score_copy = pltpu.make_async_copy(score_s, score_hbm, sems.at[1])
    score_copy.start()
    out_copy.wait()
    score_copy.wait()


def finish_back(plan, parts, routes):
    out, score = pl.pallas_call(
        functools.partial(finish_kernel, plan, len(parts)),
        out_shape=(
            jax.ShapeDtypeStruct((plan.count, plan.width), BF16),
            jax.ShapeDtypeStruct((plan.top, plan.count), F32),
        ),
        in_specs=[vmem()] * (len(parts) + 1),
        out_specs=(hbm(), hbm()),
        scratch_shapes=[
            pltpu.VMEM((plan.count, plan.width), BF16),
            pltpu.VMEM((plan.top, plan.count), F32),
            pltpu.SemaphoreType.DMA((2,)),
        ],
        compiler_params=pltpu.CompilerParams(vmem_limit_bytes=8 * MIB),
        name="finish",
    )(*parts, routes.T)
    return out, score.T


def body(
    tokens,
    routes,
    weights_fwd,
    cotangent,
    routes_back,
    weights_back,
    saved_gate,
    saved_up,
    w_gate,
    w_up,
    w_down,
):
    plan = Plan(tokens, routes, saved_gate, w_gate)
    packed = pack(plan, tokens, routes, weights_fwd)
    packed_back, saved, ready = prepare(
        plan, cotangent, routes_back, weights_back, saved_gate, saved_up, packed
    )
    gate_hbm, up_hbm = jnp.swapaxes(w_gate, 1, 2), jnp.swapaxes(w_up, 1, 2)
    if plan.paired and plan.owners > 1:
        blocks = [packed, plan.over_expert(packed, 1)]
        gate, done = fetch(plan, gate_hbm, blocks[1])
        step = 2
        while step < plan.owners:
            blocks.append(plan.over_expert(jnp.concatenate(blocks) + ready[:1], step))
            step *= 2
    else:
        blocks = gather_group(plan, packed)
        gate, done = fetch(plan, gate_hbm, packed)
    if plan.split > 1:
        blocks.append(plan.over_pair(jnp.concatenate(blocks) + done[:1]))
    blocks_back = gather_group(plan, packed_back)
    parts = forward(plan, blocks, gate, up_hbm, w_down)
    parts, blocks_back = lax.optimization_barrier((parts, blocks_back))
    if plan.split > 1:
        blocks_back = blocks_back + [plan.over_pair(jnp.concatenate(blocks_back))]
        saved[1] = plan.over_pair(saved[1])
    terms = scatter_group(plan, sum_pair(plan, parts))
    parts_back = backward(plan, blocks_back, saved, gate, up_hbm, w_down)
    parts_back, terms = lax.optimization_barrier((parts_back, terms))
    mixed = total(terms).astype(BF16)
    terms_back = scatter_steps(plan, sum_pair(plan, parts_back))
    input_grad, weight_grad = finish_back(plan, terms_back, routes_back)
    return (mixed, input_grad, weight_grad)


def solution(mesh):
    spec = P(("dp", "expert"), None)
    saved = P("dp", None, "expert", None, None)
    weight = P("expert", None, None)
    return jax.shard_map(
        body,
        mesh=mesh,
        in_specs=(spec,) * 6 + (saved,) * 2 + (weight,) * 3,
        out_specs=(spec,) * 3,
        check_vma=False,
    )
```

time: 70.1 us -> 69.1 us (0.986)
  Pallas kernels: 33.1 us -> 37.8 us
  other arithmetic: 4.63 us -> 1.19 us
  local copies, waits for them, and re-layouts: 3.24 us -> 0.12 us
  waiting for transfers between devices: 10.5 us -> 11.7 us
    pallas_call x5 -> x6, Pallas kernels: 33.1 us -> 37.8 us  [the longest x2 29.9 us: expert_call(): pl.pallas_call(kernel, out_shape=shapes, in_specs=[vmem()] * (len(inputs)...]
    add x5 -> x2, other arithmetic: 2.74 us -> 0.15 us  [the longest x1 0.1 us: body(): blocks.append(plan.over_pair(jnp.concatenate(blocks) + done[:1]))]
    transpose x1 -> x0, local copies, waits for them, and re-layouts: 1.7 us -> none  [piece(): jnp.swapaxes(rows, 0, 1)]
    ppermute x12 -> x10, waiting for transfers between devices: 7.3 us -> 8.51 us  [over_expert(): return lax.ppermute(x, ('dp', 'expert'), pairs)]
    ppermute x8 -> x5, starting transfers between devices: 2.05 us -> 0.85 us  [over_pair(): return lax.ppermute(x, 'dp', [(i, i ^ 1) for i in range(self.groups)])]
    slice x3, local copies, waits for them, and re-layouts: 1.19 us -> 0.09 us  [the longest x1 0.04 us: body(): blocks.append(plan.over_expert(jnp.concatenate(blocks) + ready[:1], step))]
    ppermute x12 -> x10, starting transfers between devices: 15.3 us -> 16.3 us  [over_expert(): return lax.ppermute(x, ('dp', 'expert'), pairs)]
    reduce_sum x2 -> x0, other arithmetic: 0.81 us -> none  [the longest x1 0.77 us: finish_back(): score = jnp.sum(jnp.where(hit, spread[None], 0.0), axis=2).T]
  transfers between devices with their start and end apart: 20 -> 15, of which waited for: 5 -> 6; matrix products, arithmetic and copies ran while one was open for 9% -> 1% of each run, Pallas kernels for 46% -> 52%
where the time goes in v4:
time: 69.1 us; the launch traced here: 68.9 us
  Pallas kernels  37.8 us (55%)
  starting transfers between devices  17.1 us (25%)
  waiting for transfers between devices  11.7 us (17%)
  other arithmetic  1.19 us (2%)
  between operations  0.99 us (1%)
    pallas_call x2, Pallas kernels, expert_call(): pl.pallas_call(kernel, out_shape=shapes, in_specs=[vmem()] * (len(inputs)...  29.9 us
    ppermute x10, starting transfers between devices, over_expert(): return lax.ppermute(x, ('dp', 'expert'), pairs)  16.3 us
    ppermute x10, waiting for transfers between devices, over_expert(): return lax.ppermute(x, ('dp', 'expert'), pairs)  8.51 us
    pallas_call x1, Pallas kernels, fetch(): pl.pallas_call(functools.partial(fetch_kernel, plan), out_shape=(pltpu.VM...  4.4 us
    ppermute x5, waiting for transfers between devices, over_pair(): return lax.ppermute(x, 'dp', [(i, i ^ 1) for i in range(self.groups)])  3.16 us
    pallas_call x1, Pallas kernels, prepare(): pl.pallas_call(functools.partial(prepare_kernel, plan), out_shape=out_sha...  1.59 us
  transfers between devices with their start and end apart: 15, of which 6 were waited for; matrix products, arithmetic and copies ran while one was open for 1% of the time, Pallas kernels for 52%

profile of v4, /device:TPU:0, one launch (start us, length us, event | category | flops | bytes accessed | tf_op | source)
XLA Modules:
  0.0 68.9 jit_solution(18284804135968972441)
XLA Ops:
  0.6 1.1 %pack.1.after.refs_0_ = bf16[32,2176]{1,0:T(8,128)(2,1)S(1)} custom-call(bf16[32,2048]{1,0:T(8,128)(2,1)} %x_hbm.2, s32[6,32]{1,0:T(8,128)} %bitcast.24, f32[6,32]{1,0:T(8,128)} %bitcast.25), custom_call_target="tpu_custom_call" | custom-call | tf_op jit(solution)/shard_map/pack/pallas_call | solution.py:133
  1.7 3.0 %collective-permute-start = (bf16[32,2176]{1,0:T(8,128)(2,1)S(1)}, bf16[32,2176]{1,0:T(8,128)(2,1)S(1)}, u32[]{:S(2)}, u32[]{:S(2)}) collective-permute-start(bf16[32,2176]{1,0:T(8,128)(2,1)S(1)} %pack.1.after.refs_0_), channel_id=1, source_target_pairs={{1,0},{0,1},{3,2},{2,3},{6,4},{7,5},{4,6},{5,7},{9,8},{8,9},{11,10... | collective-permute-start | bytes 417800 | tf_op jit(solution)/shard_map/ppermute | solution.py:87
  4.7 1.6 %prepare.1 = (bf16[32,2176]{1,0:T(8,128)(2,1)S(1)}, bf16[16,2176]{1,0:T(8,128)(2,1)S(1)}, bf16[2,128,704]{2,1,0:T(8,128)(2,1)S(1)}, bf16[2,128,704]{2,1,0:T(8,128)(2,1)S(1)}) custom-call(bf16[32,2048]{1,0:T(8,128)(2,1)} %x_hbm.3, s32[6,32]{1,0:T(8,128)} %bitcast.17, f32[6,32]{1,0:T(8,128)} %bitcast.26, bf16[224,704]{1,0:T(8,128)(2,1)} %bitcast.22, ...), custom_call_target="tpu_custom_call" | custom-call | bytes 17825792 | tf_op jit(solution)/shard_map/prepare/pallas_call | solution.py:231
  6.3 1.4 %collective-permute-done.after.refs_1_ = bf16[32,2176]{1,0:T(8,128)(2,1)S(1)} collective-permute-done((bf16[32,2176]{1,0:T(8,128)(2,1)S(1)}, bf16[32,2176]{1,0:T(8,128)(2,1)S(1)}, u32[]{:S(2)}, u32[]{:S(2)}) %collective-permute-start) | collective-permute-done | bytes 139296 | tf_op jit(solution)/shard_map/ppermute | solution.py:87
  7.8 2.1 %collective-permute-start.1 = (bf16[64,2176]{1,0:T(8,128)(2,1)S(1)}, bf16[64,2176]{1,0:T(8,128)(2,1)S(1)}, u32[]{:S(2)}, u32[]{:S(2)}) collective-permute-start(bf16[64,2176]{1,0:T(8,128)(2,1)S(1)} %maximum_add_fusion.1), channel_id=1, source_target_pairs={{2,0},{3,1},{0,2},{1,3},{5,4},{4,5},{7,6},{6,7},{10,8},{11,9},{8,1... | collective-permute-start | bytes 835592 | tf_op jit(solution)/shard_map/ppermute | solution.py:87
  9.9 4.4 %fetch.1 = (bf16[4,704,2048]{2,1,0:T(8,128)(2,1)S(1)}, bf16[16,2176]{1,0:T(8,128)(2,1)S(1)}) custom-call(bf16[8,704,2048]{2,1,0:T(8,128)(2,1)} %bitcast.21, bf16[32,2176]{1,0:T(8,128)(2,1)S(1)} %collective-permute-done.after.refs_1_), custom_call_target="tpu_custom_call" | custom-call | bytes 23068672 | tf_op jit(solution)/shard_map/fetch/pallas_call | solution.py:266
  14.4 0.1 maximum_add_fusion
  14.6 3.0 %collective-permute-start.5 = (bf16[32,2176]{1,0:T(8,128)(2,1)S(1)}, bf16[32,2176]{1,0:T(8,128)(2,1)S(1)}, u32[]{:S(2)}, u32[]{:S(2)}) collective-permute-start(bf16[32,2176]{1,0:T(8,128)(2,1)S(1)} %get-tuple-element.49.refs_0_), channel_id=1, source_target_pairs={{3,0},{2,1},{1,2},{0,3},{7,4},{6,5},{5,6},{4,7},{11,8},{10,9},{9,1... | collective-permute-start | bytes 417800 | tf_op jit(solution)/shard_map/ppermute | solution.py:87
  17.6 0.5 collective-permute-start.4
  18.1 0.1 collective-permute-start.3
  18.3 15.9 %forward.1 = (bf16[32,2048]{1,0:T(8,128)(2,1)S(1)}, bf16[32,2048]{1,0:T(8,128)(2,1)S(1)}, bf16[32,2048]{1,0:T(8,128)(2,1)S(1)}, bf16[32,2048]{1,0:T(8,128)(2,1)S(1)}, bf16[128,2048]{1,0:T(8,128)(2,1)S(1)}) custom-call(bf16[32,2176]{1,0:T(8,128)(2,1)S(1)} %pack.1.after.refs_0_, bf16[32,2176]{1,0:T(8,128)(2,1)S(1)} %collective-permute-done.after.refs_1_, ...), custom_call_target="tpu_custom_call" | custom-call | flops 2214592512 | bytes 23068672 | tf_op jit(solution)/shard_map/forward/pallas_call | solution.py:386
  34.3 0.6 collective-permute-start.6
  34.9 1.2 %collective-permute-done.8 = bf16[128,2048]{1,0:T(8,128)(2,1)S(1)} collective-permute-done((bf16[128,2048]{1,0:T(8,128)(2,1)S(1)}, bf16[128,2048]{1,0:T(8,128)(2,1)S(1)}, u32[]{:S(2)}, u32[]{:S(2)}) %collective-permute-start.8) | collective-permute-done | bytes 524320 | tf_op jit(solution)/shard_map/ppermute | solution.py:90
  36.2 2.9 %collective-permute-start.11 = (bf16[32,2048]{1,0:T(8,128)(2,1)S(1)}, bf16[32,2048]{1,0:T(8,128)(2,1)S(1)}, u32[]{:S(2)}, u32[]{:S(2)}) collective-permute-start(bf16[32,2048]{1,0:T(8,128)(2,1)S(1)} %get-tuple-element.79), channel_id=1, source_target_pairs={{0,3},{1,2},{2,1},{3,0},{4,7},{5,6},{6,5},{7,4},{8,11},{9,10},{10,... | collective-permute-start | bytes 393224 | tf_op jit(solution)/shard_map/ppermute | solution.py:87
  39.2 0.5 collective-permute-start.10
  39.7 0.1 collective-permute-start.9
  39.8 14.1 %backward.1 = (bf16[32,2176]{1,0:T(8,128)(2,1)S(1)}, bf16[32,2176]{1,0:T(8,128)(2,1)S(1)}, bf16[32,2176]{1,0:T(8,128)(2,1)S(1)}, bf16[32,2176]{1,0:T(8,128)(2,1)S(1)}, bf16[128,2176]{1,0:T(8,128)(2,1)S(1)}) custom-call(bf16[32,2176]{1,0:T(8,128)(2,1)S(1)} %get-tuple-element.49.refs_0_, bf16[32,2176]{1,0:T(8,128)(2,1)S(1)} %collective-permute-done.3.refs_1_, ...), custom_call_target="tpu_custom_call" | custom-call | flops 2214592512 | bytes 23068672 | tf_op jit(solution)/shard_map/backward/pallas_call | solution.py:386
  54.0 1.9 %collective-permute-done.12 = bf16[128,2176]{1,0:T(8,128)(2,1)S(1)} collective-permute-done((bf16[128,2176]{1,0:T(8,128)(2,1)S(1)}, bf16[128,2176]{1,0:T(8,128)(2,1)S(1)}, u32[]{:S(2)}, u32[]{:S(2)}) %collective-permute-start.12) | collective-permute-done | bytes 557088 | tf_op jit(solution)/shard_map/ppermute | solution.py:90
  56.1 1.9 %collective-permute-start.13 = (bf16[64,2176]{1,0:T(8,128)(2,1)S(1)}, bf16[64,2176]{1,0:T(8,128)(2,1)S(1)}, u32[]{:S(2)}, u32[]{:S(2)}) collective-permute-start(bf16[64,2176]{1,0:T(8,128)(2,1)S(1)} %pad_maximum_fusion.1), channel_id=1, source_target_pairs={{0,1},{1,0},{2,3},{3,2},{4,6},{5,7},{6,4},{7,5},{8,9},{9,8},{10,11... | collective-permute-start | bytes 835592 | tf_op jit(solution)/shard_map/ppermute | solution.py:87
  58.0 4.7 %collective-permute-done.13 = bf16[64,2176]{1,0:T(8,128)(2,1)S(1)} collective-permute-done((bf16[64,2176]{1,0:T(8,128)(2,1)S(1)}, bf16[64,2176]{1,0:T(8,128)(2,1)S(1)}, u32[]{:S(2)}, u32[]{:S(2)}) %collective-permute-start.13) | collective-permute-done | bytes 278560 | tf_op jit(solution)/shard_map/ppermute | solution.py:87
  62.8 2.0 %collective-permute-start.14 = (bf16[32,2176]{1,0:T(8,128)(2,1)S(1)}, bf16[32,2176]{1,0:T(8,128)(2,1)S(1)}, u32[]{:S(2)}, u32[]{:S(2)}) collective-permute-start(bf16[32,2176]{1,0:T(8,128)(2,1)S(1)} %add_convert_fusion), channel_id=1, source_target_pairs={{0,2},{1,3},{2,0},{3,1},{4,5},{5,4},{6,7},{7,6},{8,10},{9,11},{10,... | collective-permute-start | bytes 417800 | tf_op jit(solution)/shard_map/ppermute | solution.py:87
  64.7 0.7 %add_convert_fusion.3 = bf16[32,2048]{1,0:T(8,128)(2,1)} fusion(bf16[32,2048]{1,0:T(8,128)(2,1)S(1)} %collective-permute-done.11, bf16[32,2048]{1,0:T(8,128)(2,1)S(1)} %collective-permute-done.10, bf16[32,2048]{1,0:T(8,128)(2,1)S(1)} %collective-permute-done.9, bf16[32,2048]{1,0:T(8,128)(2,1)S(1)} %slice-done, bf16[32,2048]{1,0:T(8,128)(2,1)S(1)} %get-tuple-element.65), kind=kLoop, calls=%fused_computation.7 | loop fusion | flops 655360 | bytes 786432 | tf_op jit(solution)/shard_map/convert_element_type | solution.py:538
  65.5 2.4 %collective-permute-done.14.refs_3_ = bf16[32,2176]{1,0:T(8,128)(2,1)S(1)} collective-permute-done((bf16[32,2176]{1,0:T(8,128)(2,1)S(1)}, bf16[32,2176]{1,0:T(8,128)(2,1)S(1)}, u32[]{:S(2)}, u32[]{:S(2)}) %collective-permute-start.14) | collective-permute-done | bytes 139296 | tf_op jit(solution)/shard_map/ppermute | solution.py:87
  67.9 0.8 %finish.1 = (bf16[32,2048]{1,0:T(8,128)(2,1)}, f32[6,32]{1,0:T(8,128)}) custom-call(bf16[32,2176]{1,0:T(8,128)(2,1)S(1)} %get-tuple-element.70.refs_0_, bf16[32,2176]{1,0:T(8,128)(2,1)S(1)} %slice.52.refs_1_, bf16[32,2176]{1,0:T(8,128)(2,1)S(1)} %slice.55.refs_2_, bf16[32,2176]{1,0:T(8,128)(2,1)S(1)} %collective-permute-done.14.refs_3_, s32[6,32]{1,0:T(8,128)S(1)} %bitcast.18), custom_call_target="tpu_custom_call" | custom-call | tf_op jit(solution)/shard_map/finish/pallas_call | solution.py:479
  (30 shorter events, 0.9 us)
Async XLA Ops:
  1.7 6.0 %collective-permute-start = (bf16[32,2176]{1,0:T(8,128)(2,1)S(1)}, bf16[32,2176]{1,0:T(8,128)(2,1)S(1)}, u32[]{:S(2)}, u32[]{:S(2)}) collective-permute-start(bf16[32,2176]{1,0:T(8,128)(2,1)S(1)} %pack.1.after.refs_0_), channel_id=1, source_target_pairs={{1,0},{0,1},{3,2},{2,3},{6,4},{7,5},{4,6},{5,7},{9,8},{8,9},{11,10... | collective-permute-start | bytes 417800 | tf_op jit(solution)/shard_map/ppermute | solution.py:87
  7.8 6.6 %collective-permute-start.1 = (bf16[64,2176]{1,0:T(8,128)(2,1)S(1)}, bf16[64,2176]{1,0:T(8,128)(2,1)S(1)}, u32[]{:S(2)}, u32[]{:S(2)}) collective-permute-start(bf16[64,2176]{1,0:T(8,128)(2,1)S(1)} %maximum_add_fusion.1), channel_id=1, source_target_pairs={{2,0},{3,1},{0,2},{1,3},{5,4},{4,5},{7,6},{6,7},{10,8},{11,9},{8,1... | collective-permute-start | bytes 835592 | tf_op jit(solution)/shard_map/ppermute | solution.py:87
  14.5 3.7 %collective-permute-start.2 = (bf16[128,2176]{1,0:T(8,128)(2,1)S(1)}, bf16[128,2176]{1,0:T(8,128)(2,1)S(1)}, u32[]{:S(2)}, u32[]{:S(2)}) collective-permute-start(bf16[128,2176]{1,0:T(8,128)(2,1)S(1)} %maximum_add_fusion), channel_id=1, source_target_pairs={{0,4},{4,0},{8,12},{12,8},{16,20},{20,16},{24,28},{28,24},{1,5},{5... | collective-permute-start | bytes 1671176 | tf_op jit(solution)/shard_map/ppermute | solution.py:90
  14.6 19.5 %collective-permute-start.5 = (bf16[32,2176]{1,0:T(8,128)(2,1)S(1)}, bf16[32,2176]{1,0:T(8,128)(2,1)S(1)}, u32[]{:S(2)}, u32[]{:S(2)}) collective-permute-start(bf16[32,2176]{1,0:T(8,128)(2,1)S(1)} %get-tuple-element.49.refs_0_), channel_id=1, source_target_pairs={{3,0},{2,1},{1,2},{0,3},{7,4},{6,5},{5,6},{4,7},{11,8},{10,9},{9,1... | collective-permute-start | bytes 417800 | tf_op jit(solution)/shard_map/ppermute | solution.py:87
  17.6 16.5 %collective-permute-start.4 = (bf16[32,2176]{1,0:T(8,128)(2,1)S(1)}, bf16[32,2176]{1,0:T(8,128)(2,1)S(1)}, u32[]{:S(2)}, u32[]{:S(2)}) collective-permute-start(bf16[32,2176]{1,0:T(8,128)(2,1)S(1)} %get-tuple-element.49.refs_0_), channel_id=1, source_target_pairs={{2,0},{3,1},{0,2},{1,3},{5,4},{4,5},{7,6},{6,7},{10,8},{11,9},{8,1... | collective-permute-start | bytes 417800 | tf_op jit(solution)/shard_map/ppermute | solution.py:87
  18.1 16.0 %collective-permute-start.3 = (bf16[32,2176]{1,0:T(8,128)(2,1)S(1)}, bf16[32,2176]{1,0:T(8,128)(2,1)S(1)}, u32[]{:S(2)}, u32[]{:S(2)}) collective-permute-start(bf16[32,2176]{1,0:T(8,128)(2,1)S(1)} %get-tuple-element.49.refs_0_), channel_id=1, source_target_pairs={{1,0},{0,1},{3,2},{2,3},{6,4},{7,5},{4,6},{5,7},{9,8},{8,9},{11,10... | collective-permute-start | bytes 417800 | tf_op jit(solution)/shard_map/ppermute | solution.py:87
  34.2 2.0 %collective-permute-start.8 = (bf16[128,2048]{1,0:T(8,128)(2,1)S(1)}, bf16[128,2048]{1,0:T(8,128)(2,1)S(1)}, u32[]{:S(2)}, u32[]{:S(2)}) collective-permute-start(bf16[128,2048]{1,0:T(8,128)(2,1)S(1)} %get-tuple-element.61), channel_id=1, source_target_pairs={{0,4},{4,0},{8,12},{12,8},{16,20},{20,16},{24,28},{28,24},{1,5},{5... | collective-permute-start | bytes 1572872 | tf_op jit(solution)/shard_map/ppermute | solution.py:90
  34.3 5.5 %collective-permute-start.6 = (bf16[128,2176]{1,0:T(8,128)(2,1)S(1)}, bf16[128,2176]{1,0:T(8,128)(2,1)S(1)}, u32[]{:S(2)}, u32[]{:S(2)}) collective-permute-start(bf16[128,2176]{1,0:T(8,128)(2,1)S(1)} %pad_maximum_fusion), channel_id=1, source_target_pairs={{0,4},{4,0},{8,12},{12,8},{16,20},{20,16},{24,28},{28,24},{1,5},{5... | collective-permute-start | bytes 1671176 | tf_op jit(solution)/shard_map/ppermute | solution.py:90
  34.9 5.0 %collective-permute-start.7 = (bf16[2,128,704]{2,1,0:T(8,128)(2,1)S(1)}, bf16[2,128,704]{2,1,0:T(8,128)(2,1)S(1)}, u32[]{:S(2)}, u32[]{:S(2)}) collective-permute-start(bf16[2,128,704]{2,1,0:T(8,128)(2,1)S(1)} %get-tuple-element.54), channel_id=1, source_target_pairs={{0,4},{4,0},{8,12},{12,8},{16,20},{20,16},{24,28},{28,24},{1,5},{5... | collective-permute-start | bytes 1081352 | tf_op jit(solution)/shard_map/ppermute | solution.py:90
  36.1 17.7 %copy-start.1 = (bf16[128,2048]{1,0:T(8,128)(2,1)}, bf16[128,2048]{1,0:T(8,128)(2,1)S(1)}, u32[]{:S(2)}) copy-start(bf16[128,2048]{1,0:T(8,128)(2,1)S(1)} %collective-permute-done.8) | copy-start | bytes 1572868
  36.2 17.6 %collective-permute-start.11 = (bf16[32,2048]{1,0:T(8,128)(2,1)S(1)}, bf16[32,2048]{1,0:T(8,128)(2,1)S(1)}, u32[]{:S(2)}, u32[]{:S(2)}) collective-permute-start(bf16[32,2048]{1,0:T(8,128)(2,1)S(1)} %get-tuple-element.79), channel_id=1, source_target_pairs={{0,3},{1,2},{2,1},{3,0},{4,7},{5,6},{6,5},{7,4},{8,11},{9,10},{10,... | collective-permute-start | bytes 393224 | tf_op jit(solution)/shard_map/ppermute | solution.py:87
  39.2 14.8 %collective-permute-start.10 = (bf16[32,2048]{1,0:T(8,128)(2,1)S(1)}, bf16[32,2048]{1,0:T(8,128)(2,1)S(1)}, u32[]{:S(2)}, u32[]{:S(2)}) collective-permute-start(bf16[32,2048]{1,0:T(8,128)(2,1)S(1)} %get-tuple-element.80), channel_id=1, source_target_pairs={{0,2},{1,3},{2,0},{3,1},{4,5},{5,4},{6,7},{7,6},{8,10},{9,11},{10,... | collective-permute-start | bytes 393224 | tf_op jit(solution)/shard_map/ppermute | solution.py:87
  39.7 14.3 %collective-permute-start.9 = (bf16[32,2048]{1,0:T(8,128)(2,1)S(1)}, bf16[32,2048]{1,0:T(8,128)(2,1)S(1)}, u32[]{:S(2)}, u32[]{:S(2)}) collective-permute-start(bf16[32,2048]{1,0:T(8,128)(2,1)S(1)} %get-tuple-element.81), channel_id=1, source_target_pairs={{0,1},{1,0},{2,3},{3,2},{4,6},{5,7},{6,4},{7,5},{8,9},{9,8},{10,11... | collective-permute-start | bytes 393224 | tf_op jit(solution)/shard_map/ppermute | solution.py:87
  53.9 10.8 %slice-start = ((bf16[128,2048]{1,0:T(8,128)(2,1)}), bf16[32,2048]{1,0:T(8,128)(2,1)S(1)}, s32[]{:S(2)}) async-start(bf16[128,2048]{1,0:T(8,128)(2,1)} %copy-done.1), calls=%async_computation | async-start | bytes 262144 | tf_op jit(solution)/shard_map/slice | solution.py:428
  53.9 2.0 %collective-permute-start.12 = (bf16[128,2176]{1,0:T(8,128)(2,1)S(1)}, bf16[128,2176]{1,0:T(8,128)(2,1)S(1)}, u32[]{:S(2)}, u32[]{:S(2)}) collective-permute-start(bf16[128,2176]{1,0:T(8,128)(2,1)S(1)} %get-tuple-element.71), channel_id=1, source_target_pairs={{0,4},{4,0},{8,12},{12,8},{16,20},{20,16},{24,28},{28,24},{1,5},{5... | collective-permute-start | bytes 1671176 | tf_op jit(solution)/shard_map/ppermute | solution.py:90
  56.0 11.8 %copy-start = (s32[32,6]{0,1:T(8,128)S(1)}, s32[32,6]{0,1:T(8,128)}, u32[]{:S(2)}) copy-start(s32[32,6]{0,1:T(8,128)} %param.15) | copy-start | bytes 2308
  56.1 6.6 %collective-permute-start.13 = (bf16[64,2176]{1,0:T(8,128)(2,1)S(1)}, bf16[64,2176]{1,0:T(8,128)(2,1)S(1)}, u32[]{:S(2)}, u32[]{:S(2)}) collective-permute-start(bf16[64,2176]{1,0:T(8,128)(2,1)S(1)} %pad_maximum_fusion.1), channel_id=1, source_target_pairs={{0,1},{1,0},{2,3},{3,2},{4,6},{5,7},{6,4},{7,5},{8,9},{9,8},{10,11... | collective-permute-start | bytes 835592 | tf_op jit(solution)/shard_map/ppermute | solution.py:87
  62.8 5.1 %collective-permute-start.14 = (bf16[32,2176]{1,0:T(8,128)(2,1)S(1)}, bf16[32,2176]{1,0:T(8,128)(2,1)S(1)}, u32[]{:S(2)}, u32[]{:S(2)}) collective-permute-start(bf16[32,2176]{1,0:T(8,128)(2,1)S(1)} %add_convert_fusion), channel_id=1, source_target_pairs={{0,2},{1,3},{2,0},{3,1},{4,5},{5,4},{6,7},{7,6},{8,10},{9,11},{10,... | collective-permute-start | bytes 417800 | tf_op jit(solution)/shard_map/ppermute | solution.py:87

commit v5 on v4

--- a/solution.py
+++ b/solution.py
@@ -67,6 +67,7 @@
         self.expert_rows = self.split * self.source_rows
         self.paired = self.owners & (self.owners - 1) == 0
         self.sent = self.width + self.meta
+        self.half = round_up(self.width // 2, LANES)
         self.rows = self.mine * self.expert_rows
         self.cols = self.blocks * self.count
 
@@ -174,13 +175,10 @@
 
 def weight_copies(plan, array, ref, sems):
     offset = first_expert(plan)[1]
-    copies = [
+    return [
         pltpu.make_async_copy(array.at[offset + e], ref.at[e], sems.at[e])
         for e in range(plan.mine)
     ]
-    for copy in copies:
-        copy.start()
-    return copies
 
 
 def prepare_kernel(plan, x_hbm, routes_hbm, factors_hbm, gate_hbm, up_hbm, after, *refs):
@@ -257,6 +255,8 @@
 
 def fetch_kernel(plan, w_hbm, after, w_ref, done_ref, sems):
     copies = weight_copies(plan, w_hbm, w_ref, sems)
+    for copy in copies:
+        copy.start()
     done_ref[...] = jnp.zeros_like(done_ref)
     for copy in copies:
         copy.wait()
@@ -300,11 +300,16 @@
     first, _ = first_expert(plan)
     up_copies = weight_copies(plan, up_hbm, up_s, sems.at[0])
     down_copies = weight_copies(plan, down_hbm, down_s, sems.at[1])
+    up_copies[0].start()
+    down_copies[0].start()
     table, factor, rows = arrived(plan, blocks, first)
     x_s[...] = dot(table, rows).astype(BF16)
     n = plan.expert_rows
     for e in range(plan.mine):
         gate_s[e] = dot_tb(x_s[e * n : (e + 1) * n, :], gate_ref[e])
+        if e + 1 < plan.mine:
+            up_copies[e + 1].start()
+            down_copies[e + 1].start()
     for e in range(plan.mine):
         up_copies[e].wait()
         up = dot_tb(x_s[e * n : (e + 1) * n, :], up_s[e])
@@ -313,10 +318,10 @@
         down_copies[e].wait()
         out = dot(hidden, down_s[e])
         y_s[e * n : (e + 1) * n, :] = (out * factor[e * n : (e + 1) * n]).astype(BF16)
-    put_rows(plan, outs, slice(None), dot_ta(table, y_s[...]).astype(BF16))
-
-
-def put_rows(plan, outs, columns, rows):
+    put_rows(outs, slice(None), dot_ta(table, y_s[...]).astype(BF16))
+
+
+def put_rows(outs, columns, rows):
     start = 0
     for out in outs:
         stop = start + out.shape[0]
@@ -330,14 +335,12 @@
     gate_ref, up_hbm, down_hbm, *refs = refs
     held = plan.source_rows
     outs, (up_s, down_s, x_s, y_s, score_s, sems) = refs[:-6], refs[-6:]
-    first, offset = first_expert(plan)
-    copies = []
-    for e in range(plan.mine):
-        for i, (array, slot) in enumerate(((down_hbm, down_s), (up_hbm, up_s))):
-            copy = pltpu.make_async_copy(array.at[offset + e], slot.at[e], sems.at[i, e])
-            copy.start()
-            copies.append(copy)
+    first, _ = first_expert(plan)
+    up_copies = weight_copies(plan, up_hbm, up_s, sems.at[0])
+    down_copies = weight_copies(plan, down_hbm, down_s, sems.at[1])
+    down_copies[0].start()
     table, factor, rows = arrived(plan, blocks, first)
+    up_copies[0].start()
     x_s[...] = dot(table, rows).astype(BF16)
     n = plan.expert_rows
     lane = iota((n, plan.meta), 1)
@@ -351,13 +354,16 @@
         act, up = act.astype(F32), up.astype(F32)
         sig = 1.0 / (1.0 + jnp.exp(-act))
         silu = act * sig
-        copies[2 * e].wait()
+        down_copies[e].wait()
+        if e + 1 < plan.mine:
+            down_copies[e + 1].start()
+            up_copies[e + 1].start()
         grad = dot_tb(x, down_s[e])
         score = jnp.sum(silu * up * grad, axis=1, keepdims=True)
         grad_gate = (grad * up * sig * (1.0 + act * (1.0 - sig))).astype(BF16)
         grad_up = (grad * silu).astype(BF16)
         result = dot(grad_gate, gate_ref[e])
-        copies[2 * e + 1].wait()
+        up_copies[e].wait()
         result = result + dot(grad_up, up_s[e])
         y_s[e * n : (e + 1) * n, :] = (result * factor[e * n : (e + 1) * n]).astype(BF16)
         expert = first + e
@@ -368,9 +374,13 @@
         spread = jnp.where(lane == expert + plan.experts, middle, spread)
         spread = jnp.where(lane == expert + 2 * plan.experts, low, spread)
         score_s[e * n : (e + 1) * n, :] = spread.astype(BF16)
-    put_rows(plan, outs, slice(0, plan.width), dot_ta(table, y_s[...]).astype(BF16))
+    half, near = plan.half, outs[: len(outs) // 2]
+    far = outs[len(outs) // 2 :]
+    put_rows(near, slice(0, half), dot_ta(table, y_s[:, :half]).astype(BF16))
+    rest = plan.width - half
+    put_rows(far, slice(0, rest), dot_ta(table, y_s[:, half:]).astype(BF16))
     scores = dot_ta(table, score_s[...]).astype(BF16)
-    put_rows(plan, outs, slice(plan.width, plan.width + plan.meta), scores)
+    put_rows(far, slice(rest, rest + plan.meta), scores)
 
 
 def part_shapes(plan, width):
@@ -379,8 +389,8 @@
     return [block] * plan.owners + [other] * (plan.split - 1)
 
 
-def expert_call(plan, kernel, name, inputs, gate, up_hbm, down_hbm, width, scratch):
-    shapes = part_shapes(plan, width)
+def expert_call(plan, kernel, name, inputs, gate, up_hbm, down_hbm, widths, scratch):
+    shapes = [shape for width in widths for shape in part_shapes(plan, width)]
     weight = pltpu.VMEM((plan.mine, plan.hidden, plan.width), BF16)
     rows = pltpu.VMEM((plan.rows, plan.width), BF16)
     return pl.pallas_call(
@@ -406,14 +416,16 @@
 def forward(plan, blocks, *weights):
     kernel = functools.partial(forward_kernel, plan, len(blocks))
     gates = pltpu.VMEM((plan.mine, plan.expert_rows, plan.hidden), F32)
-    return expert_call(plan, kernel, "forward", blocks, *weights, plan.width, gates)
+    return expert_call(plan, kernel, "forward", blocks, *weights, [plan.width], gates)
 
 
 def backward(plan, blocks, saved, *weights):
     kernel = functools.partial(backward_kernel, plan, len(blocks))
     scores = pltpu.VMEM((plan.rows, plan.meta), BF16)
+    widths = [plan.half, plan.sent - plan.half]
     inputs = [*blocks, *saved]
-    return expert_call(plan, kernel, "backward", inputs, *weights, plan.sent, scores)
+    parts = expert_call(plan, kernel, "backward", inputs, *weights, widths, scores)
+    return parts[: len(parts) // 2], parts[len(parts) // 2 :]
 
 
 def gather_group(plan, block):
@@ -438,31 +450,33 @@
     return own[0] + [plan.over_expert(x, d, True) for d, x in enumerate(sent, 1)]
 
 
-def scatter_steps(plan, own):
+def scatter_steps(plan, owns):
     if not plan.paired:
-        return scatter_group(plan, own)
+        return [scatter_group(plan, own) for own in owns]
     step = 1
     while step < plan.owners:
         away = [d for d in range(0, plan.owners, step) if d & step]
-        sent = jnp.concatenate([total(own[d]).astype(BF16) for d in away])
-        back = plan.over_expert(sent, step, True)
-        for i, d in enumerate(away):
-            own[d ^ step].append(back[i * plan.count : (i + 1) * plan.count])
+        for own in owns:
+            sent = jnp.concatenate([total(own[d]).astype(BF16) for d in away])
+            back = plan.over_expert(sent, step, True)
+            for i, d in enumerate(away):
+                own[d ^ step].append(back[i * plan.count : (i + 1) * plan.count])
         step *= 2
-    return own[0]
+    return [own[0] for own in owns]
 
 
 def finish_kernel(plan, count, *refs):
     parts, (routes_ref, out_hbm, score_hbm, out_s, score_s, sems) = refs[:count], refs[count:]
-    whole = parts[0][: plan.count, :].astype(F32)
-    for part in parts[1:]:
-        whole = whole + part[: plan.count, :].astype(F32)
-    out_s[...] = whole[:, : plan.width].astype(BF16)
+    half, rest = plan.half, plan.width - plan.half
+    near = total([part[...] for part in parts[: count // 2]])
+    far = total([part[...] for part in parts[count // 2 :]])
+    out_s[:, :half] = near.astype(BF16)
+    out_s[:, half:] = far[:, :rest].astype(BF16)
     out_copy = pltpu.make_async_copy(out_s, out_hbm, sems.at[0])
     out_copy.start()
     shape = (plan.meta, plan.meta)
     same = jnp.where(iota(shape, 0) == iota(shape, 1), 1.0, 0.0).astype(BF16)
-    spread = dot_tb(same, whole[:, plan.width :].astype(BF16))
+    spread = dot_tb(same, far[:, rest:].astype(BF16))
     experts = plan.experts
     score = spread[:experts] + spread[experts : 2 * experts] + spread[2 * experts : 3 * experts]
     row = iota((experts, plan.count), 0)
@@ -536,8 +550,8 @@
     parts_back = backward(plan, blocks_back, saved, gate, up_hbm, w_down)
     parts_back, terms = lax.optimization_barrier((parts_back, terms))
     mixed = total(terms).astype(BF16)
-    terms_back = scatter_steps(plan, sum_pair(plan, parts_back))
-    input_grad, weight_grad = finish_back(plan, terms_back, routes_back)
+    near, far = scatter_steps(plan, [sum_pair(plan, parts) for parts in parts_back])
+    input_grad, weight_grad = finish_back(plan, near + far, routes_back)
     return (mixed, input_grad, weight_grad)
 
 

time: 69.1 us -> 66.3 us (0.959)
  waiting for transfers between devices: 11.7 us -> 8.6 us
  starting transfers between devices: 17.1 us -> 19.6 us
  Pallas kernels: 37.8 us -> 35.6 us
    pallas_call x2, Pallas kernels: 29.9 us -> 27.8 us  [expert_call(): pl.pallas_call(kernel, out_shape=shapes, in_specs=[vmem()] * (len(inputs)...]
    ppermute x10 -> x12, waiting for transfers between devices: 8.51 us -> 6.36 us  [over_expert(): return lax.ppermute(x, ('dp', 'expert'), pairs)]
    ppermute x10 -> x12, starting transfers between devices: 16.3 us -> 18.2 us  [over_expert(): return lax.ppermute(x, ('dp', 'expert'), pairs)]
    ppermute x5 -> x6, waiting for transfers between devices: 3.16 us -> 2.25 us  [over_pair(): return lax.ppermute(x, 'dp', [(i, i ^ 1) for i in range(self.groups)])]
  transfers between devices with their start and end apart: 15 -> 18, of which waited for: 6 -> 7; matrix products, arithmetic and copies ran while one was open for 1% -> 2% of each run, Pallas kernels for 52% -> 51%
where the time goes in v5:
time: 66.3 us; the launch traced here: 66.1 us
  Pallas kernels  35.6 us (54%)
  starting transfers between devices  19.6 us (30%)
  waiting for transfers between devices  8.6 us (13%)
  other arithmetic  1.2 us (2%)
  between operations  1.02 us (2%)
    pallas_call x2, Pallas kernels, expert_call(): pl.pallas_call(kernel, out_shape=shapes, in_specs=[vmem()] * (len(inputs)...  27.8 us
    ppermute x12, starting transfers between devices, over_expert(): return lax.ppermute(x, ('dp', 'expert'), pairs)  18.2 us
    ppermute x12, waiting for transfers between devices, over_expert(): return lax.ppermute(x, ('dp', 'expert'), pairs)  6.36 us
    pallas_call x1, Pallas kernels, fetch(): pl.pallas_call(functools.partial(fetch_kernel, plan), out_shape=(pltpu.VM...  4.4 us
    ppermute x6, waiting for transfers between devices, over_pair(): return lax.ppermute(x, 'dp', [(i, i ^ 1) for i in range(self.groups)])  2.25 us
    pallas_call x1, Pallas kernels, prepare(): pl.pallas_call(functools.partial(prepare_kernel, plan), out_shape=out_sha...  1.59 us
    ppermute x6, starting transfers between devices, over_pair(): return lax.ppermute(x, 'dp', [(i, i ^ 1) for i in range(self.groups)])  1.35 us
  transfers between devices with their start and end apart: 18, of which 7 were waited for; matrix products, arithmetic and copies ran while one was open for 2% of the time, Pallas kernels for 51%

profile of v5, /device:TPU:0, one launch (start us, length us, event | category | flops | bytes accessed | tf_op | source)
XLA Modules:
  0.0 66.1 jit_solution(16651493721603807833)
XLA Ops:
  0.6 1.1 %pack.1.after.refs_0_ = bf16[32,2176]{1,0:T(8,128)(2,1)S(1)} custom-call(bf16[32,2048]{1,0:T(8,128)(2,1)} %x_hbm.2, s32[6,32]{1,0:T(8,128)} %bitcast.24, f32[6,32]{1,0:T(8,128)} %bitcast.25), custom_call_target="tpu_custom_call" | custom-call | tf_op jit(solution)/shard_map/pack/pallas_call | solution.py:134
  1.7 3.0 %collective-permute-start = (bf16[32,2176]{1,0:T(8,128)(2,1)S(1)}, bf16[32,2176]{1,0:T(8,128)(2,1)S(1)}, u32[]{:S(2)}, u32[]{:S(2)}) collective-permute-start(bf16[32,2176]{1,0:T(8,128)(2,1)S(1)} %pack.1.after.refs_0_), channel_id=1, source_target_pairs={{1,0},{0,1},{3,2},{2,3},{6,4},{7,5},{4,6},{5,7},{9,8},{8,9},{11,10... | collective-permute-start | bytes 417800 | tf_op jit(solution)/shard_map/ppermute | solution.py:88
  4.7 1.6 %prepare.1 = (bf16[32,2176]{1,0:T(8,128)(2,1)S(1)}, bf16[16,2176]{1,0:T(8,128)(2,1)S(1)}, bf16[2,128,704]{2,1,0:T(8,128)(2,1)S(1)}, bf16[2,128,704]{2,1,0:T(8,128)(2,1)S(1)}) custom-call(bf16[32,2048]{1,0:T(8,128)(2,1)} %x_hbm.3, s32[6,32]{1,0:T(8,128)} %bitcast.17, f32[6,32]{1,0:T(8,128)} %bitcast.26, bf16[224,704]{1,0:T(8,128)(2,1)} %bitcast.22, ...), custom_call_target="tpu_custom_call" | custom-call | bytes 17825792 | tf_op jit(solution)/shard_map/prepare/pallas_call | solution.py:229
  6.3 1.4 %collective-permute-done.after.refs_1_ = bf16[32,2176]{1,0:T(8,128)(2,1)S(1)} collective-permute-done((bf16[32,2176]{1,0:T(8,128)(2,1)S(1)}, bf16[32,2176]{1,0:T(8,128)(2,1)S(1)}, u32[]{:S(2)}, u32[]{:S(2)}) %collective-permute-start) | collective-permute-done | bytes 139296 | tf_op jit(solution)/shard_map/ppermute | solution.py:88
  7.8 2.1 %collective-permute-start.1 = (bf16[64,2176]{1,0:T(8,128)(2,1)S(1)}, bf16[64,2176]{1,0:T(8,128)(2,1)S(1)}, u32[]{:S(2)}, u32[]{:S(2)}) collective-permute-start(bf16[64,2176]{1,0:T(8,128)(2,1)S(1)} %maximum_add_fusion.1), channel_id=1, source_target_pairs={{2,0},{3,1},{0,2},{1,3},{5,4},{4,5},{7,6},{6,7},{10,8},{11,9},{8,1... | collective-permute-start | bytes 835592 | tf_op jit(solution)/shard_map/ppermute | solution.py:88
  9.9 4.4 %fetch.1 = (bf16[4,704,2048]{2,1,0:T(8,128)(2,1)S(1)}, bf16[16,2176]{1,0:T(8,128)(2,1)S(1)}) custom-call(bf16[8,704,2048]{2,1,0:T(8,128)(2,1)} %bitcast.21, bf16[32,2176]{1,0:T(8,128)(2,1)S(1)} %collective-permute-done.after.refs_1_), custom_call_target="tpu_custom_call" | custom-call | bytes 23068672 | tf_op jit(solution)/shard_map/fetch/pallas_call | solution.py:266
  14.6 3.0 %collective-permute-start.5 = (bf16[32,2176]{1,0:T(8,128)(2,1)S(1)}, bf16[32,2176]{1,0:T(8,128)(2,1)S(1)}, u32[]{:S(2)}, u32[]{:S(2)}) collective-permute-start(bf16[32,2176]{1,0:T(8,128)(2,1)S(1)} %get-tuple-element.59.refs_0_), channel_id=1, source_target_pairs={{3,0},{2,1},{1,2},{0,3},{7,4},{6,5},{5,6},{4,7},{11,8},{10,9},{9,1... | collective-permute-start | bytes 417800 | tf_op jit(solution)/shard_map/ppermute | solution.py:88
  17.6 0.5 collective-permute-start.4
  18.3 13.7 %forward.1 = (bf16[32,2048]{1,0:T(8,128)(2,1)S(1)}, bf16[32,2048]{1,0:T(8,128)(2,1)S(1)}, bf16[32,2048]{1,0:T(8,128)(2,1)S(1)}, bf16[32,2048]{1,0:T(8,128)(2,1)S(1)}, bf16[128,2048]{1,0:T(8,128)(2,1)S(1)}) custom-call(bf16[32,2176]{1,0:T(8,128)(2,1)S(1)} %pack.1.after.refs_0_, bf16[32,2176]{1,0:T(8,128)(2,1)S(1)} %collective-permute-done.after.refs_1_, ...), custom_call_target="tpu_custom_call" | custom-call | flops 2214592512 | bytes 23068672 | tf_op jit(solution)/shard_map/forward/pallas_call | solution.py:396
  32.1 0.6 collective-permute-start.6
  32.8 1.2 %collective-permute-done.8 = bf16[128,2048]{1,0:T(8,128)(2,1)S(1)} collective-permute-done((bf16[128,2048]{1,0:T(8,128)(2,1)S(1)}, bf16[128,2048]{1,0:T(8,128)(2,1)S(1)}, u32[]{:S(2)}, u32[]{:S(2)}) %collective-permute-start.8) | collective-permute-done | bytes 524320 | tf_op jit(solution)/shard_map/ppermute | solution.py:91
  34.1 2.9 %collective-permute-start.11 = (bf16[32,2048]{1,0:T(8,128)(2,1)S(1)}, bf16[32,2048]{1,0:T(8,128)(2,1)S(1)}, u32[]{:S(2)}, u32[]{:S(2)}) collective-permute-start(bf16[32,2048]{1,0:T(8,128)(2,1)S(1)} %get-tuple-element.97), channel_id=1, source_target_pairs={{0,3},{1,2},{2,1},{3,0},{4,7},{5,6},{6,5},{7,4},{8,11},{9,10},{10,... | collective-permute-start | bytes 393224 | tf_op jit(solution)/shard_map/ppermute | solution.py:88
  37.0 0.5 collective-permute-start.10
  37.6 14.1 %backward.1 = (bf16[32,1024]{1,0:T(8,128)(2,1)S(1)}, bf16[32,1024]{1,0:T(8,128)(2,1)S(1)}, bf16[32,1024]{1,0:T(8,128)(2,1)S(1)}, bf16[32,1024]{1,0:T(8,128)(2,1)...) custom-call(bf16[32,2176]{1,0:T(8,128)(2,1)S(1)} %get-tuple-element., ...), custom_call_target="tpu_custom_call" | custom-call | flops 2214592512 | bytes 23068672 | tf_op jit(solution)/shard_map/backward/pallas_call | solution.py:396
  51.9 0.5 collective-permute-start.15
  52.4 1.0 %collective-permute-done.12 = bf16[128,1024]{1,0:T(8,128)(2,1)S(1)} collective-permute-done((bf16[128,1024]{1,0:T(8,128)(2,1)S(1)}, bf16[128,1024]{1,0:T(8,128)(2,1)S(1)}, u32[]{:S(2)}, u32[]{:S(2)}) %collective-permute-start.12) | collective-permute-done | bytes 262176 | tf_op jit(solution)/shard_map/ppermute | solution.py:91
  53.4 2.0 %collective-permute-start.13 = (bf16[64,1024]{1,0:T(8,128)(2,1)S(1)}, bf16[64,1024]{1,0:T(8,128)(2,1)S(1)}, u32[]{:S(2)}, u32[]{:S(2)}) collective-permute-start(bf16[64,1024]{1,0:T(8,128)(2,1)S(1)} %pad_maximum_fusion.2), channel_id=1, source_target_pairs={{0,1},{1,0},{2,3},{3,2},{4,6},{5,7},{6,4},{7,5},{8,9},{9,8},{10,11... | collective-permute-start | bytes 393224 | tf_op jit(solution)/shard_map/ppermute | solution.py:88
  55.5 0.4 collective-permute-start.16
  55.8 2.6 %collective-permute-done.13 = bf16[64,1024]{1,0:T(8,128)(2,1)S(1)} collective-permute-done((bf16[64,1024]{1,0:T(8,128)(2,1)S(1)}, bf16[64,1024]{1,0:T(8,128)(2,1)S(1)}, u32[]{:S(2)}, u32[]{:S(2)}) %collective-permute-start.13) | collective-permute-done | bytes 131104 | tf_op jit(solution)/shard_map/ppermute | solution.py:88
  58.5 2.0 %collective-permute-start.14 = (bf16[32,1024]{1,0:T(8,128)(2,1)S(1)}, bf16[32,1024]{1,0:T(8,128)(2,1)S(1)}, u32[]{:S(2)}, u32[]{:S(2)}) collective-permute-start(bf16[32,1024]{1,0:T(8,128)(2,1)S(1)} %add_convert_fusion.7), channel_id=1, source_target_pairs={{0,2},{1,3},{2,0},{3,1},{4,5},{5,4},{6,7},{7,6},{8,10},{9,11},{10,... | collective-permute-start | bytes 196616 | tf_op jit(solution)/shard_map/ppermute | solution.py:88
  60.7 1.6 %collective-permute-start.17 = (bf16[32,1152]{1,0:T(8,128)(2,1)S(1)}, bf16[32,1152]{1,0:T(8,128)(2,1)S(1)}, u32[]{:S(2)}, u32[]{:S(2)}) collective-permute-start(bf16[32,1152]{1,0:T(8,128)(2,1)S(1)} %add_convert_fusion.4), channel_id=1, source_target_pairs={{0,2},{1,3},{2,0},{3,1},{4,5},{5,4},{6,7},{7,6},{8,10},{9,11},{10,... | collective-permute-start | bytes 221192 | tf_op jit(solution)/shard_map/ppermute | solution.py:88
  62.3 0.7 %add_convert_fusion = bf16[32,2048]{1,0:T(8,128)(2,1)} fusion(bf16[32,2048]{1,0:T(8,128)(2,1)S(1)} %collective-permute-done.11, bf16[32,2048]{1,0:T(8,128)(2,1)S(1)} %collective-permute-done.10, bf16[32,2048]{1,0:T(8,128)(2,1)S(1)} %collective-permute-done.9, bf16[32,2048]{1,0:T(8,128)(2,1)S(1)} %slice-done, bf16[32,2048]{1,0:T(8,128)(2,1)S(1)} %get-tuple-element.80), kind=kLoop, calls=%fused_computation.3 | loop fusion | flops 655360 | bytes 786432 | tf_op jit(solution)/shard_map/convert_element_type | solution.py:552
  63.1 2.0 %collective-permute-done.17.refs_7_ = bf16[32,1152]{1,0:T(8,128)(2,1)S(1)} collective-permute-done((bf16[32,1152]{1,0:T(8,128)(2,1)S(1)}, bf16[32,1152]{1,0:T(8,128)(2,1)S(1)}, u32[]{:S(2)}, u32[]{:S(2)}) %collective-permute-start.17) | collective-permute-done | bytes 73760 | tf_op jit(solution)/shard_map/ppermute | solution.py:88
  65.1 0.8 %finish.1 = (bf16[32,2048]{1,0:T(8,128)(2,1)}, f32[6,32]{1,0:T(8,128)}) custom-call(bf16[32,1024]{1,0:T(8,128)(2,1)S(1)} %get-tuple-element.85.refs_0_, bf16[32,1024]{1,0:T(8,128)(2,1)S(1)} %slice.76.refs_1_, bf16[32,1024]{1,0:T(8,128)(2,1)S(1)} %slice.79.refs_2_, bf16[32,1024]{1,0:T(8,128)(2,1)S(1)} %collective-permute-done.14.refs_3_, ...), custom_call_target="tpu_custom_call" | custom-call | tf_op jit(solution)/shard_map/finish/pallas_call | solution.py:493
  (41 shorter events, 1.5 us)
Async XLA Ops:
  1.7 6.0 %collective-permute-start = (bf16[32,2176]{1,0:T(8,128)(2,1)S(1)}, bf16[32,2176]{1,0:T(8,128)(2,1)S(1)}, u32[]{:S(2)}, u32[]{:S(2)}) collective-permute-start(bf16[32,2176]{1,0:T(8,128)(2,1)S(1)} %pack.1.after.refs_0_), channel_id=1, source_target_pairs={{1,0},{0,1},{3,2},{2,3},{6,4},{7,5},{4,6},{5,7},{9,8},{8,9},{11,10... | collective-permute-start | bytes 417800 | tf_op jit(solution)/shard_map/ppermute | solution.py:88
  7.8 6.6 %collective-permute-start.1 = (bf16[64,2176]{1,0:T(8,128)(2,1)S(1)}, bf16[64,2176]{1,0:T(8,128)(2,1)S(1)}, u32[]{:S(2)}, u32[]{:S(2)}) collective-permute-start(bf16[64,2176]{1,0:T(8,128)(2,1)S(1)} %maximum_add_fusion.1), channel_id=1, source_target_pairs={{2,0},{3,1},{0,2},{1,3},{5,4},{4,5},{7,6},{6,7},{10,8},{11,9},{8,1... | collective-permute-start | bytes 835592 | tf_op jit(solution)/shard_map/ppermute | solution.py:88
  14.5 3.7 %collective-permute-start.2 = (bf16[128,2176]{1,0:T(8,128)(2,1)S(1)}, bf16[128,2176]{1,0:T(8,128)(2,1)S(1)}, u32[]{:S(2)}, u32[]{:S(2)}) collective-permute-start(bf16[128,2176]{1,0:T(8,128)(2,1)S(1)} %maximum_add_fusion), channel_id=1, source_target_pairs={{0,4},{4,0},{8,12},{12,8},{16,20},{20,16},{24,28},{28,24},{1,5},{5... | collective-permute-start | bytes 1671176 | tf_op jit(solution)/shard_map/ppermute | solution.py:91
  14.6 17.3 %collective-permute-start.5 = (bf16[32,2176]{1,0:T(8,128)(2,1)S(1)}, bf16[32,2176]{1,0:T(8,128)(2,1)S(1)}, u32[]{:S(2)}, u32[]{:S(2)}) collective-permute-start(bf16[32,2176]{1,0:T(8,128)(2,1)S(1)} %get-tuple-element.59.refs_0_), channel_id=1, source_target_pairs={{3,0},{2,1},{1,2},{0,3},{7,4},{6,5},{5,6},{4,7},{11,8},{10,9},{9,1... | collective-permute-start | bytes 417800 | tf_op jit(solution)/shard_map/ppermute | solution.py:88
  17.6 14.3 %collective-permute-start.4 = (bf16[32,2176]{1,0:T(8,128)(2,1)S(1)}, bf16[32,2176]{1,0:T(8,128)(2,1)S(1)}, u32[]{:S(2)}, u32[]{:S(2)}) collective-permute-start(bf16[32,2176]{1,0:T(8,128)(2,1)S(1)} %get-tuple-element.59.refs_0_), channel_id=1, source_target_pairs={{2,0},{3,1},{0,2},{1,3},{5,4},{4,5},{7,6},{6,7},{10,8},{11,9},{8,1... | collective-permute-start | bytes 417800 | tf_op jit(solution)/shard_map/ppermute | solution.py:88
  18.1 13.8 %collective-permute-start.3 = (bf16[32,2176]{1,0:T(8,128)(2,1)S(1)}, bf16[32,2176]{1,0:T(8,128)(2,1)S(1)}, u32[]{:S(2)}, u32[]{:S(2)}) collective-permute-start(bf16[32,2176]{1,0:T(8,128)(2,1)S(1)} %get-tuple-element.59.refs_0_), channel_id=1, source_target_pairs={{1,0},{0,1},{3,2},{2,3},{6,4},{7,5},{4,6},{5,7},{9,8},{8,9},{11,10... | collective-permute-start | bytes 417800 | tf_op jit(solution)/shard_map/ppermute | solution.py:88
  32.0 2.0 %collective-permute-start.8 = (bf16[128,2048]{1,0:T(8,128)(2,1)S(1)}, bf16[128,2048]{1,0:T(8,128)(2,1)S(1)}, u32[]{:S(2)}, u32[]{:S(2)}) collective-permute-start(bf16[128,2048]{1,0:T(8,128)(2,1)S(1)} %get-tuple-element.76), channel_id=1, source_target_pairs={{0,4},{4,0},{8,12},{12,8},{16,20},{20,16},{24,28},{28,24},{1,5},{5... | collective-permute-start | bytes 1572872 | tf_op jit(solution)/shard_map/ppermute | solution.py:91
  32.1 5.5 %collective-permute-start.6 = (bf16[128,2176]{1,0:T(8,128)(2,1)S(1)}, bf16[128,2176]{1,0:T(8,128)(2,1)S(1)}, u32[]{:S(2)}, u32[]{:S(2)}) collective-permute-start(bf16[128,2176]{1,0:T(8,128)(2,1)S(1)} %pad_maximum_fusion), channel_id=1, source_target_pairs={{0,4},{4,0},{8,12},{12,8},{16,20},{20,16},{24,28},{28,24},{1,5},{5... | collective-permute-start | bytes 1671176 | tf_op jit(solution)/shard_map/ppermute | solution.py:91
  32.7 5.0 %collective-permute-start.7 = (bf16[2,128,704]{2,1,0:T(8,128)(2,1)S(1)}, bf16[2,128,704]{2,1,0:T(8,128)(2,1)S(1)}, u32[]{:S(2)}, u32[]{:S(2)}) collective-permute-start(bf16[2,128,704]{2,1,0:T(8,128)(2,1)S(1)} %get-tuple-element.64), channel_id=1, source_target_pairs={{0,4},{4,0},{8,12},{12,8},{16,20},{20,16},{24,28},{28,24},{1,5},{5... | collective-permute-start | bytes 1081352 | tf_op jit(solution)/shard_map/ppermute | solution.py:91
  34.0 17.8 %copy-start.1 = (bf16[128,2048]{1,0:T(8,128)(2,1)}, bf16[128,2048]{1,0:T(8,128)(2,1)S(1)}, u32[]{:S(2)}) copy-start(bf16[128,2048]{1,0:T(8,128)(2,1)S(1)} %collective-permute-done.8) | copy-start | bytes 1572868
  34.1 17.7 %collective-permute-start.11 = (bf16[32,2048]{1,0:T(8,128)(2,1)S(1)}, bf16[32,2048]{1,0:T(8,128)(2,1)S(1)}, u32[]{:S(2)}, u32[]{:S(2)}) collective-permute-start(bf16[32,2048]{1,0:T(8,128)(2,1)S(1)} %get-tuple-element.97), channel_id=1, source_target_pairs={{0,3},{1,2},{2,1},{3,0},{4,7},{5,6},{6,5},{7,4},{8,11},{9,10},{10,... | collective-permute-start | bytes 393224 | tf_op jit(solution)/shard_map/ppermute | solution.py:88
  37.0 14.8 %collective-permute-start.10 = (bf16[32,2048]{1,0:T(8,128)(2,1)S(1)}, bf16[32,2048]{1,0:T(8,128)(2,1)S(1)}, u32[]{:S(2)}, u32[]{:S(2)}) collective-permute-start(bf16[32,2048]{1,0:T(8,128)(2,1)S(1)} %get-tuple-element.98), channel_id=1, source_target_pairs={{0,2},{1,3},{2,0},{3,1},{4,5},{5,4},{6,7},{7,6},{8,10},{9,11},{10,... | collective-permute-start | bytes 393224 | tf_op jit(solution)/shard_map/ppermute | solution.py:88
  37.5 14.3 %collective-permute-start.9 = (bf16[32,2048]{1,0:T(8,128)(2,1)S(1)}, bf16[32,2048]{1,0:T(8,128)(2,1)S(1)}, u32[]{:S(2)}, u32[]{:S(2)}) collective-permute-start(bf16[32,2048]{1,0:T(8,128)(2,1)S(1)} %get-tuple-element.99), channel_id=1, source_target_pairs={{0,1},{1,0},{2,3},{3,2},{4,6},{5,7},{6,4},{7,5},{8,9},{9,8},{10,11... | collective-permute-start | bytes 393224 | tf_op jit(solution)/shard_map/ppermute | solution.py:88
  51.7 10.6 %slice-start = ((bf16[128,2048]{1,0:T(8,128)(2,1)}), bf16[32,2048]{1,0:T(8,128)(2,1)S(1)}, s32[]{:S(2)}) async-start(bf16[128,2048]{1,0:T(8,128)(2,1)} %copy-done.1), calls=%async_computation | async-start | bytes 262144 | tf_op jit(solution)/shard_map/slice | solution.py:440
  51.8 1.6 %collective-permute-start.12 = (bf16[128,1024]{1,0:T(8,128)(2,1)S(1)}, bf16[128,1024]{1,0:T(8,128)(2,1)S(1)}, u32[]{:S(2)}, u32[]{:S(2)}) collective-permute-start(bf16[128,1024]{1,0:T(8,128)(2,1)S(1)} %get-tuple-element.86), channel_id=1, source_target_pairs={{0,4},{4,0},{8,12},{12,8},{16,20},{20,16},{24,28},{28,24},{1,5},{5... | collective-permute-start | bytes 786440 | tf_op jit(solution)/shard_map/ppermute | solution.py:91
  51.9 3.5 %collective-permute-start.15 = (bf16[128,1152]{1,0:T(8,128)(2,1)S(1)}, bf16[128,1152]{1,0:T(8,128)(2,1)S(1)}, u32[]{:S(2)}, u32[]{:S(2)}) collective-permute-start(bf16[128,1152]{1,0:T(8,128)(2,1)S(1)} %get-tuple-element.91), channel_id=1, source_target_pairs={{0,4},{4,0},{8,12},{12,8},{16,20},{20,16},{24,28},{28,24},{1,5},{5... | collective-permute-start | bytes 884744 | tf_op jit(solution)/shard_map/ppermute | solution.py:91
  53.4 5.0 %collective-permute-start.13 = (bf16[64,1024]{1,0:T(8,128)(2,1)S(1)}, bf16[64,1024]{1,0:T(8,128)(2,1)S(1)}, u32[]{:S(2)}, u32[]{:S(2)}) collective-permute-start(bf16[64,1024]{1,0:T(8,128)(2,1)S(1)} %pad_maximum_fusion.2), channel_id=1, source_target_pairs={{0,1},{1,0},{2,3},{3,2},{4,6},{5,7},{6,4},{7,5},{8,9},{9,8},{10,11... | collective-permute-start | bytes 393224 | tf_op jit(solution)/shard_map/ppermute | solution.py:88
  55.4 9.7 %copy-start = (s32[32,6]{0,1:T(8,128)S(1)}, s32[32,6]{0,1:T(8,128)}, u32[]{:S(2)}) copy-start(s32[32,6]{0,1:T(8,128)} %param.15) | copy-start | bytes 2308
  55.5 5.2 %collective-permute-start.16 = (bf16[64,1152]{1,0:T(8,128)(2,1)S(1)}, bf16[64,1152]{1,0:T(8,128)(2,1)S(1)}, u32[]{:S(2)}, u32[]{:S(2)}) collective-permute-start(bf16[64,1152]{1,0:T(8,128)(2,1)S(1)} %pad_maximum_fusion.1), channel_id=1, source_target_pairs={{0,1},{1,0},{2,3},{3,2},{4,6},{5,7},{6,4},{7,5},{8,9},{9,8},{10,11... | collective-permute-start | bytes 442376 | tf_op jit(solution)/shard_map/ppermute | solution.py:88
  58.5 4.6 %collective-permute-start.14 = (bf16[32,1024]{1,0:T(8,128)(2,1)S(1)}, bf16[32,1024]{1,0:T(8,128)(2,1)S(1)}, u32[]{:S(2)}, u32[]{:S(2)}) collective-permute-start(bf16[32,1024]{1,0:T(8,128)(2,1)S(1)} %add_convert_fusion.7), channel_id=1, source_target_pairs={{0,2},{1,3},{2,0},{3,1},{4,5},{5,4},{6,7},{7,6},{8,10},{9,11},{10,... | collective-permute-start | bytes 196616 | tf_op jit(solution)/shard_map/ppermute | solution.py:88
  60.7 4.4 %collective-permute-start.17 = (bf16[32,1152]{1,0:T(8,128)(2,1)S(1)}, bf16[32,1152]{1,0:T(8,128)(2,1)S(1)}, u32[]{:S(2)}, u32[]{:S(2)}) collective-permute-start(bf16[32,1152]{1,0:T(8,128)(2,1)S(1)} %add_convert_fusion.4), channel_id=1, source_target_pairs={{0,2},{1,3},{2,0},{3,1},{4,5},{5,4},{6,7},{7,6},{8,10},{9,11},{10,... | collective-permute-start | bytes 221192 | tf_op jit(solution)/shard_map/ppermute | solution.py:88

commit v6 on v5

--- a/solution.py
+++ b/solution.py
@@ -293,31 +293,51 @@
     return table, factor, jnp.concatenate(rows, axis=0)
 
 
+class Queue:
+    def __init__(self, copies, ahead):
+        self.copies, self.ahead, self.started, self.taken = copies, ahead, 0, 0
+
+    def fill(self):
+        limit = min(self.taken + self.ahead, len(self.copies))
+        while self.started < limit:
+            self.copies[self.started].start()
+            self.started += 1
+
+    def take(self):
+        self.fill()
+        self.copies[self.taken].wait()
+        self.taken += 1
+        self.fill()
+
+
 def forward_kernel(plan, count, *refs):
     blocks, refs = refs[:count], refs[count:]
     gate_ref, up_hbm, down_hbm, *refs = refs
-    outs, (up_s, down_s, x_s, y_s, gate_s, sems) = refs[:-6], refs[-6:]
+    outs, (up_s, down_s, x_s, y_s, gate_s, hidden_s, sems) = refs[:-7], refs[-7:]
     first, _ = first_expert(plan)
-    up_copies = weight_copies(plan, up_hbm, up_s, sems.at[0])
-    down_copies = weight_copies(plan, down_hbm, down_s, sems.at[1])
-    up_copies[0].start()
-    down_copies[0].start()
+    copies = weight_copies(plan, up_hbm, up_s, sems.at[0])
+    copies += weight_copies(plan, down_hbm, down_s, sems.at[1])
+    queue = Queue(copies, 3)
+    queue.fill()
     table, factor, rows = arrived(plan, blocks, first)
     x_s[...] = dot(table, rows).astype(BF16)
     n = plan.expert_rows
-    for e in range(plan.mine):
-        gate_s[e] = dot_tb(x_s[e * n : (e + 1) * n, :], gate_ref[e])
-        if e + 1 < plan.mine:
-            up_copies[e + 1].start()
-            down_copies[e + 1].start()
-    for e in range(plan.mine):
-        up_copies[e].wait()
-        up = dot_tb(x_s[e * n : (e + 1) * n, :], up_s[e])
-        gate = gate_s[e]
-        hidden = (gate / (1.0 + jnp.exp(-gate)) * up).astype(BF16)
-        down_copies[e].wait()
-        out = dot(hidden, down_s[e])
-        y_s[e * n : (e + 1) * n, :] = (out * factor[e * n : (e + 1) * n]).astype(BF16)
+    parts = [slice(e * n, (e + 1) * n) for e in range(plan.mine)]
+    for e, part in enumerate(parts):
+        gate_s[e] = dot_tb(x_s[part, :], gate_ref[e])
+    up = None
+    for e, part in enumerate(parts):
+        queue.take()
+        last, up = up, dot_tb(x_s[part, :], up_s[e])
+        if e:
+            gate = gate_s[e - 1]
+            hidden_s[e - 1] = (gate / (1.0 + jnp.exp(-gate)) * last).astype(BF16)
+    gate = gate_s[plan.mine - 1]
+    hidden_s[plan.mine - 1] = (gate / (1.0 + jnp.exp(-gate)) * up).astype(BF16)
+    for e, part in enumerate(parts):
+        queue.take()
+        out = dot(hidden_s[e], down_s[e])
+        y_s[part, :] = (out * factor[part]).astype(BF16)
     put_rows(outs, slice(None), dot_ta(table, y_s[...]).astype(BF16))
 
 
@@ -333,19 +353,19 @@
     blocks, refs = refs[:count], refs[count:]
     saved_ref, other_ref, refs = refs[0], refs[plan.split - 1], refs[plan.split :]
     gate_ref, up_hbm, down_hbm, *refs = refs
-    held = plan.source_rows
-    outs, (up_s, down_s, x_s, y_s, score_s, sems) = refs[:-6], refs[-6:]
+    outs, (up_s, down_s, x_s, y_s, score_s, grads_s, sems) = refs[:-7], refs[-7:]
     first, _ = first_expert(plan)
-    up_copies = weight_copies(plan, up_hbm, up_s, sems.at[0])
-    down_copies = weight_copies(plan, down_hbm, down_s, sems.at[1])
-    down_copies[0].start()
+    copies = weight_copies(plan, down_hbm, down_s, sems.at[0])
+    copies += weight_copies(plan, up_hbm, up_s, sems.at[1])
+    queue = Queue(copies, 2)
+    queue.fill()
     table, factor, rows = arrived(plan, blocks, first)
-    up_copies[0].start()
     x_s[...] = dot(table, rows).astype(BF16)
-    n = plan.expert_rows
+    n, held = plan.expert_rows, plan.source_rows
     lane = iota((n, plan.meta), 1)
-    for e in range(plan.mine):
-        x = x_s[e * n : (e + 1) * n, :]
+    parts = [slice(e * n, (e + 1) * n) for e in range(plan.mine)]
+
+    def through_activation(e, grad):
         own = slice(e * held, (e + 1) * held)
         act, up = saved_ref[0, own, :], saved_ref[1, own, :]
         if plan.split > 1:
@@ -354,18 +374,9 @@
         act, up = act.astype(F32), up.astype(F32)
         sig = 1.0 / (1.0 + jnp.exp(-act))
         silu = act * sig
-        down_copies[e].wait()
-        if e + 1 < plan.mine:
-            down_copies[e + 1].start()
-            up_copies[e + 1].start()
-        grad = dot_tb(x, down_s[e])
         score = jnp.sum(silu * up * grad, axis=1, keepdims=True)
-        grad_gate = (grad * up * sig * (1.0 + act * (1.0 - sig))).astype(BF16)
-        grad_up = (grad * silu).astype(BF16)
-        result = dot(grad_gate, gate_ref[e])
-        up_copies[e].wait()
-        result = result + dot(grad_up, up_s[e])
-        y_s[e * n : (e + 1) * n, :] = (result * factor[e * n : (e + 1) * n]).astype(BF16)
+        grads_s[0, e] = (grad * up * sig * (1.0 + act * (1.0 - sig))).astype(BF16)
+        grads_s[1, e] = (grad * silu).astype(BF16)
         expert = first + e
         high = score.astype(BF16).astype(F32)
         middle = (score - high).astype(BF16).astype(F32)
@@ -373,7 +384,19 @@
         spread = jnp.where(lane == expert, high, 0.0)
         spread = jnp.where(lane == expert + plan.experts, middle, spread)
         spread = jnp.where(lane == expert + 2 * plan.experts, low, spread)
-        score_s[e * n : (e + 1) * n, :] = spread.astype(BF16)
+        score_s[parts[e], :] = spread.astype(BF16)
+
+    grad = None
+    for e, part in enumerate(parts):
+        queue.take()
+        last, grad = grad, dot_tb(x_s[part, :], down_s[e])
+        if e:
+            through_activation(e - 1, last)
+    through_activation(plan.mine - 1, grad)
+    for e, part in enumerate(parts):
+        queue.take()
+        result = dot(grads_s[0, e], gate_ref[e]) + dot(grads_s[1, e], up_s[e])
+        y_s[part, :] = (result * factor[part]).astype(BF16)
     half, near = plan.half, outs[: len(outs) // 2]
     far = outs[len(outs) // 2 :]
     put_rows(near, slice(0, half), dot_ta(table, y_s[:, :half]).astype(BF16))
@@ -400,7 +423,7 @@
         out_specs=[vmem()] * len(shapes),
         scratch_shapes=[
             *[weight, weight, rows, rows],
-            scratch,
+            *scratch,
             pltpu.SemaphoreType.DMA((2, plan.mine)),
         ],
         compiler_params=pltpu.CompilerParams(vmem_limit_bytes=36 * MIB),
@@ -415,16 +438,20 @@
 
 def forward(plan, blocks, *weights):
     kernel = functools.partial(forward_kernel, plan, len(blocks))
-    gates = pltpu.VMEM((plan.mine, plan.expert_rows, plan.hidden), F32)
-    return expert_call(plan, kernel, "forward", blocks, *weights, [plan.width], gates)
+    shape = (plan.mine, plan.expert_rows, plan.hidden)
+    scratch = [pltpu.VMEM(shape, F32), pltpu.VMEM(shape, BF16)]
+    return expert_call(plan, kernel, "forward", blocks, *weights, [plan.width], scratch)
 
 
 def backward(plan, blocks, saved, *weights):
     kernel = functools.partial(backward_kernel, plan, len(blocks))
-    scores = pltpu.VMEM((plan.rows, plan.meta), BF16)
+    scratch = [
+        pltpu.VMEM((plan.rows, plan.meta), BF16),
+        pltpu.VMEM((2, plan.mine, plan.expert_rows, plan.hidden), BF16),
+    ]
     widths = [plan.half, plan.sent - plan.half]
     inputs = [*blocks, *saved]
-    parts = expert_call(plan, kernel, "backward", inputs, *weights, widths, scores)
+    parts = expert_call(plan, kernel, "backward", inputs, *weights, widths, scratch)
     return parts[: len(parts) // 2], parts[len(parts) // 2 :]
 
 

time: 66.3 us -> 64.5 us (0.973)
  Pallas kernels: 35.6 us -> 33.8 us
    pallas_call x2, Pallas kernels: 27.8 us -> 26 us  [expert_call(): pl.pallas_call(kernel, out_shape=shapes, in_specs=[vmem()] * (len(inputs)...]
  transfers between devices with their start and end apart: 18 -> 18, of which waited for: 7 -> 7; matrix products, arithmetic and copies ran while one was open for 2% -> 2% of each run, Pallas kernels for 51% -> 50%
where the time goes in v6:
time: 64.5 us; the launch traced here: 64.3 us
  Pallas kernels  33.8 us (52%)
  starting transfers between devices  19.5 us (30%)
  waiting for transfers between devices  8.63 us (13%)
  other arithmetic  1.2 us (2%)
  between operations  1.02 us (2%)
    pallas_call x2, Pallas kernels, expert_call(): pl.pallas_call(kernel, out_shape=shapes, in_specs=[vmem()] * (len(inputs)...  26 us
    ppermute x12, starting transfers between devices, over_expert(): return lax.ppermute(x, ('dp', 'expert'), pairs)  18.2 us
    ppermute x12, waiting for transfers between devices, over_expert(): return lax.ppermute(x, ('dp', 'expert'), pairs)  6.39 us
    pallas_call x1, Pallas kernels, fetch(): pl.pallas_call(functools.partial(fetch_kernel, plan), out_shape=(pltpu.VM...  4.4 us
    ppermute x6, waiting for transfers between devices, over_pair(): return lax.ppermute(x, 'dp', [(i, i ^ 1) for i in range(self.groups)])  2.25 us
    pallas_call x1, Pallas kernels, prepare(): pl.pallas_call(functools.partial(prepare_kernel, plan), out_shape=out_sha...  1.59 us
    ppermute x6, starting transfers between devices, over_pair(): return lax.ppermute(x, 'dp', [(i, i ^ 1) for i in range(self.groups)])  1.35 us
  transfers between devices with their start and end apart: 18, of which 7 were waited for; matrix products, arithmetic and copies ran while one was open for 2% of the time, Pallas kernels for 50%

profile of v6, /device:TPU:0, one launch (start us, length us, event | category | flops | bytes accessed | tf_op | source)
XLA Modules:
  0.0 64.3 jit_solution(2330235024318135406)
XLA Ops:
  0.6 1.1 %pack.1.after.refs_0_ = bf16[32,2176]{1,0:T(8,128)(2,1)S(1)} custom-call(bf16[32,2048]{1,0:T(8,128)(2,1)} %x_hbm.2, s32[6,32]{1,0:T(8,128)} %bitcast.24, f32[6,32]{1,0:T(8,128)} %bitcast.25), custom_call_target="tpu_custom_call" | custom-call | tf_op jit(solution)/shard_map/pack/pallas_call | solution.py:134
  1.7 3.0 %collective-permute-start = (bf16[32,2176]{1,0:T(8,128)(2,1)S(1)}, bf16[32,2176]{1,0:T(8,128)(2,1)S(1)}, u32[]{:S(2)}, u32[]{:S(2)}) collective-permute-start(bf16[32,2176]{1,0:T(8,128)(2,1)S(1)} %pack.1.after.refs_0_), channel_id=1, source_target_pairs={{1,0},{0,1},{3,2},{2,3},{6,4},{7,5},{4,6},{5,7},{9,8},{8,9},{11,10... | collective-permute-start | bytes 417800 | tf_op jit(solution)/shard_map/ppermute | solution.py:88
  4.7 1.6 %prepare.1 = (bf16[32,2176]{1,0:T(8,128)(2,1)S(1)}, bf16[16,2176]{1,0:T(8,128)(2,1)S(1)}, bf16[2,128,704]{2,1,0:T(8,128)(2,1)S(1)}, bf16[2,128,704]{2,1,0:T(8,128)(2,1)S(1)}) custom-call(bf16[32,2048]{1,0:T(8,128)(2,1)} %x_hbm.3, s32[6,32]{1,0:T(8,128)} %bitcast.17, f32[6,32]{1,0:T(8,128)} %bitcast.26, bf16[224,704]{1,0:T(8,128)(2,1)} %bitcast.22, ...), custom_call_target="tpu_custom_call" | custom-call | bytes 17825792 | tf_op jit(solution)/shard_map/prepare/pallas_call | solution.py:229
  6.3 1.4 %collective-permute-done.after.refs_1_ = bf16[32,2176]{1,0:T(8,128)(2,1)S(1)} collective-permute-done((bf16[32,2176]{1,0:T(8,128)(2,1)S(1)}, bf16[32,2176]{1,0:T(8,128)(2,1)S(1)}, u32[]{:S(2)}, u32[]{:S(2)}) %collective-permute-start) | collective-permute-done | bytes 139296 | tf_op jit(solution)/shard_map/ppermute | solution.py:88
  7.8 2.1 %collective-permute-start.1 = (bf16[64,2176]{1,0:T(8,128)(2,1)S(1)}, bf16[64,2176]{1,0:T(8,128)(2,1)S(1)}, u32[]{:S(2)}, u32[]{:S(2)}) collective-permute-start(bf16[64,2176]{1,0:T(8,128)(2,1)S(1)} %maximum_add_fusion.1), channel_id=1, source_target_pairs={{2,0},{3,1},{0,2},{1,3},{5,4},{4,5},{7,6},{6,7},{10,8},{11,9},{8,1... | collective-permute-start | bytes 835592 | tf_op jit(solution)/shard_map/ppermute | solution.py:88
  9.9 4.4 %fetch.1 = (bf16[4,704,2048]{2,1,0:T(8,128)(2,1)S(1)}, bf16[16,2176]{1,0:T(8,128)(2,1)S(1)}) custom-call(bf16[8,704,2048]{2,1,0:T(8,128)(2,1)} %bitcast.21, bf16[32,2176]{1,0:T(8,128)(2,1)S(1)} %collective-permute-done.after.refs_1_), custom_call_target="tpu_custom_call" | custom-call | bytes 23068672 | tf_op jit(solution)/shard_map/fetch/pallas_call | solution.py:266
  14.6 3.0 %collective-permute-start.5 = (bf16[32,2176]{1,0:T(8,128)(2,1)S(1)}, bf16[32,2176]{1,0:T(8,128)(2,1)S(1)}, u32[]{:S(2)}, u32[]{:S(2)}) collective-permute-start(bf16[32,2176]{1,0:T(8,128)(2,1)S(1)} %get-tuple-element.59.refs_0_), channel_id=1, source_target_pairs={{3,0},{2,1},{1,2},{0,3},{7,4},{6,5},{5,6},{4,7},{11,8},{10,9},{9,1... | collective-permute-start | bytes 417800 | tf_op jit(solution)/shard_map/ppermute | solution.py:88
  17.6 0.5 collective-permute-start.4
  18.3 13.3 %forward.1 = (bf16[32,2048]{1,0:T(8,128)(2,1)S(1)}, bf16[32,2048]{1,0:T(8,128)(2,1)S(1)}, bf16[32,2048]{1,0:T(8,128)(2,1)S(1)}, bf16[32,2048]{1,0:T(8,128)(2,1)S(1)}, bf16[128,2048]{1,0:T(8,128)(2,1)S(1)}) custom-call(bf16[32,2176]{1,0:T(8,128)(2,1)S(1)} %pack.1.after.refs_0_, bf16[32,2176]{1,0:T(8,128)(2,1)S(1)} %collective-permute-done.after.refs_1_, ...), custom_call_target="tpu_custom_call" | custom-call | flops 2214592512 | bytes 23068672 | tf_op jit(solution)/shard_map/forward/pallas_call | solution.py:419
  31.7 0.6 collective-permute-start.6
  32.4 1.2 %collective-permute-done.8 = bf16[128,2048]{1,0:T(8,128)(2,1)S(1)} collective-permute-done((bf16[128,2048]{1,0:T(8,128)(2,1)S(1)}, bf16[128,2048]{1,0:T(8,128)(2,1)S(1)}, u32[]{:S(2)}, u32[]{:S(2)}) %collective-permute-start.8) | collective-permute-done | bytes 524320 | tf_op jit(solution)/shard_map/ppermute | solution.py:91
  33.7 2.9 %collective-permute-start.11 = (bf16[32,2048]{1,0:T(8,128)(2,1)S(1)}, bf16[32,2048]{1,0:T(8,128)(2,1)S(1)}, u32[]{:S(2)}, u32[]{:S(2)}) collective-permute-start(bf16[32,2048]{1,0:T(8,128)(2,1)S(1)} %get-tuple-element.97), channel_id=1, source_target_pairs={{0,3},{1,2},{2,1},{3,0},{4,7},{5,6},{6,5},{7,4},{8,11},{9,10},{10,... | collective-permute-start | bytes 393224 | tf_op jit(solution)/shard_map/ppermute | solution.py:88
  36.6 0.5 collective-permute-start.10
  37.3 12.7 %backward.1 = (bf16[32,1024]{1,0:T(8,128)(2,1)S(1)}, bf16[32,1024]{1,0:T(8,128)(2,1)S(1)}, bf16[32,1024]{1,0:T(8,128)(2,1)S(1)}, bf16[32,1024]{1,0:T(8,128)(2,1)...) custom-call(bf16[32,2176]{1,0:T(8,128)(2,1)S(1)} %get-tuple-element., ...), custom_call_target="tpu_custom_call" | custom-call | flops 2214592512 | bytes 23068672 | tf_op jit(solution)/shard_map/backward/pallas_call | solution.py:419
  50.1 0.5 collective-permute-start.15
  50.6 1.0 %collective-permute-done.12 = bf16[128,1024]{1,0:T(8,128)(2,1)S(1)} collective-permute-done((bf16[128,1024]{1,0:T(8,128)(2,1)S(1)}, bf16[128,1024]{1,0:T(8,128)(2,1)S(1)}, u32[]{:S(2)}, u32[]{:S(2)}) %collective-permute-start.12) | collective-permute-done | bytes 262176 | tf_op jit(solution)/shard_map/ppermute | solution.py:91
  51.6 2.0 %collective-permute-start.13 = (bf16[64,1024]{1,0:T(8,128)(2,1)S(1)}, bf16[64,1024]{1,0:T(8,128)(2,1)S(1)}, u32[]{:S(2)}, u32[]{:S(2)}) collective-permute-start(bf16[64,1024]{1,0:T(8,128)(2,1)S(1)} %pad_maximum_fusion.2), channel_id=1, source_target_pairs={{0,1},{1,0},{2,3},{3,2},{4,6},{5,7},{6,4},{7,5},{8,9},{9,8},{10,11... | collective-permute-start | bytes 393224 | tf_op jit(solution)/shard_map/ppermute | solution.py:88
  53.7 0.4 collective-permute-start.16
  54.0 2.6 %collective-permute-done.13 = bf16[64,1024]{1,0:T(8,128)(2,1)S(1)} collective-permute-done((bf16[64,1024]{1,0:T(8,128)(2,1)S(1)}, bf16[64,1024]{1,0:T(8,128)(2,1)S(1)}, u32[]{:S(2)}, u32[]{:S(2)}) %collective-permute-start.13) | collective-permute-done | bytes 131104 | tf_op jit(solution)/shard_map/ppermute | solution.py:88
  56.7 2.0 %collective-permute-start.14 = (bf16[32,1024]{1,0:T(8,128)(2,1)S(1)}, bf16[32,1024]{1,0:T(8,128)(2,1)S(1)}, u32[]{:S(2)}, u32[]{:S(2)}) collective-permute-start(bf16[32,1024]{1,0:T(8,128)(2,1)S(1)} %add_convert_fusion.7), channel_id=1, source_target_pairs={{0,2},{1,3},{2,0},{3,1},{4,5},{5,4},{6,7},{7,6},{8,10},{9,11},{10,... | collective-permute-start | bytes 196616 | tf_op jit(solution)/shard_map/ppermute | solution.py:88
  58.9 1.6 %collective-permute-start.17 = (bf16[32,1152]{1,0:T(8,128)(2,1)S(1)}, bf16[32,1152]{1,0:T(8,128)(2,1)S(1)}, u32[]{:S(2)}, u32[]{:S(2)}) collective-permute-start(bf16[32,1152]{1,0:T(8,128)(2,1)S(1)} %add_convert_fusion.4), channel_id=1, source_target_pairs={{0,2},{1,3},{2,0},{3,1},{4,5},{5,4},{6,7},{7,6},{8,10},{9,11},{10,... | collective-permute-start | bytes 221192 | tf_op jit(solution)/shard_map/ppermute | solution.py:88
  60.5 0.7 %add_convert_fusion = bf16[32,2048]{1,0:T(8,128)(2,1)} fusion(bf16[32,2048]{1,0:T(8,128)(2,1)S(1)} %collective-permute-done.11, bf16[32,2048]{1,0:T(8,128)(2,1)S(1)} %collective-permute-done.10, bf16[32,2048]{1,0:T(8,128)(2,1)S(1)} %collective-permute-done.9, bf16[32,2048]{1,0:T(8,128)(2,1)S(1)} %slice-done, bf16[32,2048]{1,0:T(8,128)(2,1)S(1)} %get-tuple-element.80), kind=kLoop, calls=%fused_computation.3 | loop fusion | flops 655360 | bytes 786432 | tf_op jit(solution)/shard_map/convert_element_type | solution.py:579
  61.3 2.0 %collective-permute-done.17.refs_7_ = bf16[32,1152]{1,0:T(8,128)(2,1)S(1)} collective-permute-done((bf16[32,1152]{1,0:T(8,128)(2,1)S(1)}, bf16[32,1152]{1,0:T(8,128)(2,1)S(1)}, u32[]{:S(2)}, u32[]{:S(2)}) %collective-permute-start.17) | collective-permute-done | bytes 73760 | tf_op jit(solution)/shard_map/ppermute | solution.py:88
  63.4 0.8 %finish.1 = (bf16[32,2048]{1,0:T(8,128)(2,1)}, f32[6,32]{1,0:T(8,128)}) custom-call(bf16[32,1024]{1,0:T(8,128)(2,1)S(1)} %get-tuple-element.85.refs_0_, bf16[32,1024]{1,0:T(8,128)(2,1)S(1)} %slice.76.refs_1_, bf16[32,1024]{1,0:T(8,128)(2,1)S(1)} %slice.79.refs_2_, bf16[32,1024]{1,0:T(8,128)(2,1)S(1)} %collective-permute-done.14.refs_3_, ...), custom_call_target="tpu_custom_call" | custom-call | tf_op jit(solution)/shard_map/finish/pallas_call | solution.py:520
  (41 shorter events, 1.5 us)
Async XLA Ops:
  1.7 6.0 %collective-permute-start = (bf16[32,2176]{1,0:T(8,128)(2,1)S(1)}, bf16[32,2176]{1,0:T(8,128)(2,1)S(1)}, u32[]{:S(2)}, u32[]{:S(2)}) collective-permute-start(bf16[32,2176]{1,0:T(8,128)(2,1)S(1)} %pack.1.after.refs_0_), channel_id=1, source_target_pairs={{1,0},{0,1},{3,2},{2,3},{6,4},{7,5},{4,6},{5,7},{9,8},{8,9},{11,10... | collective-permute-start | bytes 417800 | tf_op jit(solution)/shard_map/ppermute | solution.py:88
  7.8 6.6 %collective-permute-start.1 = (bf16[64,2176]{1,0:T(8,128)(2,1)S(1)}, bf16[64,2176]{1,0:T(8,128)(2,1)S(1)}, u32[]{:S(2)}, u32[]{:S(2)}) collective-permute-start(bf16[64,2176]{1,0:T(8,128)(2,1)S(1)} %maximum_add_fusion.1), channel_id=1, source_target_pairs={{2,0},{3,1},{0,2},{1,3},{5,4},{4,5},{7,6},{6,7},{10,8},{11,9},{8,1... | collective-permute-start | bytes 835592 | tf_op jit(solution)/shard_map/ppermute | solution.py:88
  14.5 3.7 %collective-permute-start.2 = (bf16[128,2176]{1,0:T(8,128)(2,1)S(1)}, bf16[128,2176]{1,0:T(8,128)(2,1)S(1)}, u32[]{:S(2)}, u32[]{:S(2)}) collective-permute-start(bf16[128,2176]{1,0:T(8,128)(2,1)S(1)} %maximum_add_fusion), channel_id=1, source_target_pairs={{0,4},{4,0},{8,12},{12,8},{16,20},{20,16},{24,28},{28,24},{1,5},{5... | collective-permute-start | bytes 1671176 | tf_op jit(solution)/shard_map/ppermute | solution.py:91
  14.6 17.0 %collective-permute-start.5 = (bf16[32,2176]{1,0:T(8,128)(2,1)S(1)}, bf16[32,2176]{1,0:T(8,128)(2,1)S(1)}, u32[]{:S(2)}, u32[]{:S(2)}) collective-permute-start(bf16[32,2176]{1,0:T(8,128)(2,1)S(1)} %get-tuple-element.59.refs_0_), channel_id=1, source_target_pairs={{3,0},{2,1},{1,2},{0,3},{7,4},{6,5},{5,6},{4,7},{11,8},{10,9},{9,1... | collective-permute-start | bytes 417800 | tf_op jit(solution)/shard_map/ppermute | solution.py:88
  17.6 14.0 %collective-permute-start.4 = (bf16[32,2176]{1,0:T(8,128)(2,1)S(1)}, bf16[32,2176]{1,0:T(8,128)(2,1)S(1)}, u32[]{:S(2)}, u32[]{:S(2)}) collective-permute-start(bf16[32,2176]{1,0:T(8,128)(2,1)S(1)} %get-tuple-element.59.refs_0_), channel_id=1, source_target_pairs={{2,0},{3,1},{0,2},{1,3},{5,4},{4,5},{7,6},{6,7},{10,8},{11,9},{8,1... | collective-permute-start | bytes 417800 | tf_op jit(solution)/shard_map/ppermute | solution.py:88
  18.1 13.5 %collective-permute-start.3 = (bf16[32,2176]{1,0:T(8,128)(2,1)S(1)}, bf16[32,2176]{1,0:T(8,128)(2,1)S(1)}, u32[]{:S(2)}, u32[]{:S(2)}) collective-permute-start(bf16[32,2176]{1,0:T(8,128)(2,1)S(1)} %get-tuple-element.59.refs_0_), channel_id=1, source_target_pairs={{1,0},{0,1},{3,2},{2,3},{6,4},{7,5},{4,6},{5,7},{9,8},{8,9},{11,10... | collective-permute-start | bytes 417800 | tf_op jit(solution)/shard_map/ppermute | solution.py:88
  31.6 2.0 %collective-permute-start.8 = (bf16[128,2048]{1,0:T(8,128)(2,1)S(1)}, bf16[128,2048]{1,0:T(8,128)(2,1)S(1)}, u32[]{:S(2)}, u32[]{:S(2)}) collective-permute-start(bf16[128,2048]{1,0:T(8,128)(2,1)S(1)} %get-tuple-element.76), channel_id=1, source_target_pairs={{0,4},{4,0},{8,12},{12,8},{16,20},{20,16},{24,28},{28,24},{1,5},{5... | collective-permute-start | bytes 1572872 | tf_op jit(solution)/shard_map/ppermute | solution.py:91
  31.7 5.5 %collective-permute-start.6 = (bf16[128,2176]{1,0:T(8,128)(2,1)S(1)}, bf16[128,2176]{1,0:T(8,128)(2,1)S(1)}, u32[]{:S(2)}, u32[]{:S(2)}) collective-permute-start(bf16[128,2176]{1,0:T(8,128)(2,1)S(1)} %pad_maximum_fusion), channel_id=1, source_target_pairs={{0,4},{4,0},{8,12},{12,8},{16,20},{20,16},{24,28},{28,24},{1,5},{5... | collective-permute-start | bytes 1671176 | tf_op jit(solution)/shard_map/ppermute | solution.py:91
  32.3 5.0 %collective-permute-start.7 = (bf16[2,128,704]{2,1,0:T(8,128)(2,1)S(1)}, bf16[2,128,704]{2,1,0:T(8,128)(2,1)S(1)}, u32[]{:S(2)}, u32[]{:S(2)}) collective-permute-start(bf16[2,128,704]{2,1,0:T(8,128)(2,1)S(1)} %get-tuple-element.64), channel_id=1, source_target_pairs={{0,4},{4,0},{8,12},{12,8},{16,20},{20,16},{24,28},{28,24},{1,5},{5... | collective-permute-start | bytes 1081352 | tf_op jit(solution)/shard_map/ppermute | solution.py:91
  33.6 16.3 %copy-start.1 = (bf16[128,2048]{1,0:T(8,128)(2,1)}, bf16[128,2048]{1,0:T(8,128)(2,1)S(1)}, u32[]{:S(2)}) copy-start(bf16[128,2048]{1,0:T(8,128)(2,1)S(1)} %collective-permute-done.8) | copy-start | bytes 1572868
  33.7 16.3 %collective-permute-start.11 = (bf16[32,2048]{1,0:T(8,128)(2,1)S(1)}, bf16[32,2048]{1,0:T(8,128)(2,1)S(1)}, u32[]{:S(2)}, u32[]{:S(2)}) collective-permute-start(bf16[32,2048]{1,0:T(8,128)(2,1)S(1)} %get-tuple-element.97), channel_id=1, source_target_pairs={{0,3},{1,2},{2,1},{3,0},{4,7},{5,6},{6,5},{7,4},{8,11},{9,10},{10,... | collective-permute-start | bytes 393224 | tf_op jit(solution)/shard_map/ppermute | solution.py:88
  36.6 13.4 %collective-permute-start.10 = (bf16[32,2048]{1,0:T(8,128)(2,1)S(1)}, bf16[32,2048]{1,0:T(8,128)(2,1)S(1)}, u32[]{:S(2)}, u32[]{:S(2)}) collective-permute-start(bf16[32,2048]{1,0:T(8,128)(2,1)S(1)} %get-tuple-element.98), channel_id=1, source_target_pairs={{0,2},{1,3},{2,0},{3,1},{4,5},{5,4},{6,7},{7,6},{8,10},{9,11},{10,... | collective-permute-start | bytes 393224 | tf_op jit(solution)/shard_map/ppermute | solution.py:88
  37.1 12.9 %collective-permute-start.9 = (bf16[32,2048]{1,0:T(8,128)(2,1)S(1)}, bf16[32,2048]{1,0:T(8,128)(2,1)S(1)}, u32[]{:S(2)}, u32[]{:S(2)}) collective-permute-start(bf16[32,2048]{1,0:T(8,128)(2,1)S(1)} %get-tuple-element.99), channel_id=1, source_target_pairs={{0,1},{1,0},{2,3},{3,2},{4,6},{5,7},{6,4},{7,5},{8,9},{9,8},{10,11... | collective-permute-start | bytes 393224 | tf_op jit(solution)/shard_map/ppermute | solution.py:88
  50.0 10.6 %slice-start = ((bf16[128,2048]{1,0:T(8,128)(2,1)}), bf16[32,2048]{1,0:T(8,128)(2,1)S(1)}, s32[]{:S(2)}) async-start(bf16[128,2048]{1,0:T(8,128)(2,1)} %copy-done.1), calls=%async_computation | async-start | bytes 262144 | tf_op jit(solution)/shard_map/slice | solution.py:467
  50.0 1.6 %collective-permute-start.12 = (bf16[128,1024]{1,0:T(8,128)(2,1)S(1)}, bf16[128,1024]{1,0:T(8,128)(2,1)S(1)}, u32[]{:S(2)}, u32[]{:S(2)}) collective-permute-start(bf16[128,1024]{1,0:T(8,128)(2,1)S(1)} %get-tuple-element.86), channel_id=1, source_target_pairs={{0,4},{4,0},{8,12},{12,8},{16,20},{20,16},{24,28},{28,24},{1,5},{5... | collective-permute-start | bytes 786440 | tf_op jit(solution)/shard_map/ppermute | solution.py:91
  50.1 3.5 %collective-permute-start.15 = (bf16[128,1152]{1,0:T(8,128)(2,1)S(1)}, bf16[128,1152]{1,0:T(8,128)(2,1)S(1)}, u32[]{:S(2)}, u32[]{:S(2)}) collective-permute-start(bf16[128,1152]{1,0:T(8,128)(2,1)S(1)} %get-tuple-element.91), channel_id=1, source_target_pairs={{0,4},{4,0},{8,12},{12,8},{16,20},{20,16},{24,28},{28,24},{1,5},{5... | collective-permute-start | bytes 884744 | tf_op jit(solution)/shard_map/ppermute | solution.py:91
  51.6 5.0 %collective-permute-start.13 = (bf16[64,1024]{1,0:T(8,128)(2,1)S(1)}, bf16[64,1024]{1,0:T(8,128)(2,1)S(1)}, u32[]{:S(2)}, u32[]{:S(2)}) collective-permute-start(bf16[64,1024]{1,0:T(8,128)(2,1)S(1)} %pad_maximum_fusion.2), channel_id=1, source_target_pairs={{0,1},{1,0},{2,3},{3,2},{4,6},{5,7},{6,4},{7,5},{8,9},{9,8},{10,11... | collective-permute-start | bytes 393224 | tf_op jit(solution)/shard_map/ppermute | solution.py:88
  53.7 9.7 %copy-start = (s32[32,6]{0,1:T(8,128)S(1)}, s32[32,6]{0,1:T(8,128)}, u32[]{:S(2)}) copy-start(s32[32,6]{0,1:T(8,128)} %param.15) | copy-start | bytes 2308
  53.7 5.2 %collective-permute-start.16 = (bf16[64,1152]{1,0:T(8,128)(2,1)S(1)}, bf16[64,1152]{1,0:T(8,128)(2,1)S(1)}, u32[]{:S(2)}, u32[]{:S(2)}) collective-permute-start(bf16[64,1152]{1,0:T(8,128)(2,1)S(1)} %pad_maximum_fusion.1), channel_id=1, source_target_pairs={{0,1},{1,0},{2,3},{3,2},{4,6},{5,7},{6,4},{7,5},{8,9},{9,8},{10,11... | collective-permute-start | bytes 442376 | tf_op jit(solution)/shard_map/ppermute | solution.py:88
  56.7 4.6 %collective-permute-start.14 = (bf16[32,1024]{1,0:T(8,128)(2,1)S(1)}, bf16[32,1024]{1,0:T(8,128)(2,1)S(1)}, u32[]{:S(2)}, u32[]{:S(2)}) collective-permute-start(bf16[32,1024]{1,0:T(8,128)(2,1)S(1)} %add_convert_fusion.7), channel_id=1, source_target_pairs={{0,2},{1,3},{2,0},{3,1},{4,5},{5,4},{6,7},{7,6},{8,10},{9,11},{10,... | collective-permute-start | bytes 196616 | tf_op jit(solution)/shard_map/ppermute | solution.py:88
  58.9 4.4 %collective-permute-start.17 = (bf16[32,1152]{1,0:T(8,128)(2,1)S(1)}, bf16[32,1152]{1,0:T(8,128)(2,1)S(1)}, u32[]{:S(2)}, u32[]{:S(2)}) collective-permute-start(bf16[32,1152]{1,0:T(8,128)(2,1)S(1)} %add_convert_fusion.4), channel_id=1, source_target_pairs={{0,2},{1,3},{2,0},{3,1},{4,5},{5,4},{6,7},{7,6},{8,10},{9,11},{10,... | collective-permute-start | bytes 221192 | tf_op jit(solution)/shard_map/ppermute | solution.py:88

commit v7 on v6

--- a/solution.py
+++ b/solution.py
@@ -68,6 +68,7 @@
         self.paired = self.owners & (self.owners - 1) == 0
         self.sent = self.width + self.meta
         self.half = round_up(self.width // 2, LANES)
+        self.kept = min(self.mine, 2)
         self.rows = self.mine * self.expert_rows
         self.cols = self.blocks * self.count
 
@@ -91,14 +92,19 @@
         return lax.ppermute(x, "dp", [(i, i ^ 1) for i in range(self.groups)])
 
 
-def pack_body(plan, x_hbm, routes_hbm, factors_hbm, out_ref, routes_ref, factors_ref, sems):
-    experts, count = plan.experts, plan.count
-    x_copy = pltpu.make_async_copy(x_hbm, out_ref.at[:, : plan.width], sems.at[0])
+def pack_body(plan, sources, near_ref, far_ref, routes_ref, factors_ref, sems):
+    x_hbm, routes_hbm, factors_hbm = sources
+    experts, count, half = plan.experts, plan.count, plan.half
+    rest = plan.width - half
+    rows = [
+        pltpu.make_async_copy(x_hbm.at[:, :half], near_ref, sems.at[0]),
+        pltpu.make_async_copy(x_hbm.at[:, half:], far_ref.at[:, :rest], sems.at[3]),
+    ]
     small = [
         pltpu.make_async_copy(routes_hbm, routes_ref, sems.at[1]),
         pltpu.make_async_copy(factors_hbm, factors_ref, sems.at[2]),
     ]
-    for copy in (*small, x_copy):
+    for copy in (*small, *rows):
         copy.start()
     for copy in small:
         copy.wait()
@@ -118,24 +124,32 @@
     facts = (chosen * (before + 1.0) + parts).astype(BF16)
     shape = (plan.meta, plan.meta)
     same = jnp.where(iota(shape, 0) == iota(shape, 1), 1.0, 0.0).astype(BF16)
-    out_ref[:, plan.width :] = dot_ta(facts, same).astype(BF16)
-    x_copy.wait()
+    far_ref[:, rest:] = dot_ta(facts, same).astype(BF16)
+    for copy in rows:
+        copy.wait()
 
 
 def pack_scratch(plan):
     return [
         pltpu.VMEM((plan.top, plan.count), jnp.int32),
         pltpu.VMEM((plan.top, plan.count), F32),
-        pltpu.SemaphoreType.DMA((3,)),
+        pltpu.SemaphoreType.DMA((4,)),
     ]
+
+
+def pack_kernel(plan, *refs):
+    pack_body(plan, refs[:3], *refs[3:])
 
 
 def pack(plan, x, routes, factors):
     return pl.pallas_call(
-        functools.partial(pack_body, plan),
-        out_shape=jax.ShapeDtypeStruct((plan.count, plan.width + plan.meta), BF16),
+        functools.partial(pack_kernel, plan),
+        out_shape=(
+            jax.ShapeDtypeStruct((plan.count, plan.half), BF16),
+            jax.ShapeDtypeStruct((plan.count, plan.sent - plan.half), BF16),
+        ),
         in_specs=[hbm()] * 3,
-        out_specs=vmem(),
+        out_specs=(vmem(), vmem()),
         scratch_shapes=pack_scratch(plan),
         compiler_params=pltpu.CompilerParams(vmem_limit_bytes=4 * MIB),
         name="pack",
@@ -173,12 +187,16 @@
     return jnp.where(hit, 1.0, 0.0).astype(BF16), factor
 
 
-def weight_copies(plan, array, ref, sems):
+def weight_copies(plan, array, slots, sems):
     offset = first_expert(plan)[1]
     return [
-        pltpu.make_async_copy(array.at[offset + e], ref.at[e], sems.at[e])
-        for e in range(plan.mine)
+        pltpu.make_async_copy(array.at[offset + e], slot, sems.at[e])
+        for e, slot in enumerate(slots)
     ]
+
+
+def weight_slots(plan, *refs):
+    return [ref.at[e] for ref in refs for e in range(ref.shape[0])][: plan.mine]
 
 
 def prepare_kernel(plan, x_hbm, routes_hbm, factors_hbm, gate_hbm, up_hbm, after, *refs):
@@ -192,9 +210,9 @@
     ]
     for copy in saved:
         copy.start()
-    pack_body(
-        plan, x_hbm, routes_hbm, factors_hbm, packed_ref, routes_ref, factors_ref, pack_sems
-    )
+    halves = packed_ref.at[:, : plan.half], packed_ref.at[:, plan.half :]
+    sources = x_hbm, routes_hbm, factors_hbm
+    pack_body(plan, sources, *halves, routes_ref, factors_ref, pack_sems)
     _, offset = first_expert(plan)
     shape = (plan.mine * plan.source_rows, gate_s.shape[0])
     row, col = iota(shape, 0), iota(shape, 1)
@@ -253,8 +271,8 @@
     return packed, saved, done
 
 
-def fetch_kernel(plan, w_hbm, after, w_ref, done_ref, sems):
-    copies = weight_copies(plan, w_hbm, w_ref, sems)
+def fetch_kernel(plan, w_hbm, after, also_after, w_ref, done_ref, sems):
+    copies = weight_copies(plan, w_hbm, weight_slots(plan, w_ref), sems)
     for copy in copies:
         copy.start()
     done_ref[...] = jnp.zeros_like(done_ref)
@@ -262,14 +280,14 @@
         copy.wait()
 
 
-def fetch(plan, w, after):
+def fetch(plan, w, after, also_after):
     return pl.pallas_call(
         functools.partial(fetch_kernel, plan),
         out_shape=(
             pltpu.VMEM((plan.mine, plan.hidden, plan.width), BF16),
             jax.ShapeDtypeStruct((16, plan.sent), BF16),
         ),
-        in_specs=[hbm(), pl.BlockSpec(memory_space=pl.ANY)],
+        in_specs=[hbm()] + [pl.BlockSpec(memory_space=pl.ANY)] * 2,
         out_specs=(vmem(), vmem()),
         scratch_shapes=[pltpu.SemaphoreType.DMA((plan.mine,))],
         compiler_params=pltpu.CompilerParams(vmem_limit_bytes=MIB),
@@ -279,18 +297,18 @@
             transcendentals=0,
         ),
         name="fetch",
-    )(in_hbm(w), after)
-
-
-def arrived(plan, blocks, first):
-    left, metas, rows = plan.cols, [], []
-    for block in blocks:
-        count = min(left, block.shape[0])
-        metas.append(block[:count, plan.width :])
-        rows.append(block[:count, : plan.width])
-        left -= count
-    table, factor = tables(plan, jnp.concatenate(metas, axis=0), first)
-    return table, factor, jnp.concatenate(rows, axis=0)
+    )(in_hbm(w), after, also_after)
+
+
+def arrived(plan, nears, fars, first, x_s):
+    half, rest = plan.half, plan.width - plan.half
+    metas = jnp.concatenate([far[:, rest:] for far in fars], axis=0)
+    table, factor = tables(plan, metas, first)
+    near = jnp.concatenate([near[...] for near in nears], axis=0)
+    x_s[:, :half] = dot(table, near).astype(BF16)
+    far = jnp.concatenate([far[:, :rest] for far in fars], axis=0)
+    x_s[:, half:] = dot(table, far).astype(BF16)
+    return table, factor
 
 
 class Queue:
@@ -313,14 +331,15 @@
 def forward_kernel(plan, count, *refs):
     blocks, refs = refs[:count], refs[count:]
     gate_ref, up_hbm, down_hbm, *refs = refs
-    outs, (up_s, down_s, x_s, y_s, gate_s, hidden_s, sems) = refs[:-7], refs[-7:]
+    outs, (kept_ref, up_s, down_s, x_s, y_s, gate_s, hidden_s, sems) = refs[:-8], refs[-8:]
     first, _ = first_expert(plan)
-    copies = weight_copies(plan, up_hbm, up_s, sems.at[0])
-    copies += weight_copies(plan, down_hbm, down_s, sems.at[1])
+    downs = weight_slots(plan, kept_ref, down_s)
+    copies = weight_copies(plan, up_hbm, weight_slots(plan, up_s), sems.at[0])
+    copies += weight_copies(plan, down_hbm, downs, sems.at[1])
     queue = Queue(copies, 3)
     queue.fill()
-    table, factor, rows = arrived(plan, blocks, first)
-    x_s[...] = dot(table, rows).astype(BF16)
+    nears, fars = blocks[: count // 2], blocks[count // 2 :]
+    table, factor = arrived(plan, nears, fars, first, x_s)
     n = plan.expert_rows
     parts = [slice(e * n, (e + 1) * n) for e in range(plan.mine)]
     for e, part in enumerate(parts):
@@ -336,7 +355,7 @@
     hidden_s[plan.mine - 1] = (gate / (1.0 + jnp.exp(-gate)) * up).astype(BF16)
     for e, part in enumerate(parts):
         queue.take()
-        out = dot(hidden_s[e], down_s[e])
+        out = dot(hidden_s[e], downs[e][...])
         y_s[part, :] = (out * factor[part]).astype(BF16)
     put_rows(outs, slice(None), dot_ta(table, y_s[...]).astype(BF16))
 
@@ -352,15 +371,17 @@
 def backward_kernel(plan, count, *refs):
     blocks, refs = refs[:count], refs[count:]
     saved_ref, other_ref, refs = refs[0], refs[plan.split - 1], refs[plan.split :]
-    gate_ref, up_hbm, down_hbm, *refs = refs
+    gate_ref, kept_ref, up_hbm, down_hbm, *refs = refs
     outs, (up_s, down_s, x_s, y_s, score_s, grads_s, sems) = refs[:-7], refs[-7:]
     first, _ = first_expert(plan)
-    copies = weight_copies(plan, down_hbm, down_s, sems.at[0])
-    copies += weight_copies(plan, up_hbm, up_s, sems.at[1])
-    queue = Queue(copies, 2)
+    downs = weight_slots(plan, kept_ref, down_s)
+    copies = weight_copies(plan, down_hbm, downs, sems.at[0])[plan.kept :]
+    copies += weight_copies(plan, up_hbm, weight_slots(plan, up_s), sems.at[1])
+    queue = Queue(copies, 3)
     queue.fill()
-    table, factor, rows = arrived(plan, blocks, first)
-    x_s[...] = dot(table, rows).astype(BF16)
+    nears = [block.at[:, : plan.half] for block in blocks]
+    fars = [block.at[:, plan.half :] for block in blocks]
+    table, factor = arrived(plan, nears, fars, first, x_s)
     n, held = plan.expert_rows, plan.source_rows
     lane = iota((n, plan.meta), 1)
     parts = [slice(e * n, (e + 1) * n) for e in range(plan.mine)]
@@ -388,8 +409,9 @@
 
     grad = None
     for e, part in enumerate(parts):
-        queue.take()
-        last, grad = grad, dot_tb(x_s[part, :], down_s[e])
+        if e >= plan.kept:
+            queue.take()
+        last, grad = grad, dot_tb(x_s[part, :], downs[e][...])
         if e:
             through_activation(e - 1, last)
     through_activation(plan.mine - 1, grad)
@@ -412,46 +434,55 @@
     return [block] * plan.owners + [other] * (plan.split - 1)
 
 
-def expert_call(plan, kernel, name, inputs, gate, up_hbm, down_hbm, widths, scratch):
-    shapes = [shape for width in widths for shape in part_shapes(plan, width)]
-    weight = pltpu.VMEM((plan.mine, plan.hidden, plan.width), BF16)
+def expert_call(plan, kernel, name, inputs, up_hbm, down_hbm, shapes, scratch):
+    def weight(count):
+        return pltpu.VMEM((count, plan.hidden, plan.width), BF16)
+
     rows = pltpu.VMEM((plan.rows, plan.width), BF16)
     return pl.pallas_call(
         kernel,
         out_shape=shapes,
-        in_specs=[vmem()] * (len(inputs) + 1) + [hbm()] * 2,
+        in_specs=[vmem()] * len(inputs) + [hbm()] * 2,
         out_specs=[vmem()] * len(shapes),
         scratch_shapes=[
-            *[weight, weight, rows, rows],
+            *[weight(plan.mine), weight(max(plan.mine - plan.kept, 1)), rows, rows],
             *scratch,
             pltpu.SemaphoreType.DMA((2, plan.mine)),
         ],
-        compiler_params=pltpu.CompilerParams(vmem_limit_bytes=36 * MIB),
+        compiler_params=pltpu.CompilerParams(vmem_limit_bytes=31 * MIB),
         cost_estimate=pl.CostEstimate(
             flops=2 * 3 * plan.mine * plan.expert_rows * plan.width * plan.hidden,
             bytes_accessed=2 * 2 * plan.mine * plan.width * plan.hidden,
             transcendentals=0,
         ),
         name=name,
-    )(*inputs, in_vmem(gate), in_hbm(up_hbm), in_hbm(down_hbm))
-
-
-def forward(plan, blocks, *weights):
-    kernel = functools.partial(forward_kernel, plan, len(blocks))
+    )(*inputs, in_hbm(up_hbm), in_hbm(down_hbm))
+
+
+def forward(plan, nears, fars, gate, up_hbm, down_hbm):
+    kernel = functools.partial(forward_kernel, plan, 2 * len(nears))
     shape = (plan.mine, plan.expert_rows, plan.hidden)
     scratch = [pltpu.VMEM(shape, F32), pltpu.VMEM(shape, BF16)]
-    return expert_call(plan, kernel, "forward", blocks, *weights, [plan.width], scratch)
-
-
-def backward(plan, blocks, saved, *weights):
+    kept = pltpu.VMEM((plan.kept, plan.hidden, plan.width), BF16)
+    shapes = part_shapes(plan, plan.width) + [kept]
+    inputs = [*nears, *fars, in_vmem(gate)]
+    *parts, kept = expert_call(
+        plan, kernel, "forward", inputs, up_hbm, down_hbm, shapes, scratch
+    )
+    return parts, kept
+
+
+def backward(plan, blocks, saved, gate, kept, up_hbm, down_hbm):
     kernel = functools.partial(backward_kernel, plan, len(blocks))
     scratch = [
         pltpu.VMEM((plan.rows, plan.meta), BF16),
         pltpu.VMEM((2, plan.mine, plan.expert_rows, plan.hidden), BF16),
     ]
-    widths = [plan.half, plan.sent - plan.half]
-    inputs = [*blocks, *saved]
-    parts = expert_call(plan, kernel, "backward", inputs, *weights, widths, scratch)
+    shapes = part_shapes(plan, plan.half) + part_shapes(plan, plan.sent - plan.half)
+    inputs = [*blocks, *saved, in_vmem(gate), in_vmem(kept)]
+    parts = expert_call(
+        plan, kernel, "backward", inputs, up_hbm, down_hbm, shapes, scratch
+    )
     return parts[: len(parts) // 2], parts[len(parts) // 2 :]
 
 
@@ -550,31 +581,34 @@
     w_down,
 ):
     plan = Plan(tokens, routes, saved_gate, w_gate)
-    packed = pack(plan, tokens, routes, weights_fwd)
+    near, far = pack(plan, tokens, routes, weights_fwd)
     packed_back, saved, ready = prepare(
-        plan, cotangent, routes_back, weights_back, saved_gate, saved_up, packed
+        plan, cotangent, routes_back, weights_back, saved_gate, saved_up, far
     )
     gate_hbm, up_hbm = jnp.swapaxes(w_gate, 1, 2), jnp.swapaxes(w_up, 1, 2)
     if plan.paired and plan.owners > 1:
-        blocks = [packed, plan.over_expert(packed, 1)]
-        gate, done = fetch(plan, gate_hbm, blocks[1])
+        fars = [far, plan.over_expert(far, 1)]
+        nears = [near, plan.over_expert(near + ready[:1, : plan.half], 1)]
+        gate, done = fetch(plan, gate_hbm, nears[1], fars[1])
         step = 2
         while step < plan.owners:
-            blocks.append(plan.over_expert(jnp.concatenate(blocks) + ready[:1], step))
+            fars.append(plan.over_expert(jnp.concatenate(fars), step))
+            nears.append(plan.over_expert(jnp.concatenate(nears), step))
             step *= 2
     else:
-        blocks = gather_group(plan, packed)
-        gate, done = fetch(plan, gate_hbm, packed)
+        nears, fars = gather_group(plan, near), gather_group(plan, far)
+        gate, done = fetch(plan, gate_hbm, near, far)
     if plan.split > 1:
-        blocks.append(plan.over_pair(jnp.concatenate(blocks) + done[:1]))
+        nears.append(plan.over_pair(jnp.concatenate(nears) + done[:1, : plan.half]))
+        fars.append(plan.over_pair(jnp.concatenate(fars)))
     blocks_back = gather_group(plan, packed_back)
-    parts = forward(plan, blocks, gate, up_hbm, w_down)
+    parts, kept = forward(plan, nears, fars, gate, up_hbm, w_down)
     parts, blocks_back = lax.optimization_barrier((parts, blocks_back))
     if plan.split > 1:
         blocks_back = blocks_back + [plan.over_pair(jnp.concatenate(blocks_back))]
         saved[1] = plan.over_pair(saved[1])
     terms = scatter_group(plan, sum_pair(plan, parts))
-    parts_back = backward(plan, blocks_back, saved, gate, up_hbm, w_down)
+    parts_back = backward(plan, blocks_back, saved, gate, kept, up_hbm, w_down)
     parts_back, terms = lax.optimization_barrier((parts_back, terms))
     mixed = total(terms).astype(BF16)
     near, far = scatter_steps(plan, [sum_pair(plan, parts) for parts in parts_back])

time: 64.5 us -> 66.1 us (1.025)
  waiting for transfers between devices: 8.63 us -> 11.9 us
  Pallas kernels: 33.8 us -> 32.7 us
    ppermute x12 -> x14, waiting for transfers between devices: 6.39 us -> 9.61 us  [over_expert(): return lax.ppermute(x, ('dp', 'expert'), pairs)]
    pallas_call x3, Pallas kernels: 27 us -> 26 us  [the longest x2 24.9 us: expert_call(): pl.pallas_call(kernel, out_shape=shapes, in_specs=[vmem()] * len(inputs)...]
    ppermute x12 -> x14, starting transfers between devices: 18.2 us -> 17.2 us  [over_expert(): return lax.ppermute(x, ('dp', 'expert'), pairs)]
    ppermute x6 -> x7, starting transfers between devices: 1.35 us -> 1.9 us  [over_pair(): return lax.ppermute(x, 'dp', [(i, i ^ 1) for i in range(self.groups)])]
    ppermute x6 -> x7, waiting for transfers between devices: 2.25 us -> 2.25 us  [over_pair(): return lax.ppermute(x, 'dp', [(i, i ^ 1) for i in range(self.groups)])]
  transfers between devices with their start and end apart: 18 -> 21, of which waited for: 7 -> 8; matrix products, arithmetic and copies ran while one was open for 2% -> 2% of each run, Pallas kernels for 50% -> 47%
where the time goes in v7:
time: 66.1 us; the launch traced here: 65.9 us
  Pallas kernels  32.7 us (49%)
  starting transfers between devices  19.1 us (29%)
  waiting for transfers between devices  11.9 us (18%)
  other arithmetic  1.14 us (2%)
  between operations  1.06 us (2%)
    pallas_call x2, Pallas kernels, expert_call(): pl.pallas_call(kernel, out_shape=shapes, in_specs=[vmem()] * len(inputs)...  24.9 us
    ppermute x14, starting transfers between devices, over_expert(): return lax.ppermute(x, ('dp', 'expert'), pairs)  17.2 us
    ppermute x14, waiting for transfers between devices, over_expert(): return lax.ppermute(x, ('dp', 'expert'), pairs)  9.61 us
    pallas_call x1, Pallas kernels, fetch(): pl.pallas_call(functools.partial(fetch_kernel, plan), out_shape=(pltpu.VM...  4.4 us
    ppermute x7, waiting for transfers between devices, over_pair(): return lax.ppermute(x, 'dp', [(i, i ^ 1) for i in range(self.groups)])  2.25 us
    ppermute x7, starting transfers between devices, over_pair(): return lax.ppermute(x, 'dp', [(i, i ^ 1) for i in range(self.groups)])  1.9 us
    pallas_call x1, Pallas kernels, prepare(): pl.pallas_call(functools.partial(prepare_kernel, plan), out_shape=out_sha...  1.57 us
  transfers between devices with their start and end apart: 21, of which 8 were waited for; matrix products, arithmetic and copies ran while one was open for 2% of the time, Pallas kernels for 47%

profile of v7, /device:TPU:0, one launch (start us, length us, event | category | flops | bytes accessed | tf_op | source)
XLA Modules:
  0.0 65.9 jit_solution(11018233213964429505)
XLA Ops:
  0.6 1.1 %pack.1 = (bf16[32,1024]{1,0:T(8,128)(2,1)S(1)}, bf16[32,1152]{1,0:T(8,128)(2,1)S(1)}) custom-call(bf16[32,2048]{1,0:T(8,128)(2,1)} %refs_0_.1, s32[6,32]{1,0:T(8,128)} %bitcast.25, f32[6,32]{1,0:T(8,128)} %bitcast.26), custom_call_target="tpu_custom_call" | custom-call | tf_op jit(solution)/shard_map/pack/pallas_call | solution.py:145
  1.7 3.0 %collective-permute-start.2 = (bf16[32,1152]{1,0:T(8,128)(2,1)S(1)}, bf16[32,1152]{1,0:T(8,128)(2,1)S(1)}, u32[]{:S(2)}, u32[]{:S(2)}) collective-permute-start(bf16[32,1152]{1,0:T(8,128)(2,1)S(1)} %get-tuple-element.54.after.refs_4_), channel_id=1, source_target_pairs={{1,0},{0,1},{3,2},{2,3},{6,4},{7,5},{4,6},{5,7},{9,8},{8,9},{11,10... | collective-permute-start | bytes 221192 | tf_op jit(solution)/shard_map/ppermute | solution.py:89
  4.7 1.6 %prepare.1 = (bf16[32,2176]{1,0:T(8,128)(2,1)S(1)}, bf16[16,2176]{1,0:T(8,128)(2,1)S(1)}, bf16[2,128,704]{2,1,0:T(8,128)(2,1)S(1)}, bf16[2,128,704]{2,1,0:T(8,128)(2,1)S(1)}) custom-call(bf16[32,2048]{1,0:T(8,128)(2,1)} %x_hbm.1, s32[6,32]{1,0:T(8,128)} %bitcast.17, f32[6,32]{1,0:T(8,128)} %bitcast.24, bf16[224,704]{1,0:T(8,128)(2,1)} %bitcast.22, ...), custom_call_target="tpu_custom_call" | custom-call | bytes 17825792 | tf_op jit(solution)/shard_map/prepare/pallas_call | solution.py:247
  6.4 0.6 collective-permute-done.2.also_after.refs_5_
  7.1 2.1 %collective-permute-start.4 = (bf16[64,1152]{1,0:T(8,128)(2,1)S(1)}, bf16[64,1152]{1,0:T(8,128)(2,1)S(1)}, u32[]{:S(2)}, u32[]{:S(2)}) collective-permute-start(bf16[64,1152]{1,0:T(8,128)(2,1)S(1)} %pad_maximum_fusion.2), channel_id=1, source_target_pairs={{2,0},{3,1},{0,2},{1,3},{5,4},{4,5},{7,6},{6,7},{10,8},{11,9},{8,1... | collective-permute-start | bytes 442376 | tf_op jit(solution)/shard_map/ppermute | solution.py:89
  9.2 1.8 %collective-permute-done.after.refs_1_ = bf16[32,1024]{1,0:T(8,128)(2,1)S(1)} collective-permute-done((bf16[32,1024]{1,0:T(8,128)(2,1)S(1)}, bf16[32,1024]{1,0:T(8,128)(2,1)S(1)}, u32[]{:S(2)}, u32[]{:S(2)}) %collective-permute-start) | collective-permute-done | bytes 65568 | tf_op jit(solution)/shard_map/ppermute | solution.py:89
  11.0 2.0 %collective-permute-start.1 = (bf16[64,1024]{1,0:T(8,128)(2,1)S(1)}, bf16[64,1024]{1,0:T(8,128)(2,1)S(1)}, u32[]{:S(2)}, u32[]{:S(2)}) collective-permute-start(bf16[64,1024]{1,0:T(8,128)(2,1)S(1)} %pad_maximum_fusion.4), channel_id=1, source_target_pairs={{2,0},{3,1},{0,2},{1,3},{5,4},{4,5},{7,6},{6,7},{10,8},{11,9},{8,1... | collective-permute-start | bytes 393224 | tf_op jit(solution)/shard_map/ppermute | solution.py:89
  13.0 4.4 %fetch.1 = (bf16[4,704,2048]{2,1,0:T(8,128)(2,1)S(1)}, bf16[16,2176]{1,0:T(8,128)(2,1)S(1)}) custom-call(bf16[8,704,2048]{2,1,0:T(8,128)(2,1)} %bitcast.21, bf16[32,1024]{1,0:T(8,128)(2,1)S(1)} %collective-permute-done.after.refs_1_, bf16[32,1152]{1,0:T(8,128)(2,1)S(1)} %collective-permute-done.2.also_after.refs_5_), custom_call_target="tpu_custom_call" | custom-call | bytes 23068672 | tf_op jit(solution)/shard_map/fetch/pallas_call | solution.py:284
  18.1 2.0 %collective-permute-start.7 = (bf16[32,2176]{1,0:T(8,128)(2,1)S(1)}, bf16[32,2176]{1,0:T(8,128)(2,1)S(1)}, u32[]{:S(2)}, u32[]{:S(2)}) collective-permute-start(bf16[32,2176]{1,0:T(8,128)(2,1)S(1)} %get-tuple-element.64.refs_0_), channel_id=1, source_target_pairs={{2,0},{3,1},{0,2},{1,3},{5,4},{4,5},{7,6},{6,7},{10,8},{11,9},{8,1... | collective-permute-start | bytes 417800 | tf_op jit(solution)/shard_map/ppermute | solution.py:89
  20.1 1.5 %collective-permute-start.6 = (bf16[32,2176]{1,0:T(8,128)(2,1)S(1)}, bf16[32,2176]{1,0:T(8,128)(2,1)S(1)}, u32[]{:S(2)}, u32[]{:S(2)}) collective-permute-start(bf16[32,2176]{1,0:T(8,128)(2,1)S(1)} %get-tuple-element.64.refs_0_), channel_id=1, source_target_pairs={{1,0},{0,1},{3,2},{2,3},{6,4},{7,5},{4,6},{5,7},{9,8},{8,9},{11,10... | collective-permute-start | bytes 417800 | tf_op jit(solution)/shard_map/ppermute | solution.py:89
  21.6 13.3 %forward.1 = (bf16[32,2048]{1,0:T(8,128)(2,1)S(1)}, bf16[32,2048]{1,0:T(8,128)(2,1)S(1)}, bf16[32,2048]{1,0:T(8,128)(2,1)S(1)}, bf16[32,2048]{1,0:T(8,128)(2,1)S...) custom-call(bf16[32,1024]{1,0:T(8,128)(2,1)S(1)} %get-tuple-element.53.refs_0_, ...), custom_call_target="tpu_custom_call" | custom-call | flops 2214592512 | bytes 23068672 | tf_op jit(solution)/shard_map/forward/pallas_call | solution.py:442
  35.7 1.2 %collective-permute-done.11 = bf16[128,2048]{1,0:T(8,128)(2,1)S(1)} collective-permute-done((bf16[128,2048]{1,0:T(8,128)(2,1)S(1)}, bf16[128,2048]{1,0:T(8,128)(2,1)S(1)}, u32[]{:S(2)}, u32[]{:S(2)}) %collective-permute-start.11) | collective-permute-done | bytes 524320 | tf_op jit(solution)/shard_map/ppermute | solution.py:92
  37.1 2.0 %collective-permute-start.13 = (bf16[32,2048]{1,0:T(8,128)(2,1)S(1)}, bf16[32,2048]{1,0:T(8,128)(2,1)S(1)}, u32[]{:S(2)}, u32[]{:S(2)}) collective-permute-start(bf16[32,2048]{1,0:T(8,128)(2,1)S(1)} %get-tuple-element.104), channel_id=1, source_target_pairs={{0,2},{1,3},{2,0},{3,1},{4,5},{5,4},{6,7},{7,6},{8,10},{9,11},{10,... | collective-permute-start | bytes 393224 | tf_op jit(solution)/shard_map/ppermute | solution.py:89
  39.1 1.5 %collective-permute-start.12 = (bf16[32,2048]{1,0:T(8,128)(2,1)S(1)}, bf16[32,2048]{1,0:T(8,128)(2,1)S(1)}, u32[]{:S(2)}, u32[]{:S(2)}) collective-permute-start(bf16[32,2048]{1,0:T(8,128)(2,1)S(1)} %get-tuple-element.105), channel_id=1, source_target_pairs={{0,1},{1,0},{2,3},{3,2},{4,6},{5,7},{6,4},{7,5},{8,9},{9,8},{10,11... | collective-permute-start | bytes 393224 | tf_op jit(solution)/shard_map/ppermute | solution.py:89
  40.6 11.6 %backward.1 = (bf16[32,1024]{1,0:T(8,128)(2,1)S(1)}, bf16[32,1024]{1,0:T(8,128)(2,1)S(1)}, bf16[32,1024]{1,0:T(8,128)(2,1)S(1)}, bf16[32,1024]{1,0:T(8,128)(2,1)...) custom-call(bf16[32,2176]{1,0:T(8,128)(2,1)S(1)} %get-tuple-element., ...), custom_call_target="tpu_custom_call" | custom-call | flops 2214592512 | bytes 23068672 | tf_op jit(solution)/shard_map/backward/pallas_call | solution.py:442
  52.8 1.0 %collective-permute-done.15 = bf16[128,1024]{1,0:T(8,128)(2,1)S(1)} collective-permute-done((bf16[128,1024]{1,0:T(8,128)(2,1)S(1)}, bf16[128,1024]{1,0:T(8,128)(2,1)S(1)}, u32[]{:S(2)}, u32[]{:S(2)}) %collective-permute-start.15) | collective-permute-done | bytes 262176 | tf_op jit(solution)/shard_map/ppermute | solution.py:92
  54.6 1.6 %collective-permute-start.19 = (bf16[64,1152]{1,0:T(8,128)(2,1)S(1)}, bf16[64,1152]{1,0:T(8,128)(2,1)S(1)}, u32[]{:S(2)}, u32[]{:S(2)}) collective-permute-start(bf16[64,1152]{1,0:T(8,128)(2,1)S(1)} %pad_maximum_fusion.3), channel_id=1, source_target_pairs={{0,1},{1,0},{2,3},{3,2},{4,6},{5,7},{6,4},{7,5},{8,9},{9,8},{10,11... | collective-permute-start | bytes 442376 | tf_op jit(solution)/shard_map/ppermute | solution.py:89
  56.2 2.8 %collective-permute-done.16 = bf16[64,1024]{1,0:T(8,128)(2,1)S(1)} collective-permute-done((bf16[64,1024]{1,0:T(8,128)(2,1)S(1)}, bf16[64,1024]{1,0:T(8,128)(2,1)S(1)}, u32[]{:S(2)}, u32[]{:S(2)}) %collective-permute-start.16) | collective-permute-done | bytes 131104 | tf_op jit(solution)/shard_map/ppermute | solution.py:89
  59.2 1.3 %collective-permute-done.19 = bf16[64,1152]{1,0:T(8,128)(2,1)S(1)} collective-permute-done((bf16[64,1152]{1,0:T(8,128)(2,1)S(1)}, bf16[64,1152]{1,0:T(8,128)(2,1)S(1)}, u32[]{:S(2)}, u32[]{:S(2)}) %collective-permute-start.19) | collective-permute-done | bytes 147488 | tf_op jit(solution)/shard_map/ppermute | solution.py:89
  60.6 0.6 collective-permute-start.20
  61.2 0.7 %add_convert_fusion = bf16[32,2048]{1,0:T(8,128)(2,1)} fusion(bf16[32,2048]{1,0:T(8,128)(2,1)S(1)} %collective-permute-done.14, bf16[32,2048]{1,0:T(8,128)(2,1)S(1)} %collective-permute-done.13, bf16[32,2048]{1,0:T(8,128)(2,1)S(1)} %collective-permute-done.12, bf16[32,2048]{1,0:T(8,128)(2,1)S(1)} %slice-done, bf16[32,2048]{1,0:T(8,128)(2,1)S(1)} %get-tuple-element.86), kind=kLoop, calls=%fused_computation.3 | loop fusion | flops 655360 | bytes 786432 | tf_op jit(solution)/shard_map/convert_element_type | solution.py:613
  62.0 1.3 %collective-permute-done.17.refs_3_ = bf16[32,1024]{1,0:T(8,128)(2,1)S(1)} collective-permute-done((bf16[32,1024]{1,0:T(8,128)(2,1)S(1)}, bf16[32,1024]{1,0:T(8,128)(2,1)S(1)}, u32[]{:S(2)}, u32[]{:S(2)}) %collective-permute-start.17) | collective-permute-done | bytes 65568 | tf_op jit(solution)/shard_map/ppermute | solution.py:89
  63.3 1.7 %collective-permute-done.20.refs_7_ = bf16[32,1152]{1,0:T(8,128)(2,1)S(1)} collective-permute-done((bf16[32,1152]{1,0:T(8,128)(2,1)S(1)}, bf16[32,1152]{1,0:T(8,128)(2,1)S(1)}, u32[]{:S(2)}, u32[]{:S(2)}) %collective-permute-start.20) | collective-permute-done | bytes 73760 | tf_op jit(solution)/shard_map/ppermute | solution.py:89
  65.0 0.8 %finish.1 = (bf16[32,2048]{1,0:T(8,128)(2,1)}, f32[6,32]{1,0:T(8,128)}) custom-call(bf16[32,1024]{1,0:T(8,128)(2,1)S(1)} %get-tuple-element.91.refs_0_, bf16[32,1024]{1,0:T(8,128)(2,1)S(1)} %slice.76.refs_1_, bf16[32,1024]{1,0:T(8,128)(2,1)S(1)} %slice.79.refs_2_, bf16[32,1024]{1,0:T(8,128)(2,1)S(1)} %collective-permute-done.17.refs_3_, ...), custom_call_target="tpu_custom_call" | custom-call | tf_op jit(solution)/shard_map/finish/pallas_call | solution.py:551
  (50 shorter events, 3.4 us)
Async XLA Ops:
  1.7 5.3 %collective-permute-start.2 = (bf16[32,1152]{1,0:T(8,128)(2,1)S(1)}, bf16[32,1152]{1,0:T(8,128)(2,1)S(1)}, u32[]{:S(2)}, u32[]{:S(2)}) collective-permute-start(bf16[32,1152]{1,0:T(8,128)(2,1)S(1)} %get-tuple-element.54.after.refs_4_), channel_id=1, source_target_pairs={{1,0},{0,1},{3,2},{2,3},{6,4},{7,5},{4,6},{5,7},{9,8},{8,9},{11,10... | collective-permute-start | bytes 221192 | tf_op jit(solution)/shard_map/ppermute | solution.py:89
  6.3 4.7 %collective-permute-start = (bf16[32,1024]{1,0:T(8,128)(2,1)S(1)}, bf16[32,1024]{1,0:T(8,128)(2,1)S(1)}, u32[]{:S(2)}, u32[]{:S(2)}) collective-permute-start(bf16[32,1024]{1,0:T(8,128)(2,1)S(1)} %broadcast_add_fusion), channel_id=1, source_target_pairs={{1,0},{0,1},{3,2},{2,3},{6,4},{7,5},{4,6},{5,7},{9,8},{8,9},{11,10... | collective-permute-start | bytes 196616 | tf_op jit(solution)/shard_map/ppermute | solution.py:89
  7.1 10.3 %collective-permute-start.4 = (bf16[64,1152]{1,0:T(8,128)(2,1)S(1)}, bf16[64,1152]{1,0:T(8,128)(2,1)S(1)}, u32[]{:S(2)}, u32[]{:S(2)}) collective-permute-start(bf16[64,1152]{1,0:T(8,128)(2,1)S(1)} %pad_maximum_fusion.2), channel_id=1, source_target_pairs={{2,0},{3,1},{0,2},{1,3},{5,4},{4,5},{7,6},{6,7},{10,8},{11,9},{8,1... | collective-permute-start | bytes 442376 | tf_op jit(solution)/shard_map/ppermute | solution.py:89
  11.0 6.5 %collective-permute-start.1 = (bf16[64,1024]{1,0:T(8,128)(2,1)S(1)}, bf16[64,1024]{1,0:T(8,128)(2,1)S(1)}, u32[]{:S(2)}, u32[]{:S(2)}) collective-permute-start(bf16[64,1024]{1,0:T(8,128)(2,1)S(1)} %pad_maximum_fusion.4), channel_id=1, source_target_pairs={{2,0},{3,1},{0,2},{1,3},{5,4},{4,5},{7,6},{6,7},{10,8},{11,9},{8,1... | collective-permute-start | bytes 393224 | tf_op jit(solution)/shard_map/ppermute | solution.py:89
  17.4 4.2 %collective-permute-start.5 = (bf16[128,1152]{1,0:T(8,128)(2,1)S(1)}, bf16[128,1152]{1,0:T(8,128)(2,1)S(1)}, u32[]{:S(2)}, u32[]{:S(2)}) collective-permute-start(bf16[128,1152]{1,0:T(8,128)(2,1)S(1)} %pad_maximum_fusion.1), channel_id=1, source_target_pairs={{0,4},{4,0},{8,12},{12,8},{16,20},{20,16},{24,28},{28,24},{1,5},{5... | collective-permute-start | bytes 884744 | tf_op jit(solution)/shard_map/ppermute | solution.py:92
  17.6 4.0 %collective-permute-start.3 = (bf16[128,1024]{1,0:T(8,128)(2,1)S(1)}, bf16[128,1024]{1,0:T(8,128)(2,1)S(1)}, u32[]{:S(2)}, u32[]{:S(2)}) collective-permute-start(bf16[128,1024]{1,0:T(8,128)(2,1)S(1)} %maximum_add_fusion), channel_id=1, source_target_pairs={{0,4},{4,0},{8,12},{12,8},{16,20},{20,16},{24,28},{28,24},{1,5},{5... | collective-permute-start | bytes 786440 | tf_op jit(solution)/shard_map/ppermute | solution.py:92
  18.1 16.8 %collective-permute-start.8 = (bf16[32,2176]{1,0:T(8,128)(2,1)S(1)}, bf16[32,2176]{1,0:T(8,128)(2,1)S(1)}, u32[]{:S(2)}, u32[]{:S(2)}) collective-permute-start(bf16[32,2176]{1,0:T(8,128)(2,1)S(1)} %get-tuple-element.64.refs_0_), channel_id=1, source_target_pairs={{3,0},{2,1},{1,2},{0,3},{7,4},{6,5},{5,6},{4,7},{11,8},{10,9},{9,1... | collective-permute-start | bytes 417800 | tf_op jit(solution)/shard_map/ppermute | solution.py:89
  18.1 16.8 %collective-permute-start.7 = (bf16[32,2176]{1,0:T(8,128)(2,1)S(1)}, bf16[32,2176]{1,0:T(8,128)(2,1)S(1)}, u32[]{:S(2)}, u32[]{:S(2)}) collective-permute-start(bf16[32,2176]{1,0:T(8,128)(2,1)S(1)} %get-tuple-element.64.refs_0_), channel_id=1, source_target_pairs={{2,0},{3,1},{0,2},{1,3},{5,4},{4,5},{7,6},{6,7},{10,8},{11,9},{8,1... | collective-permute-start | bytes 417800 | tf_op jit(solution)/shard_map/ppermute | solution.py:89
  20.1 14.8 %collective-permute-start.6 = (bf16[32,2176]{1,0:T(8,128)(2,1)S(1)}, bf16[32,2176]{1,0:T(8,128)(2,1)S(1)}, u32[]{:S(2)}, u32[]{:S(2)}) collective-permute-start(bf16[32,2176]{1,0:T(8,128)(2,1)S(1)} %get-tuple-element.64.refs_0_), channel_id=1, source_target_pairs={{1,0},{0,1},{3,2},{2,3},{6,4},{7,5},{4,6},{5,7},{9,8},{8,9},{11,10... | collective-permute-start | bytes 417800 | tf_op jit(solution)/shard_map/ppermute | solution.py:89
  35.0 2.0 %collective-permute-start.11 = (bf16[128,2048]{1,0:T(8,128)(2,1)S(1)}, bf16[128,2048]{1,0:T(8,128)(2,1)S(1)}, u32[]{:S(2)}, u32[]{:S(2)}) collective-permute-start(bf16[128,2048]{1,0:T(8,128)(2,1)S(1)} %get-tuple-element.82), channel_id=1, source_target_pairs={{0,4},{4,0},{8,12},{12,8},{16,20},{20,16},{24,28},{28,24},{1,5},{5... | collective-permute-start | bytes 1572872 | tf_op jit(solution)/shard_map/ppermute | solution.py:92
  35.1 5.5 %collective-permute-start.9 = (bf16[128,2176]{1,0:T(8,128)(2,1)S(1)}, bf16[128,2176]{1,0:T(8,128)(2,1)S(1)}, u32[]{:S(2)}, u32[]{:S(2)}) collective-permute-start(bf16[128,2176]{1,0:T(8,128)(2,1)S(1)} %pad_maximum_fusion), channel_id=1, source_target_pairs={{0,4},{4,0},{8,12},{12,8},{16,20},{20,16},{24,28},{28,24},{1,5},{5... | collective-permute-start | bytes 1671176 | tf_op jit(solution)/shard_map/ppermute | solution.py:92
  35.7 4.9 %collective-permute-start.10 = (bf16[2,128,704]{2,1,0:T(8,128)(2,1)S(1)}, bf16[2,128,704]{2,1,0:T(8,128)(2,1)S(1)}, u32[]{:S(2)}, u32[]{:S(2)}) collective-permute-start(bf16[2,128,704]{2,1,0:T(8,128)(2,1)S(1)} %get-tuple-element.69), channel_id=1, source_target_pairs={{0,4},{4,0},{8,12},{12,8},{16,20},{20,16},{24,28},{28,24},{1,5},{5... | collective-permute-start | bytes 1081352 | tf_op jit(solution)/shard_map/ppermute | solution.py:92
  37.0 15.3 %copy-start.1 = (bf16[128,2048]{1,0:T(8,128)(2,1)}, bf16[128,2048]{1,0:T(8,128)(2,1)S(1)}, u32[]{:S(2)}) copy-start(bf16[128,2048]{1,0:T(8,128)(2,1)S(1)} %collective-permute-done.11) | copy-start | bytes 1572868
  37.1 15.2 %collective-permute-start.14 = (bf16[32,2048]{1,0:T(8,128)(2,1)S(1)}, bf16[32,2048]{1,0:T(8,128)(2,1)S(1)}, u32[]{:S(2)}, u32[]{:S(2)}) collective-permute-start(bf16[32,2048]{1,0:T(8,128)(2,1)S(1)} %get-tuple-element.103), channel_id=1, source_target_pairs={{0,3},{1,2},{2,1},{3,0},{4,7},{5,6},{6,5},{7,4},{8,11},{9,10},{10,... | collective-permute-start | bytes 393224 | tf_op jit(solution)/shard_map/ppermute | solution.py:89
  37.1 15.1 %collective-permute-start.13 = (bf16[32,2048]{1,0:T(8,128)(2,1)S(1)}, bf16[32,2048]{1,0:T(8,128)(2,1)S(1)}, u32[]{:S(2)}, u32[]{:S(2)}) collective-permute-start(bf16[32,2048]{1,0:T(8,128)(2,1)S(1)} %get-tuple-element.104), channel_id=1, source_target_pairs={{0,2},{1,3},{2,0},{3,1},{4,5},{5,4},{6,7},{7,6},{8,10},{9,11},{10,... | collective-permute-start | bytes 393224 | tf_op jit(solution)/shard_map/ppermute | solution.py:89
  39.1 13.1 %collective-permute-start.12 = (bf16[32,2048]{1,0:T(8,128)(2,1)S(1)}, bf16[32,2048]{1,0:T(8,128)(2,1)S(1)}, u32[]{:S(2)}, u32[]{:S(2)}) collective-permute-start(bf16[32,2048]{1,0:T(8,128)(2,1)S(1)} %get-tuple-element.105), channel_id=1, source_target_pairs={{0,1},{1,0},{2,3},{3,2},{4,6},{5,7},{6,4},{7,5},{8,9},{9,8},{10,11... | collective-permute-start | bytes 393224 | tf_op jit(solution)/shard_map/ppermute | solution.py:89
  52.2 9.0 %slice-start = ((bf16[128,2048]{1,0:T(8,128)(2,1)}), bf16[32,2048]{1,0:T(8,128)(2,1)S(1)}, s32[]{:S(2)}) async-start(bf16[128,2048]{1,0:T(8,128)(2,1)} %copy-done.1), calls=%async_computation | async-start | bytes 262144 | tf_op jit(solution)/shard_map/slice | solution.py:498
  52.3 1.6 %collective-permute-start.15 = (bf16[128,1024]{1,0:T(8,128)(2,1)S(1)}, bf16[128,1024]{1,0:T(8,128)(2,1)S(1)}, u32[]{:S(2)}, u32[]{:S(2)}) collective-permute-start(bf16[128,1024]{1,0:T(8,128)(2,1)S(1)} %get-tuple-element.92), channel_id=1, source_target_pairs={{0,4},{4,0},{8,12},{12,8},{16,20},{20,16},{24,28},{28,24},{1,5},{5... | collective-permute-start | bytes 786440 | tf_op jit(solution)/shard_map/ppermute | solution.py:92
  52.3 2.2 %collective-permute-start.18 = (bf16[128,1152]{1,0:T(8,128)(2,1)S(1)}, bf16[128,1152]{1,0:T(8,128)(2,1)S(1)}, u32[]{:S(2)}, u32[]{:S(2)}) collective-permute-start(bf16[128,1152]{1,0:T(8,128)(2,1)S(1)} %get-tuple-element.97), channel_id=1, source_target_pairs={{0,4},{4,0},{8,12},{12,8},{16,20},{20,16},{24,28},{28,24},{1,5},{5... | collective-permute-start | bytes 884744 | tf_op jit(solution)/shard_map/ppermute | solution.py:92
  53.9 5.0 %collective-permute-start.16 = (bf16[64,1024]{1,0:T(8,128)(2,1)S(1)}, bf16[64,1024]{1,0:T(8,128)(2,1)S(1)}, u32[]{:S(2)}, u32[]{:S(2)}) collective-permute-start(bf16[64,1024]{1,0:T(8,128)(2,1)S(1)} %pad_maximum_fusion.5), channel_id=1, source_target_pairs={{0,1},{1,0},{2,3},{3,2},{4,6},{5,7},{6,4},{7,5},{8,9},{9,8},{10,11... | collective-permute-start | bytes 393224 | tf_op jit(solution)/shard_map/ppermute | solution.py:89
  54.6 10.4 %copy-start = (s32[32,6]{0,1:T(8,128)S(1)}, s32[32,6]{0,1:T(8,128)}, u32[]{:S(2)}) copy-start(s32[32,6]{0,1:T(8,128)} %param.15) | copy-start | bytes 2308
  54.6 5.9 %collective-permute-start.19 = (bf16[64,1152]{1,0:T(8,128)(2,1)S(1)}, bf16[64,1152]{1,0:T(8,128)(2,1)S(1)}, u32[]{:S(2)}, u32[]{:S(2)}) collective-permute-start(bf16[64,1152]{1,0:T(8,128)(2,1)S(1)} %pad_maximum_fusion.3), channel_id=1, source_target_pairs={{0,1},{1,0},{2,3},{3,2},{4,6},{5,7},{6,4},{7,5},{8,9},{9,8},{10,11... | collective-permute-start | bytes 442376 | tf_op jit(solution)/shard_map/ppermute | solution.py:89
  59.0 4.3 %collective-permute-start.17 = (bf16[32,1024]{1,0:T(8,128)(2,1)S(1)}, bf16[32,1024]{1,0:T(8,128)(2,1)S(1)}, u32[]{:S(2)}, u32[]{:S(2)}) collective-permute-start(bf16[32,1024]{1,0:T(8,128)(2,1)S(1)} %add_convert_fusion.7), channel_id=1, source_target_pairs={{0,2},{1,3},{2,0},{3,1},{4,5},{5,4},{6,7},{7,6},{8,10},{9,11},{10,... | collective-permute-start | bytes 196616 | tf_op jit(solution)/shard_map/ppermute | solution.py:89
  60.6 4.4 %collective-permute-start.20 = (bf16[32,1152]{1,0:T(8,128)(2,1)S(1)}, bf16[32,1152]{1,0:T(8,128)(2,1)S(1)}, u32[]{:S(2)}, u32[]{:S(2)}) collective-permute-start(bf16[32,1152]{1,0:T(8,128)(2,1)S(1)} %add_convert_fusion.4), channel_id=1, source_target_pairs={{0,2},{1,3},{2,0},{3,1},{4,5},{5,4},{6,7},{7,6},{8,10},{9,11},{10,... | collective-permute-start | bytes 221192 | tf_op jit(solution)/shard_map/ppermute | solution.py:89

commit v8 on v7

--- a/solution.py
+++ b/solution.py
@@ -92,19 +92,15 @@
         return lax.ppermute(x, "dp", [(i, i ^ 1) for i in range(self.groups)])
 
 
-def pack_body(plan, sources, near_ref, far_ref, routes_ref, factors_ref, sems):
+def pack_body(plan, sources, out_ref, routes_ref, factors_ref, sems):
     x_hbm, routes_hbm, factors_hbm = sources
-    experts, count, half = plan.experts, plan.count, plan.half
-    rest = plan.width - half
-    rows = [
-        pltpu.make_async_copy(x_hbm.at[:, :half], near_ref, sems.at[0]),
-        pltpu.make_async_copy(x_hbm.at[:, half:], far_ref.at[:, :rest], sems.at[3]),
-    ]
+    experts, count = plan.experts, plan.count
+    rows = pltpu.make_async_copy(x_hbm, out_ref.at[:, : plan.width], sems.at[0])
     small = [
         pltpu.make_async_copy(routes_hbm, routes_ref, sems.at[1]),
         pltpu.make_async_copy(factors_hbm, factors_ref, sems.at[2]),
     ]
-    for copy in (*small, *rows):
+    for copy in (*small, rows):
         copy.start()
     for copy in small:
         copy.wait()
@@ -124,16 +120,15 @@
     facts = (chosen * (before + 1.0) + parts).astype(BF16)
     shape = (plan.meta, plan.meta)
     same = jnp.where(iota(shape, 0) == iota(shape, 1), 1.0, 0.0).astype(BF16)
-    far_ref[:, rest:] = dot_ta(facts, same).astype(BF16)
-    for copy in rows:
-        copy.wait()
+    out_ref[:, plan.width :] = dot_ta(facts, same).astype(BF16)
+    rows.wait()
 
 
 def pack_scratch(plan):
     return [
         pltpu.VMEM((plan.top, plan.count), jnp.int32),
         pltpu.VMEM((plan.top, plan.count), F32),
-        pltpu.SemaphoreType.DMA((4,)),
+        pltpu.SemaphoreType.DMA((3,)),
     ]
 
 
@@ -144,12 +139,9 @@
 def pack(plan, x, routes, factors):
     return pl.pallas_call(
         functools.partial(pack_kernel, plan),
-        out_shape=(
-            jax.ShapeDtypeStruct((plan.count, plan.half), BF16),
-            jax.ShapeDtypeStruct((plan.count, plan.sent - plan.half), BF16),
-        ),
+        out_shape=jax.ShapeDtypeStruct((plan.count, plan.sent), BF16),
         in_specs=[hbm()] * 3,
-        out_specs=(vmem(), vmem()),
+        out_specs=vmem(),
         scratch_shapes=pack_scratch(plan),
         compiler_params=pltpu.CompilerParams(vmem_limit_bytes=4 * MIB),
         name="pack",
@@ -164,25 +156,20 @@
 def tables(plan, meta, first):
     me = lax.axis_index("expert")
     core = lax.rem(lax.axis_index("dp"), plan.split)
-    row = iota((plan.rows, plan.meta), 0)
-    lane = iota((plan.rows, plan.meta), 1)
+    row = iota((plan.rows, 1), 0)
+    place = row % plan.expert_rows
     expert = first + row // plan.expert_rows
+    wanted_slot = (row % plan.cap_rows + 1).astype(F32)
+    wanted_block = place // plan.cap_rows
+    lane = iota((1, plan.meta), 1)
     pick_slot = jnp.where(lane == expert, 1.0, 0.0).astype(BF16)
-    pick_part = jnp.where(
-        (lane == expert + plan.experts) | (lane == expert + 2 * plan.experts), 1.0, 0.0
-    ).astype(BF16)
+    pick_part = (lane == expert + plan.experts) | (lane == expert + 2 * plan.experts)
     slot = dot_tb(pick_slot, meta)
-    part = dot_tb(pick_part, meta)
-    shape = (plan.rows, plan.cols)
-    row = iota(shape, 0)
-    col = iota(shape, 1)
-    block = col // plan.count
+    part = dot_tb(jnp.where(pick_part, 1.0, 0.0).astype(BF16), meta)
+    block = iota((1, plan.cols), 1) // plan.count
     group = block // plan.owners
     source = plan.peer(me, block % plan.owners, core ^ group)
-    place = row % plan.expert_rows
-    want = (row % plan.cap_rows + 1).astype(F32)
-    same = (place // plan.cap_rows) == group * plan.owners + source
-    hit = same & (slot == want)
+    hit = (wanted_block == group * plan.owners + source) & (slot == wanted_slot)
     factor = jnp.sum(jnp.where(hit, part, 0.0), axis=1, keepdims=True)
     return jnp.where(hit, 1.0, 0.0).astype(BF16), factor
 
@@ -210,9 +197,8 @@
     ]
     for copy in saved:
         copy.start()
-    halves = packed_ref.at[:, : plan.half], packed_ref.at[:, plan.half :]
     sources = x_hbm, routes_hbm, factors_hbm
-    pack_body(plan, sources, *halves, routes_ref, factors_ref, pack_sems)
+    pack_body(plan, sources, packed_ref, routes_ref, factors_ref, pack_sems)
     _, offset = first_expert(plan)
     shape = (plan.mine * plan.source_rows, gate_s.shape[0])
     row, col = iota(shape, 0), iota(shape, 1)
@@ -271,7 +257,7 @@
     return packed, saved, done
 
 
-def fetch_kernel(plan, w_hbm, after, also_after, w_ref, done_ref, sems):
+def fetch_kernel(plan, w_hbm, after, w_ref, done_ref, sems):
     copies = weight_copies(plan, w_hbm, weight_slots(plan, w_ref), sems)
     for copy in copies:
         copy.start()
@@ -280,14 +266,14 @@
         copy.wait()
 
 
-def fetch(plan, w, after, also_after):
+def fetch(plan, w, after):
     return pl.pallas_call(
         functools.partial(fetch_kernel, plan),
         out_shape=(
             pltpu.VMEM((plan.mine, plan.hidden, plan.width), BF16),
             jax.ShapeDtypeStruct((16, plan.sent), BF16),
         ),
-        in_specs=[hbm()] + [pl.BlockSpec(memory_space=pl.ANY)] * 2,
+        in_specs=[hbm(), pl.BlockSpec(memory_space=pl.ANY)],
         out_specs=(vmem(), vmem()),
         scratch_shapes=[pltpu.SemaphoreType.DMA((plan.mine,))],
         compiler_params=pltpu.CompilerParams(vmem_limit_bytes=MIB),
@@ -297,17 +283,14 @@
             transcendentals=0,
         ),
         name="fetch",
-    )(in_hbm(w), after, also_after)
-
-
-def arrived(plan, nears, fars, first, x_s):
-    half, rest = plan.half, plan.width - plan.half
-    metas = jnp.concatenate([far[:, rest:] for far in fars], axis=0)
+    )(in_hbm(w), after)
+
+
+def arrived(plan, blocks, first, x_s):
+    metas = jnp.concatenate([block[:, plan.width :] for block in blocks], axis=0)
     table, factor = tables(plan, metas, first)
-    near = jnp.concatenate([near[...] for near in nears], axis=0)
-    x_s[:, :half] = dot(table, near).astype(BF16)
-    far = jnp.concatenate([far[:, :rest] for far in fars], axis=0)
-    x_s[:, half:] = dot(table, far).astype(BF16)
+    rows = jnp.concatenate([block[:, : plan.width] for block in blocks], axis=0)
+    x_s[...] = dot(table, rows).astype(BF16)
     return table, factor
 
 
@@ -338,8 +321,7 @@
     copies += weight_copies(plan, down_hbm, downs, sems.at[1])
     queue = Queue(copies, 3)
     queue.fill()
-    nears, fars = blocks[: count // 2], blocks[count // 2 :]
-    table, factor = arrived(plan, nears, fars, first, x_s)
+    table, factor = arrived(plan, blocks, first, x_s)
     n = plan.expert_rows
     parts = [slice(e * n, (e + 1) * n) for e in range(plan.mine)]
     for e, part in enumerate(parts):
@@ -379,9 +361,7 @@
     copies += weight_copies(plan, up_hbm, weight_slots(plan, up_s), sems.at[1])
     queue = Queue(copies, 3)
     queue.fill()
-    nears = [block.at[:, : plan.half] for block in blocks]
-    fars = [block.at[:, plan.half :] for block in blocks]
-    table, factor = arrived(plan, nears, fars, first, x_s)
+    table, factor = arrived(plan, blocks, first, x_s)
     n, held = plan.expert_rows, plan.source_rows
     lane = iota((n, plan.meta), 1)
     parts = [slice(e * n, (e + 1) * n) for e in range(plan.mine)]
@@ -428,10 +408,12 @@
     put_rows(far, slice(rest, rest + plan.meta), scores)
 
 
-def part_shapes(plan, width):
+def part_shapes(plan, width, pieces=1):
     block = jax.ShapeDtypeStruct((plan.count, width), BF16)
-    other = jax.ShapeDtypeStruct((plan.owners * plan.count, width), BF16)
-    return [block] * plan.owners + [other] * (plan.split - 1)
+    pieces = pieces if plan.owners % pieces == 0 else 1
+    rows = plan.owners * plan.count // pieces
+    other = jax.ShapeDtypeStruct((rows, width), BF16)
+    return [block] * plan.owners + [other] * ((plan.split - 1) * pieces)
 
 
 def expert_call(plan, kernel, name, inputs, up_hbm, down_hbm, shapes, scratch):
@@ -459,13 +441,13 @@
     )(*inputs, in_hbm(up_hbm), in_hbm(down_hbm))
 
 
-def forward(plan, nears, fars, gate, up_hbm, down_hbm):
-    kernel = functools.partial(forward_kernel, plan, 2 * len(nears))
+def forward(plan, blocks, gate, up_hbm, down_hbm):
+    kernel = functools.partial(forward_kernel, plan, len(blocks))
     shape = (plan.mine, plan.expert_rows, plan.hidden)
     scratch = [pltpu.VMEM(shape, F32), pltpu.VMEM(shape, BF16)]
     kept = pltpu.VMEM((plan.kept, plan.hidden, plan.width), BF16)
-    shapes = part_shapes(plan, plan.width) + [kept]
-    inputs = [*nears, *fars, in_vmem(gate)]
+    shapes = part_shapes(plan, plan.width, 2) + [kept]
+    inputs = [*blocks, in_vmem(gate)]
     *parts, kept = expert_call(
         plan, kernel, "forward", inputs, up_hbm, down_hbm, shapes, scratch
     )
@@ -492,10 +474,12 @@
 
 def sum_pair(plan, parts):
     own = [[p] for p in parts[: plan.owners]]
-    if plan.split > 1:
-        other = plan.over_pair(parts[plan.owners])
-        for d in range(plan.owners):
-            own[d].append(other[d * plan.count : (d + 1) * plan.count])
+    d = 0
+    for piece in parts[plan.owners :]:
+        other = plan.over_pair(piece)
+        for start in range(0, piece.shape[0], plan.count):
+            own[d].append(other[start : start + plan.count])
+            d += 1
     return own
 
 
@@ -581,28 +565,25 @@
     w_down,
 ):
     plan = Plan(tokens, routes, saved_gate, w_gate)
-    near, far = pack(plan, tokens, routes, weights_fwd)
+    packed = pack(plan, tokens, routes, weights_fwd)
     packed_back, saved, ready = prepare(
-        plan, cotangent, routes_back, weights_back, saved_gate, saved_up, far
+        plan, cotangent, routes_back, weights_back, saved_gate, saved_up, packed
     )
     gate_hbm, up_hbm = jnp.swapaxes(w_gate, 1, 2), jnp.swapaxes(w_up, 1, 2)
     if plan.paired and plan.owners > 1:
-        fars = [far, plan.over_expert(far, 1)]
-        nears = [near, plan.over_expert(near + ready[:1, : plan.half], 1)]
-        gate, done = fetch(plan, gate_hbm, nears[1], fars[1])
+        blocks = [packed, plan.over_expert(packed, 1)]
+        gate, done = fetch(plan, gate_hbm, blocks[1])
         step = 2
         while step < plan.owners:
-            fars.append(plan.over_expert(jnp.concatenate(fars), step))
-            nears.append(plan.over_expert(jnp.concatenate(nears), step))
+            blocks.append(plan.over_expert(jnp.concatenate(blocks) + ready[:1], step))
             step *= 2
     else:
-        nears, fars = gather_group(plan, near), gather_group(plan, far)
-        gate, done = fetch(plan, gate_hbm, near, far)
+        blocks = gather_group(plan, packed)
+        gate, done = fetch(plan, gate_hbm, packed)
     if plan.split > 1:
-        nears.append(plan.over_pair(jnp.concatenate(nears) + done[:1, : plan.half]))
-        fars.append(plan.over_pair(jnp.concatenate(fars)))
+        blocks.append(plan.over_pair(jnp.concatenate(blocks) + done[:1]))
     blocks_back = gather_group(plan, packed_back)
-    parts, kept = forward(plan, nears, fars, gate, up_hbm, w_down)
+    parts, kept = forward(plan, blocks, gate, up_hbm, w_down)
     parts, blocks_back = lax.optimization_barrier((parts, blocks_back))
     if plan.split > 1:
         blocks_back = blocks_back + [plan.over_pair(jnp.concatenate(blocks_back))]

time: 66.1 us -> 63.2 us (0.956)
  waiting for transfers between devices: 11.9 us -> 8.07 us
  starting transfers between devices: 19.1 us -> 19.9 us
    ppermute x14 -> x12, waiting for transfers between devices: 9.61 us -> 6.49 us  [over_expert(): return lax.ppermute(x, ('dp', 'expert'), pairs)]
    ppermute x14 -> x12, starting transfers between devices: 17.2 us -> 18.1 us  [over_expert(): return lax.ppermute(x, ('dp', 'expert'), pairs)]
    ppermute x7, waiting for transfers between devices: 2.25 us -> 1.58 us  [over_pair(): return lax.ppermute(x, 'dp', [(i, i ^ 1) for i in range(self.groups)])]
  transfers between devices with their start and end apart: 21 -> 19, of which waited for: 8 -> 7; matrix products, arithmetic and copies ran while one was open for 2% -> 2% of each run, Pallas kernels for 47% -> 49%
where the time goes in v8:
time: 63.2 us; the launch traced here: 63 us
  Pallas kernels  32.7 us (52%)
  starting transfers between devices  19.9 us (31%)
  waiting for transfers between devices  8.07 us (13%)
  other arithmetic  1.19 us (2%)
  between operations  1.01 us (2%)
    pallas_call x2, Pallas kernels, expert_call(): pl.pallas_call(kernel, out_shape=shapes, in_specs=[vmem()] * len(inputs)...  24.9 us
    ppermute x12, starting transfers between devices, over_expert(): return lax.ppermute(x, ('dp', 'expert'), pairs)  18.1 us
    ppermute x12, waiting for transfers between devices, over_expert(): return lax.ppermute(x, ('dp', 'expert'), pairs)  6.49 us
    pallas_call x1, Pallas kernels, fetch(): pl.pallas_call(functools.partial(fetch_kernel, plan), out_shape=(pltpu.VM...  4.4 us
    ppermute x7, starting transfers between devices, over_pair(): return lax.ppermute(x, 'dp', [(i, i ^ 1) for i in range(self.groups)])  1.79 us
    pallas_call x1, Pallas kernels, prepare(): pl.pallas_call(functools.partial(prepare_kernel, plan), out_shape=out_sha...  1.59 us
    ppermute x7, waiting for transfers between devices, over_pair(): return lax.ppermute(x, 'dp', [(i, i ^ 1) for i in range(self.groups)])  1.58 us
  transfers between devices with their start and end apart: 19, of which 7 were waited for; matrix products, arithmetic and copies ran while one was open for 2% of the time, Pallas kernels for 49%

profile of v8, /device:TPU:0, one launch (start us, length us, event | category | flops | bytes accessed | tf_op | source)
XLA Modules:
  0.0 63.0 jit_solution(7857872895084833225)
XLA Ops:
  0.6 1.1 %pack.1.after.refs_0_ = bf16[32,2176]{1,0:T(8,128)(2,1)S(1)} custom-call(bf16[32,2048]{1,0:T(8,128)(2,1)} %refs_0_.1, s32[6,32]{1,0:T(8,128)} %bitcast.24, f32[6,32]{1,0:T(8,128)} %bitcast.25), custom_call_target="tpu_custom_call" | custom-call | tf_op jit(solution)/shard_map/pack/pallas_call | solution.py:140
  1.7 3.0 %collective-permute-start = (bf16[32,2176]{1,0:T(8,128)(2,1)S(1)}, bf16[32,2176]{1,0:T(8,128)(2,1)S(1)}, u32[]{:S(2)}, u32[]{:S(2)}) collective-permute-start(bf16[32,2176]{1,0:T(8,128)(2,1)S(1)} %pack.1.after.refs_0_), channel_id=1, source_target_pairs={{1,0},{0,1},{3,2},{2,3},{6,4},{7,5},{4,6},{5,7},{9,8},{8,9},{11,10... | collective-permute-start | bytes 417800 | tf_op jit(solution)/shard_map/ppermute | solution.py:89
  4.7 1.6 %prepare.1 = (bf16[32,2176]{1,0:T(8,128)(2,1)S(1)}, bf16[16,2176]{1,0:T(8,128)(2,1)S(1)}, bf16[2,128,704]{2,1,0:T(8,128)(2,1)S(1)}, bf16[2,128,704]{2,1,0:T(8,128)(2,1)S(1)}) custom-call(bf16[32,2048]{1,0:T(8,128)(2,1)} %x_hbm.1, s32[6,32]{1,0:T(8,128)} %bitcast.17, f32[6,32]{1,0:T(8,128)} %bitcast.26, bf16[224,704]{1,0:T(8,128)(2,1)} %bitcast.22, ...), custom_call_target="tpu_custom_call" | custom-call | bytes 17825792 | tf_op jit(solution)/shard_map/prepare/pallas_call | solution.py:233
  6.3 1.4 %collective-permute-done.after.refs_1_ = bf16[32,2176]{1,0:T(8,128)(2,1)S(1)} collective-permute-done((bf16[32,2176]{1,0:T(8,128)(2,1)S(1)}, bf16[32,2176]{1,0:T(8,128)(2,1)S(1)}, u32[]{:S(2)}, u32[]{:S(2)}) %collective-permute-start) | collective-permute-done | bytes 139296 | tf_op jit(solution)/shard_map/ppermute | solution.py:89
  7.8 2.1 %collective-permute-start.1 = (bf16[64,2176]{1,0:T(8,128)(2,1)S(1)}, bf16[64,2176]{1,0:T(8,128)(2,1)S(1)}, u32[]{:S(2)}, u32[]{:S(2)}) collective-permute-start(bf16[64,2176]{1,0:T(8,128)(2,1)S(1)} %maximum_add_fusion.1), channel_id=1, source_target_pairs={{2,0},{3,1},{0,2},{1,3},{5,4},{4,5},{7,6},{6,7},{10,8},{11,9},{8,1... | collective-permute-start | bytes 835592 | tf_op jit(solution)/shard_map/ppermute | solution.py:89
  9.9 4.4 %fetch.1 = (bf16[4,704,2048]{2,1,0:T(8,128)(2,1)S(1)}, bf16[16,2176]{1,0:T(8,128)(2,1)S(1)}) custom-call(bf16[8,704,2048]{2,1,0:T(8,128)(2,1)} %bitcast.21, bf16[32,2176]{1,0:T(8,128)(2,1)S(1)} %collective-permute-done.after.refs_1_), custom_call_target="tpu_custom_call" | custom-call | bytes 23068672 | tf_op jit(solution)/shard_map/fetch/pallas_call | solution.py:270
  14.6 3.0 %collective-permute-start.5 = (bf16[32,2176]{1,0:T(8,128)(2,1)S(1)}, bf16[32,2176]{1,0:T(8,128)(2,1)S(1)}, u32[]{:S(2)}, u32[]{:S(2)}) collective-permute-start(bf16[32,2176]{1,0:T(8,128)(2,1)S(1)} %get-tuple-element.63.refs_0_), channel_id=1, source_target_pairs={{3,0},{2,1},{1,2},{0,3},{7,4},{6,5},{5,6},{4,7},{11,8},{10,9},{9,1... | collective-permute-start | bytes 417800 | tf_op jit(solution)/shard_map/ppermute | solution.py:89
  17.6 0.5 collective-permute-start.4
  18.3 13.3 %forward.1 = (bf16[32,2048]{1,0:T(8,128)(2,1)S(1)}, bf16[32,2048]{1,0:T(8,128)(2,1)S(1)}, bf16[32,2048]{1,0:T(8,128)(2,1)S(1)}, bf16[32,2048]{1,0:T(8,128)(2,1)S...) custom-call(bf16[32,2176]{1,0:T(8,128)(2,1)S(1)} %pack.1.after.refs_0_, ...), custom_call_target="tpu_custom_call" | custom-call | flops 2214592512 | bytes 23068672 | tf_op jit(solution)/shard_map/forward/pallas_call | solution.py:424
  31.6 0.6 collective-permute-start.8
  32.3 0.5 collective-permute-start.6
  32.8 0.5 collective-permute-done.8
  33.4 1.9 %collective-permute-start.9 = (bf16[32,2048]{1,0:T(8,128)(2,1)S(1)}, bf16[32,2048]{1,0:T(8,128)(2,1)S(1)}, u32[]{:S(2)}, u32[]{:S(2)}) collective-permute-start(bf16[32,2048]{1,0:T(8,128)(2,1)S(1)} %add_convert_fusion.3), channel_id=1, source_target_pairs={{0,1},{1,0},{2,3},{3,2},{4,6},{5,7},{6,4},{7,5},{8,9},{9,8},{10,11... | collective-permute-start | bytes 393224 | tf_op jit(solution)/shard_map/ppermute | solution.py:89
  35.4 1.6 %collective-permute-start.12 = (bf16[32,2048]{1,0:T(8,128)(2,1)S(1)}, bf16[32,2048]{1,0:T(8,128)(2,1)S(1)}, u32[]{:S(2)}, u32[]{:S(2)}) collective-permute-start(bf16[32,2048]{1,0:T(8,128)(2,1)S(1)} %get-tuple-element.107), channel_id=1, source_target_pairs={{0,3},{1,2},{2,1},{3,0},{4,7},{5,6},{6,5},{7,4},{8,11},{9,10},{10,... | collective-permute-start | bytes 393224 | tf_op jit(solution)/shard_map/ppermute | solution.py:89
  37.2 11.6 %backward.1 = (bf16[32,1024]{1,0:T(8,128)(2,1)S(1)}, bf16[32,1024]{1,0:T(8,128)(2,1)S(1)}, bf16[32,1024]{1,0:T(8,128)(2,1)S(1)}, bf16[32,1024]{1,0:T(8,128)(2,1)...) custom-call(bf16[32,2176]{1,0:T(8,128)(2,1)S(1)} %get-tuple-element., ...), custom_call_target="tpu_custom_call" | custom-call | flops 2214592512 | bytes 23068672 | tf_op jit(solution)/shard_map/backward/pallas_call | solution.py:424
  48.9 0.5 collective-permute-start.16
  49.4 1.0 %collective-permute-done.13 = bf16[128,1024]{1,0:T(8,128)(2,1)S(1)} collective-permute-done((bf16[128,1024]{1,0:T(8,128)(2,1)S(1)}, bf16[128,1024]{1,0:T(8,128)(2,1)S(1)}, u32[]{:S(2)}, u32[]{:S(2)}) %collective-permute-start.13) | collective-permute-done | bytes 262176 | tf_op jit(solution)/shard_map/ppermute | solution.py:92
  50.5 1.8 %collective-permute-start.14 = (bf16[64,1024]{1,0:T(8,128)(2,1)S(1)}, bf16[64,1024]{1,0:T(8,128)(2,1)S(1)}, u32[]{:S(2)}, u32[]{:S(2)}) collective-permute-start(bf16[64,1024]{1,0:T(8,128)(2,1)S(1)} %pad_maximum_fusion.2), channel_id=1, source_target_pairs={{0,1},{1,0},{2,3},{3,2},{4,6},{5,7},{6,4},{7,5},{8,9},{9,8},{10,11... | collective-permute-start | bytes 393224 | tf_op jit(solution)/shard_map/ppermute | solution.py:89
  52.8 2.8 %collective-permute-done.14 = bf16[64,1024]{1,0:T(8,128)(2,1)S(1)} collective-permute-done((bf16[64,1024]{1,0:T(8,128)(2,1)S(1)}, bf16[64,1024]{1,0:T(8,128)(2,1)S(1)}, u32[]{:S(2)}, u32[]{:S(2)}) %collective-permute-start.14) | collective-permute-done | bytes 131104 | tf_op jit(solution)/shard_map/ppermute | solution.py:89
  55.6 1.9 %collective-permute-start.15 = (bf16[32,1024]{1,0:T(8,128)(2,1)S(1)}, bf16[32,1024]{1,0:T(8,128)(2,1)S(1)}, u32[]{:S(2)}, u32[]{:S(2)}) collective-permute-start(bf16[32,1024]{1,0:T(8,128)(2,1)S(1)} %add_convert_fusion.7), channel_id=1, source_target_pairs={{0,2},{1,3},{2,0},{3,1},{4,5},{5,4},{6,7},{7,6},{8,10},{9,11},{10,... | collective-permute-start | bytes 196616 | tf_op jit(solution)/shard_map/ppermute | solution.py:89
  57.7 1.6 %collective-permute-start.18 = (bf16[32,1152]{1,0:T(8,128)(2,1)S(1)}, bf16[32,1152]{1,0:T(8,128)(2,1)S(1)}, u32[]{:S(2)}, u32[]{:S(2)}) collective-permute-start(bf16[32,1152]{1,0:T(8,128)(2,1)S(1)} %add_convert_fusion.4), channel_id=1, source_target_pairs={{0,2},{1,3},{2,0},{3,1},{4,5},{5,4},{6,7},{7,6},{8,10},{9,11},{10,... | collective-permute-start | bytes 221192 | tf_op jit(solution)/shard_map/ppermute | solution.py:89
  59.2 0.7 %add_convert_fusion = bf16[32,2048]{1,0:T(8,128)(2,1)} fusion(bf16[32,2048]{1,0:T(8,128)(2,1)S(1)} %collective-permute-done.12, bf16[32,2048]{1,0:T(8,128)(2,1)S(1)} %collective-permute-done.11, bf16[32,2048]{1,0:T(8,128)(2,1)S(1)} %collective-permute-done.9, bf16[32,2048]{1,0:T(8,128)(2,1)S(1)} %slice-done, bf16[32,2048]{1,0:T(8,128)(2,1)S(1)} %get-tuple-element.86), kind=kLoop, calls=%fused_computation.3 | loop fusion | flops 655360 | bytes 786432 | tf_op jit(solution)/shard_map/convert_element_type | solution.py:594
  60.0 2.0 %collective-permute-done.18.refs_7_ = bf16[32,1152]{1,0:T(8,128)(2,1)S(1)} collective-permute-done((bf16[32,1152]{1,0:T(8,128)(2,1)S(1)}, bf16[32,1152]{1,0:T(8,128)(2,1)S(1)}, u32[]{:S(2)}, u32[]{:S(2)}) %collective-permute-start.18) | collective-permute-done | bytes 73760 | tf_op jit(solution)/shard_map/ppermute | solution.py:89
  62.1 0.8 %finish.1 = (bf16[32,2048]{1,0:T(8,128)(2,1)}, f32[6,32]{1,0:T(8,128)}) custom-call(bf16[32,1024]{1,0:T(8,128)(2,1)S(1)} %get-tuple-element.91.refs_0_, bf16[32,1024]{1,0:T(8,128)(2,1)S(1)} %slice.76.refs_1_, bf16[32,1024]{1,0:T(8,128)(2,1)S(1)} %slice.79.refs_2_, bf16[32,1024]{1,0:T(8,128)(2,1)S(1)} %collective-permute-done.15.refs_3_, ...), custom_call_target="tpu_custom_call" | custom-call | tf_op jit(solution)/shard_map/finish/pallas_call | solution.py:535
  (44 shorter events, 1.8 us)
Async XLA Ops:
  1.7 6.0 %collective-permute-start = (bf16[32,2176]{1,0:T(8,128)(2,1)S(1)}, bf16[32,2176]{1,0:T(8,128)(2,1)S(1)}, u32[]{:S(2)}, u32[]{:S(2)}) collective-permute-start(bf16[32,2176]{1,0:T(8,128)(2,1)S(1)} %pack.1.after.refs_0_), channel_id=1, source_target_pairs={{1,0},{0,1},{3,2},{2,3},{6,4},{7,5},{4,6},{5,7},{9,8},{8,9},{11,10... | collective-permute-start | bytes 417800 | tf_op jit(solution)/shard_map/ppermute | solution.py:89
  7.8 6.6 %collective-permute-start.1 = (bf16[64,2176]{1,0:T(8,128)(2,1)S(1)}, bf16[64,2176]{1,0:T(8,128)(2,1)S(1)}, u32[]{:S(2)}, u32[]{:S(2)}) collective-permute-start(bf16[64,2176]{1,0:T(8,128)(2,1)S(1)} %maximum_add_fusion.1), channel_id=1, source_target_pairs={{2,0},{3,1},{0,2},{1,3},{5,4},{4,5},{7,6},{6,7},{10,8},{11,9},{8,1... | collective-permute-start | bytes 835592 | tf_op jit(solution)/shard_map/ppermute | solution.py:89
  14.5 3.7 %collective-permute-start.2 = (bf16[128,2176]{1,0:T(8,128)(2,1)S(1)}, bf16[128,2176]{1,0:T(8,128)(2,1)S(1)}, u32[]{:S(2)}, u32[]{:S(2)}) collective-permute-start(bf16[128,2176]{1,0:T(8,128)(2,1)S(1)} %maximum_add_fusion), channel_id=1, source_target_pairs={{0,4},{4,0},{8,12},{12,8},{16,20},{20,16},{24,28},{28,24},{1,5},{5... | collective-permute-start | bytes 1671176 | tf_op jit(solution)/shard_map/ppermute | solution.py:92
  14.6 17.0 %collective-permute-start.5 = (bf16[32,2176]{1,0:T(8,128)(2,1)S(1)}, bf16[32,2176]{1,0:T(8,128)(2,1)S(1)}, u32[]{:S(2)}, u32[]{:S(2)}) collective-permute-start(bf16[32,2176]{1,0:T(8,128)(2,1)S(1)} %get-tuple-element.63.refs_0_), channel_id=1, source_target_pairs={{3,0},{2,1},{1,2},{0,3},{7,4},{6,5},{5,6},{4,7},{11,8},{10,9},{9,1... | collective-permute-start | bytes 417800 | tf_op jit(solution)/shard_map/ppermute | solution.py:89
  17.6 14.0 %collective-permute-start.4 = (bf16[32,2176]{1,0:T(8,128)(2,1)S(1)}, bf16[32,2176]{1,0:T(8,128)(2,1)S(1)}, u32[]{:S(2)}, u32[]{:S(2)}) collective-permute-start(bf16[32,2176]{1,0:T(8,128)(2,1)S(1)} %get-tuple-element.63.refs_0_), channel_id=1, source_target_pairs={{2,0},{3,1},{0,2},{1,3},{5,4},{4,5},{7,6},{6,7},{10,8},{11,9},{8,1... | collective-permute-start | bytes 417800 | tf_op jit(solution)/shard_map/ppermute | solution.py:89
  18.1 13.5 %collective-permute-start.3 = (bf16[32,2176]{1,0:T(8,128)(2,1)S(1)}, bf16[32,2176]{1,0:T(8,128)(2,1)S(1)}, u32[]{:S(2)}, u32[]{:S(2)}) collective-permute-start(bf16[32,2176]{1,0:T(8,128)(2,1)S(1)} %get-tuple-element.63.refs_0_), channel_id=1, source_target_pairs={{1,0},{0,1},{3,2},{2,3},{6,4},{7,5},{4,6},{5,7},{9,8},{8,9},{11,10... | collective-permute-start | bytes 417800 | tf_op jit(solution)/shard_map/ppermute | solution.py:89
  18.3 18.9 %collective-permute-start.7 = (bf16[2,128,704]{2,1,0:T(8,128)(2,1)S(1)}, bf16[2,128,704]{2,1,0:T(8,128)(2,1)S(1)}, u32[]{:S(2)}, u32[]{:S(2)}) collective-permute-start(bf16[2,128,704]{2,1,0:T(8,128)(2,1)S(1)} %get-tuple-element.68), channel_id=1, source_target_pairs={{0,4},{4,0},{8,12},{12,8},{16,20},{20,16},{24,28},{28,24},{1,5},{5... | collective-permute-start | bytes 1081352 | tf_op jit(solution)/shard_map/ppermute | solution.py:92
  31.6 1.7 %collective-permute-start.8 = (bf16[64,2048]{1,0:T(8,128)(2,1)S(1)}, bf16[64,2048]{1,0:T(8,128)(2,1)S(1)}, u32[]{:S(2)}, u32[]{:S(2)}) collective-permute-start(bf16[64,2048]{1,0:T(8,128)(2,1)S(1)} %get-tuple-element.81), channel_id=1, source_target_pairs={{0,4},{4,0},{8,12},{12,8},{16,20},{20,16},{24,28},{28,24},{1,5},{5... | collective-permute-start | bytes 786440 | tf_op jit(solution)/shard_map/ppermute | solution.py:92
  32.2 3.2 %collective-permute-start.10 = (bf16[64,2048]{1,0:T(8,128)(2,1)S(1)}, bf16[64,2048]{1,0:T(8,128)(2,1)S(1)}, u32[]{:S(2)}, u32[]{:S(2)}) collective-permute-start(bf16[64,2048]{1,0:T(8,128)(2,1)S(1)} %get-tuple-element.84), channel_id=1, source_target_pairs={{0,4},{4,0},{8,12},{12,8},{16,20},{20,16},{24,28},{28,24},{1,5},{5... | collective-permute-start | bytes 786440 | tf_op jit(solution)/shard_map/ppermute | solution.py:92
  32.3 4.9 %collective-permute-start.6 = (bf16[128,2176]{1,0:T(8,128)(2,1)S(1)}, bf16[128,2176]{1,0:T(8,128)(2,1)S(1)}, u32[]{:S(2)}, u32[]{:S(2)}) collective-permute-start(bf16[128,2176]{1,0:T(8,128)(2,1)S(1)} %pad_maximum_fusion), channel_id=1, source_target_pairs={{0,4},{4,0},{8,12},{12,8},{16,20},{20,16},{24,28},{28,24},{1,5},{5... | collective-permute-start | bytes 1671176 | tf_op jit(solution)/shard_map/ppermute | solution.py:92
  33.4 15.4 %copy-start.1 = (bf16[64,2048]{1,0:T(8,128)(2,1)}, bf16[64,2048]{1,0:T(8,128)(2,1)S(1)}, u32[]{:S(2)}) copy-start(bf16[64,2048]{1,0:T(8,128)(2,1)S(1)} %collective-permute-done.8) | copy-start | bytes 786436
  33.4 15.4 %collective-permute-start.9 = (bf16[32,2048]{1,0:T(8,128)(2,1)S(1)}, bf16[32,2048]{1,0:T(8,128)(2,1)S(1)}, u32[]{:S(2)}, u32[]{:S(2)}) collective-permute-start(bf16[32,2048]{1,0:T(8,128)(2,1)S(1)} %add_convert_fusion.3), channel_id=1, source_target_pairs={{0,1},{1,0},{2,3},{3,2},{4,6},{5,7},{6,4},{7,5},{8,9},{9,8},{10,11... | collective-permute-start | bytes 393224 | tf_op jit(solution)/shard_map/ppermute | solution.py:89
  35.4 13.4 %collective-permute-start.12 = (bf16[32,2048]{1,0:T(8,128)(2,1)S(1)}, bf16[32,2048]{1,0:T(8,128)(2,1)S(1)}, u32[]{:S(2)}, u32[]{:S(2)}) collective-permute-start(bf16[32,2048]{1,0:T(8,128)(2,1)S(1)} %get-tuple-element.107), channel_id=1, source_target_pairs={{0,3},{1,2},{2,1},{3,0},{4,7},{5,6},{6,5},{7,4},{8,11},{9,10},{10,... | collective-permute-start | bytes 393224 | tf_op jit(solution)/shard_map/ppermute | solution.py:89
  37.0 11.9 %collective-permute-start.11 = (bf16[32,2048]{1,0:T(8,128)(2,1)S(1)}, bf16[32,2048]{1,0:T(8,128)(2,1)S(1)}, u32[]{:S(2)}, u32[]{:S(2)}) collective-permute-start(bf16[32,2048]{1,0:T(8,128)(2,1)S(1)} %get-tuple-element.108), channel_id=1, source_target_pairs={{0,2},{1,3},{2,0},{3,1},{4,5},{5,4},{6,7},{7,6},{8,10},{9,11},{10,... | collective-permute-start | bytes 393224 | tf_op jit(solution)/shard_map/ppermute | solution.py:89
  48.8 10.4 %slice-start = ((bf16[64,2048]{1,0:T(8,128)(2,1)}), bf16[32,2048]{1,0:T(8,128)(2,1)S(1)}, s32[]{:S(2)}) async-start(bf16[64,2048]{1,0:T(8,128)(2,1)} %copy-done.1), calls=%async_computation | async-start | bytes 262144 | tf_op jit(solution)/shard_map/slice | solution.py:481
  48.8 1.6 %collective-permute-start.13 = (bf16[128,1024]{1,0:T(8,128)(2,1)S(1)}, bf16[128,1024]{1,0:T(8,128)(2,1)S(1)}, u32[]{:S(2)}, u32[]{:S(2)}) collective-permute-start(bf16[128,1024]{1,0:T(8,128)(2,1)S(1)} %get-tuple-element.92), channel_id=1, source_target_pairs={{0,4},{4,0},{8,12},{12,8},{16,20},{20,16},{24,28},{28,24},{1,5},{5... | collective-permute-start | bytes 786440 | tf_op jit(solution)/shard_map/ppermute | solution.py:92
  48.9 3.4 %collective-permute-start.16 = (bf16[128,1152]{1,0:T(8,128)(2,1)S(1)}, bf16[128,1152]{1,0:T(8,128)(2,1)S(1)}, u32[]{:S(2)}, u32[]{:S(2)}) collective-permute-start(bf16[128,1152]{1,0:T(8,128)(2,1)S(1)} %get-tuple-element.97), channel_id=1, source_target_pairs={{0,4},{4,0},{8,12},{12,8},{16,20},{20,16},{24,28},{28,24},{1,5},{5... | collective-permute-start | bytes 884744 | tf_op jit(solution)/shard_map/ppermute | solution.py:92
  50.5 5.0 %collective-permute-start.14 = (bf16[64,1024]{1,0:T(8,128)(2,1)S(1)}, bf16[64,1024]{1,0:T(8,128)(2,1)S(1)}, u32[]{:S(2)}, u32[]{:S(2)}) collective-permute-start(bf16[64,1024]{1,0:T(8,128)(2,1)S(1)} %pad_maximum_fusion.2), channel_id=1, source_target_pairs={{0,1},{1,0},{2,3},{3,2},{4,6},{5,7},{6,4},{7,5},{8,9},{9,8},{10,11... | collective-permute-start | bytes 393224 | tf_op jit(solution)/shard_map/ppermute | solution.py:89
  52.4 9.7 %copy-start = (s32[32,6]{0,1:T(8,128)S(1)}, s32[32,6]{0,1:T(8,128)}, u32[]{:S(2)}) copy-start(s32[32,6]{0,1:T(8,128)} %param.15) | copy-start | bytes 2308
  52.4 5.2 %collective-permute-start.17 = (bf16[64,1152]{1,0:T(8,128)(2,1)S(1)}, bf16[64,1152]{1,0:T(8,128)(2,1)S(1)}, u32[]{:S(2)}, u32[]{:S(2)}) collective-permute-start(bf16[64,1152]{1,0:T(8,128)(2,1)S(1)} %pad_maximum_fusion.1), channel_id=1, source_target_pairs={{0,1},{1,0},{2,3},{3,2},{4,6},{5,7},{6,4},{7,5},{8,9},{9,8},{10,11... | collective-permute-start | bytes 442376 | tf_op jit(solution)/shard_map/ppermute | solution.py:89
  55.6 4.5 %collective-permute-start.15 = (bf16[32,1024]{1,0:T(8,128)(2,1)S(1)}, bf16[32,1024]{1,0:T(8,128)(2,1)S(1)}, u32[]{:S(2)}, u32[]{:S(2)}) collective-permute-start(bf16[32,1024]{1,0:T(8,128)(2,1)S(1)} %add_convert_fusion.7), channel_id=1, source_target_pairs={{0,2},{1,3},{2,0},{3,1},{4,5},{5,4},{6,7},{7,6},{8,10},{9,11},{10,... | collective-permute-start | bytes 196616 | tf_op jit(solution)/shard_map/ppermute | solution.py:89
  57.7 4.4 %collective-permute-start.18 = (bf16[32,1152]{1,0:T(8,128)(2,1)S(1)}, bf16[32,1152]{1,0:T(8,128)(2,1)S(1)}, u32[]{:S(2)}, u32[]{:S(2)}) collective-permute-start(bf16[32,1152]{1,0:T(8,128)(2,1)S(1)} %add_convert_fusion.4), channel_id=1, source_target_pairs={{0,2},{1,3},{2,0},{3,1},{4,5},{5,4},{6,7},{7,6},{8,10},{9,11},{10,... | collective-permute-start | bytes 221192 | tf_op jit(solution)/shard_map/ppermute | solution.py:89

commit v9 on v8

--- a/solution.py
+++ b/solution.py
@@ -133,15 +133,20 @@
 
 
 def pack_kernel(plan, *refs):
-    pack_body(plan, refs[:3], *refs[3:])
+    sources, (out_ref, facts_ref), scratch = refs[:3], refs[3:5], refs[5:]
+    pack_body(plan, sources, out_ref, *scratch)
+    facts_ref[...] = out_ref[:, plan.width :]
 
 
 def pack(plan, x, routes, factors):
     return pl.pallas_call(
         functools.partial(pack_kernel, plan),
-        out_shape=jax.ShapeDtypeStruct((plan.count, plan.sent), BF16),
+        out_shape=(
+            jax.ShapeDtypeStruct((plan.count, plan.sent), BF16),
+            jax.ShapeDtypeStruct((plan.count, plan.meta), BF16),
+        ),
         in_specs=[hbm()] * 3,
-        out_specs=vmem(),
+        out_specs=(vmem(), vmem()),
         scratch_shapes=pack_scratch(plan),
         compiler_params=pltpu.CompilerParams(vmem_limit_bytes=4 * MIB),
         name="pack",
@@ -257,7 +262,7 @@
     return packed, saved, done
 
 
-def fetch_kernel(plan, w_hbm, after, w_ref, done_ref, sems):
+def fetch_kernel(plan, w_hbm, after, also_after, w_ref, done_ref, sems):
     copies = weight_copies(plan, w_hbm, weight_slots(plan, w_ref), sems)
     for copy in copies:
         copy.start()
@@ -266,14 +271,14 @@
         copy.wait()
 
 
-def fetch(plan, w, after):
+def fetch(plan, w, after, also_after):
     return pl.pallas_call(
         functools.partial(fetch_kernel, plan),
         out_shape=(
             pltpu.VMEM((plan.mine, plan.hidden, plan.width), BF16),
             jax.ShapeDtypeStruct((16, plan.sent), BF16),
         ),
-        in_specs=[hbm(), pl.BlockSpec(memory_space=pl.ANY)],
+        in_specs=[hbm()] + [pl.BlockSpec(memory_space=pl.ANY)] * 2,
         out_specs=(vmem(), vmem()),
         scratch_shapes=[pltpu.SemaphoreType.DMA((plan.mine,))],
         compiler_params=pltpu.CompilerParams(vmem_limit_bytes=MIB),
@@ -283,7 +288,7 @@
             transcendentals=0,
         ),
         name="fetch",
-    )(in_hbm(w), after)
+    )(in_hbm(w), after, also_after)
 
 
 def arrived(plan, blocks, first, x_s):
@@ -565,21 +570,24 @@
     w_down,
 ):
     plan = Plan(tokens, routes, saved_gate, w_gate)
-    packed = pack(plan, tokens, routes, weights_fwd)
+    packed, facts = pack(plan, tokens, routes, weights_fwd)
     packed_back, saved, ready = prepare(
         plan, cotangent, routes_back, weights_back, saved_gate, saved_up, packed
     )
+    if plan.split > 1:
+        saved[1] = plan.over_pair(saved[1])
     gate_hbm, up_hbm = jnp.swapaxes(w_gate, 1, 2), jnp.swapaxes(w_up, 1, 2)
     if plan.paired and plan.owners > 1:
-        blocks = [packed, plan.over_expert(packed, 1)]
-        gate, done = fetch(plan, gate_hbm, blocks[1])
+        first = plan.over_expert(tokens, 1), plan.over_expert(facts, 1)
+        blocks = [packed, jnp.concatenate(first, axis=1)]
+        gate, done = fetch(plan, gate_hbm, first[0], saved[-1])
         step = 2
         while step < plan.owners:
             blocks.append(plan.over_expert(jnp.concatenate(blocks) + ready[:1], step))
             step *= 2
     else:
         blocks = gather_group(plan, packed)
-        gate, done = fetch(plan, gate_hbm, packed)
+        gate, done = fetch(plan, gate_hbm, packed, saved[-1])
     if plan.split > 1:
         blocks.append(plan.over_pair(jnp.concatenate(blocks) + done[:1]))
     blocks_back = gather_group(plan, packed_back)
@@ -587,7 +595,6 @@
     parts, blocks_back = lax.optimization_barrier((parts, blocks_back))
     if plan.split > 1:
         blocks_back = blocks_back + [plan.over_pair(jnp.concatenate(blocks_back))]
-        saved[1] = plan.over_pair(saved[1])
     terms = scatter_group(plan, sum_pair(plan, parts))
     parts_back = backward(plan, blocks_back, saved, gate, kept, up_hbm, w_down)
     parts_back, terms = lax.optimization_barrier((parts_back, terms))

time: 63.2 us -> 63 us (level)
  starting transfers between devices: 19.9 us -> 18.6 us
  waiting for transfers between devices: 8.07 us -> 9.24 us
    ppermute x12 -> x13, starting transfers between devices: 18.1 us -> 17.1 us  [over_expert(): return lax.ppermute(x, ('dp', 'expert'), pairs)]
    ppermute x12 -> x13, waiting for transfers between devices: 6.49 us -> 7.36 us  [over_expert(): return lax.ppermute(x, ('dp', 'expert'), pairs)]
  transfers between devices with their start and end apart: 19 -> 20, of which waited for: 7 -> 8; matrix products, arithmetic and copies ran while one was open for 2% -> 2% of each run, Pallas kernels for 49% -> 51%
where the time goes in v9:
time: 63 us; the launch traced here: 62.9 us
  Pallas kernels  32.7 us (52%)
  starting transfers between devices  18.6 us (30%)
  waiting for transfers between devices  9.24 us (15%)
  other arithmetic  1.2 us (2%)
  between operations  1.02 us (2%)
    pallas_call x2, Pallas kernels, expert_call(): pl.pallas_call(kernel, out_shape=shapes, in_specs=[vmem()] * len(inputs)...  24.9 us
    ppermute x13, starting transfers between devices, over_expert(): return lax.ppermute(x, ('dp', 'expert'), pairs)  17.1 us
    ppermute x13, waiting for transfers between devices, over_expert(): return lax.ppermute(x, ('dp', 'expert'), pairs)  7.36 us
    pallas_call x1, Pallas kernels, fetch(): pl.pallas_call(functools.partial(fetch_kernel, plan), out_shape=(pltpu.VM...  4.4 us
    ppermute x7, waiting for transfers between devices, over_pair(): return lax.ppermute(x, 'dp', [(i, i ^ 1) for i in range(self.groups)])  1.88 us
    pallas_call x1, Pallas kernels, prepare(): pl.pallas_call(functools.partial(prepare_kernel, plan), out_shape=out_sha...  1.6 us
    ppermute x7, starting transfers between devices, over_pair(): return lax.ppermute(x, 'dp', [(i, i ^ 1) for i in range(self.groups)])  1.42 us
  transfers between devices with their start and end apart: 20, of which 8 were waited for; matrix products, arithmetic and copies ran while one was open for 2% of the time, Pallas kernels for 51%

profile of v9, /device:TPU:0, one launch (start us, length us, event | category | flops | bytes accessed | tf_op | source)
XLA Modules:
  0.0 62.9 jit_solution(13582959035519680867)
XLA Ops:
  0.6 3.0 %collective-permute-start = (bf16[32,2048]{1,0:T(8,128)(2,1)}, bf16[32,2048]{1,0:T(8,128)(2,1)S(1)}, u32[]{:S(2)}, u32[]{:S(2)}) collective-permute-start(bf16[32,2048]{1,0:T(8,128)(2,1)} %refs_0_.1), channel_id=1, source_target_pairs={{1,0},{0,1},{3,2},{2,3},{6,4},{7,5},{4,6},{5,7},{9,8},{8,9},{11,10... | collective-permute-start | bytes 393224 | tf_op jit(solution)/shard_map/ppermute | solution.py:89
  3.6 1.1 %pack.1 = (bf16[32,2176]{1,0:T(8,128)(2,1)S(1)}, bf16[32,128]{1,0:T(8,128)(2,1)S(1)}) custom-call(bf16[32,2048]{1,0:T(8,128)(2,1)} %refs_0_.1, s32[6,32]{1,0:T(8,128)} %bitcast.25, f32[6,32]{1,0:T(8,128)} %bitcast.26), custom_call_target="tpu_custom_call" | custom-call | tf_op jit(solution)/shard_map/pack/pallas_call | solution.py:142
  4.8 1.6 %prepare.1 = (bf16[32,2176]{1,0:T(8,128)(2,1)S(1)}, bf16[16,2176]{1,0:T(8,128)(2,1)S(1)}, bf16[2,128,704]{2,1,0:T(8,128)(2,1)S(1)}, bf16[2,128,704]{2,1,0:T(8,128)(2,1)S(1)}) custom-call(bf16[32,2048]{1,0:T(8,128)(2,1)} %x_hbm.1, s32[6,32]{1,0:T(8,128)} %bitcast.17, f32[6,32]{1,0:T(8,128)} %bitcast.24, bf16[224,704]{1,0:T(8,128)(2,1)} %bitcast.22, ...), custom_call_target="tpu_custom_call" | custom-call | bytes 17825792 | tf_op jit(solution)/shard_map/prepare/pallas_call | solution.py:238
  6.8 1.6 %collective-permute-done.1 = bf16[32,128]{1,0:T(8,128)(2,1)S(1)} collective-permute-done((bf16[32,128]{1,0:T(8,128)(2,1)S(1)}, bf16[32,128]{1,0:T(8,128)(2,1)S(1)}, u32[]{:S(2)}, u32[]{:S(2)}) %collective-permute-start.1) | collective-permute-done | bytes 8224 | tf_op jit(solution)/shard_map/ppermute | solution.py:89
  8.5 1.6 %collective-permute-start.2 = (bf16[64,2176]{1,0:T(8,128)(2,1)S(1)}, bf16[64,2176]{1,0:T(8,128)(2,1)S(1)}, u32[]{:S(2)}, u32[]{:S(2)}) collective-permute-start(bf16[64,2176]{1,0:T(8,128)(2,1)S(1)} %maximum_add_fusion.1), channel_id=1, source_target_pairs={{2,0},{3,1},{0,2},{1,3},{5,4},{4,5},{7,6},{6,7},{10,8},{11,9},{8,1... | collective-permute-start | bytes 835592 | tf_op jit(solution)/shard_map/ppermute | solution.py:89
  10.1 4.4 %fetch.1 = (bf16[4,704,2048]{2,1,0:T(8,128)(2,1)S(1)}, bf16[16,2176]{1,0:T(8,128)(2,1)S(1)}) custom-call(bf16[8,704,2048]{2,1,0:T(8,128)(2,1)} %bitcast.21, bf16[32,2048]{1,0:T(8,128)(2,1)S(1)} %collective-permute-done.after, bf16[2,128,704]{2,1,0:T(8,128)(2,1)S(1)} %collective-permute-done.3.also_after.refs_6_), custom_call_target="tpu_custom_call" | custom-call | bytes 23068672 | tf_op jit(solution)/shard_map/fetch/pallas_call | solution.py:275
  14.5 0.6 collective-permute-done.2.refs_2_
  15.3 1.6 %collective-permute-start.7 = (bf16[32,2176]{1,0:T(8,128)(2,1)S(1)}, bf16[32,2176]{1,0:T(8,128)(2,1)S(1)}, u32[]{:S(2)}, u32[]{:S(2)}) collective-permute-start(bf16[32,2176]{1,0:T(8,128)(2,1)S(1)} %get-tuple-element.68.refs_0_), channel_id=1, source_target_pairs={{3,0},{2,1},{1,2},{0,3},{7,4},{6,5},{5,6},{4,7},{11,8},{10,9},{9,1... | collective-permute-start | bytes 417800 | tf_op jit(solution)/shard_map/ppermute | solution.py:89
  17.3 1.6 %collective-permute-start.5 = (bf16[32,2176]{1,0:T(8,128)(2,1)S(1)}, bf16[32,2176]{1,0:T(8,128)(2,1)S(1)}, u32[]{:S(2)}, u32[]{:S(2)}) collective-permute-start(bf16[32,2176]{1,0:T(8,128)(2,1)S(1)} %get-tuple-element.68.refs_0_), channel_id=1, source_target_pairs={{1,0},{0,1},{3,2},{2,3},{6,4},{7,5},{4,6},{5,7},{9,8},{8,9},{11,10... | collective-permute-start | bytes 417800 | tf_op jit(solution)/shard_map/ppermute | solution.py:89
  18.9 13.3 %forward.1 = (bf16[32,2048]{1,0:T(8,128)(2,1)S(1)}, bf16[32,2048]{1,0:T(8,128)(2,1)S(1)}, bf16[32,2048]{1,0:T(8,128)(2,1)S(1)}, bf16[32,2048]{1,0:T(8,128)(2,1)S...) custom-call(bf16[32,2176]{1,0:T(8,128)(2,1)S(1)} %get-tuple-element.55.after.refs, ...), custom_call_target="tpu_custom_call" | custom-call | flops 2214592512 | bytes 23068672 | tf_op jit(solution)/shard_map/forward/pallas_call | solution.py:429
  32.9 0.8 %collective-permute-done.9 = bf16[64,2048]{1,0:T(8,128)(2,1)S(1)} collective-permute-done((bf16[64,2048]{1,0:T(8,128)(2,1)S(1)}, bf16[64,2048]{1,0:T(8,128)(2,1)S(1)}, u32[]{:S(2)}, u32[]{:S(2)}) %collective-permute-start.9) | collective-permute-done | bytes 262176 | tf_op jit(solution)/shard_map/ppermute | solution.py:92
  33.8 0.5 collective-permute-start.10
  34.4 2.6 %collective-permute-start.13 = (bf16[32,2048]{1,0:T(8,128)(2,1)S(1)}, bf16[32,2048]{1,0:T(8,128)(2,1)S(1)}, u32[]{:S(2)}, u32[]{:S(2)}) collective-permute-start(bf16[32,2048]{1,0:T(8,128)(2,1)S(1)} %get-tuple-element.111), channel_id=1, source_target_pairs={{0,3},{1,2},{2,1},{3,0},{4,7},{5,6},{6,5},{7,4},{8,11},{9,10},{10,... | collective-permute-start | bytes 393224 | tf_op jit(solution)/shard_map/ppermute | solution.py:89
  37.0 0.5 collective-permute-start.12
  37.5 11.6 %backward.1 = (bf16[32,1024]{1,0:T(8,128)(2,1)S(1)}, bf16[32,1024]{1,0:T(8,128)(2,1)S(1)}, bf16[32,1024]{1,0:T(8,128)(2,1)S(1)}, bf16[32,1024]{1,0:T(8,128)(2,1)...) custom-call(bf16[32,2176]{1,0:T(8,128)(2,1)S(1)} %get-tuple-element., ...), custom_call_target="tpu_custom_call" | custom-call | flops 2214592512 | bytes 23068672 | tf_op jit(solution)/shard_map/backward/pallas_call | solution.py:429
  49.7 1.0 %collective-permute-done.14 = bf16[128,1024]{1,0:T(8,128)(2,1)S(1)} collective-permute-done((bf16[128,1024]{1,0:T(8,128)(2,1)S(1)}, bf16[128,1024]{1,0:T(8,128)(2,1)S(1)}, u32[]{:S(2)}, u32[]{:S(2)}) %collective-permute-start.14) | collective-permute-done | bytes 262176 | tf_op jit(solution)/shard_map/ppermute | solution.py:92
  50.8 0.5 collective-permute-start.15
  51.4 1.6 %collective-permute-start.18 = (bf16[64,1152]{1,0:T(8,128)(2,1)S(1)}, bf16[64,1152]{1,0:T(8,128)(2,1)S(1)}, u32[]{:S(2)}, u32[]{:S(2)}) collective-permute-start(bf16[64,1152]{1,0:T(8,128)(2,1)S(1)} %pad_maximum_fusion.1), channel_id=1, source_target_pairs={{0,1},{1,0},{2,3},{3,2},{4,6},{5,7},{6,4},{7,5},{8,9},{9,8},{10,11... | collective-permute-start | bytes 442376 | tf_op jit(solution)/shard_map/ppermute | solution.py:89
  53.1 2.8 %collective-permute-done.15 = bf16[64,1024]{1,0:T(8,128)(2,1)S(1)} collective-permute-done((bf16[64,1024]{1,0:T(8,128)(2,1)S(1)}, bf16[64,1024]{1,0:T(8,128)(2,1)S(1)}, u32[]{:S(2)}, u32[]{:S(2)}) %collective-permute-start.15) | collective-permute-done | bytes 131104 | tf_op jit(solution)/shard_map/ppermute | solution.py:89
  55.9 1.6 %collective-permute-start.16 = (bf16[32,1024]{1,0:T(8,128)(2,1)S(1)}, bf16[32,1024]{1,0:T(8,128)(2,1)S(1)}, u32[]{:S(2)}, u32[]{:S(2)}) collective-permute-start(bf16[32,1024]{1,0:T(8,128)(2,1)S(1)} %add_convert_fusion.7), channel_id=1, source_target_pairs={{0,2},{1,3},{2,0},{3,1},{4,5},{5,4},{6,7},{7,6},{8,10},{9,11},{10,... | collective-permute-start | bytes 196616 | tf_op jit(solution)/shard_map/ppermute | solution.py:89
  57.5 1.5 %collective-permute-start.19 = (bf16[32,1152]{1,0:T(8,128)(2,1)S(1)}, bf16[32,1152]{1,0:T(8,128)(2,1)S(1)}, u32[]{:S(2)}, u32[]{:S(2)}) collective-permute-start(bf16[32,1152]{1,0:T(8,128)(2,1)S(1)} %add_convert_fusion.4), channel_id=1, source_target_pairs={{0,2},{1,3},{2,0},{3,1},{4,5},{5,4},{6,7},{7,6},{8,10},{9,11},{10,... | collective-permute-start | bytes 221192 | tf_op jit(solution)/shard_map/ppermute | solution.py:89
  59.0 0.7 %add_convert_fusion = bf16[32,2048]{1,0:T(8,128)(2,1)} fusion(bf16[32,2048]{1,0:T(8,128)(2,1)S(1)} %collective-permute-done.13, bf16[32,2048]{1,0:T(8,128)(2,1)S(1)} %collective-permute-done.12, bf16[32,2048]{1,0:T(8,128)(2,1)S(1)} %collective-permute-done.10, bf16[32,2048]{1,0:T(8,128)(2,1)S(1)} %slice-done, bf16[32,2048]{1,0:T(8,128)(2,1)S(1)} %get-tuple-element.90), kind=kLoop, calls=%fused_computation.3 | loop fusion | flops 655360 | bytes 786432 | tf_op jit(solution)/shard_map/convert_element_type | solution.py:601
  60.2 1.7 %collective-permute-done.19.refs_7_ = bf16[32,1152]{1,0:T(8,128)(2,1)S(1)} collective-permute-done((bf16[32,1152]{1,0:T(8,128)(2,1)S(1)}, bf16[32,1152]{1,0:T(8,128)(2,1)S(1)}, u32[]{:S(2)}, u32[]{:S(2)}) %collective-permute-start.19) | collective-permute-done | bytes 73760 | tf_op jit(solution)/shard_map/ppermute | solution.py:89
  61.9 0.8 %finish.1 = (bf16[32,2048]{1,0:T(8,128)(2,1)}, f32[6,32]{1,0:T(8,128)}) custom-call(bf16[32,1024]{1,0:T(8,128)(2,1)S(1)} %get-tuple-element.95.refs_0_, bf16[32,1024]{1,0:T(8,128)(2,1)S(1)} %slice.76.refs_1_, bf16[32,1024]{1,0:T(8,128)(2,1)S(1)} %slice.79.refs_2_, bf16[32,1024]{1,0:T(8,128)(2,1)S(1)} %collective-permute-done.16.refs_3_, ...), custom_call_target="tpu_custom_call" | custom-call | tf_op jit(solution)/shard_map/finish/pallas_call | solution.py:540
  (48 shorter events, 3.3 us)
Async XLA Ops:
  0.6 6.2 %collective-permute-start = (bf16[32,2048]{1,0:T(8,128)(2,1)}, bf16[32,2048]{1,0:T(8,128)(2,1)S(1)}, u32[]{:S(2)}, u32[]{:S(2)}) collective-permute-start(bf16[32,2048]{1,0:T(8,128)(2,1)} %refs_0_.1), channel_id=1, source_target_pairs={{1,0},{0,1},{3,2},{2,3},{6,4},{7,5},{4,6},{5,7},{9,8},{8,9},{11,10... | collective-permute-start | bytes 393224 | tf_op jit(solution)/shard_map/ppermute | solution.py:89
  4.7 3.7 %collective-permute-start.1 = (bf16[32,128]{1,0:T(8,128)(2,1)S(1)}, bf16[32,128]{1,0:T(8,128)(2,1)S(1)}, u32[]{:S(2)}, u32[]{:S(2)}) collective-permute-start(bf16[32,128]{1,0:T(8,128)(2,1)S(1)} %get-tuple-element.56), channel_id=1, source_target_pairs={{1,0},{0,1},{3,2},{2,3},{6,4},{7,5},{4,6},{5,7},{9,8},{8,9},{11,10... | collective-permute-start | bytes 24584 | tf_op jit(solution)/shard_map/ppermute | solution.py:89
  6.4 3.7 %collective-permute-start.3 = (bf16[2,128,704]{2,1,0:T(8,128)(2,1)S(1)}, bf16[2,128,704]{2,1,0:T(8,128)(2,1)S(1)}, u32[]{:S(2)}, u32[]{:S(2)}) collective-permute-start(bf16[2,128,704]{2,1,0:T(8,128)(2,1)S(1)} %get-tuple-element.58), channel_id=1, source_target_pairs={{0,4},{4,0},{8,12},{12,8},{16,20},{20,16},{24,28},{28,24},{1,5},{5... | collective-permute-start | bytes 1081352 | tf_op jit(solution)/shard_map/ppermute | solution.py:92
  8.5 6.6 %collective-permute-start.2 = (bf16[64,2176]{1,0:T(8,128)(2,1)S(1)}, bf16[64,2176]{1,0:T(8,128)(2,1)S(1)}, u32[]{:S(2)}, u32[]{:S(2)}) collective-permute-start(bf16[64,2176]{1,0:T(8,128)(2,1)S(1)} %maximum_add_fusion.1), channel_id=1, source_target_pairs={{2,0},{3,1},{0,2},{1,3},{5,4},{4,5},{7,6},{6,7},{10,8},{11,9},{8,1... | collective-permute-start | bytes 835592 | tf_op jit(solution)/shard_map/ppermute | solution.py:89
  15.2 3.7 %collective-permute-start.4 = (bf16[128,2176]{1,0:T(8,128)(2,1)S(1)}, bf16[128,2176]{1,0:T(8,128)(2,1)S(1)}, u32[]{:S(2)}, u32[]{:S(2)}) collective-permute-start(bf16[128,2176]{1,0:T(8,128)(2,1)S(1)} %maximum_add_fusion), channel_id=1, source_target_pairs={{0,4},{4,0},{8,12},{12,8},{16,20},{20,16},{24,28},{28,24},{1,5},{5... | collective-permute-start | bytes 1671176 | tf_op jit(solution)/shard_map/ppermute | solution.py:92
  15.3 16.9 %collective-permute-start.7 = (bf16[32,2176]{1,0:T(8,128)(2,1)S(1)}, bf16[32,2176]{1,0:T(8,128)(2,1)S(1)}, u32[]{:S(2)}, u32[]{:S(2)}) collective-permute-start(bf16[32,2176]{1,0:T(8,128)(2,1)S(1)} %get-tuple-element.68.refs_0_), channel_id=1, source_target_pairs={{3,0},{2,1},{1,2},{0,3},{7,4},{6,5},{5,6},{4,7},{11,8},{10,9},{9,1... | collective-permute-start | bytes 417800 | tf_op jit(solution)/shard_map/ppermute | solution.py:89
  16.8 15.3 %collective-permute-start.6 = (bf16[32,2176]{1,0:T(8,128)(2,1)S(1)}, bf16[32,2176]{1,0:T(8,128)(2,1)S(1)}, u32[]{:S(2)}, u32[]{:S(2)}) collective-permute-start(bf16[32,2176]{1,0:T(8,128)(2,1)S(1)} %get-tuple-element.68.refs_0_), channel_id=1, source_target_pairs={{2,0},{3,1},{0,2},{1,3},{5,4},{4,5},{7,6},{6,7},{10,8},{11,9},{8,1... | collective-permute-start | bytes 417800 | tf_op jit(solution)/shard_map/ppermute | solution.py:89
  17.3 14.9 %collective-permute-start.5 = (bf16[32,2176]{1,0:T(8,128)(2,1)S(1)}, bf16[32,2176]{1,0:T(8,128)(2,1)S(1)}, u32[]{:S(2)}, u32[]{:S(2)}) collective-permute-start(bf16[32,2176]{1,0:T(8,128)(2,1)S(1)} %get-tuple-element.68.refs_0_), channel_id=1, source_target_pairs={{1,0},{0,1},{3,2},{2,3},{6,4},{7,5},{4,6},{5,7},{9,8},{8,9},{11,10... | collective-permute-start | bytes 417800 | tf_op jit(solution)/shard_map/ppermute | solution.py:89
  32.2 1.6 %collective-permute-start.9 = (bf16[64,2048]{1,0:T(8,128)(2,1)S(1)}, bf16[64,2048]{1,0:T(8,128)(2,1)S(1)}, u32[]{:S(2)}, u32[]{:S(2)}) collective-permute-start(bf16[64,2048]{1,0:T(8,128)(2,1)S(1)} %get-tuple-element.85), channel_id=1, source_target_pairs={{0,4},{4,0},{8,12},{12,8},{16,20},{20,16},{24,28},{28,24},{1,5},{5... | collective-permute-start | bytes 786440 | tf_op jit(solution)/shard_map/ppermute | solution.py:92
  32.3 2.1 %collective-permute-start.11 = (bf16[64,2048]{1,0:T(8,128)(2,1)S(1)}, bf16[64,2048]{1,0:T(8,128)(2,1)S(1)}, u32[]{:S(2)}, u32[]{:S(2)}) collective-permute-start(bf16[64,2048]{1,0:T(8,128)(2,1)S(1)} %get-tuple-element.88), channel_id=1, source_target_pairs={{0,4},{4,0},{8,12},{12,8},{16,20},{20,16},{24,28},{28,24},{1,5},{5... | collective-permute-start | bytes 786440 | tf_op jit(solution)/shard_map/ppermute | solution.py:92
  32.8 4.7 %collective-permute-start.8 = (bf16[128,2176]{1,0:T(8,128)(2,1)S(1)}, bf16[128,2176]{1,0:T(8,128)(2,1)S(1)}, u32[]{:S(2)}, u32[]{:S(2)}) collective-permute-start(bf16[128,2176]{1,0:T(8,128)(2,1)S(1)} %pad_maximum_fusion), channel_id=1, source_target_pairs={{0,4},{4,0},{8,12},{12,8},{16,20},{20,16},{24,28},{28,24},{1,5},{5... | collective-permute-start | bytes 1671176 | tf_op jit(solution)/shard_map/ppermute | solution.py:92
  33.8 15.3 %copy-start.1 = (bf16[64,2048]{1,0:T(8,128)(2,1)}, bf16[64,2048]{1,0:T(8,128)(2,1)S(1)}, u32[]{:S(2)}) copy-start(bf16[64,2048]{1,0:T(8,128)(2,1)S(1)} %collective-permute-done.9) | copy-start | bytes 786436
  33.8 15.3 %collective-permute-start.10 = (bf16[32,2048]{1,0:T(8,128)(2,1)S(1)}, bf16[32,2048]{1,0:T(8,128)(2,1)S(1)}, u32[]{:S(2)}, u32[]{:S(2)}) collective-permute-start(bf16[32,2048]{1,0:T(8,128)(2,1)S(1)} %add_convert_fusion.3), channel_id=1, source_target_pairs={{0,1},{1,0},{2,3},{3,2},{4,6},{5,7},{6,4},{7,5},{8,9},{9,8},{10,11... | collective-permute-start | bytes 393224 | tf_op jit(solution)/shard_map/ppermute | solution.py:89
  34.4 14.7 %collective-permute-start.13 = (bf16[32,2048]{1,0:T(8,128)(2,1)S(1)}, bf16[32,2048]{1,0:T(8,128)(2,1)S(1)}, u32[]{:S(2)}, u32[]{:S(2)}) collective-permute-start(bf16[32,2048]{1,0:T(8,128)(2,1)S(1)} %get-tuple-element.111), channel_id=1, source_target_pairs={{0,3},{1,2},{2,1},{3,0},{4,7},{5,6},{6,5},{7,4},{8,11},{9,10},{10,... | collective-permute-start | bytes 393224 | tf_op jit(solution)/shard_map/ppermute | solution.py:89
  37.0 12.1 %collective-permute-start.12 = (bf16[32,2048]{1,0:T(8,128)(2,1)S(1)}, bf16[32,2048]{1,0:T(8,128)(2,1)S(1)}, u32[]{:S(2)}, u32[]{:S(2)}) collective-permute-start(bf16[32,2048]{1,0:T(8,128)(2,1)S(1)} %get-tuple-element.112), channel_id=1, source_target_pairs={{0,2},{1,3},{2,0},{3,1},{4,5},{5,4},{6,7},{7,6},{8,10},{9,11},{10,... | collective-permute-start | bytes 393224 | tf_op jit(solution)/shard_map/ppermute | solution.py:89
  49.1 9.9 %slice-start = ((bf16[64,2048]{1,0:T(8,128)(2,1)}), bf16[32,2048]{1,0:T(8,128)(2,1)S(1)}, s32[]{:S(2)}) async-start(bf16[64,2048]{1,0:T(8,128)(2,1)} %copy-done.1), calls=%async_computation | async-start | bytes 262144 | tf_op jit(solution)/shard_map/slice | solution.py:486
  49.1 1.6 %collective-permute-start.14 = (bf16[128,1024]{1,0:T(8,128)(2,1)S(1)}, bf16[128,1024]{1,0:T(8,128)(2,1)S(1)}, u32[]{:S(2)}, u32[]{:S(2)}) collective-permute-start(bf16[128,1024]{1,0:T(8,128)(2,1)S(1)} %get-tuple-element.96), channel_id=1, source_target_pairs={{0,4},{4,0},{8,12},{12,8},{16,20},{20,16},{24,28},{28,24},{1,5},{5... | collective-permute-start | bytes 786440 | tf_op jit(solution)/shard_map/ppermute | solution.py:92
  49.2 2.1 %collective-permute-start.17 = (bf16[128,1152]{1,0:T(8,128)(2,1)S(1)}, bf16[128,1152]{1,0:T(8,128)(2,1)S(1)}, u32[]{:S(2)}, u32[]{:S(2)}) collective-permute-start(bf16[128,1152]{1,0:T(8,128)(2,1)S(1)} %get-tuple-element.101), channel_id=1, source_target_pairs={{0,4},{4,0},{8,12},{12,8},{16,20},{20,16},{24,28},{28,24},{1,5},{5... | collective-permute-start | bytes 884744 | tf_op jit(solution)/shard_map/ppermute | solution.py:92
  50.8 5.0 %collective-permute-start.15 = (bf16[64,1024]{1,0:T(8,128)(2,1)S(1)}, bf16[64,1024]{1,0:T(8,128)(2,1)S(1)}, u32[]{:S(2)}, u32[]{:S(2)}) collective-permute-start(bf16[64,1024]{1,0:T(8,128)(2,1)S(1)} %pad_maximum_fusion.2), channel_id=1, source_target_pairs={{0,1},{1,0},{2,3},{3,2},{4,6},{5,7},{6,4},{7,5},{8,9},{9,8},{10,11... | collective-permute-start | bytes 393224 | tf_op jit(solution)/shard_map/ppermute | solution.py:89
  51.4 10.5 %copy-start = (s32[32,6]{0,1:T(8,128)S(1)}, s32[32,6]{0,1:T(8,128)}, u32[]{:S(2)}) copy-start(s32[32,6]{0,1:T(8,128)} %param.15) | copy-start | bytes 2308
  51.4 6.0 %collective-permute-start.18 = (bf16[64,1152]{1,0:T(8,128)(2,1)S(1)}, bf16[64,1152]{1,0:T(8,128)(2,1)S(1)}, u32[]{:S(2)}, u32[]{:S(2)}) collective-permute-start(bf16[64,1152]{1,0:T(8,128)(2,1)S(1)} %pad_maximum_fusion.1), channel_id=1, source_target_pairs={{0,1},{1,0},{2,3},{3,2},{4,6},{5,7},{6,4},{7,5},{8,9},{9,8},{10,11... | collective-permute-start | bytes 442376 | tf_op jit(solution)/shard_map/ppermute | solution.py:89
  55.9 4.3 %collective-permute-start.16 = (bf16[32,1024]{1,0:T(8,128)(2,1)S(1)}, bf16[32,1024]{1,0:T(8,128)(2,1)S(1)}, u32[]{:S(2)}, u32[]{:S(2)}) collective-permute-start(bf16[32,1024]{1,0:T(8,128)(2,1)S(1)} %add_convert_fusion.7), channel_id=1, source_target_pairs={{0,2},{1,3},{2,0},{3,1},{4,5},{5,4},{6,7},{7,6},{8,10},{9,11},{10,... | collective-permute-start | bytes 196616 | tf_op jit(solution)/shard_map/ppermute | solution.py:89
  57.5 4.4 %collective-permute-start.19 = (bf16[32,1152]{1,0:T(8,128)(2,1)S(1)}, bf16[32,1152]{1,0:T(8,128)(2,1)S(1)}, u32[]{:S(2)}, u32[]{:S(2)}) collective-permute-start(bf16[32,1152]{1,0:T(8,128)(2,1)S(1)} %add_convert_fusion.4), channel_id=1, source_target_pairs={{0,2},{1,3},{2,0},{3,1},{4,5},{5,4},{6,7},{7,6},{8,10},{9,11},{10,... | collective-permute-start | bytes 221192 | tf_op jit(solution)/shard_map/ppermute | solution.py:89

commit v10 on v8

--- a/solution.py
+++ b/solution.py
@@ -69,6 +69,7 @@
         self.sent = self.width + self.meta
         self.half = round_up(self.width // 2, LANES)
         self.kept = min(self.mine, 2)
+        self.held = 1
         self.rows = self.mine * self.expert_rows
         self.cols = self.blocks * self.count
 
@@ -257,8 +258,10 @@
     return packed, saved, done
 
 
-def fetch_kernel(plan, w_hbm, after, w_ref, done_ref, sems):
-    copies = weight_copies(plan, w_hbm, weight_slots(plan, w_ref), sems)
+def fetch_kernel(plan, gate_hbm, up_hbm, after, also_after, *refs):
+    gate_ref, held_ref, done_ref, sems = refs
+    copies = weight_copies(plan, gate_hbm, weight_slots(plan, gate_ref), sems.at[0])
+    copies += weight_copies(plan, up_hbm, weight_slots(plan, held_ref), sems.at[1])
     for copy in copies:
         copy.start()
     done_ref[...] = jnp.zeros_like(done_ref)
@@ -266,16 +269,17 @@
         copy.wait()
 
 
-def fetch(plan, w, after):
+def fetch(plan, gate_hbm, up_hbm, after, also_after):
     return pl.pallas_call(
         functools.partial(fetch_kernel, plan),
         out_shape=(
             pltpu.VMEM((plan.mine, plan.hidden, plan.width), BF16),
+            pltpu.VMEM((plan.held, plan.hidden, plan.width), BF16),
             jax.ShapeDtypeStruct((16, plan.sent), BF16),
         ),
-        in_specs=[hbm(), pl.BlockSpec(memory_space=pl.ANY)],
-        out_specs=(vmem(), vmem()),
-        scratch_shapes=[pltpu.SemaphoreType.DMA((plan.mine,))],
+        in_specs=[hbm()] * 2 + [pl.BlockSpec(memory_space=pl.ANY)] * 2,
+        out_specs=(vmem(),) * 3,
+        scratch_shapes=[pltpu.SemaphoreType.DMA((2, plan.mine))],
         compiler_params=pltpu.CompilerParams(vmem_limit_bytes=MIB),
         cost_estimate=pl.CostEstimate(
             flops=0,
@@ -283,7 +287,7 @@
             transcendentals=0,
         ),
         name="fetch",
-    )(in_hbm(w), after)
+    )(in_hbm(gate_hbm), in_hbm(up_hbm), after, also_after)
 
 
 def arrived(plan, blocks, first, x_s):
@@ -313,11 +317,12 @@
 
 def forward_kernel(plan, count, *refs):
     blocks, refs = refs[:count], refs[count:]
-    gate_ref, up_hbm, down_hbm, *refs = refs
+    gate_ref, held_ref, up_hbm, down_hbm, *refs = refs
     outs, (kept_ref, up_s, down_s, x_s, y_s, gate_s, hidden_s, sems) = refs[:-8], refs[-8:]
     first, _ = first_expert(plan)
     downs = weight_slots(plan, kept_ref, down_s)
-    copies = weight_copies(plan, up_hbm, weight_slots(plan, up_s), sems.at[0])
+    ups = weight_slots(plan, held_ref, up_s)
+    copies = weight_copies(plan, up_hbm, ups, sems.at[0])[plan.held :]
     copies += weight_copies(plan, down_hbm, downs, sems.at[1])
     queue = Queue(copies, 3)
     queue.fill()
@@ -328,8 +333,9 @@
         gate_s[e] = dot_tb(x_s[part, :], gate_ref[e])
     up = None
     for e, part in enumerate(parts):
-        queue.take()
-        last, up = up, dot_tb(x_s[part, :], up_s[e])
+        if e >= plan.held:
+            queue.take()
+        last, up = up, dot_tb(x_s[part, :], ups[e][...])
         if e:
             gate = gate_s[e - 1]
             hidden_s[e - 1] = (gate / (1.0 + jnp.exp(-gate)) * last).astype(BF16)
@@ -353,12 +359,13 @@
 def backward_kernel(plan, count, *refs):
     blocks, refs = refs[:count], refs[count:]
     saved_ref, other_ref, refs = refs[0], refs[plan.split - 1], refs[plan.split :]
-    gate_ref, kept_ref, up_hbm, down_hbm, *refs = refs
+    gate_ref, held_ref, kept_ref, up_hbm, down_hbm, *refs = refs
     outs, (up_s, down_s, x_s, y_s, score_s, grads_s, sems) = refs[:-7], refs[-7:]
     first, _ = first_expert(plan)
     downs = weight_slots(plan, kept_ref, down_s)
     copies = weight_copies(plan, down_hbm, downs, sems.at[0])[plan.kept :]
-    copies += weight_copies(plan, up_hbm, weight_slots(plan, up_s), sems.at[1])
+    ups = weight_slots(plan, held_ref, up_s)
+    copies += weight_copies(plan, up_hbm, ups, sems.at[1])[plan.held :]
     queue = Queue(copies, 3)
     queue.fill()
     table, factor = arrived(plan, blocks, first, x_s)
@@ -396,8 +403,9 @@
             through_activation(e - 1, last)
     through_activation(plan.mine - 1, grad)
     for e, part in enumerate(parts):
-        queue.take()
-        result = dot(grads_s[0, e], gate_ref[e]) + dot(grads_s[1, e], up_s[e])
+        if e >= plan.held:
+            queue.take()
+        result = dot(grads_s[0, e], gate_ref[e]) + dot(grads_s[1, e], ups[e][...])
         y_s[part, :] = (result * factor[part]).astype(BF16)
     half, near = plan.half, outs[: len(outs) // 2]
     far = outs[len(outs) // 2 :]
@@ -427,7 +435,9 @@
         in_specs=[vmem()] * len(inputs) + [hbm()] * 2,
         out_specs=[vmem()] * len(shapes),
         scratch_shapes=[
-            *[weight(plan.mine), weight(max(plan.mine - plan.kept, 1)), rows, rows],
+            weight(max(plan.mine - plan.held, 1)),
+            weight(max(plan.mine - plan.kept, 1)),
+            *[rows, rows],
             *scratch,
             pltpu.SemaphoreType.DMA((2, plan.mine)),
         ],
@@ -441,27 +451,27 @@
     )(*inputs, in_hbm(up_hbm), in_hbm(down_hbm))
 
 
-def forward(plan, blocks, gate, up_hbm, down_hbm):
+def forward(plan, blocks, gate, held, up_hbm, down_hbm):
     kernel = functools.partial(forward_kernel, plan, len(blocks))
     shape = (plan.mine, plan.expert_rows, plan.hidden)
     scratch = [pltpu.VMEM(shape, F32), pltpu.VMEM(shape, BF16)]
     kept = pltpu.VMEM((plan.kept, plan.hidden, plan.width), BF16)
     shapes = part_shapes(plan, plan.width, 2) + [kept]
-    inputs = [*blocks, in_vmem(gate)]
+    inputs = [*blocks, in_vmem(gate), in_vmem(held)]
     *parts, kept = expert_call(
         plan, kernel, "forward", inputs, up_hbm, down_hbm, shapes, scratch
     )
     return parts, kept
 
 
-def backward(plan, blocks, saved, gate, kept, up_hbm, down_hbm):
+def backward(plan, blocks, saved, resident, up_hbm, down_hbm):
     kernel = functools.partial(backward_kernel, plan, len(blocks))
     scratch = [
         pltpu.VMEM((plan.rows, plan.meta), BF16),
         pltpu.VMEM((2, plan.mine, plan.expert_rows, plan.hidden), BF16),
     ]
     shapes = part_shapes(plan, plan.half) + part_shapes(plan, plan.sent - plan.half)
-    inputs = [*blocks, *saved, in_vmem(gate), in_vmem(kept)]
+    inputs = [*blocks, *saved, *[in_vmem(w) for w in resident]]
     parts = expert_call(
         plan, kernel, "backward", inputs, up_hbm, down_hbm, shapes, scratch
     )
@@ -569,27 +579,28 @@
     packed_back, saved, ready = prepare(
         plan, cotangent, routes_back, weights_back, saved_gate, saved_up, packed
     )
+    if plan.split > 1:
+        saved[1] = plan.over_pair(saved[1])
     gate_hbm, up_hbm = jnp.swapaxes(w_gate, 1, 2), jnp.swapaxes(w_up, 1, 2)
     if plan.paired and plan.owners > 1:
         blocks = [packed, plan.over_expert(packed, 1)]
-        gate, done = fetch(plan, gate_hbm, blocks[1])
+        gate, held, done = fetch(plan, gate_hbm, up_hbm, blocks[1], saved[-1])
         step = 2
         while step < plan.owners:
             blocks.append(plan.over_expert(jnp.concatenate(blocks) + ready[:1], step))
             step *= 2
     else:
         blocks = gather_group(plan, packed)
-        gate, done = fetch(plan, gate_hbm, packed)
+        gate, held, done = fetch(plan, gate_hbm, up_hbm, packed, saved[-1])
     if plan.split > 1:
         blocks.append(plan.over_pair(jnp.concatenate(blocks) + done[:1]))
     blocks_back = gather_group(plan, packed_back)
-    parts, kept = forward(plan, blocks, gate, up_hbm, w_down)
+    parts, kept = forward(plan, blocks, gate, held, up_hbm, w_down)
     parts, blocks_back = lax.optimization_barrier((parts, blocks_back))
     if plan.split > 1:
         blocks_back = blocks_back + [plan.over_pair(jnp.concatenate(blocks_back))]
-        saved[1] = plan.over_pair(saved[1])
     terms = scatter_group(plan, sum_pair(plan, parts))
-    parts_back = backward(plan, blocks_back, saved, gate, kept, up_hbm, w_down)
+    parts_back = backward(plan, blocks_back, saved, (gate, held, kept), up_hbm, w_down)
     parts_back, terms = lax.optimization_barrier((parts_back, terms))
     mixed = total(terms).astype(BF16)
     near, far = scatter_steps(plan, [sum_pair(plan, parts) for parts in parts_back])

time: 63.2 us -> 67.4 us (1.066)
  local copies, waits for them, and re-layouts: 0.12 us -> 4.4 us
  starting transfers between devices: 19.9 us -> 18.5 us
  waiting for transfers between devices: 8.07 us -> 8.82 us
    unnamed x4 -> x8, local copies, waits for them, and re-layouts: 0.01 us -> 4.29 us
    ppermute x12, starting transfers between devices: 18.1 us -> 17 us  [over_expert(): return lax.ppermute(x, ('dp', 'expert'), pairs)]
    pallas_call x1, Pallas kernels: 4.4 us -> 5.26 us  [fetch(): pl.pallas_call(functools.partial(fetch_kernel, plan), out_shape=(pltpu.VM...]
  transfers between devices with their start and end apart: 19 -> 19, of which waited for: 7 -> 7; matrix products, arithmetic and copies ran while one was open for 2% -> 2% of each run, Pallas kernels for 49% -> 47%
where the time goes in v10:
time: 67.4 us; the launch traced here: 67.2 us
  Pallas kernels  33.3 us (49%)
  starting transfers between devices  18.5 us (27%)
  waiting for transfers between devices  8.82 us (13%)
  local copies, waits for them, and re-layouts  4.4 us (7%)
  other arithmetic  1.2 us (2%)
  between operations  1.04 us (2%)
    pallas_call x2, Pallas kernels, expert_call(): pl.pallas_call(kernel, out_shape=shapes, in_specs=[vmem()] * len(inputs)...  24.6 us
    ppermute x12, starting transfers between devices, over_expert(): return lax.ppermute(x, ('dp', 'expert'), pairs)  17 us
    ppermute x12, waiting for transfers between devices, over_expert(): return lax.ppermute(x, ('dp', 'expert'), pairs)  6.95 us
    pallas_call x1, Pallas kernels, fetch(): pl.pallas_call(functools.partial(fetch_kernel, plan), out_shape=(pltpu.VM...  5.26 us
    unnamed x8, local copies, waits for them, and re-layouts  4.29 us
    ppermute x7, waiting for transfers between devices, over_pair(): return lax.ppermute(x, 'dp', [(i, i ^ 1) for i in range(self.groups)])  1.88 us
    pallas_call x1, Pallas kernels, prepare(): pl.pallas_call(functools.partial(prepare_kernel, plan), out_shape=out_sha...  1.59 us
    ppermute x7, starting transfers between devices, over_pair(): return lax.ppermute(x, 'dp', [(i, i ^ 1) for i in range(self.groups)])  1.42 us
  transfers between devices with their start and end apart: 19, of which 7 were waited for; matrix products, arithmetic and copies ran while one was open for 2% of the time, Pallas kernels for 47%

profile of v10, /device:TPU:0, one launch (start us, length us, event | category | flops | bytes accessed | tf_op | source)
XLA Modules:
  0.0 67.2 jit_solution(10461916258217912486)
XLA Ops:
  0.6 1.1 %pack.1.after.refs_0_ = bf16[32,2176]{1,0:T(8,128)(2,1)S(1)} custom-call(bf16[32,2048]{1,0:T(8,128)(2,1)} %refs_0_.1, s32[6,32]{1,0:T(8,128)} %bitcast.25, f32[6,32]{1,0:T(8,128)} %bitcast.26), custom_call_target="tpu_custom_call" | custom-call | tf_op jit(solution)/shard_map/pack/pallas_call | solution.py:141
  1.7 3.0 %collective-permute-start = (bf16[32,2176]{1,0:T(8,128)(2,1)S(1)}, bf16[32,2176]{1,0:T(8,128)(2,1)S(1)}, u32[]{:S(2)}, u32[]{:S(2)}) collective-permute-start(bf16[32,2176]{1,0:T(8,128)(2,1)S(1)} %pack.1.after.refs_0_), channel_id=1, source_target_pairs={{1,0},{0,1},{3,2},{2,3},{6,4},{7,5},{4,6},{5,7},{9,8},{8,9},{11,10... | collective-permute-start | bytes 417800 | tf_op jit(solution)/shard_map/ppermute | solution.py:90
  4.7 1.6 %prepare.1 = (bf16[32,2176]{1,0:T(8,128)(2,1)S(1)}, bf16[16,2176]{1,0:T(8,128)(2,1)S(1)}, bf16[2,128,704]{2,1,0:T(8,128)(2,1)S(1)}, bf16[2,128,704]{2,1,0:T(8,128)(2,1)S(1)}) custom-call(bf16[32,2048]{1,0:T(8,128)(2,1)} %x_hbm.1, s32[6,32]{1,0:T(8,128)} %bitcast.17, f32[6,32]{1,0:T(8,128)} %bitcast.27, bf16[224,704]{1,0:T(8,128)(2,1)} %bitcast.23, ...), custom_call_target="tpu_custom_call" | custom-call | bytes 17825792 | tf_op jit(solution)/shard_map/prepare/pallas_call | solution.py:234
  6.4 1.3 %collective-permute-done.after.refs_1_ = bf16[32,2176]{1,0:T(8,128)(2,1)S(1)} collective-permute-done((bf16[32,2176]{1,0:T(8,128)(2,1)S(1)}, bf16[32,2176]{1,0:T(8,128)(2,1)S(1)}, u32[]{:S(2)}, u32[]{:S(2)}) %collective-permute-start) | collective-permute-done | bytes 139296 | tf_op jit(solution)/shard_map/ppermute | solution.py:90
  7.8 2.1 %collective-permute-start.1 = (bf16[64,2176]{1,0:T(8,128)(2,1)S(1)}, bf16[64,2176]{1,0:T(8,128)(2,1)S(1)}, u32[]{:S(2)}, u32[]{:S(2)}) collective-permute-start(bf16[64,2176]{1,0:T(8,128)(2,1)S(1)} %maximum_add_fusion.1), channel_id=1, source_target_pairs={{2,0},{3,1},{0,2},{1,3},{5,4},{4,5},{7,6},{6,7},{10,8},{11,9},{8,1... | collective-permute-start | bytes 835592 | tf_op jit(solution)/shard_map/ppermute | solution.py:90
  9.9 5.3 %fetch.1 = (bf16[4,704,2048]{2,1,0:T(8,128)(2,1)S(1)}, bf16[1,704,2048]{2,1,0:T(8,128)(2,1)S(1)}, bf16[16,2176]{1,0:T(8,128)(2,1)S(1)}) custom-call(bf16[8,704,2048]{2,1,0:T(8,128)(2,1)} %bitcast.22, bf16[8,704,2048]{2,1,0:T(8,128)(2,1)} %bitcast.19, bf16[32,2176]{1,0:T(8,128)(2,1)S(1)} %collective-permute-done.after.refs_1_, ...), custom_call_target="tpu_custom_call" | custom-call | bytes 23068672 | tf_op jit(solution)/shard_map/fetch/pallas_call | solution.py:273
  15.4 2.2 %collective-permute-start.6 = (bf16[32,2176]{1,0:T(8,128)(2,1)S(1)}, bf16[32,2176]{1,0:T(8,128)(2,1)S(1)}, u32[]{:S(2)}, u32[]{:S(2)}) collective-permute-start(bf16[32,2176]{1,0:T(8,128)(2,1)S(1)} %get-tuple-element.66.refs_0_), channel_id=1, source_target_pairs={{3,0},{2,1},{1,2},{0,3},{7,4},{6,5},{5,6},{4,7},{11,8},{10,9},{9,1... | collective-permute-start | bytes 417800 | tf_op jit(solution)/shard_map/ppermute | solution.py:90
  17.6 0.8 %collective-permute-start.5 = (bf16[32,2176]{1,0:T(8,128)(2,1)S(1)}, bf16[32,2176]{1,0:T(8,128)(2,1)S(1)}, u32[]{:S(2)}, u32[]{:S(2)}) collective-permute-start(bf16[32,2176]{1,0:T(8,128)(2,1)S(1)} %get-tuple-element.66.refs_0_), channel_id=1, source_target_pairs={{2,0},{3,1},{0,2},{1,3},{5,4},{4,5},{7,6},{6,7},{10,8},{11,9},{8,1... | collective-permute-start | bytes 417800 | tf_op jit(solution)/shard_map/ppermute | solution.py:90
  19.0 13.1 %forward.1 = (bf16[32,2048]{1,0:T(8,128)(2,1)S(1)}, bf16[32,2048]{1,0:T(8,128)(2,1)S(1)}, bf16[32,2048]{1,0:T(8,128)(2,1)S(1)}, bf16[32,2048]{1,0:T(8,128)(2,1)S...) custom-call(bf16[32,2176]{1,0:T(8,128)(2,1)S(1)} %pack.1.after.refs_0_, ...), custom_call_target="tpu_custom_call" | custom-call | flops 2214592512 | bytes 23068672 | tf_op jit(solution)/shard_map/forward/pallas_call | solution.py:432
  32.9 0.8 %collective-permute-done.8 = bf16[64,2048]{1,0:T(8,128)(2,1)S(1)} collective-permute-done((bf16[64,2048]{1,0:T(8,128)(2,1)S(1)}, bf16[64,2048]{1,0:T(8,128)(2,1)S(1)}, u32[]{:S(2)}, u32[]{:S(2)}) %collective-permute-start.8) | collective-permute-done | bytes 262176 | tf_op jit(solution)/shard_map/ppermute | solution.py:93
  33.8 1.6 %collective-permute-start.9 = (bf16[32,2048]{1,0:T(8,128)(2,1)S(1)}, bf16[32,2048]{1,0:T(8,128)(2,1)S(1)}, u32[]{:S(2)}, u32[]{:S(2)}) collective-permute-start(bf16[32,2048]{1,0:T(8,128)(2,1)S(1)} %add_convert_fusion.3), channel_id=1, source_target_pairs={{0,1},{1,0},{2,3},{3,2},{4,6},{5,7},{6,4},{7,5},{8,9},{9,8},{10,11... | collective-permute-start | bytes 393224 | tf_op jit(solution)/shard_map/ppermute | solution.py:90
  35.4 1.3 %collective-permute-start.12 = (bf16[32,2048]{1,0:T(8,128)(2,1)S(1)}, bf16[32,2048]{1,0:T(8,128)(2,1)S(1)}, u32[]{:S(2)}, u32[]{:S(2)}) collective-permute-start(bf16[32,2048]{1,0:T(8,128)(2,1)S(1)} %get-tuple-element.109), channel_id=1, source_target_pairs={{0,3},{1,2},{2,1},{3,0},{4,7},{5,6},{6,5},{7,4},{8,11},{9,10},{10,... | collective-permute-start | bytes 393224 | tf_op jit(solution)/shard_map/ppermute | solution.py:90
  36.7 0.8 %collective-permute-start.11 = (bf16[32,2048]{1,0:T(8,128)(2,1)S(1)}, bf16[32,2048]{1,0:T(8,128)(2,1)S(1)}, u32[]{:S(2)}, u32[]{:S(2)}) collective-permute-start(bf16[32,2048]{1,0:T(8,128)(2,1)S(1)} %get-tuple-element.110), channel_id=1, source_target_pairs={{0,2},{1,3},{2,0},{3,1},{4,5},{5,4},{6,7},{7,6},{8,10},{9,11},{10,... | collective-permute-start | bytes 393224 | tf_op jit(solution)/shard_map/ppermute | solution.py:90
  37.5 4.3 %copy-done.1 = bf16[4,704,2048]{2,1,0:T(8,128)(2,1)S(1)} copy-done((bf16[4,704,2048]{2,1,0:T(8,128)(2,1)S(1)}, bf16[4,704,2048]{2,1,0:T(8,128)(2,1)}, u32[]{:S(2)}) %copy-start.1) | copy-done | bytes 11534360
  41.8 11.5 %backward.1 = (bf16[32,1024]{1,0:T(8,128)(2,1)S(1)}, bf16[32,1024]{1,0:T(8,128)(2,1)S(1)}, bf16[32,1024]{1,0:T(8,128)(2,1)S(1)}, bf16[32,1024]{1,0:T(8,128)(2,1)...) custom-call(bf16[32,2176]{1,0:T(8,128)(2,1)S(1)} %get-tuple-element., ...), custom_call_target="tpu_custom_call" | custom-call | flops 2214592512 | bytes 23068672 | tf_op jit(solution)/shard_map/backward/pallas_call | solution.py:432
  53.9 1.0 %collective-permute-done.13 = bf16[128,1024]{1,0:T(8,128)(2,1)S(1)} collective-permute-done((bf16[128,1024]{1,0:T(8,128)(2,1)S(1)}, bf16[128,1024]{1,0:T(8,128)(2,1)S(1)}, u32[]{:S(2)}, u32[]{:S(2)}) %collective-permute-start.13) | collective-permute-done | bytes 262176 | tf_op jit(solution)/shard_map/ppermute | solution.py:93
  54.9 1.6 %collective-permute-start.14 = (bf16[64,1024]{1,0:T(8,128)(2,1)S(1)}, bf16[64,1024]{1,0:T(8,128)(2,1)S(1)}, u32[]{:S(2)}, u32[]{:S(2)}) collective-permute-start(bf16[64,1024]{1,0:T(8,128)(2,1)S(1)} %pad_maximum_fusion.2), channel_id=1, source_target_pairs={{0,1},{1,0},{2,3},{3,2},{4,6},{5,7},{6,4},{7,5},{8,9},{9,8},{10,11... | collective-permute-start | bytes 393224 | tf_op jit(solution)/shard_map/ppermute | solution.py:90
  56.6 0.6 collective-permute-start.17
  57.2 2.8 %collective-permute-done.14 = bf16[64,1024]{1,0:T(8,128)(2,1)S(1)} collective-permute-done((bf16[64,1024]{1,0:T(8,128)(2,1)S(1)}, bf16[64,1024]{1,0:T(8,128)(2,1)S(1)}, u32[]{:S(2)}, u32[]{:S(2)}) %collective-permute-start.14) | collective-permute-done | bytes 131104 | tf_op jit(solution)/shard_map/ppermute | solution.py:90
  60.0 1.3 %collective-permute-start.15 = (bf16[32,1024]{1,0:T(8,128)(2,1)S(1)}, bf16[32,1024]{1,0:T(8,128)(2,1)S(1)}, u32[]{:S(2)}, u32[]{:S(2)}) collective-permute-start(bf16[32,1024]{1,0:T(8,128)(2,1)S(1)} %add_convert_fusion.7), channel_id=1, source_target_pairs={{0,2},{1,3},{2,0},{3,1},{4,5},{5,4},{6,7},{7,6},{8,10},{9,11},{10,... | collective-permute-start | bytes 196616 | tf_op jit(solution)/shard_map/ppermute | solution.py:90
  61.8 1.3 %collective-permute-start.18 = (bf16[32,1152]{1,0:T(8,128)(2,1)S(1)}, bf16[32,1152]{1,0:T(8,128)(2,1)S(1)}, u32[]{:S(2)}, u32[]{:S(2)}) collective-permute-start(bf16[32,1152]{1,0:T(8,128)(2,1)S(1)} %add_convert_fusion.4), channel_id=1, source_target_pairs={{0,2},{1,3},{2,0},{3,1},{4,5},{5,4},{6,7},{7,6},{8,10},{9,11},{10,... | collective-permute-start | bytes 221192 | tf_op jit(solution)/shard_map/ppermute | solution.py:90
  63.1 0.7 %add_convert_fusion = bf16[32,2048]{1,0:T(8,128)(2,1)} fusion(bf16[32,2048]{1,0:T(8,128)(2,1)S(1)} %collective-permute-done.12, bf16[32,2048]{1,0:T(8,128)(2,1)S(1)} %collective-permute-done.11, bf16[32,2048]{1,0:T(8,128)(2,1)S(1)} %collective-permute-done.9, bf16[32,2048]{1,0:T(8,128)(2,1)S(1)} %slice-done, bf16[32,2048]{1,0:T(8,128)(2,1)S(1)} %get-tuple-element.88), kind=kLoop, calls=%fused_computation.3 | loop fusion | flops 655360 | bytes 786432 | tf_op jit(solution)/shard_map/convert_element_type | solution.py:605
  64.3 1.9 %collective-permute-done.18.refs_7_ = bf16[32,1152]{1,0:T(8,128)(2,1)S(1)} collective-permute-done((bf16[32,1152]{1,0:T(8,128)(2,1)S(1)}, bf16[32,1152]{1,0:T(8,128)(2,1)S(1)}, u32[]{:S(2)}, u32[]{:S(2)}) %collective-permute-start.18) | collective-permute-done | bytes 73760 | tf_op jit(solution)/shard_map/ppermute | solution.py:90
  66.2 0.8 %finish.1 = (bf16[32,2048]{1,0:T(8,128)(2,1)}, f32[6,32]{1,0:T(8,128)}) custom-call(bf16[32,1024]{1,0:T(8,128)(2,1)S(1)} %get-tuple-element.93.refs_0_, bf16[32,1024]{1,0:T(8,128)(2,1)S(1)} %slice.76.refs_1_, bf16[32,1024]{1,0:T(8,128)(2,1)S(1)} %slice.79.refs_2_, bf16[32,1024]{1,0:T(8,128)(2,1)S(1)} %collective-permute-done.15.refs_3_, ...), custom_call_target="tpu_custom_call" | custom-call | tf_op jit(solution)/shard_map/finish/pallas_call | solution.py:545
  (48 shorter events, 3.5 us)
Async XLA Ops:
  1.7 6.0 %collective-permute-start = (bf16[32,2176]{1,0:T(8,128)(2,1)S(1)}, bf16[32,2176]{1,0:T(8,128)(2,1)S(1)}, u32[]{:S(2)}, u32[]{:S(2)}) collective-permute-start(bf16[32,2176]{1,0:T(8,128)(2,1)S(1)} %pack.1.after.refs_0_), channel_id=1, source_target_pairs={{1,0},{0,1},{3,2},{2,3},{6,4},{7,5},{4,6},{5,7},{9,8},{8,9},{11,10... | collective-permute-start | bytes 417800 | tf_op jit(solution)/shard_map/ppermute | solution.py:90
  6.3 3.6 %collective-permute-start.2 = (bf16[2,128,704]{2,1,0:T(8,128)(2,1)S(1)}, bf16[2,128,704]{2,1,0:T(8,128)(2,1)S(1)}, u32[]{:S(2)}, u32[]{:S(2)}) collective-permute-start(bf16[2,128,704]{2,1,0:T(8,128)(2,1)S(1)} %get-tuple-element.55), channel_id=1, source_target_pairs={{0,4},{4,0},{8,12},{12,8},{16,20},{20,16},{24,28},{28,24},{1,5},{5... | collective-permute-start | bytes 1081352 | tf_op jit(solution)/shard_map/ppermute | solution.py:93
  7.8 7.4 %collective-permute-start.1 = (bf16[64,2176]{1,0:T(8,128)(2,1)S(1)}, bf16[64,2176]{1,0:T(8,128)(2,1)S(1)}, u32[]{:S(2)}, u32[]{:S(2)}) collective-permute-start(bf16[64,2176]{1,0:T(8,128)(2,1)S(1)} %maximum_add_fusion.1), channel_id=1, source_target_pairs={{2,0},{3,1},{0,2},{1,3},{5,4},{4,5},{7,6},{6,7},{10,8},{11,9},{8,1... | collective-permute-start | bytes 835592 | tf_op jit(solution)/shard_map/ppermute | solution.py:90
  15.2 16.9 %copy-start = (bf16[4,704,2048]{2,1,0:T(8,128)(2,1)}, bf16[4,704,2048]{2,1,0:T(8,128)(2,1)S(1)}, u32[]{:S(2)}) copy-start(bf16[4,704,2048]{2,1,0:T(8,128)(2,1)S(1)} %get-tuple-element.57.refs_4_.refs_7_) | copy-start | bytes 34603012
  15.3 3.6 %collective-permute-start.3 = (bf16[128,2176]{1,0:T(8,128)(2,1)S(1)}, bf16[128,2176]{1,0:T(8,128)(2,1)S(1)}, u32[]{:S(2)}, u32[]{:S(2)}) collective-permute-start(bf16[128,2176]{1,0:T(8,128)(2,1)S(1)} %maximum_add_fusion), channel_id=1, source_target_pairs={{0,4},{4,0},{8,12},{12,8},{16,20},{20,16},{24,28},{28,24},{1,5},{5... | collective-permute-start | bytes 1671176 | tf_op jit(solution)/shard_map/ppermute | solution.py:93
  15.4 16.7 %collective-permute-start.6 = (bf16[32,2176]{1,0:T(8,128)(2,1)S(1)}, bf16[32,2176]{1,0:T(8,128)(2,1)S(1)}, u32[]{:S(2)}, u32[]{:S(2)}) collective-permute-start(bf16[32,2176]{1,0:T(8,128)(2,1)S(1)} %get-tuple-element.66.refs_0_), channel_id=1, source_target_pairs={{3,0},{2,1},{1,2},{0,3},{7,4},{6,5},{5,6},{4,7},{11,8},{10,9},{9,1... | collective-permute-start | bytes 417800 | tf_op jit(solution)/shard_map/ppermute | solution.py:90
  17.6 14.5 %collective-permute-start.5 = (bf16[32,2176]{1,0:T(8,128)(2,1)S(1)}, bf16[32,2176]{1,0:T(8,128)(2,1)S(1)}, u32[]{:S(2)}, u32[]{:S(2)}) collective-permute-start(bf16[32,2176]{1,0:T(8,128)(2,1)S(1)} %get-tuple-element.66.refs_0_), channel_id=1, source_target_pairs={{2,0},{3,1},{0,2},{1,3},{5,4},{4,5},{7,6},{6,7},{10,8},{11,9},{8,1... | collective-permute-start | bytes 417800 | tf_op jit(solution)/shard_map/ppermute | solution.py:90
  18.4 13.7 %collective-permute-start.4 = (bf16[32,2176]{1,0:T(8,128)(2,1)S(1)}, bf16[32,2176]{1,0:T(8,128)(2,1)S(1)}, u32[]{:S(2)}, u32[]{:S(2)}) collective-permute-start(bf16[32,2176]{1,0:T(8,128)(2,1)S(1)} %get-tuple-element.66.refs_0_), channel_id=1, source_target_pairs={{1,0},{0,1},{3,2},{2,3},{6,4},{7,5},{4,6},{5,7},{9,8},{8,9},{11,10... | collective-permute-start | bytes 417800 | tf_op jit(solution)/shard_map/ppermute | solution.py:90
  32.2 1.6 %collective-permute-start.8 = (bf16[64,2048]{1,0:T(8,128)(2,1)S(1)}, bf16[64,2048]{1,0:T(8,128)(2,1)S(1)}, u32[]{:S(2)}, u32[]{:S(2)}) collective-permute-start(bf16[64,2048]{1,0:T(8,128)(2,1)S(1)} %get-tuple-element.83), channel_id=1, source_target_pairs={{0,4},{4,0},{8,12},{12,8},{16,20},{20,16},{24,28},{28,24},{1,5},{5... | collective-permute-start | bytes 786440 | tf_op jit(solution)/shard_map/ppermute | solution.py:93
  32.2 3.1 %collective-permute-start.10 = (bf16[64,2048]{1,0:T(8,128)(2,1)S(1)}, bf16[64,2048]{1,0:T(8,128)(2,1)S(1)}, u32[]{:S(2)}, u32[]{:S(2)}) collective-permute-start(bf16[64,2048]{1,0:T(8,128)(2,1)S(1)} %get-tuple-element.86), channel_id=1, source_target_pairs={{0,4},{4,0},{8,12},{12,8},{16,20},{20,16},{24,28},{28,24},{1,5},{5... | collective-permute-start | bytes 786440 | tf_op jit(solution)/shard_map/ppermute | solution.py:93
  32.8 4.7 %collective-permute-start.7 = (bf16[128,2176]{1,0:T(8,128)(2,1)S(1)}, bf16[128,2176]{1,0:T(8,128)(2,1)S(1)}, u32[]{:S(2)}, u32[]{:S(2)}) collective-permute-start(bf16[128,2176]{1,0:T(8,128)(2,1)S(1)} %pad_maximum_fusion), channel_id=1, source_target_pairs={{0,4},{4,0},{8,12},{12,8},{16,20},{20,16},{24,28},{28,24},{1,5},{5... | collective-permute-start | bytes 1671176 | tf_op jit(solution)/shard_map/ppermute | solution.py:93
  33.8 19.5 %copy-start.3 = (bf16[64,2048]{1,0:T(8,128)(2,1)}, bf16[64,2048]{1,0:T(8,128)(2,1)S(1)}, u32[]{:S(2)}) copy-start(bf16[64,2048]{1,0:T(8,128)(2,1)S(1)} %collective-permute-done.8) | copy-start | bytes 786436
  33.8 19.4 %collective-permute-start.9 = (bf16[32,2048]{1,0:T(8,128)(2,1)S(1)}, bf16[32,2048]{1,0:T(8,128)(2,1)S(1)}, u32[]{:S(2)}, u32[]{:S(2)}) collective-permute-start(bf16[32,2048]{1,0:T(8,128)(2,1)S(1)} %add_convert_fusion.3), channel_id=1, source_target_pairs={{0,1},{1,0},{2,3},{3,2},{4,6},{5,7},{6,4},{7,5},{8,9},{9,8},{10,11... | collective-permute-start | bytes 393224 | tf_op jit(solution)/shard_map/ppermute | solution.py:90
  35.4 17.8 %collective-permute-start.12 = (bf16[32,2048]{1,0:T(8,128)(2,1)S(1)}, bf16[32,2048]{1,0:T(8,128)(2,1)S(1)}, u32[]{:S(2)}, u32[]{:S(2)}) collective-permute-start(bf16[32,2048]{1,0:T(8,128)(2,1)S(1)} %get-tuple-element.109), channel_id=1, source_target_pairs={{0,3},{1,2},{2,1},{3,0},{4,7},{5,6},{6,5},{7,4},{8,11},{9,10},{10,... | collective-permute-start | bytes 393224 | tf_op jit(solution)/shard_map/ppermute | solution.py:90
  36.7 16.6 %collective-permute-start.11 = (bf16[32,2048]{1,0:T(8,128)(2,1)S(1)}, bf16[32,2048]{1,0:T(8,128)(2,1)S(1)}, u32[]{:S(2)}, u32[]{:S(2)}) collective-permute-start(bf16[32,2048]{1,0:T(8,128)(2,1)S(1)} %get-tuple-element.110), channel_id=1, source_target_pairs={{0,2},{1,3},{2,0},{3,1},{4,5},{5,4},{6,7},{7,6},{8,10},{9,11},{10,... | collective-permute-start | bytes 393224 | tf_op jit(solution)/shard_map/ppermute | solution.py:90
  37.5 4.3 %copy-start.1 = (bf16[4,704,2048]{2,1,0:T(8,128)(2,1)S(1)}, bf16[4,704,2048]{2,1,0:T(8,128)(2,1)}, u32[]{:S(2)}) copy-start(bf16[4,704,2048]{2,1,0:T(8,128)(2,1)} %copy-done) | copy-start | bytes 34603012
  53.3 9.9 %slice-start = ((bf16[64,2048]{1,0:T(8,128)(2,1)}), bf16[32,2048]{1,0:T(8,128)(2,1)S(1)}, s32[]{:S(2)}) async-start(bf16[64,2048]{1,0:T(8,128)(2,1)} %copy-done.3), calls=%async_computation | async-start | bytes 262144 | tf_op jit(solution)/shard_map/slice | solution.py:491
  53.3 1.6 %collective-permute-start.13 = (bf16[128,1024]{1,0:T(8,128)(2,1)S(1)}, bf16[128,1024]{1,0:T(8,128)(2,1)S(1)}, u32[]{:S(2)}, u32[]{:S(2)}) collective-permute-start(bf16[128,1024]{1,0:T(8,128)(2,1)S(1)} %get-tuple-element.94), channel_id=1, source_target_pairs={{0,4},{4,0},{8,12},{12,8},{16,20},{20,16},{24,28},{28,24},{1,5},{5... | collective-permute-start | bytes 786440 | tf_op jit(solution)/shard_map/ppermute | solution.py:93
  53.4 3.1 %collective-permute-start.16 = (bf16[128,1152]{1,0:T(8,128)(2,1)S(1)}, bf16[128,1152]{1,0:T(8,128)(2,1)S(1)}, u32[]{:S(2)}, u32[]{:S(2)}) collective-permute-start(bf16[128,1152]{1,0:T(8,128)(2,1)S(1)} %get-tuple-element.99), channel_id=1, source_target_pairs={{0,4},{4,0},{8,12},{12,8},{16,20},{20,16},{24,28},{28,24},{1,5},{5... | collective-permute-start | bytes 884744 | tf_op jit(solution)/shard_map/ppermute | solution.py:93
  54.9 5.0 %collective-permute-start.14 = (bf16[64,1024]{1,0:T(8,128)(2,1)S(1)}, bf16[64,1024]{1,0:T(8,128)(2,1)S(1)}, u32[]{:S(2)}, u32[]{:S(2)}) collective-permute-start(bf16[64,1024]{1,0:T(8,128)(2,1)S(1)} %pad_maximum_fusion.2), channel_id=1, source_target_pairs={{0,1},{1,0},{2,3},{3,2},{4,6},{5,7},{6,4},{7,5},{8,9},{9,8},{10,11... | collective-permute-start | bytes 393224 | tf_op jit(solution)/shard_map/ppermute | solution.py:90
  56.5 9.7 %copy-start.2 = (s32[32,6]{0,1:T(8,128)S(1)}, s32[32,6]{0,1:T(8,128)}, u32[]{:S(2)}) copy-start(s32[32,6]{0,1:T(8,128)} %param.15) | copy-start | bytes 2308
  56.6 5.2 %collective-permute-start.17 = (bf16[64,1152]{1,0:T(8,128)(2,1)S(1)}, bf16[64,1152]{1,0:T(8,128)(2,1)S(1)}, u32[]{:S(2)}, u32[]{:S(2)}) collective-permute-start(bf16[64,1152]{1,0:T(8,128)(2,1)S(1)} %pad_maximum_fusion.1), channel_id=1, source_target_pairs={{0,1},{1,0},{2,3},{3,2},{4,6},{5,7},{6,4},{7,5},{8,9},{9,8},{10,11... | collective-permute-start | bytes 442376 | tf_op jit(solution)/shard_map/ppermute | solution.py:90
  60.0 4.3 %collective-permute-start.15 = (bf16[32,1024]{1,0:T(8,128)(2,1)S(1)}, bf16[32,1024]{1,0:T(8,128)(2,1)S(1)}, u32[]{:S(2)}, u32[]{:S(2)}) collective-permute-start(bf16[32,1024]{1,0:T(8,128)(2,1)S(1)} %add_convert_fusion.7), channel_id=1, source_target_pairs={{0,2},{1,3},{2,0},{3,1},{4,5},{5,4},{6,7},{7,6},{8,10},{9,11},{10,... | collective-permute-start | bytes 196616 | tf_op jit(solution)/shard_map/ppermute | solution.py:90
  61.8 4.4 %collective-permute-start.18 = (bf16[32,1152]{1,0:T(8,128)(2,1)S(1)}, bf16[32,1152]{1,0:T(8,128)(2,1)S(1)}, u32[]{:S(2)}, u32[]{:S(2)}) collective-permute-start(bf16[32,1152]{1,0:T(8,128)(2,1)S(1)} %add_convert_fusion.4), channel_id=1, source_target_pairs={{0,2},{1,3},{2,0},{3,1},{4,5},{5,4},{6,7},{7,6},{8,10},{9,11},{10,... | collective-permute-start | bytes 221192 | tf_op jit(solution)/shard_map/ppermute | solution.py:90

commit v11 on v10

--- a/solution.py
+++ b/solution.py
@@ -441,7 +441,7 @@
             *scratch,
             pltpu.SemaphoreType.DMA((2, plan.mine)),
         ],
-        compiler_params=pltpu.CompilerParams(vmem_limit_bytes=31 * MIB),
+        compiler_params=pltpu.CompilerParams(vmem_limit_bytes=26 * MIB),
         cost_estimate=pl.CostEstimate(
             flops=2 * 3 * plan.mine * plan.expert_rows * plan.width * plan.hidden,
             bytes_accessed=2 * 2 * plan.mine * plan.width * plan.hidden,

time: 67.4 us -> 63.1 us (0.936)
  local copies, waits for them, and re-layouts: 4.4 us -> 0.12 us
    unnamed x8 -> x4, local copies, waits for them, and re-layouts: 4.29 us -> 0.01 us
  transfers between devices with their start and end apart: 19 -> 19, of which waited for: 7 -> 7; matrix products, arithmetic and copies ran while one was open for 2% -> 2% of each run, Pallas kernels for 47% -> 50%
where the time goes in v11:
time: 63.1 us; the launch traced here: 62.9 us
  Pallas kernels  33.2 us (53%)
  starting transfers between devices  18.5 us (29%)
  waiting for transfers between devices  8.81 us (14%)
  other arithmetic  1.2 us (2%)
  between operations  1.02 us (2%)
    pallas_call x2, Pallas kernels, expert_call(): pl.pallas_call(kernel, out_shape=shapes, in_specs=[vmem()] * len(inputs)...  24.5 us
    ppermute x12, starting transfers between devices, over_expert(): return lax.ppermute(x, ('dp', 'expert'), pairs)  17 us
    ppermute x12, waiting for transfers between devices, over_expert(): return lax.ppermute(x, ('dp', 'expert'), pairs)  6.94 us
    pallas_call x1, Pallas kernels, fetch(): pl.pallas_call(functools.partial(fetch_kernel, plan), out_shape=(pltpu.VM...  5.26 us
    ppermute x7, waiting for transfers between devices, over_pair(): return lax.ppermute(x, 'dp', [(i, i ^ 1) for i in range(self.groups)])  1.87 us
    pallas_call x1, Pallas kernels, prepare(): pl.pallas_call(functools.partial(prepare_kernel, plan), out_shape=out_sha...  1.59 us
    ppermute x7, starting transfers between devices, over_pair(): return lax.ppermute(x, 'dp', [(i, i ^ 1) for i in range(self.groups)])  1.42 us
  transfers between devices with their start and end apart: 19, of which 7 were waited for; matrix products, arithmetic and copies ran while one was open for 2% of the time, Pallas kernels for 50%

profile of v11, /device:TPU:0, one launch (start us, length us, event | category | flops | bytes accessed | tf_op | source)
XLA Modules:
  0.0 62.9 jit_solution(3265237893448669209)
XLA Ops:
  0.6 1.1 %pack.1.after.refs_0_ = bf16[32,2176]{1,0:T(8,128)(2,1)S(1)} custom-call(bf16[32,2048]{1,0:T(8,128)(2,1)} %refs_0_.1, s32[6,32]{1,0:T(8,128)} %bitcast.25, f32[6,32]{1,0:T(8,128)} %bitcast.26), custom_call_target="tpu_custom_call" | custom-call | tf_op jit(solution)/shard_map/pack/pallas_call | solution.py:141
  1.7 3.0 %collective-permute-start = (bf16[32,2176]{1,0:T(8,128)(2,1)S(1)}, bf16[32,2176]{1,0:T(8,128)(2,1)S(1)}, u32[]{:S(2)}, u32[]{:S(2)}) collective-permute-start(bf16[32,2176]{1,0:T(8,128)(2,1)S(1)} %pack.1.after.refs_0_), channel_id=1, source_target_pairs={{1,0},{0,1},{3,2},{2,3},{6,4},{7,5},{4,6},{5,7},{9,8},{8,9},{11,10... | collective-permute-start | bytes 417800 | tf_op jit(solution)/shard_map/ppermute | solution.py:90
  4.7 1.6 %prepare.1 = (bf16[32,2176]{1,0:T(8,128)(2,1)S(1)}, bf16[16,2176]{1,0:T(8,128)(2,1)S(1)}, bf16[2,128,704]{2,1,0:T(8,128)(2,1)S(1)}, bf16[2,128,704]{2,1,0:T(8,128)(2,1)S(1)}) custom-call(bf16[32,2048]{1,0:T(8,128)(2,1)} %x_hbm.1, s32[6,32]{1,0:T(8,128)} %bitcast.17, f32[6,32]{1,0:T(8,128)} %bitcast.27, bf16[224,704]{1,0:T(8,128)(2,1)} %bitcast.23, ...), custom_call_target="tpu_custom_call" | custom-call | bytes 17825792 | tf_op jit(solution)/shard_map/prepare/pallas_call | solution.py:234
  6.4 1.3 %collective-permute-done.after.refs_1_ = bf16[32,2176]{1,0:T(8,128)(2,1)S(1)} collective-permute-done((bf16[32,2176]{1,0:T(8,128)(2,1)S(1)}, bf16[32,2176]{1,0:T(8,128)(2,1)S(1)}, u32[]{:S(2)}, u32[]{:S(2)}) %collective-permute-start) | collective-permute-done | bytes 139296 | tf_op jit(solution)/shard_map/ppermute | solution.py:90
  7.8 2.1 %collective-permute-start.1 = (bf16[64,2176]{1,0:T(8,128)(2,1)S(1)}, bf16[64,2176]{1,0:T(8,128)(2,1)S(1)}, u32[]{:S(2)}, u32[]{:S(2)}) collective-permute-start(bf16[64,2176]{1,0:T(8,128)(2,1)S(1)} %maximum_add_fusion.1), channel_id=1, source_target_pairs={{2,0},{3,1},{0,2},{1,3},{5,4},{4,5},{7,6},{6,7},{10,8},{11,9},{8,1... | collective-permute-start | bytes 835592 | tf_op jit(solution)/shard_map/ppermute | solution.py:90
  9.9 5.3 %fetch.1 = (bf16[4,704,2048]{2,1,0:T(8,128)(2,1)S(1)}, bf16[1,704,2048]{2,1,0:T(8,128)(2,1)S(1)}, bf16[16,2176]{1,0:T(8,128)(2,1)S(1)}) custom-call(bf16[8,704,2048]{2,1,0:T(8,128)(2,1)} %bitcast.22, bf16[8,704,2048]{2,1,0:T(8,128)(2,1)} %bitcast.19, bf16[32,2176]{1,0:T(8,128)(2,1)S(1)} %collective-permute-done.after.refs_1_, ...), custom_call_target="tpu_custom_call" | custom-call | bytes 23068672 | tf_op jit(solution)/shard_map/fetch/pallas_call | solution.py:273
  15.4 2.2 %collective-permute-start.6 = (bf16[32,2176]{1,0:T(8,128)(2,1)S(1)}, bf16[32,2176]{1,0:T(8,128)(2,1)S(1)}, u32[]{:S(2)}, u32[]{:S(2)}) collective-permute-start(bf16[32,2176]{1,0:T(8,128)(2,1)S(1)} %get-tuple-element.66.refs_0_), channel_id=1, source_target_pairs={{3,0},{2,1},{1,2},{0,3},{7,4},{6,5},{5,6},{4,7},{11,8},{10,9},{9,1... | collective-permute-start | bytes 417800 | tf_op jit(solution)/shard_map/ppermute | solution.py:90
  17.6 0.8 %collective-permute-start.5 = (bf16[32,2176]{1,0:T(8,128)(2,1)S(1)}, bf16[32,2176]{1,0:T(8,128)(2,1)S(1)}, u32[]{:S(2)}, u32[]{:S(2)}) collective-permute-start(bf16[32,2176]{1,0:T(8,128)(2,1)S(1)} %get-tuple-element.66.refs_0_), channel_id=1, source_target_pairs={{2,0},{3,1},{0,2},{1,3},{5,4},{4,5},{7,6},{6,7},{10,8},{11,9},{8,1... | collective-permute-start | bytes 417800 | tf_op jit(solution)/shard_map/ppermute | solution.py:90
  18.4 0.5 collective-permute-start.4
  19.0 13.1 %forward.1 = (bf16[32,2048]{1,0:T(8,128)(2,1)S(1)}, bf16[32,2048]{1,0:T(8,128)(2,1)S(1)}, bf16[32,2048]{1,0:T(8,128)(2,1)S(1)}, bf16[32,2048]{1,0:T(8,128)(2,1)S...) custom-call(bf16[32,2176]{1,0:T(8,128)(2,1)S(1)} %pack.1.after.refs_0_, ...), custom_call_target="tpu_custom_call" | custom-call | flops 2214592512 | bytes 23068672 | tf_op jit(solution)/shard_map/forward/pallas_call | solution.py:432
  32.9 0.8 %collective-permute-done.8 = bf16[64,2048]{1,0:T(8,128)(2,1)S(1)} collective-permute-done((bf16[64,2048]{1,0:T(8,128)(2,1)S(1)}, bf16[64,2048]{1,0:T(8,128)(2,1)S(1)}, u32[]{:S(2)}, u32[]{:S(2)}) %collective-permute-start.8) | collective-permute-done | bytes 262176 | tf_op jit(solution)/shard_map/ppermute | solution.py:93
  33.8 1.6 %collective-permute-start.9 = (bf16[32,2048]{1,0:T(8,128)(2,1)S(1)}, bf16[32,2048]{1,0:T(8,128)(2,1)S(1)}, u32[]{:S(2)}, u32[]{:S(2)}) collective-permute-start(bf16[32,2048]{1,0:T(8,128)(2,1)S(1)} %add_convert_fusion.3), channel_id=1, source_target_pairs={{0,1},{1,0},{2,3},{3,2},{4,6},{5,7},{6,4},{7,5},{8,9},{9,8},{10,11... | collective-permute-start | bytes 393224 | tf_op jit(solution)/shard_map/ppermute | solution.py:90
  35.4 1.3 %collective-permute-start.12 = (bf16[32,2048]{1,0:T(8,128)(2,1)S(1)}, bf16[32,2048]{1,0:T(8,128)(2,1)S(1)}, u32[]{:S(2)}, u32[]{:S(2)}) collective-permute-start(bf16[32,2048]{1,0:T(8,128)(2,1)S(1)} %get-tuple-element.109), channel_id=1, source_target_pairs={{0,3},{1,2},{2,1},{3,0},{4,7},{5,6},{6,5},{7,4},{8,11},{9,10},{10,... | collective-permute-start | bytes 393224 | tf_op jit(solution)/shard_map/ppermute | solution.py:90
  36.7 0.8 %collective-permute-start.11 = (bf16[32,2048]{1,0:T(8,128)(2,1)S(1)}, bf16[32,2048]{1,0:T(8,128)(2,1)S(1)}, u32[]{:S(2)}, u32[]{:S(2)}) collective-permute-start(bf16[32,2048]{1,0:T(8,128)(2,1)S(1)} %get-tuple-element.110), channel_id=1, source_target_pairs={{0,2},{1,3},{2,0},{3,1},{4,5},{5,4},{6,7},{7,6},{8,10},{9,11},{10,... | collective-permute-start | bytes 393224 | tf_op jit(solution)/shard_map/ppermute | solution.py:90
  37.5 11.4 %backward.1 = (bf16[32,1024]{1,0:T(8,128)(2,1)S(1)}, bf16[32,1024]{1,0:T(8,128)(2,1)S(1)}, bf16[32,1024]{1,0:T(8,128)(2,1)S(1)}, bf16[32,1024]{1,0:T(8,128)(2,1)...) custom-call(bf16[32,2176]{1,0:T(8,128)(2,1)S(1)} %get-tuple-element., ...), custom_call_target="tpu_custom_call" | custom-call | flops 2214592512 | bytes 23068672 | tf_op jit(solution)/shard_map/backward/pallas_call | solution.py:432
  49.5 1.0 %collective-permute-done.13 = bf16[128,1024]{1,0:T(8,128)(2,1)S(1)} collective-permute-done((bf16[128,1024]{1,0:T(8,128)(2,1)S(1)}, bf16[128,1024]{1,0:T(8,128)(2,1)S(1)}, u32[]{:S(2)}, u32[]{:S(2)}) %collective-permute-start.13) | collective-permute-done | bytes 262176 | tf_op jit(solution)/shard_map/ppermute | solution.py:93
  50.6 1.6 %collective-permute-start.14 = (bf16[64,1024]{1,0:T(8,128)(2,1)S(1)}, bf16[64,1024]{1,0:T(8,128)(2,1)S(1)}, u32[]{:S(2)}, u32[]{:S(2)}) collective-permute-start(bf16[64,1024]{1,0:T(8,128)(2,1)S(1)} %pad_maximum_fusion.2), channel_id=1, source_target_pairs={{0,1},{1,0},{2,3},{3,2},{4,6},{5,7},{6,4},{7,5},{8,9},{9,8},{10,11... | collective-permute-start | bytes 393224 | tf_op jit(solution)/shard_map/ppermute | solution.py:90
  52.2 0.6 collective-permute-start.17
  52.8 2.8 %collective-permute-done.14 = bf16[64,1024]{1,0:T(8,128)(2,1)S(1)} collective-permute-done((bf16[64,1024]{1,0:T(8,128)(2,1)S(1)}, bf16[64,1024]{1,0:T(8,128)(2,1)S(1)}, u32[]{:S(2)}, u32[]{:S(2)}) %collective-permute-start.14) | collective-permute-done | bytes 131104 | tf_op jit(solution)/shard_map/ppermute | solution.py:90
  55.7 1.3 %collective-permute-start.15 = (bf16[32,1024]{1,0:T(8,128)(2,1)S(1)}, bf16[32,1024]{1,0:T(8,128)(2,1)S(1)}, u32[]{:S(2)}, u32[]{:S(2)}) collective-permute-start(bf16[32,1024]{1,0:T(8,128)(2,1)S(1)} %add_convert_fusion.7), channel_id=1, source_target_pairs={{0,2},{1,3},{2,0},{3,1},{4,5},{5,4},{6,7},{7,6},{8,10},{9,11},{10,... | collective-permute-start | bytes 196616 | tf_op jit(solution)/shard_map/ppermute | solution.py:90
  57.5 1.3 %collective-permute-start.18 = (bf16[32,1152]{1,0:T(8,128)(2,1)S(1)}, bf16[32,1152]{1,0:T(8,128)(2,1)S(1)}, u32[]{:S(2)}, u32[]{:S(2)}) collective-permute-start(bf16[32,1152]{1,0:T(8,128)(2,1)S(1)} %add_convert_fusion.4), channel_id=1, source_target_pairs={{0,2},{1,3},{2,0},{3,1},{4,5},{5,4},{6,7},{7,6},{8,10},{9,11},{10,... | collective-permute-start | bytes 221192 | tf_op jit(solution)/shard_map/ppermute | solution.py:90
  58.8 0.7 %add_convert_fusion = bf16[32,2048]{1,0:T(8,128)(2,1)} fusion(bf16[32,2048]{1,0:T(8,128)(2,1)S(1)} %collective-permute-done.12, bf16[32,2048]{1,0:T(8,128)(2,1)S(1)} %collective-permute-done.11, bf16[32,2048]{1,0:T(8,128)(2,1)S(1)} %collective-permute-done.9, bf16[32,2048]{1,0:T(8,128)(2,1)S(1)} %slice-done, bf16[32,2048]{1,0:T(8,128)(2,1)S(1)} %get-tuple-element.88), kind=kLoop, calls=%fused_computation.3 | loop fusion | flops 655360 | bytes 786432 | tf_op jit(solution)/shard_map/convert_element_type | solution.py:605
  60.0 1.9 %collective-permute-done.18.refs_7_ = bf16[32,1152]{1,0:T(8,128)(2,1)S(1)} collective-permute-done((bf16[32,1152]{1,0:T(8,128)(2,1)S(1)}, bf16[32,1152]{1,0:T(8,128)(2,1)S(1)}, u32[]{:S(2)}, u32[]{:S(2)}) %collective-permute-start.18) | collective-permute-done | bytes 73760 | tf_op jit(solution)/shard_map/ppermute | solution.py:90
  61.9 0.8 %finish.1 = (bf16[32,2048]{1,0:T(8,128)(2,1)}, f32[6,32]{1,0:T(8,128)}) custom-call(bf16[32,1024]{1,0:T(8,128)(2,1)S(1)} %get-tuple-element.93.refs_0_, bf16[32,1024]{1,0:T(8,128)(2,1)S(1)} %slice.76.refs_1_, bf16[32,1024]{1,0:T(8,128)(2,1)S(1)} %slice.79.refs_2_, bf16[32,1024]{1,0:T(8,128)(2,1)S(1)} %collective-permute-done.15.refs_3_, ...), custom_call_target="tpu_custom_call" | custom-call | tf_op jit(solution)/shard_map/finish/pallas_call | solution.py:545
  (44 shorter events, 2.9 us)
Async XLA Ops:
  1.7 6.0 %collective-permute-start = (bf16[32,2176]{1,0:T(8,128)(2,1)S(1)}, bf16[32,2176]{1,0:T(8,128)(2,1)S(1)}, u32[]{:S(2)}, u32[]{:S(2)}) collective-permute-start(bf16[32,2176]{1,0:T(8,128)(2,1)S(1)} %pack.1.after.refs_0_), channel_id=1, source_target_pairs={{1,0},{0,1},{3,2},{2,3},{6,4},{7,5},{4,6},{5,7},{9,8},{8,9},{11,10... | collective-permute-start | bytes 417800 | tf_op jit(solution)/shard_map/ppermute | solution.py:90
  6.3 3.6 %collective-permute-start.2 = (bf16[2,128,704]{2,1,0:T(8,128)(2,1)S(1)}, bf16[2,128,704]{2,1,0:T(8,128)(2,1)S(1)}, u32[]{:S(2)}, u32[]{:S(2)}) collective-permute-start(bf16[2,128,704]{2,1,0:T(8,128)(2,1)S(1)} %get-tuple-element.55), channel_id=1, source_target_pairs={{0,4},{4,0},{8,12},{12,8},{16,20},{20,16},{24,28},{28,24},{1,5},{5... | collective-permute-start | bytes 1081352 | tf_op jit(solution)/shard_map/ppermute | solution.py:93
  7.8 7.4 %collective-permute-start.1 = (bf16[64,2176]{1,0:T(8,128)(2,1)S(1)}, bf16[64,2176]{1,0:T(8,128)(2,1)S(1)}, u32[]{:S(2)}, u32[]{:S(2)}) collective-permute-start(bf16[64,2176]{1,0:T(8,128)(2,1)S(1)} %maximum_add_fusion.1), channel_id=1, source_target_pairs={{2,0},{3,1},{0,2},{1,3},{5,4},{4,5},{7,6},{6,7},{10,8},{11,9},{8,1... | collective-permute-start | bytes 835592 | tf_op jit(solution)/shard_map/ppermute | solution.py:90
  15.3 3.6 %collective-permute-start.3 = (bf16[128,2176]{1,0:T(8,128)(2,1)S(1)}, bf16[128,2176]{1,0:T(8,128)(2,1)S(1)}, u32[]{:S(2)}, u32[]{:S(2)}) collective-permute-start(bf16[128,2176]{1,0:T(8,128)(2,1)S(1)} %maximum_add_fusion), channel_id=1, source_target_pairs={{0,4},{4,0},{8,12},{12,8},{16,20},{20,16},{24,28},{28,24},{1,5},{5... | collective-permute-start | bytes 1671176 | tf_op jit(solution)/shard_map/ppermute | solution.py:93
  15.4 16.7 %collective-permute-start.6 = (bf16[32,2176]{1,0:T(8,128)(2,1)S(1)}, bf16[32,2176]{1,0:T(8,128)(2,1)S(1)}, u32[]{:S(2)}, u32[]{:S(2)}) collective-permute-start(bf16[32,2176]{1,0:T(8,128)(2,1)S(1)} %get-tuple-element.66.refs_0_), channel_id=1, source_target_pairs={{3,0},{2,1},{1,2},{0,3},{7,4},{6,5},{5,6},{4,7},{11,8},{10,9},{9,1... | collective-permute-start | bytes 417800 | tf_op jit(solution)/shard_map/ppermute | solution.py:90
  17.6 14.5 %collective-permute-start.5 = (bf16[32,2176]{1,0:T(8,128)(2,1)S(1)}, bf16[32,2176]{1,0:T(8,128)(2,1)S(1)}, u32[]{:S(2)}, u32[]{:S(2)}) collective-permute-start(bf16[32,2176]{1,0:T(8,128)(2,1)S(1)} %get-tuple-element.66.refs_0_), channel_id=1, source_target_pairs={{2,0},{3,1},{0,2},{1,3},{5,4},{4,5},{7,6},{6,7},{10,8},{11,9},{8,1... | collective-permute-start | bytes 417800 | tf_op jit(solution)/shard_map/ppermute | solution.py:90
  18.4 13.7 %collective-permute-start.4 = (bf16[32,2176]{1,0:T(8,128)(2,1)S(1)}, bf16[32,2176]{1,0:T(8,128)(2,1)S(1)}, u32[]{:S(2)}, u32[]{:S(2)}) collective-permute-start(bf16[32,2176]{1,0:T(8,128)(2,1)S(1)} %get-tuple-element.66.refs_0_), channel_id=1, source_target_pairs={{1,0},{0,1},{3,2},{2,3},{6,4},{7,5},{4,6},{5,7},{9,8},{8,9},{11,10... | collective-permute-start | bytes 417800 | tf_op jit(solution)/shard_map/ppermute | solution.py:90
  32.1 1.6 %collective-permute-start.8 = (bf16[64,2048]{1,0:T(8,128)(2,1)S(1)}, bf16[64,2048]{1,0:T(8,128)(2,1)S(1)}, u32[]{:S(2)}, u32[]{:S(2)}) collective-permute-start(bf16[64,2048]{1,0:T(8,128)(2,1)S(1)} %get-tuple-element.83), channel_id=1, source_target_pairs={{0,4},{4,0},{8,12},{12,8},{16,20},{20,16},{24,28},{28,24},{1,5},{5... | collective-permute-start | bytes 786440 | tf_op jit(solution)/shard_map/ppermute | solution.py:93
  32.2 3.1 %collective-permute-start.10 = (bf16[64,2048]{1,0:T(8,128)(2,1)S(1)}, bf16[64,2048]{1,0:T(8,128)(2,1)S(1)}, u32[]{:S(2)}, u32[]{:S(2)}) collective-permute-start(bf16[64,2048]{1,0:T(8,128)(2,1)S(1)} %get-tuple-element.86), channel_id=1, source_target_pairs={{0,4},{4,0},{8,12},{12,8},{16,20},{20,16},{24,28},{28,24},{1,5},{5... | collective-permute-start | bytes 786440 | tf_op jit(solution)/shard_map/ppermute | solution.py:93
  32.8 4.7 %collective-permute-start.7 = (bf16[128,2176]{1,0:T(8,128)(2,1)S(1)}, bf16[128,2176]{1,0:T(8,128)(2,1)S(1)}, u32[]{:S(2)}, u32[]{:S(2)}) collective-permute-start(bf16[128,2176]{1,0:T(8,128)(2,1)S(1)} %pad_maximum_fusion), channel_id=1, source_target_pairs={{0,4},{4,0},{8,12},{12,8},{16,20},{20,16},{24,28},{28,24},{1,5},{5... | collective-permute-start | bytes 1671176 | tf_op jit(solution)/shard_map/ppermute | solution.py:93
  33.7 15.2 %copy-start.1 = (bf16[64,2048]{1,0:T(8,128)(2,1)}, bf16[64,2048]{1,0:T(8,128)(2,1)S(1)}, u32[]{:S(2)}) copy-start(bf16[64,2048]{1,0:T(8,128)(2,1)S(1)} %collective-permute-done.8) | copy-start | bytes 786436
  33.8 15.1 %collective-permute-start.9 = (bf16[32,2048]{1,0:T(8,128)(2,1)S(1)}, bf16[32,2048]{1,0:T(8,128)(2,1)S(1)}, u32[]{:S(2)}, u32[]{:S(2)}) collective-permute-start(bf16[32,2048]{1,0:T(8,128)(2,1)S(1)} %add_convert_fusion.3), channel_id=1, source_target_pairs={{0,1},{1,0},{2,3},{3,2},{4,6},{5,7},{6,4},{7,5},{8,9},{9,8},{10,11... | collective-permute-start | bytes 393224 | tf_op jit(solution)/shard_map/ppermute | solution.py:90
  35.4 13.5 %collective-permute-start.12 = (bf16[32,2048]{1,0:T(8,128)(2,1)S(1)}, bf16[32,2048]{1,0:T(8,128)(2,1)S(1)}, u32[]{:S(2)}, u32[]{:S(2)}) collective-permute-start(bf16[32,2048]{1,0:T(8,128)(2,1)S(1)} %get-tuple-element.109), channel_id=1, source_target_pairs={{0,3},{1,2},{2,1},{3,0},{4,7},{5,6},{6,5},{7,4},{8,11},{9,10},{10,... | collective-permute-start | bytes 393224 | tf_op jit(solution)/shard_map/ppermute | solution.py:90
  36.7 12.3 %collective-permute-start.11 = (bf16[32,2048]{1,0:T(8,128)(2,1)S(1)}, bf16[32,2048]{1,0:T(8,128)(2,1)S(1)}, u32[]{:S(2)}, u32[]{:S(2)}) collective-permute-start(bf16[32,2048]{1,0:T(8,128)(2,1)S(1)} %get-tuple-element.110), channel_id=1, source_target_pairs={{0,2},{1,3},{2,0},{3,1},{4,5},{5,4},{6,7},{7,6},{8,10},{9,11},{10,... | collective-permute-start | bytes 393224 | tf_op jit(solution)/shard_map/ppermute | solution.py:90
  48.9 9.9 %slice-start = ((bf16[64,2048]{1,0:T(8,128)(2,1)}), bf16[32,2048]{1,0:T(8,128)(2,1)S(1)}, s32[]{:S(2)}) async-start(bf16[64,2048]{1,0:T(8,128)(2,1)} %copy-done.1), calls=%async_computation | async-start | bytes 262144 | tf_op jit(solution)/shard_map/slice | solution.py:491
  48.9 1.6 %collective-permute-start.13 = (bf16[128,1024]{1,0:T(8,128)(2,1)S(1)}, bf16[128,1024]{1,0:T(8,128)(2,1)S(1)}, u32[]{:S(2)}, u32[]{:S(2)}) collective-permute-start(bf16[128,1024]{1,0:T(8,128)(2,1)S(1)} %get-tuple-element.94), channel_id=1, source_target_pairs={{0,4},{4,0},{8,12},{12,8},{16,20},{20,16},{24,28},{28,24},{1,5},{5... | collective-permute-start | bytes 786440 | tf_op jit(solution)/shard_map/ppermute | solution.py:93
  49.0 3.1 %collective-permute-start.16 = (bf16[128,1152]{1,0:T(8,128)(2,1)S(1)}, bf16[128,1152]{1,0:T(8,128)(2,1)S(1)}, u32[]{:S(2)}, u32[]{:S(2)}) collective-permute-start(bf16[128,1152]{1,0:T(8,128)(2,1)S(1)} %get-tuple-element.99), channel_id=1, source_target_pairs={{0,4},{4,0},{8,12},{12,8},{16,20},{20,16},{24,28},{28,24},{1,5},{5... | collective-permute-start | bytes 884744 | tf_op jit(solution)/shard_map/ppermute | solution.py:93
  50.6 5.0 %collective-permute-start.14 = (bf16[64,1024]{1,0:T(8,128)(2,1)S(1)}, bf16[64,1024]{1,0:T(8,128)(2,1)S(1)}, u32[]{:S(2)}, u32[]{:S(2)}) collective-permute-start(bf16[64,1024]{1,0:T(8,128)(2,1)S(1)} %pad_maximum_fusion.2), channel_id=1, source_target_pairs={{0,1},{1,0},{2,3},{3,2},{4,6},{5,7},{6,4},{7,5},{8,9},{9,8},{10,11... | collective-permute-start | bytes 393224 | tf_op jit(solution)/shard_map/ppermute | solution.py:90
  52.2 9.7 %copy-start = (s32[32,6]{0,1:T(8,128)S(1)}, s32[32,6]{0,1:T(8,128)}, u32[]{:S(2)}) copy-start(s32[32,6]{0,1:T(8,128)} %param.15) | copy-start | bytes 2308
  52.2 5.2 %collective-permute-start.17 = (bf16[64,1152]{1,0:T(8,128)(2,1)S(1)}, bf16[64,1152]{1,0:T(8,128)(2,1)S(1)}, u32[]{:S(2)}, u32[]{:S(2)}) collective-permute-start(bf16[64,1152]{1,0:T(8,128)(2,1)S(1)} %pad_maximum_fusion.1), channel_id=1, source_target_pairs={{0,1},{1,0},{2,3},{3,2},{4,6},{5,7},{6,4},{7,5},{8,9},{9,8},{10,11... | collective-permute-start | bytes 442376 | tf_op jit(solution)/shard_map/ppermute | solution.py:90
  55.7 4.3 %collective-permute-start.15 = (bf16[32,1024]{1,0:T(8,128)(2,1)S(1)}, bf16[32,1024]{1,0:T(8,128)(2,1)S(1)}, u32[]{:S(2)}, u32[]{:S(2)}) collective-permute-start(bf16[32,1024]{1,0:T(8,128)(2,1)S(1)} %add_convert_fusion.7), channel_id=1, source_target_pairs={{0,2},{1,3},{2,0},{3,1},{4,5},{5,4},{6,7},{7,6},{8,10},{9,11},{10,... | collective-permute-start | bytes 196616 | tf_op jit(solution)/shard_map/ppermute | solution.py:90
  57.5 4.4 %collective-permute-start.18 = (bf16[32,1152]{1,0:T(8,128)(2,1)S(1)}, bf16[32,1152]{1,0:T(8,128)(2,1)S(1)}, u32[]{:S(2)}, u32[]{:S(2)}) collective-permute-start(bf16[32,1152]{1,0:T(8,128)(2,1)S(1)} %add_convert_fusion.4), channel_id=1, source_target_pairs={{0,2},{1,3},{2,0},{3,1},{4,5},{5,4},{6,7},{7,6},{8,10},{9,11},{10,... | collective-permute-start | bytes 221192 | tf_op jit(solution)/shard_map/ppermute | solution.py:90

commit v12 on v8

--- a/solution.py
+++ b/solution.py
@@ -257,7 +257,7 @@
     return packed, saved, done
 
 
-def fetch_kernel(plan, w_hbm, after, w_ref, done_ref, sems):
+def fetch_kernel(plan, w_hbm, after, also_after, w_ref, done_ref, sems):
     copies = weight_copies(plan, w_hbm, weight_slots(plan, w_ref), sems)
     for copy in copies:
         copy.start()
@@ -266,14 +266,14 @@
         copy.wait()
 
 
-def fetch(plan, w, after):
+def fetch(plan, w, after, also_after):
     return pl.pallas_call(
         functools.partial(fetch_kernel, plan),
         out_shape=(
             pltpu.VMEM((plan.mine, plan.hidden, plan.width), BF16),
             jax.ShapeDtypeStruct((16, plan.sent), BF16),
         ),
-        in_specs=[hbm(), pl.BlockSpec(memory_space=pl.ANY)],
+        in_specs=[hbm()] + [pl.BlockSpec(memory_space=pl.ANY)] * 2,
         out_specs=(vmem(), vmem()),
         scratch_shapes=[pltpu.SemaphoreType.DMA((plan.mine,))],
         compiler_params=pltpu.CompilerParams(vmem_limit_bytes=MIB),
@@ -283,7 +283,7 @@
             transcendentals=0,
         ),
         name="fetch",
-    )(in_hbm(w), after)
+    )(in_hbm(w), after, also_after)
 
 
 def arrived(plan, blocks, first, x_s):
@@ -304,10 +304,11 @@
             self.copies[self.started].start()
             self.started += 1
 
-    def take(self):
+    def take(self, count):
         self.fill()
-        self.copies[self.taken].wait()
-        self.taken += 1
+        for _ in range(count):
+            self.copies[self.taken].wait()
+            self.taken += 1
         self.fill()
 
 
@@ -319,7 +320,7 @@
     downs = weight_slots(plan, kept_ref, down_s)
     copies = weight_copies(plan, up_hbm, weight_slots(plan, up_s), sems.at[0])
     copies += weight_copies(plan, down_hbm, downs, sems.at[1])
-    queue = Queue(copies, 3)
+    queue = Queue(copies, 4)
     queue.fill()
     table, factor = arrived(plan, blocks, first, x_s)
     n = plan.expert_rows
@@ -328,7 +329,8 @@
         gate_s[e] = dot_tb(x_s[part, :], gate_ref[e])
     up = None
     for e, part in enumerate(parts):
-        queue.take()
+        if e % 2 == 0:
+            queue.take(min(2, plan.mine - e))
         last, up = up, dot_tb(x_s[part, :], up_s[e])
         if e:
             gate = gate_s[e - 1]
@@ -336,7 +338,8 @@
     gate = gate_s[plan.mine - 1]
     hidden_s[plan.mine - 1] = (gate / (1.0 + jnp.exp(-gate)) * up).astype(BF16)
     for e, part in enumerate(parts):
-        queue.take()
+        if e % 2 == 0:
+            queue.take(min(2, plan.mine - e))
         out = dot(hidden_s[e], downs[e][...])
         y_s[part, :] = (out * factor[part]).astype(BF16)
     put_rows(outs, slice(None), dot_ta(table, y_s[...]).astype(BF16))
@@ -359,7 +362,7 @@
     downs = weight_slots(plan, kept_ref, down_s)
     copies = weight_copies(plan, down_hbm, downs, sems.at[0])[plan.kept :]
     copies += weight_copies(plan, up_hbm, weight_slots(plan, up_s), sems.at[1])
-    queue = Queue(copies, 3)
+    queue = Queue(copies, 4)
     queue.fill()
     table, factor = arrived(plan, blocks, first, x_s)
     n, held = plan.expert_rows, plan.source_rows
@@ -389,14 +392,15 @@
 
     grad = None
     for e, part in enumerate(parts):
-        if e >= plan.kept:
-            queue.take()
+        if e == plan.kept:
+            queue.take(plan.mine - plan.kept)
         last, grad = grad, dot_tb(x_s[part, :], downs[e][...])
         if e:
             through_activation(e - 1, last)
     through_activation(plan.mine - 1, grad)
     for e, part in enumerate(parts):
-        queue.take()
+        if e % 2 == 0:
+            queue.take(min(2, plan.mine - e))
         result = dot(grads_s[0, e], gate_ref[e]) + dot(grads_s[1, e], up_s[e])
         y_s[part, :] = (result * factor[part]).astype(BF16)
     half, near = plan.half, outs[: len(outs) // 2]
@@ -569,17 +573,19 @@
     packed_back, saved, ready = prepare(
         plan, cotangent, routes_back, weights_back, saved_gate, saved_up, packed
     )
+    if plan.split > 1:
+        saved[1] = plan.over_pair(saved[1])
     gate_hbm, up_hbm = jnp.swapaxes(w_gate, 1, 2), jnp.swapaxes(w_up, 1, 2)
     if plan.paired and plan.owners > 1:
         blocks = [packed, plan.over_expert(packed, 1)]
-        gate, done = fetch(plan, gate_hbm, blocks[1])
+        gate, done = fetch(plan, gate_hbm, blocks[1], saved[-1])
         step = 2
         while step < plan.owners:
             blocks.append(plan.over_expert(jnp.concatenate(blocks) + ready[:1], step))
             step *= 2
     else:
         blocks = gather_group(plan, packed)
-        gate, done = fetch(plan, gate_hbm, packed)
+        gate, done = fetch(plan, gate_hbm, packed, saved[-1])
     if plan.split > 1:
         blocks.append(plan.over_pair(jnp.concatenate(blocks) + done[:1]))
     blocks_back = gather_group(plan, packed_back)
@@ -587,7 +593,6 @@
     parts, blocks_back = lax.optimization_barrier((parts, blocks_back))
     if plan.split > 1:
         blocks_back = blocks_back + [plan.over_pair(jnp.concatenate(blocks_back))]
-        saved[1] = plan.over_pair(saved[1])
     terms = scatter_group(plan, sum_pair(plan, parts))
     parts_back = backward(plan, blocks_back, saved, gate, kept, up_hbm, w_down)
     parts_back, terms = lax.optimization_barrier((parts_back, terms))

time: 63.2 us -> 63.2 us (level)
  no operation moved by 1% of the time
where the time goes in v12:
time: 63.2 us; the launch traced here: 63 us
  Pallas kernels  32.8 us (52%)
  starting transfers between devices  19.6 us (31%)
  waiting for transfers between devices  8.28 us (13%)
  other arithmetic  1.2 us (2%)
  between operations  1.03 us (2%)
    pallas_call x2, Pallas kernels, expert_call(): pl.pallas_call(kernel, out_shape=shapes, in_specs=[vmem()] * len(inputs)...  25 us
    ppermute x12, starting transfers between devices, over_expert(): return lax.ppermute(x, ('dp', 'expert'), pairs)  18.1 us
    ppermute x12, waiting for transfers between devices, over_expert(): return lax.ppermute(x, ('dp', 'expert'), pairs)  6.41 us
    pallas_call x1, Pallas kernels, fetch(): pl.pallas_call(functools.partial(fetch_kernel, plan), out_shape=(pltpu.VM...  4.4 us
    ppermute x7, waiting for transfers between devices, over_pair(): return lax.ppermute(x, 'dp', [(i, i ^ 1) for i in range(self.groups)])  1.87 us
    pallas_call x1, Pallas kernels, prepare(): pl.pallas_call(functools.partial(prepare_kernel, plan), out_shape=out_sha...  1.59 us
    ppermute x7, starting transfers between devices, over_pair(): return lax.ppermute(x, 'dp', [(i, i ^ 1) for i in range(self.groups)])  1.42 us
  transfers between devices with their start and end apart: 19, of which 7 were waited for; matrix products, arithmetic and copies ran while one was open for 2% of the time, Pallas kernels for 49%

profile of v12, /device:TPU:0, one launch (start us, length us, event | category | flops | bytes accessed | tf_op | source)
XLA Modules:
  0.0 63.0 jit_solution(4372593883659663429)
XLA Ops:
  0.6 1.1 %pack.1.after.refs_0_ = bf16[32,2176]{1,0:T(8,128)(2,1)S(1)} custom-call(bf16[32,2048]{1,0:T(8,128)(2,1)} %refs_0_.1, s32[6,32]{1,0:T(8,128)} %bitcast.24, f32[6,32]{1,0:T(8,128)} %bitcast.25), custom_call_target="tpu_custom_call" | custom-call | tf_op jit(solution)/shard_map/pack/pallas_call | solution.py:140
  1.7 3.0 %collective-permute-start = (bf16[32,2176]{1,0:T(8,128)(2,1)S(1)}, bf16[32,2176]{1,0:T(8,128)(2,1)S(1)}, u32[]{:S(2)}, u32[]{:S(2)}) collective-permute-start(bf16[32,2176]{1,0:T(8,128)(2,1)S(1)} %pack.1.after.refs_0_), channel_id=1, source_target_pairs={{1,0},{0,1},{3,2},{2,3},{6,4},{7,5},{4,6},{5,7},{9,8},{8,9},{11,10... | collective-permute-start | bytes 417800 | tf_op jit(solution)/shard_map/ppermute | solution.py:89
  4.7 1.6 %prepare.1 = (bf16[32,2176]{1,0:T(8,128)(2,1)S(1)}, bf16[16,2176]{1,0:T(8,128)(2,1)S(1)}, bf16[2,128,704]{2,1,0:T(8,128)(2,1)S(1)}, bf16[2,128,704]{2,1,0:T(8,128)(2,1)S(1)}) custom-call(bf16[32,2048]{1,0:T(8,128)(2,1)} %x_hbm.1, s32[6,32]{1,0:T(8,128)} %bitcast.17, f32[6,32]{1,0:T(8,128)} %bitcast.26, bf16[224,704]{1,0:T(8,128)(2,1)} %bitcast.22, ...), custom_call_target="tpu_custom_call" | custom-call | bytes 17825792 | tf_op jit(solution)/shard_map/prepare/pallas_call | solution.py:233
  6.4 1.3 %collective-permute-done.after.refs_1_ = bf16[32,2176]{1,0:T(8,128)(2,1)S(1)} collective-permute-done((bf16[32,2176]{1,0:T(8,128)(2,1)S(1)}, bf16[32,2176]{1,0:T(8,128)(2,1)S(1)}, u32[]{:S(2)}, u32[]{:S(2)}) %collective-permute-start) | collective-permute-done | bytes 139296 | tf_op jit(solution)/shard_map/ppermute | solution.py:89
  7.8 2.1 %collective-permute-start.1 = (bf16[64,2176]{1,0:T(8,128)(2,1)S(1)}, bf16[64,2176]{1,0:T(8,128)(2,1)S(1)}, u32[]{:S(2)}, u32[]{:S(2)}) collective-permute-start(bf16[64,2176]{1,0:T(8,128)(2,1)S(1)} %maximum_add_fusion.1), channel_id=1, source_target_pairs={{2,0},{3,1},{0,2},{1,3},{5,4},{4,5},{7,6},{6,7},{10,8},{11,9},{8,1... | collective-permute-start | bytes 835592 | tf_op jit(solution)/shard_map/ppermute | solution.py:89
  9.9 4.4 %fetch.1 = (bf16[4,704,2048]{2,1,0:T(8,128)(2,1)S(1)}, bf16[16,2176]{1,0:T(8,128)(2,1)S(1)}) custom-call(bf16[8,704,2048]{2,1,0:T(8,128)(2,1)} %bitcast.21, bf16[32,2176]{1,0:T(8,128)(2,1)S(1)} %collective-permute-done.after.refs_1_, bf16[2,128,704]{2,1,0:T(8,128)(2,1)S(1)} %collective-permute-done.2.also_after.refs_6_), custom_call_target="tpu_custom_call" | custom-call | bytes 23068672 | tf_op jit(solution)/shard_map/fetch/pallas_call | solution.py:270
  14.6 3.0 %collective-permute-start.6 = (bf16[32,2176]{1,0:T(8,128)(2,1)S(1)}, bf16[32,2176]{1,0:T(8,128)(2,1)S(1)}, u32[]{:S(2)}, u32[]{:S(2)}) collective-permute-start(bf16[32,2176]{1,0:T(8,128)(2,1)S(1)} %get-tuple-element.64.refs_0_), channel_id=1, source_target_pairs={{3,0},{2,1},{1,2},{0,3},{7,4},{6,5},{5,6},{4,7},{11,8},{10,9},{9,1... | collective-permute-start | bytes 417800 | tf_op jit(solution)/shard_map/ppermute | solution.py:89
  17.6 0.5 collective-permute-start.5
  18.3 13.1 %forward.1 = (bf16[32,2048]{1,0:T(8,128)(2,1)S(1)}, bf16[32,2048]{1,0:T(8,128)(2,1)S(1)}, bf16[32,2048]{1,0:T(8,128)(2,1)S(1)}, bf16[32,2048]{1,0:T(8,128)(2,1)S...) custom-call(bf16[32,2176]{1,0:T(8,128)(2,1)S(1)} %pack.1.after.refs_0_, ...), custom_call_target="tpu_custom_call" | custom-call | flops 2214592512 | bytes 23068672 | tf_op jit(solution)/shard_map/forward/pallas_call | solution.py:428
  31.5 0.5 collective-permute-start.10
  32.2 0.8 %collective-permute-done.8 = bf16[64,2048]{1,0:T(8,128)(2,1)S(1)} collective-permute-done((bf16[64,2048]{1,0:T(8,128)(2,1)S(1)}, bf16[64,2048]{1,0:T(8,128)(2,1)S(1)}, u32[]{:S(2)}, u32[]{:S(2)}) %collective-permute-start.8) | collective-permute-done | bytes 262176 | tf_op jit(solution)/shard_map/ppermute | solution.py:92
  33.0 2.0 %collective-permute-start.9 = (bf16[32,2048]{1,0:T(8,128)(2,1)S(1)}, bf16[32,2048]{1,0:T(8,128)(2,1)S(1)}, u32[]{:S(2)}, u32[]{:S(2)}) collective-permute-start(bf16[32,2048]{1,0:T(8,128)(2,1)S(1)} %add_convert_fusion.3), channel_id=1, source_target_pairs={{0,1},{1,0},{2,3},{3,2},{4,6},{5,7},{6,4},{7,5},{8,9},{9,8},{10,11... | collective-permute-start | bytes 393224 | tf_op jit(solution)/shard_map/ppermute | solution.py:89
  35.1 1.6 %collective-permute-start.12 = (bf16[32,2048]{1,0:T(8,128)(2,1)S(1)}, bf16[32,2048]{1,0:T(8,128)(2,1)S(1)}, u32[]{:S(2)}, u32[]{:S(2)}) collective-permute-start(bf16[32,2048]{1,0:T(8,128)(2,1)S(1)} %get-tuple-element.107), channel_id=1, source_target_pairs={{0,3},{1,2},{2,1},{3,0},{4,7},{5,6},{6,5},{7,4},{8,11},{9,10},{10,... | collective-permute-start | bytes 393224 | tf_op jit(solution)/shard_map/ppermute | solution.py:89
  36.9 11.9 %backward.1 = (bf16[32,1024]{1,0:T(8,128)(2,1)S(1)}, bf16[32,1024]{1,0:T(8,128)(2,1)S(1)}, bf16[32,1024]{1,0:T(8,128)(2,1)S(1)}, bf16[32,1024]{1,0:T(8,128)(2,1)...) custom-call(bf16[32,2176]{1,0:T(8,128)(2,1)S(1)} %get-tuple-element., ...), custom_call_target="tpu_custom_call" | custom-call | flops 2214592512 | bytes 23068672 | tf_op jit(solution)/shard_map/backward/pallas_call | solution.py:428
  48.9 0.5 collective-permute-start.16
  49.4 1.0 %collective-permute-done.13 = bf16[128,1024]{1,0:T(8,128)(2,1)S(1)} collective-permute-done((bf16[128,1024]{1,0:T(8,128)(2,1)S(1)}, bf16[128,1024]{1,0:T(8,128)(2,1)S(1)}, u32[]{:S(2)}, u32[]{:S(2)}) %collective-permute-start.13) | collective-permute-done | bytes 262176 | tf_op jit(solution)/shard_map/ppermute | solution.py:92
  50.5 1.8 %collective-permute-start.14 = (bf16[64,1024]{1,0:T(8,128)(2,1)S(1)}, bf16[64,1024]{1,0:T(8,128)(2,1)S(1)}, u32[]{:S(2)}, u32[]{:S(2)}) collective-permute-start(bf16[64,1024]{1,0:T(8,128)(2,1)S(1)} %pad_maximum_fusion.2), channel_id=1, source_target_pairs={{0,1},{1,0},{2,3},{3,2},{4,6},{5,7},{6,4},{7,5},{8,9},{9,8},{10,11... | collective-permute-start | bytes 393224 | tf_op jit(solution)/shard_map/ppermute | solution.py:89
  52.4 0.4 collective-permute-start.17
  52.7 2.8 %collective-permute-done.14 = bf16[64,1024]{1,0:T(8,128)(2,1)S(1)} collective-permute-done((bf16[64,1024]{1,0:T(8,128)(2,1)S(1)}, bf16[64,1024]{1,0:T(8,128)(2,1)S(1)}, u32[]{:S(2)}, u32[]{:S(2)}) %collective-permute-start.14) | collective-permute-done | bytes 131104 | tf_op jit(solution)/shard_map/ppermute | solution.py:89
  55.5 1.9 %collective-permute-start.15 = (bf16[32,1024]{1,0:T(8,128)(2,1)S(1)}, bf16[32,1024]{1,0:T(8,128)(2,1)S(1)}, u32[]{:S(2)}, u32[]{:S(2)}) collective-permute-start(bf16[32,1024]{1,0:T(8,128)(2,1)S(1)} %add_convert_fusion.7), channel_id=1, source_target_pairs={{0,2},{1,3},{2,0},{3,1},{4,5},{5,4},{6,7},{7,6},{8,10},{9,11},{10,... | collective-permute-start | bytes 196616 | tf_op jit(solution)/shard_map/ppermute | solution.py:89
  57.6 1.6 %collective-permute-start.18 = (bf16[32,1152]{1,0:T(8,128)(2,1)S(1)}, bf16[32,1152]{1,0:T(8,128)(2,1)S(1)}, u32[]{:S(2)}, u32[]{:S(2)}) collective-permute-start(bf16[32,1152]{1,0:T(8,128)(2,1)S(1)} %add_convert_fusion.4), channel_id=1, source_target_pairs={{0,2},{1,3},{2,0},{3,1},{4,5},{5,4},{6,7},{7,6},{8,10},{9,11},{10,... | collective-permute-start | bytes 221192 | tf_op jit(solution)/shard_map/ppermute | solution.py:89
  59.2 0.7 %add_convert_fusion = bf16[32,2048]{1,0:T(8,128)(2,1)} fusion(bf16[32,2048]{1,0:T(8,128)(2,1)S(1)} %collective-permute-done.12, bf16[32,2048]{1,0:T(8,128)(2,1)S(1)} %collective-permute-done.11, bf16[32,2048]{1,0:T(8,128)(2,1)S(1)} %collective-permute-done.9, bf16[32,2048]{1,0:T(8,128)(2,1)S(1)} %slice-done, bf16[32,2048]{1,0:T(8,128)(2,1)S(1)} %get-tuple-element.86), kind=kLoop, calls=%fused_computation.3 | loop fusion | flops 655360 | bytes 786432 | tf_op jit(solution)/shard_map/convert_element_type | solution.py:599
  60.0 2.0 %collective-permute-done.18.refs_7_ = bf16[32,1152]{1,0:T(8,128)(2,1)S(1)} collective-permute-done((bf16[32,1152]{1,0:T(8,128)(2,1)S(1)}, bf16[32,1152]{1,0:T(8,128)(2,1)S(1)}, u32[]{:S(2)}, u32[]{:S(2)}) %collective-permute-start.18) | collective-permute-done | bytes 73760 | tf_op jit(solution)/shard_map/ppermute | solution.py:89
  62.0 0.8 %finish.1 = (bf16[32,2048]{1,0:T(8,128)(2,1)}, f32[6,32]{1,0:T(8,128)}) custom-call(bf16[32,1024]{1,0:T(8,128)(2,1)S(1)} %get-tuple-element.91.refs_0_, bf16[32,1024]{1,0:T(8,128)(2,1)S(1)} %slice.76.refs_1_, bf16[32,1024]{1,0:T(8,128)(2,1)S(1)} %slice.79.refs_2_, bf16[32,1024]{1,0:T(8,128)(2,1)S(1)} %collective-permute-done.15.refs_3_, ...), custom_call_target="tpu_custom_call" | custom-call | tf_op jit(solution)/shard_map/finish/pallas_call | solution.py:539
  (44 shorter events, 1.7 us)
Async XLA Ops:
  1.7 6.0 %collective-permute-start = (bf16[32,2176]{1,0:T(8,128)(2,1)S(1)}, bf16[32,2176]{1,0:T(8,128)(2,1)S(1)}, u32[]{:S(2)}, u32[]{:S(2)}) collective-permute-start(bf16[32,2176]{1,0:T(8,128)(2,1)S(1)} %pack.1.after.refs_0_), channel_id=1, source_target_pairs={{1,0},{0,1},{3,2},{2,3},{6,4},{7,5},{4,6},{5,7},{9,8},{8,9},{11,10... | collective-permute-start | bytes 417800 | tf_op jit(solution)/shard_map/ppermute | solution.py:89
  6.3 3.6 %collective-permute-start.2 = (bf16[2,128,704]{2,1,0:T(8,128)(2,1)S(1)}, bf16[2,128,704]{2,1,0:T(8,128)(2,1)S(1)}, u32[]{:S(2)}, u32[]{:S(2)}) collective-permute-start(bf16[2,128,704]{2,1,0:T(8,128)(2,1)S(1)} %get-tuple-element.54), channel_id=1, source_target_pairs={{0,4},{4,0},{8,12},{12,8},{16,20},{20,16},{24,28},{28,24},{1,5},{5... | collective-permute-start | bytes 1081352 | tf_op jit(solution)/shard_map/ppermute | solution.py:92
  7.8 6.6 %collective-permute-start.1 = (bf16[64,2176]{1,0:T(8,128)(2,1)S(1)}, bf16[64,2176]{1,0:T(8,128)(2,1)S(1)}, u32[]{:S(2)}, u32[]{:S(2)}) collective-permute-start(bf16[64,2176]{1,0:T(8,128)(2,1)S(1)} %maximum_add_fusion.1), channel_id=1, source_target_pairs={{2,0},{3,1},{0,2},{1,3},{5,4},{4,5},{7,6},{6,7},{10,8},{11,9},{8,1... | collective-permute-start | bytes 835592 | tf_op jit(solution)/shard_map/ppermute | solution.py:89
  14.5 3.7 %collective-permute-start.3 = (bf16[128,2176]{1,0:T(8,128)(2,1)S(1)}, bf16[128,2176]{1,0:T(8,128)(2,1)S(1)}, u32[]{:S(2)}, u32[]{:S(2)}) collective-permute-start(bf16[128,2176]{1,0:T(8,128)(2,1)S(1)} %maximum_add_fusion), channel_id=1, source_target_pairs={{0,4},{4,0},{8,12},{12,8},{16,20},{20,16},{24,28},{28,24},{1,5},{5... | collective-permute-start | bytes 1671176 | tf_op jit(solution)/shard_map/ppermute | solution.py:92
  14.6 16.8 %collective-permute-start.6 = (bf16[32,2176]{1,0:T(8,128)(2,1)S(1)}, bf16[32,2176]{1,0:T(8,128)(2,1)S(1)}, u32[]{:S(2)}, u32[]{:S(2)}) collective-permute-start(bf16[32,2176]{1,0:T(8,128)(2,1)S(1)} %get-tuple-element.64.refs_0_), channel_id=1, source_target_pairs={{3,0},{2,1},{1,2},{0,3},{7,4},{6,5},{5,6},{4,7},{11,8},{10,9},{9,1... | collective-permute-start | bytes 417800 | tf_op jit(solution)/shard_map/ppermute | solution.py:89
  17.6 13.8 %collective-permute-start.5 = (bf16[32,2176]{1,0:T(8,128)(2,1)S(1)}, bf16[32,2176]{1,0:T(8,128)(2,1)S(1)}, u32[]{:S(2)}, u32[]{:S(2)}) collective-permute-start(bf16[32,2176]{1,0:T(8,128)(2,1)S(1)} %get-tuple-element.64.refs_0_), channel_id=1, source_target_pairs={{2,0},{3,1},{0,2},{1,3},{5,4},{4,5},{7,6},{6,7},{10,8},{11,9},{8,1... | collective-permute-start | bytes 417800 | tf_op jit(solution)/shard_map/ppermute | solution.py:89
  18.1 13.3 %collective-permute-start.4 = (bf16[32,2176]{1,0:T(8,128)(2,1)S(1)}, bf16[32,2176]{1,0:T(8,128)(2,1)S(1)}, u32[]{:S(2)}, u32[]{:S(2)}) collective-permute-start(bf16[32,2176]{1,0:T(8,128)(2,1)S(1)} %get-tuple-element.64.refs_0_), channel_id=1, source_target_pairs={{1,0},{0,1},{3,2},{2,3},{6,4},{7,5},{4,6},{5,7},{9,8},{8,9},{11,10... | collective-permute-start | bytes 417800 | tf_op jit(solution)/shard_map/ppermute | solution.py:89
  31.4 1.6 %collective-permute-start.8 = (bf16[64,2048]{1,0:T(8,128)(2,1)S(1)}, bf16[64,2048]{1,0:T(8,128)(2,1)S(1)}, u32[]{:S(2)}, u32[]{:S(2)}) collective-permute-start(bf16[64,2048]{1,0:T(8,128)(2,1)S(1)} %get-tuple-element.81), channel_id=1, source_target_pairs={{0,4},{4,0},{8,12},{12,8},{16,20},{20,16},{24,28},{28,24},{1,5},{5... | collective-permute-start | bytes 786440 | tf_op jit(solution)/shard_map/ppermute | solution.py:92
  31.5 3.5 %collective-permute-start.10 = (bf16[64,2048]{1,0:T(8,128)(2,1)S(1)}, bf16[64,2048]{1,0:T(8,128)(2,1)S(1)}, u32[]{:S(2)}, u32[]{:S(2)}) collective-permute-start(bf16[64,2048]{1,0:T(8,128)(2,1)S(1)} %get-tuple-element.84), channel_id=1, source_target_pairs={{0,4},{4,0},{8,12},{12,8},{16,20},{20,16},{24,28},{28,24},{1,5},{5... | collective-permute-start | bytes 786440 | tf_op jit(solution)/shard_map/ppermute | solution.py:92
  32.0 4.8 %collective-permute-start.7 = (bf16[128,2176]{1,0:T(8,128)(2,1)S(1)}, bf16[128,2176]{1,0:T(8,128)(2,1)S(1)}, u32[]{:S(2)}, u32[]{:S(2)}) collective-permute-start(bf16[128,2176]{1,0:T(8,128)(2,1)S(1)} %pad_maximum_fusion), channel_id=1, source_target_pairs={{0,4},{4,0},{8,12},{12,8},{16,20},{20,16},{24,28},{28,24},{1,5},{5... | collective-permute-start | bytes 1671176 | tf_op jit(solution)/shard_map/ppermute | solution.py:92
  33.0 15.8 %copy-start.1 = (bf16[64,2048]{1,0:T(8,128)(2,1)}, bf16[64,2048]{1,0:T(8,128)(2,1)S(1)}, u32[]{:S(2)}) copy-start(bf16[64,2048]{1,0:T(8,128)(2,1)S(1)} %collective-permute-done.8) | copy-start | bytes 786436
  33.0 15.7 %collective-permute-start.9 = (bf16[32,2048]{1,0:T(8,128)(2,1)S(1)}, bf16[32,2048]{1,0:T(8,128)(2,1)S(1)}, u32[]{:S(2)}, u32[]{:S(2)}) collective-permute-start(bf16[32,2048]{1,0:T(8,128)(2,1)S(1)} %add_convert_fusion.3), channel_id=1, source_target_pairs={{0,1},{1,0},{2,3},{3,2},{4,6},{5,7},{6,4},{7,5},{8,9},{9,8},{10,11... | collective-permute-start | bytes 393224 | tf_op jit(solution)/shard_map/ppermute | solution.py:89
  35.1 13.7 %collective-permute-start.12 = (bf16[32,2048]{1,0:T(8,128)(2,1)S(1)}, bf16[32,2048]{1,0:T(8,128)(2,1)S(1)}, u32[]{:S(2)}, u32[]{:S(2)}) collective-permute-start(bf16[32,2048]{1,0:T(8,128)(2,1)S(1)} %get-tuple-element.107), channel_id=1, source_target_pairs={{0,3},{1,2},{2,1},{3,0},{4,7},{5,6},{6,5},{7,4},{8,11},{9,10},{10,... | collective-permute-start | bytes 393224 | tf_op jit(solution)/shard_map/ppermute | solution.py:89
  36.6 12.2 %collective-permute-start.11 = (bf16[32,2048]{1,0:T(8,128)(2,1)S(1)}, bf16[32,2048]{1,0:T(8,128)(2,1)S(1)}, u32[]{:S(2)}, u32[]{:S(2)}) collective-permute-start(bf16[32,2048]{1,0:T(8,128)(2,1)S(1)} %get-tuple-element.108), channel_id=1, source_target_pairs={{0,2},{1,3},{2,0},{3,1},{4,5},{5,4},{6,7},{7,6},{8,10},{9,11},{10,... | collective-permute-start | bytes 393224 | tf_op jit(solution)/shard_map/ppermute | solution.py:89
  48.8 10.4 %slice-start = ((bf16[64,2048]{1,0:T(8,128)(2,1)}), bf16[32,2048]{1,0:T(8,128)(2,1)S(1)}, s32[]{:S(2)}) async-start(bf16[64,2048]{1,0:T(8,128)(2,1)} %copy-done.1), calls=%async_computation | async-start | bytes 262144 | tf_op jit(solution)/shard_map/slice | solution.py:485
  48.8 1.6 %collective-permute-start.13 = (bf16[128,1024]{1,0:T(8,128)(2,1)S(1)}, bf16[128,1024]{1,0:T(8,128)(2,1)S(1)}, u32[]{:S(2)}, u32[]{:S(2)}) collective-permute-start(bf16[128,1024]{1,0:T(8,128)(2,1)S(1)} %get-tuple-element.92), channel_id=1, source_target_pairs={{0,4},{4,0},{8,12},{12,8},{16,20},{20,16},{24,28},{28,24},{1,5},{5... | collective-permute-start | bytes 786440 | tf_op jit(solution)/shard_map/ppermute | solution.py:92
  48.9 3.4 %collective-permute-start.16 = (bf16[128,1152]{1,0:T(8,128)(2,1)S(1)}, bf16[128,1152]{1,0:T(8,128)(2,1)S(1)}, u32[]{:S(2)}, u32[]{:S(2)}) collective-permute-start(bf16[128,1152]{1,0:T(8,128)(2,1)S(1)} %get-tuple-element.97), channel_id=1, source_target_pairs={{0,4},{4,0},{8,12},{12,8},{16,20},{20,16},{24,28},{28,24},{1,5},{5... | collective-permute-start | bytes 884744 | tf_op jit(solution)/shard_map/ppermute | solution.py:92
  50.5 5.0 %collective-permute-start.14 = (bf16[64,1024]{1,0:T(8,128)(2,1)S(1)}, bf16[64,1024]{1,0:T(8,128)(2,1)S(1)}, u32[]{:S(2)}, u32[]{:S(2)}) collective-permute-start(bf16[64,1024]{1,0:T(8,128)(2,1)S(1)} %pad_maximum_fusion.2), channel_id=1, source_target_pairs={{0,1},{1,0},{2,3},{3,2},{4,6},{5,7},{6,4},{7,5},{8,9},{9,8},{10,11... | collective-permute-start | bytes 393224 | tf_op jit(solution)/shard_map/ppermute | solution.py:89
  52.3 9.7 %copy-start = (s32[32,6]{0,1:T(8,128)S(1)}, s32[32,6]{0,1:T(8,128)}, u32[]{:S(2)}) copy-start(s32[32,6]{0,1:T(8,128)} %param.15) | copy-start | bytes 2308
  52.4 5.2 %collective-permute-start.17 = (bf16[64,1152]{1,0:T(8,128)(2,1)S(1)}, bf16[64,1152]{1,0:T(8,128)(2,1)S(1)}, u32[]{:S(2)}, u32[]{:S(2)}) collective-permute-start(bf16[64,1152]{1,0:T(8,128)(2,1)S(1)} %pad_maximum_fusion.1), channel_id=1, source_target_pairs={{0,1},{1,0},{2,3},{3,2},{4,6},{5,7},{6,4},{7,5},{8,9},{9,8},{10,11... | collective-permute-start | bytes 442376 | tf_op jit(solution)/shard_map/ppermute | solution.py:89
  55.5 4.5 %collective-permute-start.15 = (bf16[32,1024]{1,0:T(8,128)(2,1)S(1)}, bf16[32,1024]{1,0:T(8,128)(2,1)S(1)}, u32[]{:S(2)}, u32[]{:S(2)}) collective-permute-start(bf16[32,1024]{1,0:T(8,128)(2,1)S(1)} %add_convert_fusion.7), channel_id=1, source_target_pairs={{0,2},{1,3},{2,0},{3,1},{4,5},{5,4},{6,7},{7,6},{8,10},{9,11},{10,... | collective-permute-start | bytes 196616 | tf_op jit(solution)/shard_map/ppermute | solution.py:89
  57.6 4.4 %collective-permute-start.18 = (bf16[32,1152]{1,0:T(8,128)(2,1)S(1)}, bf16[32,1152]{1,0:T(8,128)(2,1)S(1)}, u32[]{:S(2)}, u32[]{:S(2)}) collective-permute-start(bf16[32,1152]{1,0:T(8,128)(2,1)S(1)} %add_convert_fusion.4), channel_id=1, source_target_pairs={{0,2},{1,3},{2,0},{3,1},{4,5},{5,4},{6,7},{7,6},{8,10},{9,11},{10,... | collective-permute-start | bytes 221192 | tf_op jit(solution)/shard_map/ppermute | solution.py:89

commit v13 on v12

--- a/solution.py
+++ b/solution.py
@@ -496,19 +496,24 @@
     return own[0] + [plan.over_expert(x, d, True) for d, x in enumerate(sent, 1)]
 
 
-def scatter_steps(plan, owns):
-    if not plan.paired:
-        return [scatter_group(plan, own) for own in owns]
-    step = 1
-    while step < plan.owners:
-        away = [d for d in range(0, plan.owners, step) if d & step]
-        for own in owns:
-            sent = jnp.concatenate([total(own[d]).astype(BF16) for d in away])
-            back = plan.over_expert(sent, step, True)
-            for i, d in enumerate(away):
-                own[d ^ step].append(back[i * plan.count : (i + 1) * plan.count])
-        step *= 2
-    return [own[0] for own in owns]
+def away(plan, step):
+    return [d for d in range(0, plan.owners, step) if d & step]
+
+
+def send_step(plan, own, step):
+    sent = [total(own[d]).astype(BF16) for d in away(plan, step)]
+    return plan.over_expert(jnp.concatenate(sent), step, True)
+
+
+def take_step(plan, own, step, back):
+    kept = [list(terms) for terms in own]
+    for i, d in enumerate(away(plan, step)):
+        kept[d ^ step].append(back[i * plan.count : (i + 1) * plan.count])
+    return kept
+
+
+def exchange(plan, own, step):
+    return take_step(plan, own, step, send_step(plan, own, step))
 
 
 def finish_kernel(plan, count, *refs):
@@ -593,12 +598,27 @@
     parts, blocks_back = lax.optimization_barrier((parts, blocks_back))
     if plan.split > 1:
         blocks_back = blocks_back + [plan.over_pair(jnp.concatenate(blocks_back))]
-    terms = scatter_group(plan, sum_pair(plan, parts))
+    own = sum_pair(plan, parts)
+    steps = [1 << i for i in range(plan.owners.bit_length() - 1)] if plan.paired else []
+    back = send_step(plan, own, 1) if steps else scatter_group(plan, own)
     parts_back = backward(plan, blocks_back, saved, gate, kept, up_hbm, w_down)
-    parts_back, terms = lax.optimization_barrier((parts_back, terms))
-    mixed = total(terms).astype(BF16)
-    near, far = scatter_steps(plan, [sum_pair(plan, parts) for parts in parts_back])
-    input_grad, weight_grad = finish_back(plan, near + far, routes_back)
+    parts_back, back = lax.optimization_barrier((parts_back, back))
+    near, far = [sum_pair(plan, half) for half in parts_back]
+    if steps:
+        own = take_step(plan, own, 1, back)
+        for step in steps[1:-1]:
+            own = exchange(plan, own, step)
+        back = send_step(plan, own, steps[-1])
+        near_back, far_back = send_step(plan, near, 1), send_step(plan, far, 1)
+        near_back, back = lax.optimization_barrier((near_back, back))
+        own = take_step(plan, own, steps[-1], back)
+        near, far = take_step(plan, near, 1, near_back), take_step(plan, far, 1, far_back)
+        for step in steps[1:]:
+            near, far = exchange(plan, near, step), exchange(plan, far, step)
+    else:
+        own, near, far = [back], [scatter_group(plan, near)], [scatter_group(plan, far)]
+    mixed = total(own[0]).astype(BF16)
+    input_grad, weight_grad = finish_back(plan, near[0] + far[0], routes_back)
     return (mixed, input_grad, weight_grad)
 
 

time: 63.2 us -> 61.5 us (0.973)
  starting transfers between devices: 19.6 us -> 17.7 us
    ppermute x12 -> x11, starting transfers between devices: 18.1 us -> 16.8 us  [over_expert(): return lax.ppermute(x, ('dp', 'expert'), pairs)]
    ppermute x12 -> x11, waiting for transfers between devices: 6.41 us -> 6.67 us  [over_expert(): return lax.ppermute(x, ('dp', 'expert'), pairs)]
  transfers between devices with their start and end apart: 19 -> 18, of which waited for: 7 -> 10; matrix products, arithmetic and copies ran while one was open for 2% -> 2% of each run, Pallas kernels for 49% -> 50%
where the time goes in v13:
time: 61.5 us; the launch traced here: 61.3 us
  Pallas kernels  32.8 us (53%)
  starting transfers between devices  17.7 us (29%)
  waiting for transfers between devices  8.44 us (14%)
  other arithmetic  1.22 us (2%)
  between operations  0.98 us (2%)
    pallas_call x2, Pallas kernels, expert_call(): pl.pallas_call(kernel, out_shape=shapes, in_specs=[vmem()] * len(inputs)...  25 us
    ppermute x11, starting transfers between devices, over_expert(): return lax.ppermute(x, ('dp', 'expert'), pairs)  16.8 us
    ppermute x11, waiting for transfers between devices, over_expert(): return lax.ppermute(x, ('dp', 'expert'), pairs)  6.67 us
    pallas_call x1, Pallas kernels, fetch(): pl.pallas_call(functools.partial(fetch_kernel, plan), out_shape=(pltpu.VM...  4.4 us
    ppermute x7, waiting for transfers between devices, over_pair(): return lax.ppermute(x, 'dp', [(i, i ^ 1) for i in range(self.groups)])  1.76 us
    pallas_call x1, Pallas kernels, prepare(): pl.pallas_call(functools.partial(prepare_kernel, plan), out_shape=out_sha...  1.59 us
  transfers between devices with their start and end apart: 18, of which 10 were waited for; matrix products, arithmetic and copies ran while one was open for 2% of the time, Pallas kernels for 50%

profile of v13, /device:TPU:0, one launch (start us, length us, event | category | flops | bytes accessed | tf_op | source)
XLA Modules:
  0.0 61.3 jit_solution(15514029627640824007)
XLA Ops:
  0.6 1.1 %pack.1.after.refs_0_ = bf16[32,2176]{1,0:T(8,128)(2,1)S(1)} custom-call(bf16[32,2048]{1,0:T(8,128)(2,1)} %refs_0_.1, s32[6,32]{1,0:T(8,128)} %bitcast.24, f32[6,32]{1,0:T(8,128)} %bitcast.25), custom_call_target="tpu_custom_call" | custom-call | tf_op jit(solution)/shard_map/pack/pallas_call | solution.py:140
  1.7 3.0 %collective-permute-start = (bf16[32,2176]{1,0:T(8,128)(2,1)S(1)}, bf16[32,2176]{1,0:T(8,128)(2,1)S(1)}, u32[]{:S(2)}, u32[]{:S(2)}) collective-permute-start(bf16[32,2176]{1,0:T(8,128)(2,1)S(1)} %pack.1.after.refs_0_), channel_id=1, source_target_pairs={{1,0},{0,1},{3,2},{2,3},{6,4},{7,5},{4,6},{5,7},{9,8},{8,9},{11,10... | collective-permute-start | bytes 417800 | tf_op jit(solution)/shard_map/ppermute | solution.py:89
  4.7 1.6 %prepare.1 = (bf16[32,2176]{1,0:T(8,128)(2,1)S(1)}, bf16[16,2176]{1,0:T(8,128)(2,1)S(1)}, bf16[2,128,704]{2,1,0:T(8,128)(2,1)S(1)}, bf16[2,128,704]{2,1,0:T(8,128)(2,1)S(1)}) custom-call(bf16[32,2048]{1,0:T(8,128)(2,1)} %x_hbm.1, s32[6,32]{1,0:T(8,128)} %bitcast.17, f32[6,32]{1,0:T(8,128)} %bitcast.26, bf16[224,704]{1,0:T(8,128)(2,1)} %bitcast.22, ...), custom_call_target="tpu_custom_call" | custom-call | bytes 17825792 | tf_op jit(solution)/shard_map/prepare/pallas_call | solution.py:233
  6.4 1.3 %collective-permute-done.after.refs_1_ = bf16[32,2176]{1,0:T(8,128)(2,1)S(1)} collective-permute-done((bf16[32,2176]{1,0:T(8,128)(2,1)S(1)}, bf16[32,2176]{1,0:T(8,128)(2,1)S(1)}, u32[]{:S(2)}, u32[]{:S(2)}) %collective-permute-start) | collective-permute-done | bytes 139296 | tf_op jit(solution)/shard_map/ppermute | solution.py:89
  7.8 2.1 %collective-permute-start.1 = (bf16[64,2176]{1,0:T(8,128)(2,1)S(1)}, bf16[64,2176]{1,0:T(8,128)(2,1)S(1)}, u32[]{:S(2)}, u32[]{:S(2)}) collective-permute-start(bf16[64,2176]{1,0:T(8,128)(2,1)S(1)} %maximum_add_fusion.1), channel_id=1, source_target_pairs={{2,0},{3,1},{0,2},{1,3},{5,4},{4,5},{7,6},{6,7},{10,8},{11,9},{8,1... | collective-permute-start | bytes 835592 | tf_op jit(solution)/shard_map/ppermute | solution.py:89
  9.9 4.4 %fetch.1 = (bf16[4,704,2048]{2,1,0:T(8,128)(2,1)S(1)}, bf16[16,2176]{1,0:T(8,128)(2,1)S(1)}) custom-call(bf16[8,704,2048]{2,1,0:T(8,128)(2,1)} %bitcast.21, bf16[32,2176]{1,0:T(8,128)(2,1)S(1)} %collective-permute-done.after.refs_1_, bf16[2,128,704]{2,1,0:T(8,128)(2,1)S(1)} %collective-permute-done.2.also_after.refs_6_), custom_call_target="tpu_custom_call" | custom-call | bytes 23068672 | tf_op jit(solution)/shard_map/fetch/pallas_call | solution.py:270
  14.6 3.0 %collective-permute-start.6 = (bf16[32,2176]{1,0:T(8,128)(2,1)S(1)}, bf16[32,2176]{1,0:T(8,128)(2,1)S(1)}, u32[]{:S(2)}, u32[]{:S(2)}) collective-permute-start(bf16[32,2176]{1,0:T(8,128)(2,1)S(1)} %get-tuple-element.64.refs_0_), channel_id=1, source_target_pairs={{3,0},{2,1},{1,2},{0,3},{7,4},{6,5},{5,6},{4,7},{11,8},{10,9},{9,1... | collective-permute-start | bytes 417800 | tf_op jit(solution)/shard_map/ppermute | solution.py:89
  17.6 0.5 collective-permute-start.5
  18.3 13.1 %forward.1 = (bf16[32,2048]{1,0:T(8,128)(2,1)S(1)}, bf16[32,2048]{1,0:T(8,128)(2,1)S(1)}, bf16[32,2048]{1,0:T(8,128)(2,1)S(1)}, bf16[32,2048]{1,0:T(8,128)(2,1)S...) custom-call(bf16[32,2176]{1,0:T(8,128)(2,1)S(1)} %pack.1.after.refs_0_, ...), custom_call_target="tpu_custom_call" | custom-call | flops 2214592512 | bytes 23068672 | tf_op jit(solution)/shard_map/forward/pallas_call | solution.py:428
  32.2 0.8 %collective-permute-done.7 = bf16[64,2048]{1,0:T(8,128)(2,1)S(1)} collective-permute-done((bf16[64,2048]{1,0:T(8,128)(2,1)S(1)}, bf16[64,2048]{1,0:T(8,128)(2,1)S(1)}, u32[]{:S(2)}, u32[]{:S(2)}) %collective-permute-start.7) | collective-permute-done | bytes 262176 | tf_op jit(solution)/shard_map/ppermute | solution.py:92
  33.4 2.0 %collective-permute-start.10 = (bf16[64,2048]{1,0:T(8,128)(2,1)S(1)}, bf16[64,2048]{1,0:T(8,128)(2,1)S(1)}, u32[]{:S(2)}, u32[]{:S(2)}) collective-permute-start(bf16[64,2048]{1,0:T(8,128)(2,1)S(1)} %pad_maximum_fusion.1), channel_id=1, source_target_pairs={{0,1},{1,0},{2,3},{3,2},{4,6},{5,7},{6,4},{7,5},{8,9},{9,8},{10,11... | collective-permute-start | bytes 786440 | tf_op jit(solution)/shard_map/ppermute | solution.py:89
  35.4 11.9 %backward.1 = (bf16[32,1024]{1,0:T(8,128)(2,1)S(1)}, bf16[32,1024]{1,0:T(8,128)(2,1)S(1)}, bf16[32,1024]{1,0:T(8,128)(2,1)S(1)}, bf16[32,1024]{1,0:T(8,128)(2,1)...) custom-call(bf16[32,2176]{1,0:T(8,128)(2,1)S(1)} %get-tuple-element., ...), custom_call_target="tpu_custom_call" | custom-call | flops 2214592512 | bytes 23068672 | tf_op jit(solution)/shard_map/backward/pallas_call | solution.py:428
  47.4 1.6 %collective-permute-start.13 = (bf16[32,2048]{1,0:T(8,128)(2,1)S(1)}, bf16[32,2048]{1,0:T(8,128)(2,1)S(1)}, u32[]{:S(2)}, u32[]{:S(2)}) collective-permute-start(bf16[32,2048]{1,0:T(8,128)(2,1)S(1)} %add_convert_fusion.1), channel_id=1, source_target_pairs={{0,2},{1,3},{2,0},{3,1},{4,5},{5,4},{6,7},{7,6},{8,10},{9,11},{10,... | collective-permute-start | bytes 393224 | tf_op jit(solution)/shard_map/ppermute | solution.py:89
  49.1 0.9 %collective-permute-start.12 = (bf16[64,1024]{1,0:T(8,128)(2,1)S(1)}, bf16[64,1024]{1,0:T(8,128)(2,1)S(1)}, u32[]{:S(2)}, u32[]{:S(2)}) collective-permute-start(bf16[64,1024]{1,0:T(8,128)(2,1)S(1)} %pad_maximum_fusion.3), channel_id=1, source_target_pairs={{0,1},{1,0},{2,3},{3,2},{4,6},{5,7},{6,4},{7,5},{8,9},{9,8},{10,11... | collective-permute-start | bytes 393224 | tf_op jit(solution)/shard_map/ppermute | solution.py:89
  50.0 0.6 collective-permute-done.15
  50.7 0.8 %collective-permute-start.16 = (bf16[64,1152]{1,0:T(8,128)(2,1)S(1)}, bf16[64,1152]{1,0:T(8,128)(2,1)S(1)}, u32[]{:S(2)}, u32[]{:S(2)}) collective-permute-start(bf16[64,1152]{1,0:T(8,128)(2,1)S(1)} %pad_maximum_fusion.2), channel_id=1, source_target_pairs={{0,1},{1,0},{2,3},{3,2},{4,6},{5,7},{6,4},{7,5},{8,9},{9,8},{10,11... | collective-permute-start | bytes 442376 | tf_op jit(solution)/shard_map/ppermute | solution.py:89
  51.5 1.1 %collective-permute-done.13 = bf16[32,2048]{1,0:T(8,128)(2,1)S(1)} collective-permute-done((bf16[32,2048]{1,0:T(8,128)(2,1)S(1)}, bf16[32,2048]{1,0:T(8,128)(2,1)S(1)}, u32[]{:S(2)}, u32[]{:S(2)}) %collective-permute-start.13) | collective-permute-done | bytes 131104 | tf_op jit(solution)/shard_map/ppermute | solution.py:89
  52.7 1.5 %collective-permute-done.12 = bf16[64,1024]{1,0:T(8,128)(2,1)S(1)} collective-permute-done((bf16[64,1024]{1,0:T(8,128)(2,1)S(1)}, bf16[64,1024]{1,0:T(8,128)(2,1)S(1)}, u32[]{:S(2)}, u32[]{:S(2)}) %collective-permute-start.12) | collective-permute-done | bytes 131104 | tf_op jit(solution)/shard_map/ppermute | solution.py:89
  54.2 1.5 %collective-permute-start.14 = (bf16[32,1024]{1,0:T(8,128)(2,1)S(1)}, bf16[32,1024]{1,0:T(8,128)(2,1)S(1)}, u32[]{:S(2)}, u32[]{:S(2)}) collective-permute-start(bf16[32,1024]{1,0:T(8,128)(2,1)S(1)} %add_convert_fusion.7), channel_id=1, source_target_pairs={{0,2},{1,3},{2,0},{3,1},{4,5},{5,4},{6,7},{7,6},{8,10},{9,11},{10,... | collective-permute-start | bytes 196616 | tf_op jit(solution)/shard_map/ppermute | solution.py:89
  55.9 1.3 %collective-permute-start.17 = (bf16[32,1152]{1,0:T(8,128)(2,1)S(1)}, bf16[32,1152]{1,0:T(8,128)(2,1)S(1)}, u32[]{:S(2)}, u32[]{:S(2)}) collective-permute-start(bf16[32,1152]{1,0:T(8,128)(2,1)S(1)} %add_convert_fusion.4), channel_id=1, source_target_pairs={{0,2},{1,3},{2,0},{3,1},{4,5},{5,4},{6,7},{7,6},{8,10},{9,11},{10,... | collective-permute-start | bytes 221192 | tf_op jit(solution)/shard_map/ppermute | solution.py:89
  57.2 0.7 %add_convert_fusion = bf16[32,2048]{1,0:T(8,128)(2,1)} fusion(bf16[32,2048]{1,0:T(8,128)(2,1)S(1)} %collective-permute-done.13, bf16[32,2048]{1,0:T(8,128)(2,1)S(1)} %get-tuple-element.62, bf16[64,2048]{1,0:T(8,128)(2,1)S(1)} %collective-permute-done.7, bf16[64,2048]{1,0:T(8,128)(2,1)S(1)} %collective-permute-done.10), kind=kLoop, calls=%fused_computation.4 | loop fusion | flops 524288 | bytes 655360 | tf_op jit(solution)/shard_map/convert_element_type | solution.py:620
  57.9 0.6 collective-permute-done.14.refs_3_
  58.5 1.8 %collective-permute-done.17.refs_7_ = bf16[32,1152]{1,0:T(8,128)(2,1)S(1)} collective-permute-done((bf16[32,1152]{1,0:T(8,128)(2,1)S(1)}, bf16[32,1152]{1,0:T(8,128)(2,1)S(1)}, u32[]{:S(2)}, u32[]{:S(2)}) %collective-permute-start.17) | collective-permute-done | bytes 73760 | tf_op jit(solution)/shard_map/ppermute | solution.py:89
  60.3 0.8 %finish.1 = (bf16[32,2048]{1,0:T(8,128)(2,1)}, f32[6,32]{1,0:T(8,128)}) custom-call(bf16[32,1024]{1,0:T(8,128)(2,1)S(1)} %get-tuple-element.89.refs_0_, bf16[32,1024]{1,0:T(8,128)(2,1)S(1)} %slice.86.refs_1_, bf16[32,1024]{1,0:T(8,128)(2,1)S(1)} %slice.71.refs_2_, bf16[32,1024]{1,0:T(8,128)(2,1)S(1)} %collective-permute-done.14.refs_3_, ...), custom_call_target="tpu_custom_call" | custom-call | tf_op jit(solution)/shard_map/finish/pallas_call | solution.py:544
  (40 shorter events, 2.4 us)
Async XLA Ops:
  1.7 6.0 %collective-permute-start = (bf16[32,2176]{1,0:T(8,128)(2,1)S(1)}, bf16[32,2176]{1,0:T(8,128)(2,1)S(1)}, u32[]{:S(2)}, u32[]{:S(2)}) collective-permute-start(bf16[32,2176]{1,0:T(8,128)(2,1)S(1)} %pack.1.after.refs_0_), channel_id=1, source_target_pairs={{1,0},{0,1},{3,2},{2,3},{6,4},{7,5},{4,6},{5,7},{9,8},{8,9},{11,10... | collective-permute-start | bytes 417800 | tf_op jit(solution)/shard_map/ppermute | solution.py:89
  6.3 3.6 %collective-permute-start.2 = (bf16[2,128,704]{2,1,0:T(8,128)(2,1)S(1)}, bf16[2,128,704]{2,1,0:T(8,128)(2,1)S(1)}, u32[]{:S(2)}, u32[]{:S(2)}) collective-permute-start(bf16[2,128,704]{2,1,0:T(8,128)(2,1)S(1)} %get-tuple-element.52), channel_id=1, source_target_pairs={{0,4},{4,0},{8,12},{12,8},{16,20},{20,16},{24,28},{28,24},{1,5},{5... | collective-permute-start | bytes 1081352 | tf_op jit(solution)/shard_map/ppermute | solution.py:92
  7.8 6.6 %collective-permute-start.1 = (bf16[64,2176]{1,0:T(8,128)(2,1)S(1)}, bf16[64,2176]{1,0:T(8,128)(2,1)S(1)}, u32[]{:S(2)}, u32[]{:S(2)}) collective-permute-start(bf16[64,2176]{1,0:T(8,128)(2,1)S(1)} %maximum_add_fusion.1), channel_id=1, source_target_pairs={{2,0},{3,1},{0,2},{1,3},{5,4},{4,5},{7,6},{6,7},{10,8},{11,9},{8,1... | collective-permute-start | bytes 835592 | tf_op jit(solution)/shard_map/ppermute | solution.py:89
  14.5 3.7 %collective-permute-start.3 = (bf16[128,2176]{1,0:T(8,128)(2,1)S(1)}, bf16[128,2176]{1,0:T(8,128)(2,1)S(1)}, u32[]{:S(2)}, u32[]{:S(2)}) collective-permute-start(bf16[128,2176]{1,0:T(8,128)(2,1)S(1)} %maximum_add_fusion), channel_id=1, source_target_pairs={{0,4},{4,0},{8,12},{12,8},{16,20},{20,16},{24,28},{28,24},{1,5},{5... | collective-permute-start | bytes 1671176 | tf_op jit(solution)/shard_map/ppermute | solution.py:92
  14.6 16.8 %collective-permute-start.6 = (bf16[32,2176]{1,0:T(8,128)(2,1)S(1)}, bf16[32,2176]{1,0:T(8,128)(2,1)S(1)}, u32[]{:S(2)}, u32[]{:S(2)}) collective-permute-start(bf16[32,2176]{1,0:T(8,128)(2,1)S(1)} %get-tuple-element.64.refs_0_), channel_id=1, source_target_pairs={{3,0},{2,1},{1,2},{0,3},{7,4},{6,5},{5,6},{4,7},{11,8},{10,9},{9,1... | collective-permute-start | bytes 417800 | tf_op jit(solution)/shard_map/ppermute | solution.py:89
  17.6 13.8 %collective-permute-start.5 = (bf16[32,2176]{1,0:T(8,128)(2,1)S(1)}, bf16[32,2176]{1,0:T(8,128)(2,1)S(1)}, u32[]{:S(2)}, u32[]{:S(2)}) collective-permute-start(bf16[32,2176]{1,0:T(8,128)(2,1)S(1)} %get-tuple-element.64.refs_0_), channel_id=1, source_target_pairs={{2,0},{3,1},{0,2},{1,3},{5,4},{4,5},{7,6},{6,7},{10,8},{11,9},{8,1... | collective-permute-start | bytes 417800 | tf_op jit(solution)/shard_map/ppermute | solution.py:89
  18.1 13.3 %collective-permute-start.4 = (bf16[32,2176]{1,0:T(8,128)(2,1)S(1)}, bf16[32,2176]{1,0:T(8,128)(2,1)S(1)}, u32[]{:S(2)}, u32[]{:S(2)}) collective-permute-start(bf16[32,2176]{1,0:T(8,128)(2,1)S(1)} %get-tuple-element.64.refs_0_), channel_id=1, source_target_pairs={{1,0},{0,1},{3,2},{2,3},{6,4},{7,5},{4,6},{5,7},{9,8},{8,9},{11,10... | collective-permute-start | bytes 417800 | tf_op jit(solution)/shard_map/ppermute | solution.py:89
  31.4 1.6 %collective-permute-start.7 = (bf16[64,2048]{1,0:T(8,128)(2,1)S(1)}, bf16[64,2048]{1,0:T(8,128)(2,1)S(1)}, u32[]{:S(2)}, u32[]{:S(2)}) collective-permute-start(bf16[64,2048]{1,0:T(8,128)(2,1)S(1)} %get-tuple-element.63), channel_id=1, source_target_pairs={{0,4},{4,0},{8,12},{12,8},{16,20},{20,16},{24,28},{28,24},{1,5},{5... | collective-permute-start | bytes 786440 | tf_op jit(solution)/shard_map/ppermute | solution.py:92
  31.5 1.9 %collective-permute-start.9 = (bf16[64,2048]{1,0:T(8,128)(2,1)S(1)}, bf16[64,2048]{1,0:T(8,128)(2,1)S(1)}, u32[]{:S(2)}, u32[]{:S(2)}) collective-permute-start(bf16[64,2048]{1,0:T(8,128)(2,1)S(1)} %get-tuple-element.82), channel_id=1, source_target_pairs={{0,4},{4,0},{8,12},{12,8},{16,20},{20,16},{24,28},{28,24},{1,5},{5... | collective-permute-start | bytes 786440 | tf_op jit(solution)/shard_map/ppermute | solution.py:92
  32.0 3.4 %collective-permute-start.8 = (bf16[128,2176]{1,0:T(8,128)(2,1)S(1)}, bf16[128,2176]{1,0:T(8,128)(2,1)S(1)}, u32[]{:S(2)}, u32[]{:S(2)}) collective-permute-start(bf16[128,2176]{1,0:T(8,128)(2,1)S(1)} %pad_maximum_fusion), channel_id=1, source_target_pairs={{0,4},{4,0},{8,12},{12,8},{16,20},{20,16},{24,28},{28,24},{1,5},{5... | collective-permute-start | bytes 1671176 | tf_op jit(solution)/shard_map/ppermute | solution.py:92
  33.4 13.8 %collective-permute-start.10 = (bf16[64,2048]{1,0:T(8,128)(2,1)S(1)}, bf16[64,2048]{1,0:T(8,128)(2,1)S(1)}, u32[]{:S(2)}, u32[]{:S(2)}) collective-permute-start(bf16[64,2048]{1,0:T(8,128)(2,1)S(1)} %pad_maximum_fusion.1), channel_id=1, source_target_pairs={{0,1},{1,0},{2,3},{3,2},{4,6},{5,7},{6,4},{7,5},{8,9},{9,8},{10,11... | collective-permute-start | bytes 786440 | tf_op jit(solution)/shard_map/ppermute | solution.py:89
  47.3 1.7 %collective-permute-start.11 = (bf16[128,1024]{1,0:T(8,128)(2,1)S(1)}, bf16[128,1024]{1,0:T(8,128)(2,1)S(1)}, u32[]{:S(2)}, u32[]{:S(2)}) collective-permute-start(bf16[128,1024]{1,0:T(8,128)(2,1)S(1)} %get-tuple-element.85), channel_id=1, source_target_pairs={{0,4},{4,0},{8,12},{12,8},{16,20},{20,16},{24,28},{28,24},{1,5},{5... | collective-permute-start | bytes 786440 | tf_op jit(solution)/shard_map/ppermute | solution.py:92
  47.4 5.2 %collective-permute-start.13 = (bf16[32,2048]{1,0:T(8,128)(2,1)S(1)}, bf16[32,2048]{1,0:T(8,128)(2,1)S(1)}, u32[]{:S(2)}, u32[]{:S(2)}) collective-permute-start(bf16[32,2048]{1,0:T(8,128)(2,1)S(1)} %add_convert_fusion.1), channel_id=1, source_target_pairs={{0,2},{1,3},{2,0},{3,1},{4,5},{5,4},{6,7},{7,6},{8,10},{9,11},{10,... | collective-permute-start | bytes 393224 | tf_op jit(solution)/shard_map/ppermute | solution.py:89
  49.0 1.6 %collective-permute-start.15 = (bf16[128,1152]{1,0:T(8,128)(2,1)S(1)}, bf16[128,1152]{1,0:T(8,128)(2,1)S(1)}, u32[]{:S(2)}, u32[]{:S(2)}) collective-permute-start(bf16[128,1152]{1,0:T(8,128)(2,1)S(1)} %get-tuple-element.93), channel_id=1, source_target_pairs={{0,4},{4,0},{8,12},{12,8},{16,20},{20,16},{24,28},{28,24},{1,5},{5... | collective-permute-start | bytes 884744 | tf_op jit(solution)/shard_map/ppermute | solution.py:92
  49.1 5.0 %collective-permute-start.12 = (bf16[64,1024]{1,0:T(8,128)(2,1)S(1)}, bf16[64,1024]{1,0:T(8,128)(2,1)S(1)}, u32[]{:S(2)}, u32[]{:S(2)}) collective-permute-start(bf16[64,1024]{1,0:T(8,128)(2,1)S(1)} %pad_maximum_fusion.3), channel_id=1, source_target_pairs={{0,1},{1,0},{2,3},{3,2},{4,6},{5,7},{6,4},{7,5},{8,9},{9,8},{10,11... | collective-permute-start | bytes 393224 | tf_op jit(solution)/shard_map/ppermute | solution.py:89
  50.0 10.3 %copy-start = (s32[32,6]{0,1:T(8,128)S(1)}, s32[32,6]{0,1:T(8,128)}, u32[]{:S(2)}) copy-start(s32[32,6]{0,1:T(8,128)} %param.15) | copy-start | bytes 2308
  50.7 5.2 %collective-permute-start.16 = (bf16[64,1152]{1,0:T(8,128)(2,1)S(1)}, bf16[64,1152]{1,0:T(8,128)(2,1)S(1)}, u32[]{:S(2)}, u32[]{:S(2)}) collective-permute-start(bf16[64,1152]{1,0:T(8,128)(2,1)S(1)} %pad_maximum_fusion.2), channel_id=1, source_target_pairs={{0,1},{1,0},{2,3},{3,2},{4,6},{5,7},{6,4},{7,5},{8,9},{9,8},{10,11... | collective-permute-start | bytes 442376 | tf_op jit(solution)/shard_map/ppermute | solution.py:89
  54.2 4.3 %collective-permute-start.14 = (bf16[32,1024]{1,0:T(8,128)(2,1)S(1)}, bf16[32,1024]{1,0:T(8,128)(2,1)S(1)}, u32[]{:S(2)}, u32[]{:S(2)}) collective-permute-start(bf16[32,1024]{1,0:T(8,128)(2,1)S(1)} %add_convert_fusion.7), channel_id=1, source_target_pairs={{0,2},{1,3},{2,0},{3,1},{4,5},{5,4},{6,7},{7,6},{8,10},{9,11},{10,... | collective-permute-start | bytes 196616 | tf_op jit(solution)/shard_map/ppermute | solution.py:89
  55.9 4.4 %collective-permute-start.17 = (bf16[32,1152]{1,0:T(8,128)(2,1)S(1)}, bf16[32,1152]{1,0:T(8,128)(2,1)S(1)}, u32[]{:S(2)}, u32[]{:S(2)}) collective-permute-start(bf16[32,1152]{1,0:T(8,128)(2,1)S(1)} %add_convert_fusion.4), channel_id=1, source_target_pairs={{0,2},{1,3},{2,0},{3,1},{4,5},{5,4},{6,7},{7,6},{8,10},{9,11},{10,... | collective-permute-start | bytes 221192 | tf_op jit(solution)/shard_map/ppermute | solution.py:89

commit v14 on v13

--- a/solution.py
+++ b/solution.py
@@ -362,7 +362,7 @@
     downs = weight_slots(plan, kept_ref, down_s)
     copies = weight_copies(plan, down_hbm, downs, sems.at[0])[plan.kept :]
     copies += weight_copies(plan, up_hbm, weight_slots(plan, up_s), sems.at[1])
-    queue = Queue(copies, 4)
+    queue = Queue(copies, 3)
     queue.fill()
     table, factor = arrived(plan, blocks, first, x_s)
     n, held = plan.expert_rows, plan.source_rows
@@ -392,15 +392,14 @@
 
     grad = None
     for e, part in enumerate(parts):
-        if e == plan.kept:
-            queue.take(plan.mine - plan.kept)
+        if e >= plan.kept:
+            queue.take(1)
         last, grad = grad, dot_tb(x_s[part, :], downs[e][...])
         if e:
             through_activation(e - 1, last)
     through_activation(plan.mine - 1, grad)
     for e, part in enumerate(parts):
-        if e % 2 == 0:
-            queue.take(min(2, plan.mine - e))
+        queue.take(1)
         result = dot(grads_s[0, e], gate_ref[e]) + dot(grads_s[1, e], up_s[e])
         y_s[part, :] = (result * factor[part]).astype(BF16)
     half, near = plan.half, outs[: len(outs) // 2]

time: 61.5 us -> 61.2 us (level)
  no operation moved by 1% of the time
where the time goes in v14:
time: 61.2 us; the launch traced here: 61 us
  Pallas kernels  32.5 us (53%)
  starting transfers between devices  17.8 us (29%)
  waiting for transfers between devices  8.42 us (14%)
  other arithmetic  1.22 us (2%)
  between operations  0.98 us (2%)
    pallas_call x2, Pallas kernels, expert_call(): pl.pallas_call(kernel, out_shape=shapes, in_specs=[vmem()] * len(inputs)...  24.7 us
    ppermute x11, starting transfers between devices, over_expert(): return lax.ppermute(x, ('dp', 'expert'), pairs)  16.8 us
    ppermute x11, waiting for transfers between devices, over_expert(): return lax.ppermute(x, ('dp', 'expert'), pairs)  6.66 us
    pallas_call x1, Pallas kernels, fetch(): pl.pallas_call(functools.partial(fetch_kernel, plan), out_shape=(pltpu.VM...  4.4 us
    ppermute x7, waiting for transfers between devices, over_pair(): return lax.ppermute(x, 'dp', [(i, i ^ 1) for i in range(self.groups)])  1.75 us
    pallas_call x1, Pallas kernels, prepare(): pl.pallas_call(functools.partial(prepare_kernel, plan), out_shape=out_sha...  1.59 us
  transfers between devices with their start and end apart: 18, of which 10 were waited for; matrix products, arithmetic and copies ran while one was open for 2% of the time, Pallas kernels for 50%

profile of v14, /device:TPU:0, one launch (start us, length us, event | category | flops | bytes accessed | tf_op | source)
XLA Modules:
  0.0 61.0 jit_solution(13061811186532777834)
XLA Ops:
  0.6 1.1 %pack.1.after.refs_0_ = bf16[32,2176]{1,0:T(8,128)(2,1)S(1)} custom-call(bf16[32,2048]{1,0:T(8,128)(2,1)} %refs_0_.1, s32[6,32]{1,0:T(8,128)} %bitcast.24, f32[6,32]{1,0:T(8,128)} %bitcast.25), custom_call_target="tpu_custom_call" | custom-call | tf_op jit(solution)/shard_map/pack/pallas_call | solution.py:140
  1.7 3.0 %collective-permute-start = (bf16[32,2176]{1,0:T(8,128)(2,1)S(1)}, bf16[32,2176]{1,0:T(8,128)(2,1)S(1)}, u32[]{:S(2)}, u32[]{:S(2)}) collective-permute-start(bf16[32,2176]{1,0:T(8,128)(2,1)S(1)} %pack.1.after.refs_0_), channel_id=1, source_target_pairs={{1,0},{0,1},{3,2},{2,3},{6,4},{7,5},{4,6},{5,7},{9,8},{8,9},{11,10... | collective-permute-start | bytes 417800 | tf_op jit(solution)/shard_map/ppermute | solution.py:89
  4.7 1.6 %prepare.1 = (bf16[32,2176]{1,0:T(8,128)(2,1)S(1)}, bf16[16,2176]{1,0:T(8,128)(2,1)S(1)}, bf16[2,128,704]{2,1,0:T(8,128)(2,1)S(1)}, bf16[2,128,704]{2,1,0:T(8,128)(2,1)S(1)}) custom-call(bf16[32,2048]{1,0:T(8,128)(2,1)} %x_hbm.1, s32[6,32]{1,0:T(8,128)} %bitcast.17, f32[6,32]{1,0:T(8,128)} %bitcast.26, bf16[224,704]{1,0:T(8,128)(2,1)} %bitcast.22, ...), custom_call_target="tpu_custom_call" | custom-call | bytes 17825792 | tf_op jit(solution)/shard_map/prepare/pallas_call | solution.py:233
  6.4 1.3 %collective-permute-done.after.refs_1_ = bf16[32,2176]{1,0:T(8,128)(2,1)S(1)} collective-permute-done((bf16[32,2176]{1,0:T(8,128)(2,1)S(1)}, bf16[32,2176]{1,0:T(8,128)(2,1)S(1)}, u32[]{:S(2)}, u32[]{:S(2)}) %collective-permute-start) | collective-permute-done | bytes 139296 | tf_op jit(solution)/shard_map/ppermute | solution.py:89
  7.8 2.1 %collective-permute-start.1 = (bf16[64,2176]{1,0:T(8,128)(2,1)S(1)}, bf16[64,2176]{1,0:T(8,128)(2,1)S(1)}, u32[]{:S(2)}, u32[]{:S(2)}) collective-permute-start(bf16[64,2176]{1,0:T(8,128)(2,1)S(1)} %maximum_add_fusion.1), channel_id=1, source_target_pairs={{2,0},{3,1},{0,2},{1,3},{5,4},{4,5},{7,6},{6,7},{10,8},{11,9},{8,1... | collective-permute-start | bytes 835592 | tf_op jit(solution)/shard_map/ppermute | solution.py:89
  9.9 4.4 %fetch.1 = (bf16[4,704,2048]{2,1,0:T(8,128)(2,1)S(1)}, bf16[16,2176]{1,0:T(8,128)(2,1)S(1)}) custom-call(bf16[8,704,2048]{2,1,0:T(8,128)(2,1)} %bitcast.21, bf16[32,2176]{1,0:T(8,128)(2,1)S(1)} %collective-permute-done.after.refs_1_, bf16[2,128,704]{2,1,0:T(8,128)(2,1)S(1)} %collective-permute-done.2.also_after.refs_6_), custom_call_target="tpu_custom_call" | custom-call | bytes 23068672 | tf_op jit(solution)/shard_map/fetch/pallas_call | solution.py:270
  14.6 3.0 %collective-permute-start.6 = (bf16[32,2176]{1,0:T(8,128)(2,1)S(1)}, bf16[32,2176]{1,0:T(8,128)(2,1)S(1)}, u32[]{:S(2)}, u32[]{:S(2)}) collective-permute-start(bf16[32,2176]{1,0:T(8,128)(2,1)S(1)} %get-tuple-element.64.refs_0_), channel_id=1, source_target_pairs={{3,0},{2,1},{1,2},{0,3},{7,4},{6,5},{5,6},{4,7},{11,8},{10,9},{9,1... | collective-permute-start | bytes 417800 | tf_op jit(solution)/shard_map/ppermute | solution.py:89
  17.6 0.5 collective-permute-start.5
  18.3 13.1 %forward.1 = (bf16[32,2048]{1,0:T(8,128)(2,1)S(1)}, bf16[32,2048]{1,0:T(8,128)(2,1)S(1)}, bf16[32,2048]{1,0:T(8,128)(2,1)S(1)}, bf16[32,2048]{1,0:T(8,128)(2,1)S...) custom-call(bf16[32,2176]{1,0:T(8,128)(2,1)S(1)} %pack.1.after.refs_0_, ...), custom_call_target="tpu_custom_call" | custom-call | flops 2214592512 | bytes 23068672 | tf_op jit(solution)/shard_map/forward/pallas_call | solution.py:427
  32.2 0.8 %collective-permute-done.7 = bf16[64,2048]{1,0:T(8,128)(2,1)S(1)} collective-permute-done((bf16[64,2048]{1,0:T(8,128)(2,1)S(1)}, bf16[64,2048]{1,0:T(8,128)(2,1)S(1)}, u32[]{:S(2)}, u32[]{:S(2)}) %collective-permute-start.7) | collective-permute-done | bytes 262176 | tf_op jit(solution)/shard_map/ppermute | solution.py:92
  33.4 2.0 %collective-permute-start.10 = (bf16[64,2048]{1,0:T(8,128)(2,1)S(1)}, bf16[64,2048]{1,0:T(8,128)(2,1)S(1)}, u32[]{:S(2)}, u32[]{:S(2)}) collective-permute-start(bf16[64,2048]{1,0:T(8,128)(2,1)S(1)} %pad_maximum_fusion.1), channel_id=1, source_target_pairs={{0,1},{1,0},{2,3},{3,2},{4,6},{5,7},{6,4},{7,5},{8,9},{9,8},{10,11... | collective-permute-start | bytes 786440 | tf_op jit(solution)/shard_map/ppermute | solution.py:89
  35.4 11.6 %backward.1 = (bf16[32,1024]{1,0:T(8,128)(2,1)S(1)}, bf16[32,1024]{1,0:T(8,128)(2,1)S(1)}, bf16[32,1024]{1,0:T(8,128)(2,1)S(1)}, bf16[32,1024]{1,0:T(8,128)(2,1)...) custom-call(bf16[32,2176]{1,0:T(8,128)(2,1)S(1)} %get-tuple-element., ...), custom_call_target="tpu_custom_call" | custom-call | flops 2214592512 | bytes 23068672 | tf_op jit(solution)/shard_map/backward/pallas_call | solution.py:427
  47.1 1.6 %collective-permute-start.13 = (bf16[32,2048]{1,0:T(8,128)(2,1)S(1)}, bf16[32,2048]{1,0:T(8,128)(2,1)S(1)}, u32[]{:S(2)}, u32[]{:S(2)}) collective-permute-start(bf16[32,2048]{1,0:T(8,128)(2,1)S(1)} %add_convert_fusion.1), channel_id=1, source_target_pairs={{0,2},{1,3},{2,0},{3,1},{4,5},{5,4},{6,7},{7,6},{8,10},{9,11},{10,... | collective-permute-start | bytes 393224 | tf_op jit(solution)/shard_map/ppermute | solution.py:89
  48.8 0.9 %collective-permute-start.12 = (bf16[64,1024]{1,0:T(8,128)(2,1)S(1)}, bf16[64,1024]{1,0:T(8,128)(2,1)S(1)}, u32[]{:S(2)}, u32[]{:S(2)}) collective-permute-start(bf16[64,1024]{1,0:T(8,128)(2,1)S(1)} %pad_maximum_fusion.3), channel_id=1, source_target_pairs={{0,1},{1,0},{2,3},{3,2},{4,6},{5,7},{6,4},{7,5},{8,9},{9,8},{10,11... | collective-permute-start | bytes 393224 | tf_op jit(solution)/shard_map/ppermute | solution.py:89
  49.7 0.6 collective-permute-done.15
  50.4 0.8 %collective-permute-start.16 = (bf16[64,1152]{1,0:T(8,128)(2,1)S(1)}, bf16[64,1152]{1,0:T(8,128)(2,1)S(1)}, u32[]{:S(2)}, u32[]{:S(2)}) collective-permute-start(bf16[64,1152]{1,0:T(8,128)(2,1)S(1)} %pad_maximum_fusion.2), channel_id=1, source_target_pairs={{0,1},{1,0},{2,3},{3,2},{4,6},{5,7},{6,4},{7,5},{8,9},{9,8},{10,11... | collective-permute-start | bytes 442376 | tf_op jit(solution)/shard_map/ppermute | solution.py:89
  51.2 1.2 %collective-permute-done.13 = bf16[32,2048]{1,0:T(8,128)(2,1)S(1)} collective-permute-done((bf16[32,2048]{1,0:T(8,128)(2,1)S(1)}, bf16[32,2048]{1,0:T(8,128)(2,1)S(1)}, u32[]{:S(2)}, u32[]{:S(2)}) %collective-permute-start.13) | collective-permute-done | bytes 131104 | tf_op jit(solution)/shard_map/ppermute | solution.py:89
  52.4 1.4 %collective-permute-done.12 = bf16[64,1024]{1,0:T(8,128)(2,1)S(1)} collective-permute-done((bf16[64,1024]{1,0:T(8,128)(2,1)S(1)}, bf16[64,1024]{1,0:T(8,128)(2,1)S(1)}, u32[]{:S(2)}, u32[]{:S(2)}) %collective-permute-start.12) | collective-permute-done | bytes 131104 | tf_op jit(solution)/shard_map/ppermute | solution.py:89
  53.8 1.5 %collective-permute-start.14 = (bf16[32,1024]{1,0:T(8,128)(2,1)S(1)}, bf16[32,1024]{1,0:T(8,128)(2,1)S(1)}, u32[]{:S(2)}, u32[]{:S(2)}) collective-permute-start(bf16[32,1024]{1,0:T(8,128)(2,1)S(1)} %add_convert_fusion.7), channel_id=1, source_target_pairs={{0,2},{1,3},{2,0},{3,1},{4,5},{5,4},{6,7},{7,6},{8,10},{9,11},{10,... | collective-permute-start | bytes 196616 | tf_op jit(solution)/shard_map/ppermute | solution.py:89
  55.6 1.3 %collective-permute-start.17 = (bf16[32,1152]{1,0:T(8,128)(2,1)S(1)}, bf16[32,1152]{1,0:T(8,128)(2,1)S(1)}, u32[]{:S(2)}, u32[]{:S(2)}) collective-permute-start(bf16[32,1152]{1,0:T(8,128)(2,1)S(1)} %add_convert_fusion.4), channel_id=1, source_target_pairs={{0,2},{1,3},{2,0},{3,1},{4,5},{5,4},{6,7},{7,6},{8,10},{9,11},{10,... | collective-permute-start | bytes 221192 | tf_op jit(solution)/shard_map/ppermute | solution.py:89
  56.9 0.7 %add_convert_fusion = bf16[32,2048]{1,0:T(8,128)(2,1)} fusion(bf16[32,2048]{1,0:T(8,128)(2,1)S(1)} %collective-permute-done.13, bf16[32,2048]{1,0:T(8,128)(2,1)S(1)} %get-tuple-element.62, bf16[64,2048]{1,0:T(8,128)(2,1)S(1)} %collective-permute-done.7, bf16[64,2048]{1,0:T(8,128)(2,1)S(1)} %collective-permute-done.10), kind=kLoop, calls=%fused_computation.4 | loop fusion | flops 524288 | bytes 655360 | tf_op jit(solution)/shard_map/convert_element_type | solution.py:619
  57.6 0.6 collective-permute-done.14.refs_3_
  58.2 1.8 %collective-permute-done.17.refs_7_ = bf16[32,1152]{1,0:T(8,128)(2,1)S(1)} collective-permute-done((bf16[32,1152]{1,0:T(8,128)(2,1)S(1)}, bf16[32,1152]{1,0:T(8,128)(2,1)S(1)}, u32[]{:S(2)}, u32[]{:S(2)}) %collective-permute-start.17) | collective-permute-done | bytes 73760 | tf_op jit(solution)/shard_map/ppermute | solution.py:89
  60.0 0.8 %finish.1 = (bf16[32,2048]{1,0:T(8,128)(2,1)}, f32[6,32]{1,0:T(8,128)}) custom-call(bf16[32,1024]{1,0:T(8,128)(2,1)S(1)} %get-tuple-element.89.refs_0_, bf16[32,1024]{1,0:T(8,128)(2,1)S(1)} %slice.86.refs_1_, bf16[32,1024]{1,0:T(8,128)(2,1)S(1)} %slice.71.refs_2_, bf16[32,1024]{1,0:T(8,128)(2,1)S(1)} %collective-permute-done.14.refs_3_, ...), custom_call_target="tpu_custom_call" | custom-call | tf_op jit(solution)/shard_map/finish/pallas_call | solution.py:543
  (40 shorter events, 2.4 us)
Async XLA Ops:
  1.7 6.0 %collective-permute-start = (bf16[32,2176]{1,0:T(8,128)(2,1)S(1)}, bf16[32,2176]{1,0:T(8,128)(2,1)S(1)}, u32[]{:S(2)}, u32[]{:S(2)}) collective-permute-start(bf16[32,2176]{1,0:T(8,128)(2,1)S(1)} %pack.1.after.refs_0_), channel_id=1, source_target_pairs={{1,0},{0,1},{3,2},{2,3},{6,4},{7,5},{4,6},{5,7},{9,8},{8,9},{11,10... | collective-permute-start | bytes 417800 | tf_op jit(solution)/shard_map/ppermute | solution.py:89
  6.3 3.6 %collective-permute-start.2 = (bf16[2,128,704]{2,1,0:T(8,128)(2,1)S(1)}, bf16[2,128,704]{2,1,0:T(8,128)(2,1)S(1)}, u32[]{:S(2)}, u32[]{:S(2)}) collective-permute-start(bf16[2,128,704]{2,1,0:T(8,128)(2,1)S(1)} %get-tuple-element.52), channel_id=1, source_target_pairs={{0,4},{4,0},{8,12},{12,8},{16,20},{20,16},{24,28},{28,24},{1,5},{5... | collective-permute-start | bytes 1081352 | tf_op jit(solution)/shard_map/ppermute | solution.py:92
  7.8 6.6 %collective-permute-start.1 = (bf16[64,2176]{1,0:T(8,128)(2,1)S(1)}, bf16[64,2176]{1,0:T(8,128)(2,1)S(1)}, u32[]{:S(2)}, u32[]{:S(2)}) collective-permute-start(bf16[64,2176]{1,0:T(8,128)(2,1)S(1)} %maximum_add_fusion.1), channel_id=1, source_target_pairs={{2,0},{3,1},{0,2},{1,3},{5,4},{4,5},{7,6},{6,7},{10,8},{11,9},{8,1... | collective-permute-start | bytes 835592 | tf_op jit(solution)/shard_map/ppermute | solution.py:89
  14.5 3.7 %collective-permute-start.3 = (bf16[128,2176]{1,0:T(8,128)(2,1)S(1)}, bf16[128,2176]{1,0:T(8,128)(2,1)S(1)}, u32[]{:S(2)}, u32[]{:S(2)}) collective-permute-start(bf16[128,2176]{1,0:T(8,128)(2,1)S(1)} %maximum_add_fusion), channel_id=1, source_target_pairs={{0,4},{4,0},{8,12},{12,8},{16,20},{20,16},{24,28},{28,24},{1,5},{5... | collective-permute-start | bytes 1671176 | tf_op jit(solution)/shard_map/ppermute | solution.py:92
  14.6 16.8 %collective-permute-start.6 = (bf16[32,2176]{1,0:T(8,128)(2,1)S(1)}, bf16[32,2176]{1,0:T(8,128)(2,1)S(1)}, u32[]{:S(2)}, u32[]{:S(2)}) collective-permute-start(bf16[32,2176]{1,0:T(8,128)(2,1)S(1)} %get-tuple-element.64.refs_0_), channel_id=1, source_target_pairs={{3,0},{2,1},{1,2},{0,3},{7,4},{6,5},{5,6},{4,7},{11,8},{10,9},{9,1... | collective-permute-start | bytes 417800 | tf_op jit(solution)/shard_map/ppermute | solution.py:89
  17.6 13.8 %collective-permute-start.5 = (bf16[32,2176]{1,0:T(8,128)(2,1)S(1)}, bf16[32,2176]{1,0:T(8,128)(2,1)S(1)}, u32[]{:S(2)}, u32[]{:S(2)}) collective-permute-start(bf16[32,2176]{1,0:T(8,128)(2,1)S(1)} %get-tuple-element.64.refs_0_), channel_id=1, source_target_pairs={{2,0},{3,1},{0,2},{1,3},{5,4},{4,5},{7,6},{6,7},{10,8},{11,9},{8,1... | collective-permute-start | bytes 417800 | tf_op jit(solution)/shard_map/ppermute | solution.py:89
  18.1 13.3 %collective-permute-start.4 = (bf16[32,2176]{1,0:T(8,128)(2,1)S(1)}, bf16[32,2176]{1,0:T(8,128)(2,1)S(1)}, u32[]{:S(2)}, u32[]{:S(2)}) collective-permute-start(bf16[32,2176]{1,0:T(8,128)(2,1)S(1)} %get-tuple-element.64.refs_0_), channel_id=1, source_target_pairs={{1,0},{0,1},{3,2},{2,3},{6,4},{7,5},{4,6},{5,7},{9,8},{8,9},{11,10... | collective-permute-start | bytes 417800 | tf_op jit(solution)/shard_map/ppermute | solution.py:89
  31.4 1.6 %collective-permute-start.7 = (bf16[64,2048]{1,0:T(8,128)(2,1)S(1)}, bf16[64,2048]{1,0:T(8,128)(2,1)S(1)}, u32[]{:S(2)}, u32[]{:S(2)}) collective-permute-start(bf16[64,2048]{1,0:T(8,128)(2,1)S(1)} %get-tuple-element.63), channel_id=1, source_target_pairs={{0,4},{4,0},{8,12},{12,8},{16,20},{20,16},{24,28},{28,24},{1,5},{5... | collective-permute-start | bytes 786440 | tf_op jit(solution)/shard_map/ppermute | solution.py:92
  31.5 1.9 %collective-permute-start.9 = (bf16[64,2048]{1,0:T(8,128)(2,1)S(1)}, bf16[64,2048]{1,0:T(8,128)(2,1)S(1)}, u32[]{:S(2)}, u32[]{:S(2)}) collective-permute-start(bf16[64,2048]{1,0:T(8,128)(2,1)S(1)} %get-tuple-element.82), channel_id=1, source_target_pairs={{0,4},{4,0},{8,12},{12,8},{16,20},{20,16},{24,28},{28,24},{1,5},{5... | collective-permute-start | bytes 786440 | tf_op jit(solution)/shard_map/ppermute | solution.py:92
  32.0 3.4 %collective-permute-start.8 = (bf16[128,2176]{1,0:T(8,128)(2,1)S(1)}, bf16[128,2176]{1,0:T(8,128)(2,1)S(1)}, u32[]{:S(2)}, u32[]{:S(2)}) collective-permute-start(bf16[128,2176]{1,0:T(8,128)(2,1)S(1)} %pad_maximum_fusion), channel_id=1, source_target_pairs={{0,4},{4,0},{8,12},{12,8},{16,20},{20,16},{24,28},{28,24},{1,5},{5... | collective-permute-start | bytes 1671176 | tf_op jit(solution)/shard_map/ppermute | solution.py:92
  33.4 13.6 %collective-permute-start.10 = (bf16[64,2048]{1,0:T(8,128)(2,1)S(1)}, bf16[64,2048]{1,0:T(8,128)(2,1)S(1)}, u32[]{:S(2)}, u32[]{:S(2)}) collective-permute-start(bf16[64,2048]{1,0:T(8,128)(2,1)S(1)} %pad_maximum_fusion.1), channel_id=1, source_target_pairs={{0,1},{1,0},{2,3},{3,2},{4,6},{5,7},{6,4},{7,5},{8,9},{9,8},{10,11... | collective-permute-start | bytes 786440 | tf_op jit(solution)/shard_map/ppermute | solution.py:89
  47.0 1.7 %collective-permute-start.11 = (bf16[128,1024]{1,0:T(8,128)(2,1)S(1)}, bf16[128,1024]{1,0:T(8,128)(2,1)S(1)}, u32[]{:S(2)}, u32[]{:S(2)}) collective-permute-start(bf16[128,1024]{1,0:T(8,128)(2,1)S(1)} %get-tuple-element.85), channel_id=1, source_target_pairs={{0,4},{4,0},{8,12},{12,8},{16,20},{20,16},{24,28},{28,24},{1,5},{5... | collective-permute-start | bytes 786440 | tf_op jit(solution)/shard_map/ppermute | solution.py:92
  47.1 5.2 %collective-permute-start.13 = (bf16[32,2048]{1,0:T(8,128)(2,1)S(1)}, bf16[32,2048]{1,0:T(8,128)(2,1)S(1)}, u32[]{:S(2)}, u32[]{:S(2)}) collective-permute-start(bf16[32,2048]{1,0:T(8,128)(2,1)S(1)} %add_convert_fusion.1), channel_id=1, source_target_pairs={{0,2},{1,3},{2,0},{3,1},{4,5},{5,4},{6,7},{7,6},{8,10},{9,11},{10,... | collective-permute-start | bytes 393224 | tf_op jit(solution)/shard_map/ppermute | solution.py:89
  48.7 1.6 %collective-permute-start.15 = (bf16[128,1152]{1,0:T(8,128)(2,1)S(1)}, bf16[128,1152]{1,0:T(8,128)(2,1)S(1)}, u32[]{:S(2)}, u32[]{:S(2)}) collective-permute-start(bf16[128,1152]{1,0:T(8,128)(2,1)S(1)} %get-tuple-element.93), channel_id=1, source_target_pairs={{0,4},{4,0},{8,12},{12,8},{16,20},{20,16},{24,28},{28,24},{1,5},{5... | collective-permute-start | bytes 884744 | tf_op jit(solution)/shard_map/ppermute | solution.py:92
  48.8 5.0 %collective-permute-start.12 = (bf16[64,1024]{1,0:T(8,128)(2,1)S(1)}, bf16[64,1024]{1,0:T(8,128)(2,1)S(1)}, u32[]{:S(2)}, u32[]{:S(2)}) collective-permute-start(bf16[64,1024]{1,0:T(8,128)(2,1)S(1)} %pad_maximum_fusion.3), channel_id=1, source_target_pairs={{0,1},{1,0},{2,3},{3,2},{4,6},{5,7},{6,4},{7,5},{8,9},{9,8},{10,11... | collective-permute-start | bytes 393224 | tf_op jit(solution)/shard_map/ppermute | solution.py:89
  49.7 10.3 %copy-start = (s32[32,6]{0,1:T(8,128)S(1)}, s32[32,6]{0,1:T(8,128)}, u32[]{:S(2)}) copy-start(s32[32,6]{0,1:T(8,128)} %param.15) | copy-start | bytes 2308
  50.4 5.2 %collective-permute-start.16 = (bf16[64,1152]{1,0:T(8,128)(2,1)S(1)}, bf16[64,1152]{1,0:T(8,128)(2,1)S(1)}, u32[]{:S(2)}, u32[]{:S(2)}) collective-permute-start(bf16[64,1152]{1,0:T(8,128)(2,1)S(1)} %pad_maximum_fusion.2), channel_id=1, source_target_pairs={{0,1},{1,0},{2,3},{3,2},{4,6},{5,7},{6,4},{7,5},{8,9},{9,8},{10,11... | collective-permute-start | bytes 442376 | tf_op jit(solution)/shard_map/ppermute | solution.py:89
  53.8 4.3 %collective-permute-start.14 = (bf16[32,1024]{1,0:T(8,128)(2,1)S(1)}, bf16[32,1024]{1,0:T(8,128)(2,1)S(1)}, u32[]{:S(2)}, u32[]{:S(2)}) collective-permute-start(bf16[32,1024]{1,0:T(8,128)(2,1)S(1)} %add_convert_fusion.7), channel_id=1, source_target_pairs={{0,2},{1,3},{2,0},{3,1},{4,5},{5,4},{6,7},{7,6},{8,10},{9,11},{10,... | collective-permute-start | bytes 196616 | tf_op jit(solution)/shard_map/ppermute | solution.py:89
  55.6 4.4 %collective-permute-start.17 = (bf16[32,1152]{1,0:T(8,128)(2,1)S(1)}, bf16[32,1152]{1,0:T(8,128)(2,1)S(1)}, u32[]{:S(2)}, u32[]{:S(2)}) collective-permute-start(bf16[32,1152]{1,0:T(8,128)(2,1)S(1)} %add_convert_fusion.4), channel_id=1, source_target_pairs={{0,2},{1,3},{2,0},{3,1},{4,5},{5,4},{6,7},{7,6},{8,10},{9,11},{10,... | collective-permute-start | bytes 221192 | tf_op jit(solution)/shard_map/ppermute | solution.py:89

commit v15 on v14

--- a/solution.py
+++ b/solution.py
@@ -69,6 +69,7 @@
         self.sent = self.width + self.meta
         self.half = round_up(self.width // 2, LANES)
         self.kept = min(self.mine, 2)
+        self.order = [*range(1, self.owners, 2), *range(0, self.owners, 2)]
         self.rows = self.mine * self.expert_rows
         self.cols = self.blocks * self.count
 
@@ -342,7 +343,11 @@
             queue.take(min(2, plan.mine - e))
         out = dot(hidden_s[e], downs[e][...])
         y_s[part, :] = (out * factor[part]).astype(BF16)
-    put_rows(outs, slice(None), dot_ta(table, y_s[...]).astype(BF16))
+    mixed = dot_ta(table, y_s[...]).astype(BF16)
+    order = [*range(plan.owners), *[plan.owners + d for d in plan.order]]
+    order = order[: plan.blocks]
+    mixed = [mixed[b * plan.count : (b + 1) * plan.count, :] for b in order]
+    put_rows(outs, slice(None), jnp.concatenate(mixed, axis=0))
 
 
 def put_rows(outs, columns, rows):
@@ -475,14 +480,13 @@
     return [block] + [plan.over_expert(block, d) for d in range(1, plan.owners)]
 
 
-def sum_pair(plan, parts):
+def sum_pair(plan, parts, order=None):
     own = [[p] for p in parts[: plan.owners]]
-    d = 0
+    order = iter(order or range(plan.owners))
     for piece in parts[plan.owners :]:
         other = plan.over_pair(piece)
         for start in range(0, piece.shape[0], plan.count):
-            own[d].append(other[start : start + plan.count])
-            d += 1
+            own[next(order)].append(other[start : start + plan.count])
     return own
 
 
@@ -597,7 +601,7 @@
     parts, blocks_back = lax.optimization_barrier((parts, blocks_back))
     if plan.split > 1:
         blocks_back = blocks_back + [plan.over_pair(jnp.concatenate(blocks_back))]
-    own = sum_pair(plan, parts)
+    own = sum_pair(plan, parts, plan.order)
     steps = [1 << i for i in range(plan.owners.bit_length() - 1)] if plan.paired else []
     back = send_step(plan, own, 1) if steps else scatter_group(plan, own)
     parts_back = backward(plan, blocks_back, saved, gate, kept, up_hbm, w_down)

time: 61.2 us -> 61.3 us (level)
  waiting for transfers between devices: 8.42 us -> 9.19 us
  starting transfers between devices: 17.8 us -> 17.1 us
    ppermute x11, starting transfers between devices: 16.8 us -> 15.8 us  [over_expert(): return lax.ppermute(x, ('dp', 'expert'), pairs)]
    ppermute x11, waiting for transfers between devices: 6.66 us -> 7.57 us  [over_expert(): return lax.ppermute(x, ('dp', 'expert'), pairs)]
  transfers between devices with their start and end apart: 18 -> 18, of which waited for: 10 -> 9; matrix products, arithmetic and copies ran while one was open for 2% -> 2% of each run, Pallas kernels for 50% -> 50%
where the time goes in v15:
time: 61.3 us; the launch traced here: 61.1 us
  Pallas kernels  32.5 us (53%)
  starting transfers between devices  17.1 us (28%)
  waiting for transfers between devices  9.19 us (15%)
  other arithmetic  1.21 us (2%)
  between operations  0.97 us (2%)
    pallas_call x2, Pallas kernels, expert_call(): pl.pallas_call(kernel, out_shape=shapes, in_specs=[vmem()] * len(inputs)...  24.7 us
    ppermute x11, starting transfers between devices, over_expert(): return lax.ppermute(x, ('dp', 'expert'), pairs)  15.8 us
    ppermute x11, waiting for transfers between devices, over_expert(): return lax.ppermute(x, ('dp', 'expert'), pairs)  7.57 us
    pallas_call x1, Pallas kernels, fetch(): pl.pallas_call(functools.partial(fetch_kernel, plan), out_shape=(pltpu.VM...  4.4 us
    ppermute x7, waiting for transfers between devices, over_pair(): return lax.ppermute(x, 'dp', [(i, i ^ 1) for i in range(self.groups)])  1.62 us
    pallas_call x1, Pallas kernels, prepare(): pl.pallas_call(functools.partial(prepare_kernel, plan), out_shape=out_sha...  1.59 us
    ppermute x7, starting transfers between devices, over_pair(): return lax.ppermute(x, 'dp', [(i, i ^ 1) for i in range(self.groups)])  1.35 us
  transfers between devices with their start and end apart: 18, of which 9 were waited for; matrix products, arithmetic and copies ran while one was open for 2% of the time, Pallas kernels for 50%

profile of v15, /device:TPU:0, one launch (start us, length us, event | category | flops | bytes accessed | tf_op | source)
XLA Modules:
  0.0 61.1 jit_solution(6336714000824953241)
XLA Ops:
  0.6 1.1 %pack.1.after.refs_0_ = bf16[32,2176]{1,0:T(8,128)(2,1)S(1)} custom-call(bf16[32,2048]{1,0:T(8,128)(2,1)} %refs_0_.1, s32[6,32]{1,0:T(8,128)} %bitcast.24, f32[6,32]{1,0:T(8,128)} %bitcast.25), custom_call_target="tpu_custom_call" | custom-call | tf_op jit(solution)/shard_map/pack/pallas_call | solution.py:141
  1.7 3.0 %collective-permute-start = (bf16[32,2176]{1,0:T(8,128)(2,1)S(1)}, bf16[32,2176]{1,0:T(8,128)(2,1)S(1)}, u32[]{:S(2)}, u32[]{:S(2)}) collective-permute-start(bf16[32,2176]{1,0:T(8,128)(2,1)S(1)} %pack.1.after.refs_0_), channel_id=1, source_target_pairs={{1,0},{0,1},{3,2},{2,3},{6,4},{7,5},{4,6},{5,7},{9,8},{8,9},{11,10... | collective-permute-start | bytes 417800 | tf_op jit(solution)/shard_map/ppermute | solution.py:90
  4.7 1.6 %prepare.1 = (bf16[32,2176]{1,0:T(8,128)(2,1)S(1)}, bf16[16,2176]{1,0:T(8,128)(2,1)S(1)}, bf16[2,128,704]{2,1,0:T(8,128)(2,1)S(1)}, bf16[2,128,704]{2,1,0:T(8,128)(2,1)S(1)}) custom-call(bf16[32,2048]{1,0:T(8,128)(2,1)} %x_hbm.1, s32[6,32]{1,0:T(8,128)} %bitcast.17, f32[6,32]{1,0:T(8,128)} %bitcast.26, bf16[224,704]{1,0:T(8,128)(2,1)} %bitcast.22, ...), custom_call_target="tpu_custom_call" | custom-call | bytes 17825792 | tf_op jit(solution)/shard_map/prepare/pallas_call | solution.py:234
  6.4 1.3 %collective-permute-done.after.refs_1_ = bf16[32,2176]{1,0:T(8,128)(2,1)S(1)} collective-permute-done((bf16[32,2176]{1,0:T(8,128)(2,1)S(1)}, bf16[32,2176]{1,0:T(8,128)(2,1)S(1)}, u32[]{:S(2)}, u32[]{:S(2)}) %collective-permute-start) | collective-permute-done | bytes 139296 | tf_op jit(solution)/shard_map/ppermute | solution.py:90
  7.8 2.1 %collective-permute-start.1 = (bf16[64,2176]{1,0:T(8,128)(2,1)S(1)}, bf16[64,2176]{1,0:T(8,128)(2,1)S(1)}, u32[]{:S(2)}, u32[]{:S(2)}) collective-permute-start(bf16[64,2176]{1,0:T(8,128)(2,1)S(1)} %maximum_add_fusion.1), channel_id=1, source_target_pairs={{2,0},{3,1},{0,2},{1,3},{5,4},{4,5},{7,6},{6,7},{10,8},{11,9},{8,1... | collective-permute-start | bytes 835592 | tf_op jit(solution)/shard_map/ppermute | solution.py:90
  9.9 4.4 %fetch.1 = (bf16[4,704,2048]{2,1,0:T(8,128)(2,1)S(1)}, bf16[16,2176]{1,0:T(8,128)(2,1)S(1)}) custom-call(bf16[8,704,2048]{2,1,0:T(8,128)(2,1)} %bitcast.21, bf16[32,2176]{1,0:T(8,128)(2,1)S(1)} %collective-permute-done.after.refs_1_, bf16[2,128,704]{2,1,0:T(8,128)(2,1)S(1)} %collective-permute-done.2.also_after.refs_6_), custom_call_target="tpu_custom_call" | custom-call | bytes 23068672 | tf_op jit(solution)/shard_map/fetch/pallas_call | solution.py:271
  14.6 3.0 %collective-permute-start.6 = (bf16[32,2176]{1,0:T(8,128)(2,1)S(1)}, bf16[32,2176]{1,0:T(8,128)(2,1)S(1)}, u32[]{:S(2)}, u32[]{:S(2)}) collective-permute-start(bf16[32,2176]{1,0:T(8,128)(2,1)S(1)} %get-tuple-element.64.refs_0_), channel_id=1, source_target_pairs={{3,0},{2,1},{1,2},{0,3},{7,4},{6,5},{5,6},{4,7},{11,8},{10,9},{9,1... | collective-permute-start | bytes 417800 | tf_op jit(solution)/shard_map/ppermute | solution.py:90
  18.3 13.1 %forward.1 = (bf16[32,2048]{1,0:T(8,128)(2,1)S(1)}, bf16[32,2048]{1,0:T(8,128)(2,1)S(1)}, bf16[32,2048]{1,0:T(8,128)(2,1)S(1)}, bf16[32,2048]{1,0:T(8,128)(2,1)S...) custom-call(bf16[32,2176]{1,0:T(8,128)(2,1)S(1)} %pack.1.after.refs_0_, ...), custom_call_target="tpu_custom_call" | custom-call | flops 2214592512 | bytes 23068672 | tf_op jit(solution)/shard_map/forward/pallas_call | solution.py:432
  32.1 0.9 %collective-permute-done.9 = bf16[64,2048]{1,0:T(8,128)(2,1)S(1)} collective-permute-done((bf16[64,2048]{1,0:T(8,128)(2,1)S(1)}, bf16[64,2048]{1,0:T(8,128)(2,1)S(1)}, u32[]{:S(2)}, u32[]{:S(2)}) %collective-permute-start.9) | collective-permute-done | bytes 262176 | tf_op jit(solution)/shard_map/ppermute | solution.py:93
  33.1 2.0 %collective-permute-start.10 = (bf16[64,2048]{1,0:T(8,128)(2,1)S(1)}, bf16[64,2048]{1,0:T(8,128)(2,1)S(1)}, u32[]{:S(2)}, u32[]{:S(2)}) collective-permute-start(bf16[64,2048]{1,0:T(8,128)(2,1)S(1)} %pad_maximum_fusion.1), channel_id=1, source_target_pairs={{0,1},{1,0},{2,3},{3,2},{4,6},{5,7},{6,4},{7,5},{8,9},{9,8},{10,11... | collective-permute-start | bytes 786440 | tf_op jit(solution)/shard_map/ppermute | solution.py:90
  35.1 11.6 %backward.1 = (bf16[32,1024]{1,0:T(8,128)(2,1)S(1)}, bf16[32,1024]{1,0:T(8,128)(2,1)S(1)}, bf16[32,1024]{1,0:T(8,128)(2,1)S(1)}, bf16[32,1024]{1,0:T(8,128)(2,1)...) custom-call(bf16[32,2176]{1,0:T(8,128)(2,1)S(1)} %get-tuple-element., ...), custom_call_target="tpu_custom_call" | custom-call | flops 2214592512 | bytes 23068672 | tf_op jit(solution)/shard_map/backward/pallas_call | solution.py:432
  47.3 1.6 %collective-permute-start.13 = (bf16[32,2048]{1,0:T(8,128)(2,1)S(1)}, bf16[32,2048]{1,0:T(8,128)(2,1)S(1)}, u32[]{:S(2)}, u32[]{:S(2)}) collective-permute-start(bf16[32,2048]{1,0:T(8,128)(2,1)S(1)} %add_convert_fusion.1), channel_id=1, source_target_pairs={{0,2},{1,3},{2,0},{3,1},{4,5},{5,4},{6,7},{7,6},{8,10},{9,11},{10,... | collective-permute-start | bytes 393224 | tf_op jit(solution)/shard_map/ppermute | solution.py:90
  48.9 0.8 %collective-permute-start.12 = (bf16[64,1024]{1,0:T(8,128)(2,1)S(1)}, bf16[64,1024]{1,0:T(8,128)(2,1)S(1)}, u32[]{:S(2)}, u32[]{:S(2)}) collective-permute-start(bf16[64,1024]{1,0:T(8,128)(2,1)S(1)} %pad_maximum_fusion.3), channel_id=1, source_target_pairs={{0,1},{1,0},{2,3},{3,2},{4,6},{5,7},{6,4},{7,5},{8,9},{9,8},{10,11... | collective-permute-start | bytes 393224 | tf_op jit(solution)/shard_map/ppermute | solution.py:90
  49.8 0.7 %collective-permute-done.15 = bf16[128,1152]{1,0:T(8,128)(2,1)S(1)} collective-permute-done((bf16[128,1152]{1,0:T(8,128)(2,1)S(1)}, bf16[128,1152]{1,0:T(8,128)(2,1)S(1)}, u32[]{:S(2)}, u32[]{:S(2)}) %collective-permute-start.15) | collective-permute-done | bytes 294944 | tf_op jit(solution)/shard_map/ppermute | solution.py:93
  50.5 0.7 %collective-permute-start.16 = (bf16[64,1152]{1,0:T(8,128)(2,1)S(1)}, bf16[64,1152]{1,0:T(8,128)(2,1)S(1)}, u32[]{:S(2)}, u32[]{:S(2)}) collective-permute-start(bf16[64,1152]{1,0:T(8,128)(2,1)S(1)} %pad_maximum_fusion.2), channel_id=1, source_target_pairs={{0,1},{1,0},{2,3},{3,2},{4,6},{5,7},{6,4},{7,5},{8,9},{9,8},{10,11... | collective-permute-start | bytes 442376 | tf_op jit(solution)/shard_map/ppermute | solution.py:90
  51.2 1.3 %collective-permute-done.13 = bf16[32,2048]{1,0:T(8,128)(2,1)S(1)} collective-permute-done((bf16[32,2048]{1,0:T(8,128)(2,1)S(1)}, bf16[32,2048]{1,0:T(8,128)(2,1)S(1)}, u32[]{:S(2)}, u32[]{:S(2)}) %collective-permute-start.13) | collective-permute-done | bytes 131104 | tf_op jit(solution)/shard_map/ppermute | solution.py:90
  52.5 1.4 %collective-permute-done.12 = bf16[64,1024]{1,0:T(8,128)(2,1)S(1)} collective-permute-done((bf16[64,1024]{1,0:T(8,128)(2,1)S(1)}, bf16[64,1024]{1,0:T(8,128)(2,1)S(1)}, u32[]{:S(2)}, u32[]{:S(2)}) %collective-permute-start.12) | collective-permute-done | bytes 131104 | tf_op jit(solution)/shard_map/ppermute | solution.py:90
  54.0 1.1 %collective-permute-start.14 = (bf16[32,1024]{1,0:T(8,128)(2,1)S(1)}, bf16[32,1024]{1,0:T(8,128)(2,1)S(1)}, u32[]{:S(2)}, u32[]{:S(2)}) collective-permute-start(bf16[32,1024]{1,0:T(8,128)(2,1)S(1)} %add_convert_fusion.7), channel_id=1, source_target_pairs={{0,2},{1,3},{2,0},{3,1},{4,5},{5,4},{6,7},{7,6},{8,10},{9,11},{10,... | collective-permute-start | bytes 196616 | tf_op jit(solution)/shard_map/ppermute | solution.py:90
  55.1 0.6 %collective-permute-done.16 = bf16[64,1152]{1,0:T(8,128)(2,1)S(1)} collective-permute-done((bf16[64,1152]{1,0:T(8,128)(2,1)S(1)}, bf16[64,1152]{1,0:T(8,128)(2,1)S(1)}, u32[]{:S(2)}, u32[]{:S(2)}) %collective-permute-start.16) | collective-permute-done | bytes 147488 | tf_op jit(solution)/shard_map/ppermute | solution.py:90
  55.7 0.9 %collective-permute-start.17 = (bf16[32,1152]{1,0:T(8,128)(2,1)S(1)}, bf16[32,1152]{1,0:T(8,128)(2,1)S(1)}, u32[]{:S(2)}, u32[]{:S(2)}) collective-permute-start(bf16[32,1152]{1,0:T(8,128)(2,1)S(1)} %add_convert_fusion.4), channel_id=1, source_target_pairs={{0,2},{1,3},{2,0},{3,1},{4,5},{5,4},{6,7},{7,6},{8,10},{9,11},{10,... | collective-permute-start | bytes 221192 | tf_op jit(solution)/shard_map/ppermute | solution.py:90
  56.7 0.7 %add_convert_fusion = bf16[32,2048]{1,0:T(8,128)(2,1)} fusion(bf16[32,2048]{1,0:T(8,128)(2,1)S(1)} %collective-permute-done.13, bf16[32,2048]{1,0:T(8,128)(2,1)S(1)} %get-tuple-element.62, bf16[64,2048]{1,0:T(8,128)(2,1)S(1)} %collective-permute-done.7, bf16[64,2048]{1,0:T(8,128)(2,1)S(1)} %collective-permute-done.10), kind=kLoop, calls=%fused_computation.4 | loop fusion | flops 524288 | bytes 655360 | tf_op jit(solution)/shard_map/convert_element_type | solution.py:623
  57.4 0.9 %collective-permute-done.14.refs_3_ = bf16[32,1024]{1,0:T(8,128)(2,1)S(1)} collective-permute-done((bf16[32,1024]{1,0:T(8,128)(2,1)S(1)}, bf16[32,1024]{1,0:T(8,128)(2,1)S(1)}, u32[]{:S(2)}, u32[]{:S(2)}) %collective-permute-start.14) | collective-permute-done | bytes 65568 | tf_op jit(solution)/shard_map/ppermute | solution.py:90
  58.3 1.8 %collective-permute-done.17.refs_7_ = bf16[32,1152]{1,0:T(8,128)(2,1)S(1)} collective-permute-done((bf16[32,1152]{1,0:T(8,128)(2,1)S(1)}, bf16[32,1152]{1,0:T(8,128)(2,1)S(1)}, u32[]{:S(2)}, u32[]{:S(2)}) %collective-permute-start.17) | collective-permute-done | bytes 73760 | tf_op jit(solution)/shard_map/ppermute | solution.py:90
  60.2 0.8 %finish.1 = (bf16[32,2048]{1,0:T(8,128)(2,1)}, f32[6,32]{1,0:T(8,128)}) custom-call(bf16[32,1024]{1,0:T(8,128)(2,1)S(1)} %get-tuple-element.89.refs_0_, bf16[32,1024]{1,0:T(8,128)(2,1)S(1)} %slice.86.refs_1_, bf16[32,1024]{1,0:T(8,128)(2,1)S(1)} %slice.71.refs_2_, bf16[32,1024]{1,0:T(8,128)(2,1)S(1)} %collective-permute-done.14.refs_3_, ...), custom_call_target="tpu_custom_call" | custom-call | tf_op jit(solution)/shard_map/finish/pallas_call | solution.py:547
  (39 shorter events, 2.7 us)
Async XLA Ops:
  1.7 6.0 %collective-permute-start = (bf16[32,2176]{1,0:T(8,128)(2,1)S(1)}, bf16[32,2176]{1,0:T(8,128)(2,1)S(1)}, u32[]{:S(2)}, u32[]{:S(2)}) collective-permute-start(bf16[32,2176]{1,0:T(8,128)(2,1)S(1)} %pack.1.after.refs_0_), channel_id=1, source_target_pairs={{1,0},{0,1},{3,2},{2,3},{6,4},{7,5},{4,6},{5,7},{9,8},{8,9},{11,10... | collective-permute-start | bytes 417800 | tf_op jit(solution)/shard_map/ppermute | solution.py:90
  6.3 3.6 %collective-permute-start.2 = (bf16[2,128,704]{2,1,0:T(8,128)(2,1)S(1)}, bf16[2,128,704]{2,1,0:T(8,128)(2,1)S(1)}, u32[]{:S(2)}, u32[]{:S(2)}) collective-permute-start(bf16[2,128,704]{2,1,0:T(8,128)(2,1)S(1)} %get-tuple-element.52), channel_id=1, source_target_pairs={{0,4},{4,0},{8,12},{12,8},{16,20},{20,16},{24,28},{28,24},{1,5},{5... | collective-permute-start | bytes 1081352 | tf_op jit(solution)/shard_map/ppermute | solution.py:93
  7.8 6.6 %collective-permute-start.1 = (bf16[64,2176]{1,0:T(8,128)(2,1)S(1)}, bf16[64,2176]{1,0:T(8,128)(2,1)S(1)}, u32[]{:S(2)}, u32[]{:S(2)}) collective-permute-start(bf16[64,2176]{1,0:T(8,128)(2,1)S(1)} %maximum_add_fusion.1), channel_id=1, source_target_pairs={{2,0},{3,1},{0,2},{1,3},{5,4},{4,5},{7,6},{6,7},{10,8},{11,9},{8,1... | collective-permute-start | bytes 835592 | tf_op jit(solution)/shard_map/ppermute | solution.py:90
  14.5 3.7 %collective-permute-start.3 = (bf16[128,2176]{1,0:T(8,128)(2,1)S(1)}, bf16[128,2176]{1,0:T(8,128)(2,1)S(1)}, u32[]{:S(2)}, u32[]{:S(2)}) collective-permute-start(bf16[128,2176]{1,0:T(8,128)(2,1)S(1)} %maximum_add_fusion), channel_id=1, source_target_pairs={{0,4},{4,0},{8,12},{12,8},{16,20},{20,16},{24,28},{28,24},{1,5},{5... | collective-permute-start | bytes 1671176 | tf_op jit(solution)/shard_map/ppermute | solution.py:93
  14.6 16.8 %collective-permute-start.6 = (bf16[32,2176]{1,0:T(8,128)(2,1)S(1)}, bf16[32,2176]{1,0:T(8,128)(2,1)S(1)}, u32[]{:S(2)}, u32[]{:S(2)}) collective-permute-start(bf16[32,2176]{1,0:T(8,128)(2,1)S(1)} %get-tuple-element.64.refs_0_), channel_id=1, source_target_pairs={{3,0},{2,1},{1,2},{0,3},{7,4},{6,5},{5,6},{4,7},{11,8},{10,9},{9,1... | collective-permute-start | bytes 417800 | tf_op jit(solution)/shard_map/ppermute | solution.py:90
  17.6 13.8 %collective-permute-start.5 = (bf16[32,2176]{1,0:T(8,128)(2,1)S(1)}, bf16[32,2176]{1,0:T(8,128)(2,1)S(1)}, u32[]{:S(2)}, u32[]{:S(2)}) collective-permute-start(bf16[32,2176]{1,0:T(8,128)(2,1)S(1)} %get-tuple-element.64.refs_0_), channel_id=1, source_target_pairs={{2,0},{3,1},{0,2},{1,3},{5,4},{4,5},{7,6},{6,7},{10,8},{11,9},{8,1... | collective-permute-start | bytes 417800 | tf_op jit(solution)/shard_map/ppermute | solution.py:90
  18.1 13.3 %collective-permute-start.4 = (bf16[32,2176]{1,0:T(8,128)(2,1)S(1)}, bf16[32,2176]{1,0:T(8,128)(2,1)S(1)}, u32[]{:S(2)}, u32[]{:S(2)}) collective-permute-start(bf16[32,2176]{1,0:T(8,128)(2,1)S(1)} %get-tuple-element.64.refs_0_), channel_id=1, source_target_pairs={{1,0},{0,1},{3,2},{2,3},{6,4},{7,5},{4,6},{5,7},{9,8},{8,9},{11,10... | collective-permute-start | bytes 417800 | tf_op jit(solution)/shard_map/ppermute | solution.py:90
  31.4 1.6 %collective-permute-start.9 = (bf16[64,2048]{1,0:T(8,128)(2,1)S(1)}, bf16[64,2048]{1,0:T(8,128)(2,1)S(1)}, u32[]{:S(2)}, u32[]{:S(2)}) collective-permute-start(bf16[64,2048]{1,0:T(8,128)(2,1)S(1)} %get-tuple-element.81), channel_id=1, source_target_pairs={{0,4},{4,0},{8,12},{12,8},{16,20},{20,16},{24,28},{28,24},{1,5},{5... | collective-permute-start | bytes 786440 | tf_op jit(solution)/shard_map/ppermute | solution.py:93
  31.5 3.5 %collective-permute-start.8 = (bf16[128,2176]{1,0:T(8,128)(2,1)S(1)}, bf16[128,2176]{1,0:T(8,128)(2,1)S(1)}, u32[]{:S(2)}, u32[]{:S(2)}) collective-permute-start(bf16[128,2176]{1,0:T(8,128)(2,1)S(1)} %pad_maximum_fusion), channel_id=1, source_target_pairs={{0,4},{4,0},{8,12},{12,8},{16,20},{20,16},{24,28},{28,24},{1,5},{5... | collective-permute-start | bytes 1671176 | tf_op jit(solution)/shard_map/ppermute | solution.py:93
  33.1 13.5 %collective-permute-start.10 = (bf16[64,2048]{1,0:T(8,128)(2,1)S(1)}, bf16[64,2048]{1,0:T(8,128)(2,1)S(1)}, u32[]{:S(2)}, u32[]{:S(2)}) collective-permute-start(bf16[64,2048]{1,0:T(8,128)(2,1)S(1)} %pad_maximum_fusion.1), channel_id=1, source_target_pairs={{0,1},{1,0},{2,3},{3,2},{4,6},{5,7},{6,4},{7,5},{8,9},{9,8},{10,11... | collective-permute-start | bytes 786440 | tf_op jit(solution)/shard_map/ppermute | solution.py:90
  35.1 12.2 %collective-permute-start.7 = (bf16[64,2048]{1,0:T(8,128)(2,1)S(1)}, bf16[64,2048]{1,0:T(8,128)(2,1)S(1)}, u32[]{:S(2)}, u32[]{:S(2)}) collective-permute-start(bf16[64,2048]{1,0:T(8,128)(2,1)S(1)} %get-tuple-element.63), channel_id=1, source_target_pairs={{0,4},{4,0},{8,12},{12,8},{16,20},{20,16},{24,28},{28,24},{1,5},{5... | collective-permute-start | bytes 786440 | tf_op jit(solution)/shard_map/ppermute | solution.py:93
  46.6 2.2 %collective-permute-start.11 = (bf16[128,1024]{1,0:T(8,128)(2,1)S(1)}, bf16[128,1024]{1,0:T(8,128)(2,1)S(1)}, u32[]{:S(2)}, u32[]{:S(2)}) collective-permute-start(bf16[128,1024]{1,0:T(8,128)(2,1)S(1)} %get-tuple-element.85), channel_id=1, source_target_pairs={{0,4},{4,0},{8,12},{12,8},{16,20},{20,16},{24,28},{28,24},{1,5},{5... | collective-permute-start | bytes 786440 | tf_op jit(solution)/shard_map/ppermute | solution.py:93
  47.3 5.2 %collective-permute-start.13 = (bf16[32,2048]{1,0:T(8,128)(2,1)S(1)}, bf16[32,2048]{1,0:T(8,128)(2,1)S(1)}, u32[]{:S(2)}, u32[]{:S(2)}) collective-permute-start(bf16[32,2048]{1,0:T(8,128)(2,1)S(1)} %add_convert_fusion.1), channel_id=1, source_target_pairs={{0,2},{1,3},{2,0},{3,1},{4,5},{5,4},{6,7},{7,6},{8,10},{9,11},{10,... | collective-permute-start | bytes 393224 | tf_op jit(solution)/shard_map/ppermute | solution.py:90
  48.9 1.6 %collective-permute-start.15 = (bf16[128,1152]{1,0:T(8,128)(2,1)S(1)}, bf16[128,1152]{1,0:T(8,128)(2,1)S(1)}, u32[]{:S(2)}, u32[]{:S(2)}) collective-permute-start(bf16[128,1152]{1,0:T(8,128)(2,1)S(1)} %get-tuple-element.93), channel_id=1, source_target_pairs={{0,4},{4,0},{8,12},{12,8},{16,20},{20,16},{24,28},{28,24},{1,5},{5... | collective-permute-start | bytes 884744 | tf_op jit(solution)/shard_map/ppermute | solution.py:93
  48.9 5.0 %collective-permute-start.12 = (bf16[64,1024]{1,0:T(8,128)(2,1)S(1)}, bf16[64,1024]{1,0:T(8,128)(2,1)S(1)}, u32[]{:S(2)}, u32[]{:S(2)}) collective-permute-start(bf16[64,1024]{1,0:T(8,128)(2,1)S(1)} %pad_maximum_fusion.3), channel_id=1, source_target_pairs={{0,1},{1,0},{2,3},{3,2},{4,6},{5,7},{6,4},{7,5},{8,9},{9,8},{10,11... | collective-permute-start | bytes 393224 | tf_op jit(solution)/shard_map/ppermute | solution.py:90
  49.7 10.4 %copy-start = (s32[32,6]{0,1:T(8,128)S(1)}, s32[32,6]{0,1:T(8,128)}, u32[]{:S(2)}) copy-start(s32[32,6]{0,1:T(8,128)} %param.15) | copy-start | bytes 2308
  50.5 5.2 %collective-permute-start.16 = (bf16[64,1152]{1,0:T(8,128)(2,1)S(1)}, bf16[64,1152]{1,0:T(8,128)(2,1)S(1)}, u32[]{:S(2)}, u32[]{:S(2)}) collective-permute-start(bf16[64,1152]{1,0:T(8,128)(2,1)S(1)} %pad_maximum_fusion.2), channel_id=1, source_target_pairs={{0,1},{1,0},{2,3},{3,2},{4,6},{5,7},{6,4},{7,5},{8,9},{9,8},{10,11... | collective-permute-start | bytes 442376 | tf_op jit(solution)/shard_map/ppermute | solution.py:90
  54.0 4.3 %collective-permute-start.14 = (bf16[32,1024]{1,0:T(8,128)(2,1)S(1)}, bf16[32,1024]{1,0:T(8,128)(2,1)S(1)}, u32[]{:S(2)}, u32[]{:S(2)}) collective-permute-start(bf16[32,1024]{1,0:T(8,128)(2,1)S(1)} %add_convert_fusion.7), channel_id=1, source_target_pairs={{0,2},{1,3},{2,0},{3,1},{4,5},{5,4},{6,7},{7,6},{8,10},{9,11},{10,... | collective-permute-start | bytes 196616 | tf_op jit(solution)/shard_map/ppermute | solution.py:90
  55.7 4.4 %collective-permute-start.17 = (bf16[32,1152]{1,0:T(8,128)(2,1)S(1)}, bf16[32,1152]{1,0:T(8,128)(2,1)S(1)}, u32[]{:S(2)}, u32[]{:S(2)}) collective-permute-start(bf16[32,1152]{1,0:T(8,128)(2,1)S(1)} %add_convert_fusion.4), channel_id=1, source_target_pairs={{0,2},{1,3},{2,0},{3,1},{4,5},{5,4},{6,7},{7,6},{8,10},{9,11},{10,... | collective-permute-start | bytes 221192 | tf_op jit(solution)/shard_map/ppermute | solution.py:90
